TPU v7x, 32 devices: a whole 2x2x4 slice. The times are simulated.
32 devices in a mesh: groups: 2 (over y), ctx: 4 (over x, core), head: 4 (over z).
Axes of the slice: x: 2, y: 2, z: 4, core: 2. Of those that a mesh axis runs over, the one named last changes fastest.
Arguments:
- features: bfloat16 [4, 3072, 8192], P('groups', 'ctx', 'head'), parts along dimension 0, may hold values from -6 to 6
- gate_in: bfloat16 [4, 3072, 8192], P('groups', 'ctx', 'head'), parts along dimension 0, may hold values from -240 to 240
- state_proj: bfloat16 [2, 4, 128, 3072], P(None, 'groups', 'head', 'ctx'), parts along dimension 1, may hold values from -3 to 3
- step_size: float32 [4, 128, 3072], P('groups', 'head', 'ctx'), parts along dimension 0, may hold values from 0.01 to 0.1
- log_decay: float32 [4, 128, 3072], P('groups', 'head', 'ctx'), parts along dimension 0, may hold values from -1 to 0
- skip_gain: float32 [128], P('head'), may hold values from 0.5 to 2
- norm_gain: float32 [8192], P('head'), may hold values from 0.5 to 1.5
Outputs:
- output: bfloat16 [4, 3072, 8192], P('groups', 'ctx', 'head'), parts along dimension 0
There are 2 independent parts, one for each index of `groups`. A program takes and returns all parts, laid end to end along the dimension named above; an argument that names none is the same for every part. Nothing has to cross between parts.
All inputs are finite; a program needn't handle non-finite values.
Results may differ from a plain program's by a relative error of at most 0.014.
Values may be sent and summed in bfloat16 or wider, within the bound.
No kernel may reach another device: no remote copies, remote signals or barrier semaphores. Data moves between devices by JAX's collectives and lax.ppermute only.
A program may use at most 128 MiB of HBM per device.

v0:
```python
import jax
import jax.numpy as jnp
from jax import lax
from jax.sharding import PartitionSpec as P

SPAN = 128


def passed_along(shard, axis, by):
    devices = lax.axis_size(axis)
    pairs = [(i, i + by) for i in range(devices) if 0 <= i + by < devices]
    return lax.ppermute(shard, axis, pairs)


def body(features, gate_in, state_proj, step_size, log_decay, skip_gain, norm_gain):
    gathered = lax.all_gather(state_proj, "head", axis=2, tiled=True)
    seq_count, length, channels = features.shape
    head_count = step_size.shape[1]
    head_dim = channels // head_count
    state_dim = gathered.shape[2]
    spans = length // SPAN
    feat_blocks = features.reshape(seq_count, spans, SPAN, head_count, head_dim).transpose(
        1, 0, 3, 2, 4
    )
    b_blocks = gathered[0].reshape(seq_count, state_dim, spans, SPAN).transpose(2, 0, 1, 3)
    c_blocks = gathered[1].reshape(seq_count, state_dim, spans, SPAN).transpose(2, 0, 1, 3)
    step_blocks = step_size.reshape(seq_count, head_count, spans, SPAN).transpose(2, 0, 1, 3)
    decay_blocks = log_decay.reshape(seq_count, head_count, spans, SPAN).transpose(2, 0, 1, 3)
    row_index = lax.broadcasted_iota(jnp.int32, (SPAN, SPAN), 0)
    col_index = lax.broadcasted_iota(jnp.int32, (SPAN, SPAN), 1)
    causal = (row_index >= col_index)[None, None]

    def block_state_of(weighted, b_block, cumulative):
        to_end = jnp.exp(cumulative[..., -1:] - cumulative)
        contrib = (weighted.astype(jnp.float32) * to_end[..., None]).astype(jnp.bfloat16)
        return jnp.einsum("shup,snu->shpn", contrib, b_block, preferred_element_type=jnp.float32)

    def local_terms(carried, pieces):
        feat_block, b_block, c_block, step_block, decay_block = pieces
        cumulative = jnp.cumsum(decay_block, axis=2)
        spread = jnp.where(causal, cumulative[..., :, None] - cumulative[..., None, :], 0.0)
        decay_table = jnp.where(causal, jnp.exp(spread), 0.0)
        affinity = jnp.einsum("snt,snu->stu", c_block, b_block, preferred_element_type=jnp.float32)
        scores = (decay_table * affinity[:, None]).astype(jnp.bfloat16)
        weighted = (feat_block.astype(jnp.float32) * step_block[..., None]).astype(jnp.bfloat16)
        within = jnp.einsum("shtu,shup->shtp", scores, weighted, preferred_element_type=jnp.float32)
        carried = jnp.exp(cumulative[..., -1])[..., None, None] * carried + block_state_of(
            weighted, b_block, cumulative
        )
        return (carried, within)

    initial = jnp.zeros((seq_count, head_count, head_dim, state_dim), jnp.float32)
    local_state, within_blocks = lax.scan(
        local_terms, initial, (feat_blocks, b_blocks, c_blocks, step_blocks, decay_blocks)
    )
    cumulative_all = jnp.cumsum(log_decay, axis=2)
    decay_total = jnp.exp(cumulative_all[:, :, -1])

    def chain_turn(turn_index, incoming):
        return passed_along(
            (decay_total[:, :, None, None] * incoming + local_state).astype(jnp.bfloat16), "ctx", 1
        ).astype(jnp.float32)

    incoming = lax.fori_loop(0, lax.axis_size("ctx") - 1, chain_turn, initial)

    def entering_terms(carried, pieces):
        feat_block, b_block, c_block, step_block, decay_block, within = pieces
        cumulative = jnp.cumsum(decay_block, axis=2)
        entering = carried.astype(jnp.bfloat16)
        carried_in = (
            jnp.einsum("snt,shpn->shtp", c_block, entering, preferred_element_type=jnp.float32)
            * jnp.exp(cumulative)[..., None]
        )
        weighted = (feat_block.astype(jnp.float32) * step_block[..., None]).astype(jnp.bfloat16)
        carried = jnp.exp(cumulative[..., -1])[..., None, None] * carried + block_state_of(
            weighted, b_block, cumulative
        )
        return (carried, within + carried_in)

    _, blocks = lax.scan(
        entering_terms,
        incoming,
        (feat_blocks, b_blocks, c_blocks, step_blocks, decay_blocks, within_blocks),
    )
    mixed = blocks.transpose(1, 0, 3, 2, 4).reshape(seq_count, length, channels)
    skip_wide = jnp.repeat(skip_gain, head_dim)
    mixed = mixed + features.astype(jnp.float32) * skip_wide[None, None, :]
    gated = mixed * jax.nn.silu(gate_in.astype(jnp.float32))
    square_sum = lax.psum(jnp.sum(gated * gated, axis=-1), "head")
    inv_rms = lax.rsqrt(square_sum / (channels * lax.axis_size("head")) + 1e-05)
    return (gated * inv_rms[..., None] * norm_gain[None, None, :]).astype(jnp.bfloat16)


def solution(mesh):
    in_specs = (
        P("groups", "ctx", "head"),
        P("groups", "ctx", "head"),
        P(None, "groups", "head", "ctx"),
        P("groups", "head", "ctx"),
        P("groups", "head", "ctx"),
        P("head"),
        P("head"),
    )
    out_specs = P("groups", "ctx", "head")
    return jax.shard_map(body, mesh=mesh, in_specs=in_specs, out_specs=out_specs, check_vma=False)
```

profile of v0, /device:TPU:2, one launch (start us, length us, event | category | flops | bytes accessed | tf_op | source)
XLA Modules:
  0.0 309.2 jit_solution(11279930924663844956)
XLA Ops:
  0.0 8.7 %copy.54 = bf16[2,768,2048]{1,2,0:T(8,128)(2,1)} copy(bf16[2,768,2048]{2,1,0:T(8,128)(2,1)} %param.13) | data formatting | bytes 12582912 | tf_op args[0]
  8.7 13.7 %reshape.70 = bf16[2,6,128,32,64]{2,1,4,3,0:T(8,128)(2,1)} reshape(bf16[2,768,2048]{1,2,0:T(8,128)(2,1)} %copy.54) | data formatting | bytes 12582912 | tf_op jit(solution)/shard_map/reshape | solution.py:22
  22.4 7.9 %copy.59 = bf16[6,2,32,128,64]{3,4,2,1,0:T(8,128)(2,1)} copy(bf16[6,2,32,128,64]{3,0,4,2,1:T(8,128)(2,1)} %bitcast.119) | data formatting | bytes 12582912
  30.5 19.8 %all_gather.3 = bf16[2,2,128,768]{3,1,0,2:T(2,128)(2,1)S(1)} all-gather(bf16[2,2,32,768]{3,1,0,2:T(2,128)(2,1)S(1)} %copy.55), channel_id=1, replica_groups=mesh['groups'=2,'ctx'=4,'head'=4] {'head'}, dimensions={2}, use_global_device_ids=true | all-gather | bytes 983040 | tf_op jit(solution)/shard_map/all_gather | solution.py:16
  52.3 6.2 %broadcast.25.clone = f32[6,2,32,128,64]{3,4,2,1,0:T(8,128)} broadcast(f32[]{:T(128)} %constant.52.clone.1), dimensions={} | broadcast | bytes 12582916 | tf_op jit(solution)/shard_map/broadcast.3
  58.5 42.1 %while.39 = (s32[]{:T(128)}, f32[2,32,64,128]{3,2,1,0:T(8,128)S(1)}, f32[6,2,32,128,64]{3,4,2,1,0:T(8,128)}, f32[6,2,32,128]{3,2,1,0:T(8,128)S(1)}, bf16[6,2,32,...) while((s32[]{:T(128)}, ...), condition=%wide.region_4.5_spmd.clone.clone, body=%wide.region_2.4_spmd.clone.clone.sunk | while | flops 289423360 | bytes 9311615 | solution.py:53
  59.3 3.9 %bitcast_dynamic-update-slice_fusion.5 = f32[6,2,32,128,64]{3,4,2,1,0:T(8,128)} fusion(f32[6,2,32,128,64]{3,4,2,1,0:T(8,128)} %get-tuple-element.452, s32[]{:T(128)} %get-tuple-element.450, f32[2,128,128]{2,1,0:T(8,128)S(1)} %fusion.74, f32[2,32,128]{2,1,0:T(8,128)S(1)} %reduce_window_sum.41, pred[128,128]{1,0:T(8,128)(4,1)S(1)} %fusion.75, ...), kind=kOutput, calls=%fused_computation.30.clone.1 | convolution fusion | flops 141033472 | bytes 3392512 | tf_op jit(solution)/shard_map/while/body/eval_jaxpr/shtu,shup->shtp/dot_general | solution.py:46
  66.3 3.9 %bitcast_dynamic-update-slice_fusion.5 = f32[6,2,32,128,64]{3,4,2,1,0:T(8,128)} fusion(f32[6,2,32,128,64]{3,4,2,1,0:T(8,128)} %get-tuple-element.452, s32[]{:T(128)} %get-tuple-element.450, f32[2,128,128]{2,1,0:T(8,128)S(1)} %fusion.74, f32[2,32,128]{2,1,0:T(8,128)S(1)} %reduce_window_sum.41, pred[128,128]{1,0:T(8,128)(4,1)S(1)} %fusion.75, ...), kind=kOutput, calls=%fused_computation.30.clone.1 | convolution fusion | flops 141033472 | bytes 3392512 | tf_op jit(solution)/shard_map/while/body/eval_jaxpr/shtu,shup->shtp/dot_general | solution.py:46
  73.3 3.9 %bitcast_dynamic-update-slice_fusion.5 = f32[6,2,32,128,64]{3,4,2,1,0:T(8,128)} fusion(f32[6,2,32,128,64]{3,4,2,1,0:T(8,128)} %get-tuple-element.452, s32[]{:T(128)} %get-tuple-element.450, f32[2,128,128]{2,1,0:T(8,128)S(1)} %fusion.74, f32[2,32,128]{2,1,0:T(8,128)S(1)} %reduce_window_sum.41, pred[128,128]{1,0:T(8,128)(4,1)S(1)} %fusion.75, ...), kind=kOutput, calls=%fused_computation.30.clone.1 | convolution fusion | flops 141033472 | bytes 3392512 | tf_op jit(solution)/shard_map/while/body/eval_jaxpr/shtu,shup->shtp/dot_general | solution.py:46
  80.4 3.9 %bitcast_dynamic-update-slice_fusion.5 = f32[6,2,32,128,64]{3,4,2,1,0:T(8,128)} fusion(f32[6,2,32,128,64]{3,4,2,1,0:T(8,128)} %get-tuple-element.452, s32[]{:T(128)} %get-tuple-element.450, f32[2,128,128]{2,1,0:T(8,128)S(1)} %fusion.74, f32[2,32,128]{2,1,0:T(8,128)S(1)} %reduce_window_sum.41, pred[128,128]{1,0:T(8,128)(4,1)S(1)} %fusion.75, ...), kind=kOutput, calls=%fused_computation.30.clone.1 | convolution fusion | flops 141033472 | bytes 3392512 | tf_op jit(solution)/shard_map/while/body/eval_jaxpr/shtu,shup->shtp/dot_general | solution.py:46
  87.4 3.9 %bitcast_dynamic-update-slice_fusion.5 = f32[6,2,32,128,64]{3,4,2,1,0:T(8,128)} fusion(f32[6,2,32,128,64]{3,4,2,1,0:T(8,128)} %get-tuple-element.452, s32[]{:T(128)} %get-tuple-element.450, f32[2,128,128]{2,1,0:T(8,128)S(1)} %fusion.74, f32[2,32,128]{2,1,0:T(8,128)S(1)} %reduce_window_sum.41, pred[128,128]{1,0:T(8,128)(4,1)S(1)} %fusion.75, ...), kind=kOutput, calls=%fused_computation.30.clone.1 | convolution fusion | flops 141033472 | bytes 3392512 | tf_op jit(solution)/shard_map/while/body/eval_jaxpr/shtu,shup->shtp/dot_general | solution.py:46
  94.4 3.9 %bitcast_dynamic-update-slice_fusion.5 = f32[6,2,32,128,64]{3,4,2,1,0:T(8,128)} fusion(f32[6,2,32,128,64]{3,4,2,1,0:T(8,128)} %get-tuple-element.452, s32[]{:T(128)} %get-tuple-element.450, f32[2,128,128]{2,1,0:T(8,128)S(1)} %fusion.74, f32[2,32,128]{2,1,0:T(8,128)S(1)} %reduce_window_sum.41, pred[128,128]{1,0:T(8,128)(4,1)S(1)} %fusion.75, ...), kind=kOutput, calls=%fused_computation.30.clone.1 | convolution fusion | flops 141033472 | bytes 3392512 | tf_op jit(solution)/shard_map/while/body/eval_jaxpr/shtu,shup->shtp/dot_general | solution.py:46
  102.5 6.3 %reduce-window.6 = f32[2,32,6,128]{3,1,2,0:T(8,128)S(1)} reduce-window(f32[2,32,6,128]{3,1,2,0:T(8,128)} %copy_bitcast_fusion.1, f32[]{:T(128)} %constant.52.clone.1), window={size=1x1x1x128 pad=0_0x0_0x0_0x127_0}, to_apply=%region_0.1 | reduce-window | flops 6242304 | bytes 393220 | tf_op jit(solution)/shard_map/reduce-window
  111.0 58.4 %while.38 = (s32[]{:T(128)}, f32[2,32,64,128]{3,2,1,0:T(8,128)S(1)}, f32[2,32]{1,0:T(2,128)S(1)}, f32[2,32,64,128]{3,2,1,0:T(8,128)}, s32[]{:T(128)}, /*index=5*/s32[]{:T(128)}) while((s32[]{:T(128)}, f32[2,32,64,128]{3,2,1,0:T(8,128)S(1)}, f32[2,32]{1,0:T(2,128)S(1)}, f32[2,32,64,128]{3,2,1,0:T(8,128)}, s32[]{:T(128)}, ...), condition=%wide.region_6.7_spmd.clone, body=%wide.region_5.6_spmd.clone.sunk | while | flops 2621443 | bytes 12583287 | solution.py:64
  115.9 14.4 %collective-permute-done = bf16[2,32,64,128]{3,2,1,0:T(8,128)(2,1)S(1)} collective-permute-done((bf16[2,32,64,128]{3,2,1,0:T(8,128)(2,1)}, bf16[2,32,64,128]{3,2,1,0:T(8,128)(2,1)S(1)}, u32[]{:S(2)}, u32[]{:S(2)}) %collective-permute-start) | collective-permute-done | bytes 1048608 | tf_op jit(solution)/shard_map/while/body/eval_jaxpr/ppermute | solution.py:12
  135.3 14.4 %collective-permute-done = bf16[2,32,64,128]{3,2,1,0:T(8,128)(2,1)S(1)} collective-permute-done((bf16[2,32,64,128]{3,2,1,0:T(8,128)(2,1)}, bf16[2,32,64,128]{3,2,1,0:T(8,128)(2,1)S(1)}, u32[]{:S(2)}, u32[]{:S(2)}) %collective-permute-start) | collective-permute-done | bytes 1048608 | tf_op jit(solution)/shard_map/while/body/eval_jaxpr/ppermute | solution.py:12
  154.8 14.4 %collective-permute-done = bf16[2,32,64,128]{3,2,1,0:T(8,128)(2,1)S(1)} collective-permute-done((bf16[2,32,64,128]{3,2,1,0:T(8,128)(2,1)}, bf16[2,32,64,128]{3,2,1,0:T(8,128)(2,1)S(1)}, u32[]{:S(2)}, u32[]{:S(2)}) %collective-permute-start) | collective-permute-done | bytes 1048608 | tf_op jit(solution)/shard_map/while/body/eval_jaxpr/ppermute | solution.py:12
  169.5 6.2 %broadcast.25 = f32[6,2,32,128,64]{3,4,2,1,0:T(8,128)} broadcast(f32[]{:T(128)} %constant.52.clone.1), dimensions={} | broadcast | bytes 12582916 | tf_op jit(solution)/shard_map/broadcast.3
  175.6 42.6 %while.37 = (s32[]{:T(128)}, f32[2,32,64,128]{3,2,1,0:T(8,128)S(1)}, f32[6,2,32,128,64]{3,4,2,1,0:T(8,128)}, f32[6,2,32,128]{3,2,1,0:T(8,128)}, bf16[6,2,32,128,...) while((s32[]{:T(128)}, ...), condition=%wide.region_9.10_spmd, body=%wide.region_7.9_spmd.sunk | while | flops 275251200 | bytes 12063093 | solution.py:80
  177.3 3.4 %bitcast_dynamic-update-slice_fusion.4 = f32[6,2,32,128,64]{3,4,2,1,0:T(8,128)} fusion(f32[6,2,32,128,64]{3,4,2,1,0:T(8,128)} %get-tuple-element.503, s32[]{:T(128)} %get-tuple-element.501, f32[6,2,32,128,64]{3,4,2,1,0:T(8,128)} %get-tuple-element.519, f32[2,32,128]{2,1,0:T(8,128)S(1)} %get-tuple-element.424, ...), kind=kOutput, calls=%fused_computation.6.clone.1 | convolution fusion | flops 135790592 | bytes 6390784 | tf_op jit(solution)/shard_map/while/body/eval_jaxpr/snt,shpn->shtp/dot_general | solution.py:71
  184.3 3.4 %bitcast_dynamic-update-slice_fusion.4 = f32[6,2,32,128,64]{3,4,2,1,0:T(8,128)} fusion(f32[6,2,32,128,64]{3,4,2,1,0:T(8,128)} %get-tuple-element.503, s32[]{:T(128)} %get-tuple-element.501, f32[6,2,32,128,64]{3,4,2,1,0:T(8,128)} %get-tuple-element.519, f32[2,32,128]{2,1,0:T(8,128)S(1)} %get-tuple-element.424, ...), kind=kOutput, calls=%fused_computation.6.clone.1 | convolution fusion | flops 135790592 | bytes 6390784 | tf_op jit(solution)/shard_map/while/body/eval_jaxpr/snt,shpn->shtp/dot_general | solution.py:71
  191.4 3.4 %bitcast_dynamic-update-slice_fusion.4 = f32[6,2,32,128,64]{3,4,2,1,0:T(8,128)} fusion(f32[6,2,32,128,64]{3,4,2,1,0:T(8,128)} %get-tuple-element.503, s32[]{:T(128)} %get-tuple-element.501, f32[6,2,32,128,64]{3,4,2,1,0:T(8,128)} %get-tuple-element.519, f32[2,32,128]{2,1,0:T(8,128)S(1)} %get-tuple-element.424, ...), kind=kOutput, calls=%fused_computation.6.clone.1 | convolution fusion | flops 135790592 | bytes 6390784 | tf_op jit(solution)/shard_map/while/body/eval_jaxpr/snt,shpn->shtp/dot_general | solution.py:71
  198.5 3.4 %bitcast_dynamic-update-slice_fusion.4 = f32[6,2,32,128,64]{3,4,2,1,0:T(8,128)} fusion(f32[6,2,32,128,64]{3,4,2,1,0:T(8,128)} %get-tuple-element.503, s32[]{:T(128)} %get-tuple-element.501, f32[6,2,32,128,64]{3,4,2,1,0:T(8,128)} %get-tuple-element.519, f32[2,32,128]{2,1,0:T(8,128)S(1)} %get-tuple-element.424, ...), kind=kOutput, calls=%fused_computation.6.clone.1 | convolution fusion | flops 135790592 | bytes 6390784 | tf_op jit(solution)/shard_map/while/body/eval_jaxpr/snt,shpn->shtp/dot_general | solution.py:71
  205.5 3.5 %bitcast_dynamic-update-slice_fusion.4 = f32[6,2,32,128,64]{3,4,2,1,0:T(8,128)} fusion(f32[6,2,32,128,64]{3,4,2,1,0:T(8,128)} %get-tuple-element.503, s32[]{:T(128)} %get-tuple-element.501, f32[6,2,32,128,64]{3,4,2,1,0:T(8,128)} %get-tuple-element.519, f32[2,32,128]{2,1,0:T(8,128)S(1)} %get-tuple-element.424, ...), kind=kOutput, calls=%fused_computation.6.clone.1 | convolution fusion | flops 135790592 | bytes 6390784 | tf_op jit(solution)/shard_map/while/body/eval_jaxpr/snt,shpn->shtp/dot_general | solution.py:71
  212.7 3.4 %bitcast_dynamic-update-slice_fusion.4 = f32[6,2,32,128,64]{3,4,2,1,0:T(8,128)} fusion(f32[6,2,32,128,64]{3,4,2,1,0:T(8,128)} %get-tuple-element.503, s32[]{:T(128)} %get-tuple-element.501, f32[6,2,32,128,64]{3,4,2,1,0:T(8,128)} %get-tuple-element.519, f32[2,32,128]{2,1,0:T(8,128)S(1)} %get-tuple-element.424, ...), kind=kOutput, calls=%fused_computation.6.clone.1 | convolution fusion | flops 135790592 | bytes 6390784 | tf_op jit(solution)/shard_map/while/body/eval_jaxpr/snt,shpn->shtp/dot_general | solution.py:71
  218.3 22.7 %copy.68 = f32[2,6,128,32,64]{2,1,4,3,0:T(8,128)} copy(f32[2,6,128,32,64]{2,4,3,0,1:T(8,128)} %bitcast.118) | data formatting | bytes 25165824 | tf_op jit(solution)/shard_map/transpose | solution.py:85
  241.0 15.9 %reshape.72 = f32[2,768,2048]{1,2,0:T(8,128)} reshape(f32[2,6,128,32,64]{2,1,4,3,0:T(8,128)} %copy.68) | data formatting | bytes 25165824 | tf_op jit(solution)/shard_map/reshape | solution.py:85
  256.9 8.6 %copy.70 = bf16[2,768,2048]{1,2,0:T(8,128)(2,1)} copy(bf16[2,768,2048]{2,1,0:T(8,128)(2,1)} %param.14) | data formatting | bytes 12582912 | tf_op args[1]
  265.6 16.4 %multiply_reduce_fusion = (f32[2,768]{1,0:T(2,128)S(1)}, f32[2,768,2048]{1,2,0:T(8,128)}) fusion(bf16[2,768,2048]{1,2,0:T(8,128)(2,1)} %copy.70, f32[2,768,2048]{1,2,0:T(8,128)} %reshape.72, f32[2048]{0:T(1024)S(1)} %mul.112, bf16[2,768,2048]{1,2,0:T(8,128)(2,1)} %copy.54), kind=kLoop, calls=%fused_computation.64 | loop fusion | flops 34601472 | bytes 37763072 | tf_op jit(solution)/shard_map/reduce_sum | solution.py:89
  282.0 10.2 %psum.7 = f32[2,768]{1,0:T(2,128)S(1)} all-reduce(f32[2,768]{1,0:T(2,128)S(1)} %get-tuple-element.288), channel_id=1, replica_groups=mesh['groups'=2,'ctx'=4,'head'=4] {'head'}, use_global_device_ids=true, to_apply=%region_11.12 | all-reduce | flops 1536 | bytes 12288 | tf_op jit(solution)/shard_map/psum | solution.py:89
  292.2 8.4 %multiply_convert_fusion.8 = bf16[2,768,2048]{1,2,0:T(8,128)(2,1)} fusion(f32[2,768,2048]{1,2,0:T(8,128)} %get-tuple-element.289, f32[2048]{0:T(1024)S(1)} %copy-done.7, f32[2,768]{1,0:T(2,128)S(1)} %add_rsqrt_fusion), kind=kLoop, calls=%fused_computation.63 | loop fusion | flops 9437184 | bytes 18888704 | tf_op jit(solution)/shard_map/convert_element_type | solution.py:91
  300.6 8.6 %copy.71 = bf16[2,768,2048]{2,1,0:T(8,128)(2,1)} copy(bf16[2,768,2048]{1,2,0:T(8,128)(2,1)} %multiply_convert_fusion.8) | data formatting | bytes 12582912 | tf_op jit(solution)/shard_map/convert_element_type | solution.py:91
  (133 shorter events, 61.7 us)
Async XLA Ops:
  22.4 7.9 %copy-start.6 = (bf16[2,2,32,768]{3,2,1,0:T(8,128)(2,1)S(1)}, bf16[2,2,32,768]{3,2,1,0:T(8,128)(2,1)}, u32[]{:S(2)}) copy-start(bf16[2,2,32,768]{3,2,1,0:T(8,128)(2,1)} %param.15) | copy-start | bytes 589828
  30.3 21.8 %copy-start.4 = (f32[2,32,768]{2,1,0:T(8,128)S(1)}, f32[2,32,768]{2,1,0:T(8,128)}, u32[]{:S(2)}) copy-start(f32[2,32,768]{2,1,0:T(8,128)} %param.17) | copy-start | bytes 589828
  30.3 21.9 %copy-start.5 = (f32[2,32,768]{2,1,0:T(8,128)S(1)}, f32[2,32,768]{2,1,0:T(8,128)}, u32[]{:S(2)}) copy-start(f32[2,32,768]{2,1,0:T(8,128)} %param.16) | copy-start | bytes 589828
  100.6 10.2 %copy-start = (f32[2,32,64,128]{3,2,1,0:T(8,128)}, f32[2,32,64,128]{3,2,1,0:T(8,128)S(1)}, u32[]{:S(2)}) copy-start(f32[2,32,64,128]{3,2,1,0:T(8,128)S(1)} %get-tuple-element.475) | copy-start | bytes 6291460
  100.6 10.4 %copy-start.1 = (bf16[6,2,128,128]{2,3,0,1:T(8,128)(2,1)}, bf16[6,2,128,128]{2,3,0,1:T(8,128)(2,1)S(1)}, u32[]{:S(2)}) copy-start(bf16[6,2,128,128]{2,3,0,1:T(8,128)(2,1)S(1)} %get-tuple-element.526) | copy-start | bytes 1179652
  100.6 10.4 %copy-start.2 = (f32[6,2,32,128]{3,2,1,0:T(8,128)}, f32[6,2,32,128]{3,2,1,0:T(8,128)S(1)}, u32[]{:S(2)}) copy-start(f32[6,2,32,128]{3,2,1,0:T(8,128)S(1)} %get-tuple-element.527) | copy-start | bytes 589828
  100.6 10.4 %copy-start.3 = (f32[6,2,32,128]{3,2,1,0:T(8,128)}, f32[6,2,32,128]{3,2,1,0:T(8,128)S(1)}, u32[]{:S(2)}) copy-start(f32[6,2,32,128]{3,2,1,0:T(8,128)S(1)} %get-tuple-element.528) | copy-start | bytes 589828
  113.9 16.3 %collective-permute-start = (bf16[2,32,64,128]{3,2,1,0:T(8,128)(2,1)}, bf16[2,32,64,128]{3,2,1,0:T(8,128)(2,1)S(1)}, u32[]{:S(2)}, u32[]{:S(2)}) collective-permute-start(bf16[2,32,64,128]{3,2,1,0:T(8,128)(2,1)} %fusion.68), channel_id=1, source_target_pairs={{0,4},{4,8},{8,12},{1,5},{5,9},{9,13},{2,6},{6,10},{10,14},{3,7},{... | collective-permute-start | bytes 3145736 | tf_op jit(solution)/shard_map/while/body/eval_jaxpr/ppermute | solution.py:12
  133.4 16.3 %collective-permute-start = (bf16[2,32,64,128]{3,2,1,0:T(8,128)(2,1)}, bf16[2,32,64,128]{3,2,1,0:T(8,128)(2,1)S(1)}, u32[]{:S(2)}, u32[]{:S(2)}) collective-permute-start(bf16[2,32,64,128]{3,2,1,0:T(8,128)(2,1)} %fusion.68), channel_id=1, source_target_pairs={{0,4},{4,8},{8,12},{1,5},{5,9},{9,13},{2,6},{6,10},{10,14},{3,7},{... | collective-permute-start | bytes 3145736 | tf_op jit(solution)/shard_map/while/body/eval_jaxpr/ppermute | solution.py:12
  152.9 16.3 %collective-permute-start = (bf16[2,32,64,128]{3,2,1,0:T(8,128)(2,1)}, bf16[2,32,64,128]{3,2,1,0:T(8,128)(2,1)S(1)}, u32[]{:S(2)}, u32[]{:S(2)}) collective-permute-start(bf16[2,32,64,128]{3,2,1,0:T(8,128)(2,1)} %fusion.68), channel_id=1, source_target_pairs={{0,4},{4,8},{8,12},{1,5},{5,9},{9,13},{2,6},{6,10},{10,14},{3,7},{... | collective-permute-start | bytes 3145736 | tf_op jit(solution)/shard_map/while/body/eval_jaxpr/ppermute | solution.py:12
  256.9 8.6 %copy-start.8 = (f32[32]{0:T(128)S(1)}, f32[32]{0:T(128)}, u32[]{:S(2)}) copy-start(f32[32]{0:T(128)} %param.18) | copy-start | bytes 388
  265.6 26.6 %copy-start.7 = (f32[2048]{0:T(1024)S(1)}, f32[2048]{0:T(1024)}, u32[]{:S(2)}) copy-start(f32[2048]{0:T(1024)} %param.19) | copy-start | bytes 24580
where the time goes:
time: 313 us; the launch traced here: 309 us
  local copies, waits for them, and re-layouts  111 us (35%)
  matrix products  69.1 us (22%)
  other arithmetic  48.8 us (16%)
  waiting for transfers between devices  43.2 us (14%)
  blocking collectives  30 us (10%)
  starting transfers between devices  5.72 us (2%)
    ppermute x3, waiting for transfers between devices, passed_along(): return lax.ppermute(shard, axis, pairs)  43.2 us
    unnamed x27, local copies, waits for them, and re-layouts  26.7 us
    dot_general x12, matrix products, block_state_of(): jnp.einsum('shup,snu->shpn', contrib, b_block, preferred_element_type=jnp...  24.4 us
    dot_general x6, matrix products, local_terms(): jnp.einsum('shtu,shup->shtp', scores, weighted, preferred_element_type=jn...  23.3 us
    transpose x1, local copies, waits for them, and re-layouts, body(): mixed = blocks.transpose(1, 0, 3, 2, 4).reshape(seq_count, length, channels)  22.7 us
    dot_general x6, matrix products, entering_terms(): jnp.einsum('snt,shpn->shtp', c_block, entering, preferred_element_type=jn...  20.5 us
    all_gather x1, blocking collectives, body(): gathered = lax.all_gather(state_proj, 'head', axis=2, tiled=True)  19.8 us
    reduce_sum x1, other arithmetic, body(): square_sum = lax.psum(jnp.sum(gated * gated, axis=-1), 'head')  16.4 us
  transfers between devices with their start and end apart: 3, of which 3 were waited for; matrix products, arithmetic and copies ran while one was open for 0% of the time, Pallas kernels for 0%

commit v1 on v0

v1 whole, which is shorter than its diff:
```python
import functools

import jax
import jax.numpy as jnp
from jax import lax
from jax.experimental import pallas as pl
from jax.experimental.pallas import tpu as pltpu
from jax.sharding import PartitionSpec as P

SPAN = 128
CHUNK = 256
F32 = jnp.float32
BF16 = jnp.bfloat16
VMEM_LIMIT = 40 * 1024 * 1024


def mm(a, b):
    return jnp.dot(a, b, preferred_element_type=F32)


def mm_t(a, b):
    return lax.dot_general(a, b, (((0,), (0,)), ((), ())), preferred_element_type=F32)


def split2(v):
    high = v.astype(BF16)
    low = (v - high.astype(F32)).astype(BF16)
    return jnp.concatenate([high, low], axis=0)


def exact_dot(a, b):
    return jnp.dot(a, b, precision=lax.Precision.HIGHEST, preferred_element_type=F32)


def iotas(shape):
    return (
        lax.broadcasted_iota(jnp.int32, shape, 0),
        lax.broadcasted_iota(jnp.int32, shape, 1),
    )


def widen(column, spread32):
    return jnp.sum(spread32 * column, axis=0, keepdims=True)


def to_end_kernel(x_ref, step_ref, decay_ref, spread_ref, contrib_ref, total_ref):
    block = pl.program_id(1)
    heads, length = decay_ref.shape[1:]
    channels = x_ref.shape[2]
    decay = decay_ref[0]
    start = pl.multiple_of(block * SPAN, SPAN)
    here = decay_ref[0, :, pl.ds(start, SPAN)]
    step = step_ref[0, :, pl.ds(start, SPAN)]
    row, col = iotas((SPAN, SPAN))
    after = jnp.where(row > col, 1.0, 0.0).astype(F32)
    _, position = iotas((heads, length))
    later = jnp.sum(jnp.where(position >= start + SPAN, decay, 0.0), axis=1, keepdims=True)
    scale = split2(step * jnp.exp(exact_dot(here, after) + later))
    for lo in range(0, channels, CHUNK):
        sl = slice(lo, lo + CHUNK)
        wide = mm_t(scale, spread_ref[:, sl])
        contrib_ref[0, :, sl] = (x_ref[0, :, sl].astype(F32) * wide).astype(BF16)

    @pl.when(block == 0)
    def _():
        total = jnp.exp(jnp.sum(decay, axis=1, keepdims=True))
        total_ref[0] = widen(total, spread_ref[:heads, :].astype(F32))


def to_end(features, step_size, log_decay, spread):
    seqs, length, channels = features.shape
    heads = step_size.shape[1]
    blocks = length // SPAN
    whole = pl.BlockSpec((1, heads, length), lambda s, k: (s, 0, 0))
    tile = pl.BlockSpec((1, SPAN, channels), lambda s, k: (s, k, 0))
    return pl.pallas_call(
        to_end_kernel,
        grid=(seqs, blocks),
        in_specs=[tile, whole, whole, pl.BlockSpec(spread.shape, lambda s, k: (0, 0))],
        out_specs=[tile, pl.BlockSpec((1, 1, channels), lambda s, k: (s, 0, 0))],
        out_shape=[
            jax.ShapeDtypeStruct(features.shape, BF16),
            jax.ShapeDtypeStruct((seqs, 1, channels), F32),
        ],
        compiler_params=pltpu.CompilerParams(vmem_limit_bytes=VMEM_LIMIT),
        cost_estimate=pl.CostEstimate(
            flops=2 * seqs * length * channels * 64,
            bytes_accessed=4 * seqs * length * channels,
            transcendentals=0,
        ),
        name="contrib_to_end",
    )(features, step_size, log_decay, spread)


def state_kernel(b_ref, contrib_ref, state_ref):
    state_ref[...] = mm(b_ref[...], contrib_ref[0]).astype(BF16)


def end_state(b, contrib, seq):
    states, length = b.shape
    channels = contrib.shape[2]
    width = min(512, channels)
    return pl.pallas_call(
        state_kernel,
        grid=(channels // width,),
        in_specs=[
            pl.BlockSpec((states, length), lambda j: (0, 0)),
            pl.BlockSpec((1, length, width), lambda j: (seq, 0, j)),
        ],
        out_specs=pl.BlockSpec((states, width), lambda j: (0, j)),
        out_shape=jax.ShapeDtypeStruct((states, channels), BF16),
        compiler_params=pltpu.CompilerParams(vmem_limit_bytes=VMEM_LIMIT),
        cost_estimate=pl.CostEstimate(
            flops=2 * length * channels * states,
            bytes_accessed=2 * length * channels,
            transcendentals=0,
        ),
        name="own_end_state",
    )(b, contrib)


def local_kernel(
    x_ref, gate_ref, b_ref, c_ref, step_ref, decay_ref, spread_ref, skip_ref,
    own_ref, factor_ref, state,
):
    block = pl.program_id(0)
    heads, length = decay_ref.shape[1:]
    channels = x_ref.shape[2]

    @pl.when(block == 0)
    def _():
        state[...] = jnp.zeros_like(state)

    start = pl.multiple_of(block * SPAN, SPAN)
    decay = decay_ref[0]
    here = decay_ref[0, :, pl.ds(start, SPAN)]
    step = step_ref[0, :, pl.ds(start, SPAN)]
    row, col = iotas((SPAN, SPAN))
    _, lane = iotas((heads, SPAN))
    _, position = iotas((heads, length))
    until = jnp.where(row <= col, 1.0, 0.0).astype(F32)
    summed = exact_dot(here, until)
    middle = jnp.sum(jnp.where(lane < SPAN // 2, here, 0.0), axis=1, keepdims=True)
    last = jnp.sum(here, axis=1, keepdims=True)
    before = jnp.sum(jnp.where(position < start, decay, 0.0), axis=1, keepdims=True)
    rise = split2(jnp.exp(summed - middle))
    fall = split2(step * jnp.exp(middle - summed))
    spread32 = spread_ref[:heads, :].astype(F32)
    enter_row = widen(jnp.exp(middle), spread32)
    leave_row = widen(jnp.exp(last - middle), spread32)
    first_row = widen(jnp.exp(middle + before), spread32)

    b = b_ref[...]
    c_t = c_ref[...].T
    affinity = mm(c_t, b)
    masked = jnp.where(row >= col, affinity, 0.0).astype(BF16)
    left = jnp.concatenate([masked, c_t], axis=1)
    for lo in range(0, channels, CHUNK):
        sl = slice(lo, lo + CHUNK)
        spread = spread_ref[:, sl]
        x = x_ref[0, :, sl].astype(F32)
        weighted = (x * mm_t(fall, spread)).astype(BF16)
        entering = enter_row[:, sl] * state[:, sl]
        mixed = mm(left, jnp.concatenate([weighted, entering.astype(BF16)], axis=0))
        state[:, sl] = leave_row[:, sl] * (entering + mm(b, weighted))
        wide = mm_t(rise, spread)
        half = 0.5 * gate_ref[0, :, sl].astype(F32)
        gate = half * jnp.tanh(half) + half
        own_ref[:, sl] = ((wide * mixed + skip_ref[:, sl] * x) * gate).astype(BF16)
        factor_ref[:, sl] = (wide * first_row[:, sl] * gate).astype(BF16)


def local_terms(features, gate_in, b, c, step_size, log_decay, spread, skip_row, seq):
    _, length, channels = features.shape
    heads = step_size.shape[1]
    states = b.shape[0]
    whole = pl.BlockSpec((1, heads, length), lambda k: (seq, 0, 0))
    tile = pl.BlockSpec((1, SPAN, channels), lambda k: (seq, k, 0))
    span = pl.BlockSpec((states, SPAN), lambda k: (0, k))
    out = pl.BlockSpec((SPAN, channels), lambda k: (k, 0))
    return pl.pallas_call(
        local_kernel,
        grid=(length // SPAN,),
        in_specs=[
            tile, tile, span, span, whole, whole,
            pl.BlockSpec(spread.shape, lambda k: (0, 0)),
            pl.BlockSpec(skip_row.shape, lambda k: (0, 0)),
        ],
        out_specs=[out, out],
        out_shape=[jax.ShapeDtypeStruct((length, channels), BF16)] * 2,
        scratch_shapes=[pltpu.VMEM((states, channels), F32)],
        compiler_params=pltpu.CompilerParams(vmem_limit_bytes=VMEM_LIMIT),
        cost_estimate=pl.CostEstimate(
            flops=2 * length * channels * 512,
            bytes_accessed=8 * length * channels,
            transcendentals=length * channels,
        ),
        name="local_terms",
    )(features, gate_in, b, c, step_size, log_decay, spread, skip_row)


def joined_kernel(own_ref, factor_ref, c_ref, incoming_ref, gated_ref, square_ref):
    channels = own_ref.shape[1]
    c_t = c_ref[...].T
    squares = jnp.zeros((SPAN, 128), F32)
    for lo in range(0, channels, CHUNK):
        sl = slice(lo, lo + CHUNK)
        carried = mm(c_t, incoming_ref[:, sl])
        gated = own_ref[:, sl].astype(F32) + factor_ref[:, sl].astype(F32) * carried
        gated_ref[:, sl] = gated.astype(BF16)
        power = gated * gated
        for at in range(0, CHUNK, 128):
            squares = squares + power[:, at:at + 128]
    square_ref[0] = jnp.sum(squares.T, axis=0, keepdims=True)


def joined(own, factor, c, incoming):
    length, channels = own.shape
    states = c.shape[0]
    blocks = length // SPAN
    tile = pl.BlockSpec((SPAN, channels), lambda k: (k, 0))
    return pl.pallas_call(
        joined_kernel,
        grid=(blocks,),
        in_specs=[
            tile, tile,
            pl.BlockSpec((states, SPAN), lambda k: (0, k)),
            pl.BlockSpec((states, channels), lambda k: (0, 0)),
        ],
        out_specs=[tile, pl.BlockSpec((1, 1, SPAN), lambda k: (k, 0, 0))],
        out_shape=[
            jax.ShapeDtypeStruct((length, channels), BF16),
            jax.ShapeDtypeStruct((blocks, 1, SPAN), F32),
        ],
        compiler_params=pltpu.CompilerParams(vmem_limit_bytes=VMEM_LIMIT),
        cost_estimate=pl.CostEstimate(
            flops=2 * length * channels * states,
            bytes_accessed=6 * length * channels,
            transcendentals=0,
        ),
        name="joined",
    )(own, factor, c, incoming)


def norm_kernel(all_channels, *refs):
    gated_refs, square_ref, gain_ref, out_ref = refs[:-3], refs[-3], refs[-2], refs[-1]
    channels = out_ref.shape[2]
    seq = pl.program_id(0)
    total = jnp.sum(square_ref[:, 0, 0], axis=0)
    inverse = lax.rsqrt(total / all_channels + 1e-05)
    column = jnp.broadcast_to(inverse, (128, SPAN)).T
    for number, gated_ref in enumerate(gated_refs):

        @pl.when(seq == number)
        def _():
            for lo in range(0, channels, 128):
                sl = slice(lo, lo + 128)
                out_ref[0, :, sl] = (
                    gated_ref[:, sl].astype(F32) * column * gain_ref[:, sl]
                ).astype(BF16)


def normed(gated, squares, gain_row, all_channels):
    length, channels = gated[0].shape
    seqs = len(gated)
    shards = squares.shape[0]

    def tile_of(number):
        last = length // SPAN - 1
        return pl.BlockSpec(
            (SPAN, channels),
            lambda s, k: (jnp.where(s == number, k, jnp.where(s < number, 0, last)), 0),
        )

    return pl.pallas_call(
        functools.partial(norm_kernel, all_channels),
        grid=(seqs, length // SPAN),
        in_specs=[tile_of(number) for number in range(seqs)] + [
            pl.BlockSpec((shards, 1, 1, 1, SPAN), lambda s, k: (0, s, k, 0, 0)),
            pl.BlockSpec(gain_row.shape, lambda s, k: (0, 0)),
        ],
        out_specs=pl.BlockSpec((1, SPAN, channels), lambda s, k: (s, k, 0)),
        out_shape=jax.ShapeDtypeStruct((seqs, length, channels), BF16),
        compiler_params=pltpu.CompilerParams(vmem_limit_bytes=VMEM_LIMIT),
        cost_estimate=pl.CostEstimate(
            flops=2 * seqs * length * channels,
            bytes_accessed=4 * seqs * length * channels,
            transcendentals=0,
        ),
        name="normed",
    )(*gated, squares, gain_row)


def from_all(shard, axis):
    devices = lax.axis_size(axis)
    return [shard] + [
        lax.ppermute(shard, axis, [(i, (i + by) % devices) for i in range(devices)])
        for by in range(1, devices)
    ]


def body(features, gate_in, state_proj, step_size, log_decay, skip_gain, norm_gain):
    seqs, length, channels = features.shape
    heads = step_size.shape[1]
    head_dim = channels // heads
    spread = jnp.repeat(jnp.eye(heads, dtype=BF16), head_dim, axis=1)
    spread = jnp.concatenate([spread, spread], axis=0)
    skip_row = jnp.repeat(skip_gain, head_dim)[None, :]
    gain_row = norm_gain[None, :]

    b = [jnp.concatenate(p, axis=0) for p in zip(*[
        [piece[s] for s in range(seqs)] for piece in from_all(state_proj[0], "head")
    ])]
    c = [jnp.concatenate(p, axis=0) for p in zip(*[
        [piece[s] for s in range(seqs)] for piece in from_all(state_proj[1], "head")
    ])]
    contrib, total = to_end(features, step_size, log_decay, spread)
    own_state = [end_state(b[s], contrib, s) for s in range(seqs)]
    locals_ = [
        local_terms(features, gate_in, b[s], c[s], step_size, log_decay, spread, skip_row, s)
        for s in range(seqs)
    ]
    sent = list(own_state)
    incoming = [None] * seqs
    devices = lax.axis_size("ctx")
    for turn in range(devices - 1):
        for s in range(seqs):
            received = lax.ppermute(sent[s], "ctx", [(turn, turn + 1)])
            incoming[s] = received if incoming[s] is None else incoming[s] + received
            sent[s] = (
                own_state[s].astype(F32) + total[s] * incoming[s].astype(F32)
            ).astype(BF16)
    pairs = [joined(*locals_[s], c[s], incoming[s]) for s in range(seqs)]
    squares = [jnp.stack(from_all(pairs[s][1], "head")) for s in range(seqs)]
    squares = jnp.stack(squares, axis=1)
    return normed(
        [pairs[s][0] for s in range(seqs)], squares, gain_row,
        channels * lax.axis_size("head"),
    )


def solution(mesh):
    in_specs = (
        P("groups", "ctx", "head"),
        P("groups", "ctx", "head"),
        P(None, "groups", "head", "ctx"),
        P("groups", "head", "ctx"),
        P("groups", "head", "ctx"),
        P("head"),
        P("head"),
    )
    out_specs = P("groups", "ctx", "head")
    return jax.shard_map(body, mesh=mesh, in_specs=in_specs, out_specs=out_specs, check_vma=False)
```

time: 313 us -> 110 us (0.35)
  the two profiles are of different devices: /device:TPU:2 before, /device:TPU:14 now
where the time goes in v1:
time: 110 us
  Pallas kernels  50.1 us (46%)
  starting transfers between devices  25.1 us (23%)
  local copies, waits for them, and re-layouts  15.8 us (14%)
  waiting for transfers between devices  15.1 us (14%)
  other arithmetic  3.13 us (3%)
    pallas_call x2, Pallas kernels, local_terms(): pl.pallas_call(local_kernel, grid=(length // SPAN,), in_specs=[tile, tile...  27.4 us
    ppermute x12, starting transfers between devices, from_all(): lax.ppermute(shard, axis, [(i, (i + by) % devices) for i in range(devices)])  17.3 us
    unnamed x31, local copies, waits for them, and re-layouts  14.2 us
    ppermute x6, waiting for transfers between devices, body(): received = lax.ppermute(sent[s], 'ctx', [(turn, turn + 1)])  11.5 us
    ppermute x6, starting transfers between devices, body(): received = lax.ppermute(sent[s], 'ctx', [(turn, turn + 1)])  7.8 us
    pallas_call x1, Pallas kernels, to_end(): pl.pallas_call(to_end_kernel, grid=(seqs, blocks), in_specs=[tile, whole,...  7.15 us
    pallas_call x1, Pallas kernels, normed(): pl.pallas_call(functools.partial(norm_kernel, all_channels), grid=(seqs,...  6.7 us
    pallas_call x2, Pallas kernels, joined(): pl.pallas_call(joined_kernel, grid=(blocks,), in_specs=[tile, tile, pl.Bl...  6.05 us
  transfers between devices with their start and end apart: 18, of which 4 were waited for; matrix products, arithmetic and copies ran while one was open for 3% of the time, Pallas kernels for 40%

profile of v1, /device:TPU:14, one launch (start us, length us, event | category | flops | bytes accessed | tf_op | source)
XLA Modules:
  0.0 109.8 jit_solution(16476936302895333278)
XLA Ops:
  0.0 1.0 slice_bitcast_fusion
  1.0 1.6 %collective-permute-start = (bf16[2,32,768]{2,1,0:T(8,128)(2,1)S(1)}, bf16[2,32,768]{2,1,0:T(8,128)(2,1)S(1)}, u32[]{:S(2)}, u32[]{:S(2)}) collective-permute-start(bf16[2,32,768]{2,1,0:T(8,128)(2,1)S(1)} %get-tuple-element.34), channel_id=1, source_target_pairs={{0,1},{1,2},{2,3},{3,0},{4,5},{5,6},{6,7},{7,4},{8,9},{9,10},{10,1... | collective-permute-start | bytes 294920 | tf_op jit(solution)/shard_map/ppermute | solution.py:297
  2.6 1.2 %collective-permute-start.1 = (bf16[2,32,768]{2,1,0:T(8,128)(2,1)S(1)}, bf16[2,32,768]{2,1,0:T(8,128)(2,1)S(1)}, u32[]{:S(2)}, u32[]{:S(2)}) collective-permute-start(bf16[2,32,768]{2,1,0:T(8,128)(2,1)S(1)} %get-tuple-element.34), channel_id=1, source_target_pairs={{0,2},{1,3},{2,0},{3,1},{4,6},{5,7},{6,4},{7,5},{8,10},{9,11},{10,... | collective-permute-start | bytes 294920 | tf_op jit(solution)/shard_map/ppermute | solution.py:297
  3.8 1.8 %collective-permute-start.2 = (bf16[2,32,768]{2,1,0:T(8,128)(2,1)S(1)}, bf16[2,32,768]{2,1,0:T(8,128)(2,1)S(1)}, u32[]{:S(2)}, u32[]{:S(2)}) collective-permute-start(bf16[2,32,768]{2,1,0:T(8,128)(2,1)S(1)} %get-tuple-element.34), channel_id=1, source_target_pairs={{0,3},{1,0},{2,1},{3,2},{4,7},{5,4},{6,5},{7,6},{8,11},{9,8},{10,9... | collective-permute-start | bytes 294920 | tf_op jit(solution)/shard_map/ppermute | solution.py:297
  5.8 3.5 %collective-permute-start.4 = (bf16[2,32,768]{2,1,0:T(8,128)(2,1)S(1)}, bf16[2,32,768]{2,1,0:T(8,128)(2,1)S(1)}, u32[]{:S(2)}, u32[]{:S(2)}) collective-permute-start(bf16[2,32,768]{2,1,0:T(8,128)(2,1)S(1)} %get-tuple-element.33), channel_id=1, source_target_pairs={{0,2},{1,3},{2,0},{3,1},{4,6},{5,7},{6,4},{7,5},{8,10},{9,11},{10,... | collective-permute-start | bytes 294920 | tf_op jit(solution)/shard_map/ppermute | solution.py:297
  9.9 2.8 %copy-done = bf16[2,768,2048]{2,1,0:T(8,128)(2,1)S(1)} copy-done((bf16[2,768,2048]{2,1,0:T(8,128)(2,1)S(1)}, bf16[2,768,2048]{2,1,0:T(8,128)(2,1)}, u32[]{:S(2)}) %copy-start) | copy-done | bytes 6291480
  14.5 7.1 %contrib_to_end.1 = (bf16[2,768,2048]{2,1,0:T(8,128)(2,1)S(1)}, f32[2,1,2048]{2,1,0:T(1,128)S(1)}) custom-call(bf16[2,768,2048]{2,1,0:T(8,128)(2,1)S(1)} %copy-done, f32[2,32,768]{2,1,0:T(8,128)S(1)} %copy-done.6, f32[2,32,768]{2,1,0:T(8,128)S(1)} %copy-done.8, bf16[64,2048]{1,0:T(8,128)(2,1)S(1)} %constant_dynamic-update-slice_fusion.spread_ref), custom_call_target="tpu_custom_call" | custom-call | flops 402653184 | bytes 12582912 | tf_op jit(solution)/shard_map/contrib_to_end/pallas_call | solution.py:76
  21.7 2.7 %copy-done.1 = bf16[2,768,2048]{2,1,0:T(8,128)(2,1)} copy-done((bf16[2,768,2048]{2,1,0:T(8,128)(2,1)}, bf16[2,768,2048]{2,1,0:T(8,128)(2,1)S(1)}, u32[]{:S(2)}) %copy-start.1) | copy-done | bytes 6291480
  24.7 2.8 %copy-done.2 = bf16[2,768,2048]{2,1,0:T(8,128)(2,1)S(1)} copy-done((bf16[2,768,2048]{2,1,0:T(8,128)(2,1)S(1)}, bf16[2,768,2048]{2,1,0:T(8,128)(2,1)}, u32[]{:S(2)}) %copy-start.2) | copy-done | bytes 6291480
  27.5 1.4 %own_end_state.2 = bf16[128,2048]{1,0:T(8,128)(2,1)S(1)} custom-call(bf16[128,768]{1,0:T(8,128)(2,1)S(1)} %pad_maximum_fusion.b_ref, bf16[2,768,2048]{2,1,0:T(8,128)(2,1)S(1)} %copy-done.2), custom_call_target="tpu_custom_call" | custom-call | flops 402653184 | bytes 3145728 | tf_op jit(solution)/shard_map/own_end_state/pallas_call | solution.py:103
  30.3 1.4 %own_end_state.3 = bf16[128,2048]{1,0:T(8,128)(2,1)S(1)} custom-call(bf16[128,768]{1,0:T(8,128)(2,1)S(1)} %pad_maximum_fusion.2.b_ref, bf16[2,768,2048]{2,1,0:T(8,128)(2,1)S(1)} %copy-done.3), custom_call_target="tpu_custom_call" | custom-call | flops 402653184 | bytes 3145728 | tf_op jit(solution)/shard_map/own_end_state/pallas_call | solution.py:103
  32.7 1.4 %collective-permute-start.7 = (bf16[128,2048]{1,0:T(8,128)(2,1)S(1)}, bf16[128,2048]{1,0:T(8,128)(2,1)S(1)}, u32[]{:S(2)}, u32[]{:S(2)}) collective-permute-start(bf16[128,2048]{1,0:T(8,128)(2,1)S(1)} %fusion), channel_id=1, source_target_pairs={{4,8},{5,9},{6,10},{7,11},{20,24},{21,25},{22,26},{23,27}} | collective-permute-start | bytes 1572872 | tf_op jit(solution)/shard_map/ppermute | solution.py:328
  34.3 1.4 %collective-permute-start.10 = (bf16[128,2048]{1,0:T(8,128)(2,1)S(1)}, bf16[128,2048]{1,0:T(8,128)(2,1)S(1)}, u32[]{:S(2)}, u32[]{:S(2)}) collective-permute-start(bf16[128,2048]{1,0:T(8,128)(2,1)S(1)} %fusion.2), channel_id=1, source_target_pairs={{4,8},{5,9},{6,10},{7,11},{20,24},{21,25},{22,26},{23,27}} | collective-permute-start | bytes 1572872 | tf_op jit(solution)/shard_map/ppermute | solution.py:328
  35.8 7.5 %collective-permute-done.7 = bf16[128,2048]{1,0:T(8,128)(2,1)S(1)} collective-permute-done((bf16[128,2048]{1,0:T(8,128)(2,1)S(1)}, bf16[128,2048]{1,0:T(8,128)(2,1)S(1)}, u32[]{:S(2)}, u32[]{:S(2)}) %collective-permute-start.7) | collective-permute-done | bytes 524320 | tf_op jit(solution)/shard_map/ppermute | solution.py:328
  43.6 1.3 %collective-permute-start.8 = (bf16[128,2048]{1,0:T(8,128)(2,1)S(1)}, bf16[128,2048]{1,0:T(8,128)(2,1)S(1)}, u32[]{:S(2)}, u32[]{:S(2)}) collective-permute-start(bf16[128,2048]{1,0:T(8,128)(2,1)S(1)} %get-tuple-element.27), channel_id=1, source_target_pairs={{8,12},{9,13},{10,14},{11,15},{24,28},{25,29},{26,30},{27,31}} | collective-permute-start | bytes 1572872 | tf_op jit(solution)/shard_map/ppermute | solution.py:328
  45.0 4.0 %collective-permute-done.10 = bf16[128,2048]{1,0:T(8,128)(2,1)S(1)} collective-permute-done((bf16[128,2048]{1,0:T(8,128)(2,1)S(1)}, bf16[128,2048]{1,0:T(8,128)(2,1)S(1)}, u32[]{:S(2)}, u32[]{:S(2)}) %collective-permute-start.10) | collective-permute-done | bytes 524320 | tf_op jit(solution)/shard_map/ppermute | solution.py:328
  48.9 1.1 fusion.3
  50.0 2.1 %collective-permute-start.11 = (bf16[128,2048]{1,0:T(8,128)(2,1)}, bf16[128,2048]{1,0:T(8,128)(2,1)}, u32[]{:S(2)}, u32[]{:S(2)}) collective-permute-start(bf16[128,2048]{1,0:T(8,128)(2,1)} %get-tuple-element.25), channel_id=1, source_target_pairs={{8,12},{9,13},{10,14},{11,15},{24,28},{25,29},{26,30},{27,31}} | collective-permute-start | bytes 1572872 | tf_op jit(solution)/shard_map/ppermute | solution.py:328
  52.2 13.7 %local_terms.2 = (bf16[768,2048]{1,0:T(8,128)(2,1)S(1)}, bf16[768,2048]{1,0:T(8,128)(2,1)S(1)}) custom-call(bf16[2,768,2048]{2,1,0:T(8,128)(2,1)S(1)} %bitcast.52, bf16[2,768,2048]{2,1,0:T(8,128)(2,1)} %gate_ref.3, bf16[128,768]{1,0:T(8,128)(2,1)S(1)} %pad_maximum_fusion.b_ref, bf16[128,768]{1,0:T(8,128)(2,1)S(1)} %pad_maximum_fusion.1.c_ref, ...), custom_call_target="tpu_custom_call" | custom-call | flops 1610612736 | bytes 12582912 | tf_op jit(solution)/shard_map/local_terms/pallas_call | solution.py:181
  65.9 1.7 %copy-done.4 = bf16[768,2048]{1,0:T(8,128)(2,1)} copy-done((bf16[768,2048]{1,0:T(8,128)(2,1)}, bf16[768,2048]{1,0:T(8,128)(2,1)S(1)}, u32[]{:S(2)}) %copy-start.4) | copy-done | bytes 3145752
  67.6 13.7 %local_terms.3 = (bf16[768,2048]{1,0:T(8,128)(2,1)S(1)}, bf16[768,2048]{1,0:T(8,128)(2,1)S(1)}) custom-call(bf16[2,768,2048]{2,1,0:T(8,128)(2,1)S(1)} %bitcast.52, bf16[2,768,2048]{2,1,0:T(8,128)(2,1)} %gate_ref.3, bf16[128,768]{1,0:T(8,128)(2,1)S(1)} %pad_maximum_fusion.2.b_ref, bf16[128,768]{1,0:T(8,128)(2,1)S(1)} %pad_maximum_fusion.3.c_ref, ...), custom_call_target="tpu_custom_call" | custom-call | flops 1610612736 | bytes 12582912 | tf_op jit(solution)/shard_map/local_terms/pallas_call | solution.py:181
  81.4 1.9 %copy-done.5 = bf16[768,2048]{1,0:T(8,128)(2,1)S(1)} copy-done((bf16[768,2048]{1,0:T(8,128)(2,1)S(1)}, bf16[768,2048]{1,0:T(8,128)(2,1)}, u32[]{:S(2)}) %copy-start.5) | copy-done | bytes 3145752
  83.3 3.0 %joined.2 = (bf16[768,2048]{1,0:T(8,128)(2,1)S(1)}, f32[6,1,128]{2,1,0:T(1,128)S(1)}) custom-call(bf16[768,2048]{1,0:T(8,128)(2,1)S(1)} %get-tuple-element.15.own_ref, bf16[768,2048]{1,0:T(8,128)(2,1)S(1)} %copy-done.5, bf16[128,768]{1,0:T(8,128)(2,1)S(1)} %pad_maximum_fusion.1.c_ref, bf16[128,2048]{1,0:T(8,128)(2,1)S(1)} %add.27.incoming_ref), custom_call_target="tpu_custom_call" | custom-call | flops 402653184 | bytes 9437184 | tf_op jit(solution)/shard_map/joined/pallas_call | solution.py:222
  86.3 2.1 %collective-permute-start.12 = (f32[6,1,128]{2,1,0:T(1,128)S(1)}, f32[6,1,128]{2,1,0:T(1,128)S(1)}, u32[]{:S(2)}, u32[]{:S(2)}) collective-permute-start(f32[6,1,128]{2,1,0:T(1,128)S(1)} %get-tuple-element.23), channel_id=1, source_target_pairs={{0,1},{1,2},{2,3},{3,0},{4,5},{5,6},{6,7},{7,4},{8,9},{9,10},{10,1... | collective-permute-start | bytes 9224 | tf_op jit(solution)/shard_map/ppermute | solution.py:297
  88.3 1.8 %collective-permute-start.13 = (f32[6,1,128]{2,1,0:T(1,128)S(1)}, f32[6,1,128]{2,1,0:T(1,128)S(1)}, u32[]{:S(2)}, u32[]{:S(2)}) collective-permute-start(f32[6,1,128]{2,1,0:T(1,128)S(1)} %get-tuple-element.23), channel_id=1, source_target_pairs={{0,2},{1,3},{2,0},{3,1},{4,6},{5,7},{6,4},{7,5},{8,10},{9,11},{10,... | collective-permute-start | bytes 9224 | tf_op jit(solution)/shard_map/ppermute | solution.py:297
  90.1 1.2 %add.31.incoming_ref = bf16[128,2048]{1,0:T(8,128)(2,1)S(1)} add(bf16[128,2048]{1,0:T(8,128)(2,1)S(1)} %get-tuple-element.26, bf16[128,2048]{1,0:T(8,128)(2,1)} %collective-permute-done.11) | non-fusion elementwise | flops 262144 | bytes 1572864 | tf_op jit(solution)/shard_map/add | solution.py:329
  91.3 3.1 %joined.3 = (bf16[768,2048]{1,0:T(8,128)(2,1)S(1)}, f32[6,1,128]{2,1,0:T(1,128)S(1)}) custom-call(bf16[768,2048]{1,0:T(8,128)(2,1)S(1)} %get-tuple-element.20.own_ref, bf16[768,2048]{1,0:T(8,128)(2,1)S(1)} %get-tuple-element.21.factor_ref, bf16[128,768]{1,0:T(8,128)(2,1)S(1)} %pad_maximum_fusion.3.c_ref, bf16[128,2048]{1,0:T(8,128)(2,1)S(1)} %add.31.incoming_ref), custom_call_target="tpu_custom_call" | custom-call | flops 402653184 | bytes 9437184 | tf_op jit(solution)/shard_map/joined/pallas_call | solution.py:222
  94.4 2.1 %collective-permute-start.15 = (f32[6,1,128]{2,1,0:T(1,128)S(1)}, f32[6,1,128]{2,1,0:T(1,128)S(1)}, u32[]{:S(2)}, u32[]{:S(2)}) collective-permute-start(f32[6,1,128]{2,1,0:T(1,128)S(1)} %get-tuple-element.24), channel_id=1, source_target_pairs={{0,1},{1,2},{2,3},{3,0},{4,5},{5,6},{6,7},{7,4},{8,9},{9,10},{10,1... | collective-permute-start | bytes 9224 | tf_op jit(solution)/shard_map/ppermute | solution.py:297
  96.5 2.9 %collective-permute-start.16 = (f32[6,1,128]{2,1,0:T(1,128)S(1)}, f32[6,1,128]{2,1,0:T(1,128)S(1)}, u32[]{:S(2)}, u32[]{:S(2)}) collective-permute-start(f32[6,1,128]{2,1,0:T(1,128)S(1)} %get-tuple-element.24), channel_id=1, source_target_pairs={{0,2},{1,3},{2,0},{3,1},{4,6},{5,7},{6,4},{7,5},{8,10},{9,11},{10,... | collective-permute-start | bytes 9224 | tf_op jit(solution)/shard_map/ppermute | solution.py:297
  99.5 1.5 %collective-permute-done.16 = f32[6,1,128]{2,1,0:T(1,128)S(1)} collective-permute-done((f32[6,1,128]{2,1,0:T(1,128)S(1)}, f32[6,1,128]{2,1,0:T(1,128)S(1)}, u32[]{:S(2)}, u32[]{:S(2)}) %collective-permute-start.16) | collective-permute-done | bytes 3104 | tf_op jit(solution)/shard_map/ppermute | solution.py:297
  101.0 2.0 %collective-permute-done.17 = f32[6,1,128]{2,1,0:T(1,128)S(1)} collective-permute-done((f32[6,1,128]{2,1,0:T(1,128)S(1)}, f32[6,1,128]{2,1,0:T(1,128)S(1)}, u32[]{:S(2)}, u32[]{:S(2)}) %collective-permute-start.17) | collective-permute-done | bytes 3104 | tf_op jit(solution)/shard_map/ppermute | solution.py:297
  103.1 6.7 %normed.1 = bf16[2,768,2048]{2,1,0:T(8,128)(2,1)} custom-call(bf16[768,2048]{1,0:T(8,128)(2,1)S(1)} %get-tuple-element.19.refs_0_, bf16[768,2048]{1,0:T(8,128)(2,1)S(1)} %get-tuple-element.22.refs_1_, f32[4,2,6,1,128]{4,3,2,1,0:T(1,128)S(1)} %pad_maximum_fusion.4.refs_2_, f32[1,2048]{1,0:T(1,128)S(1)} %bitcast.53), custom_call_target="tpu_custom_call" | custom-call | flops 6291456 | bytes 12582912 | tf_op jit(solution)/shard_map/normed/pallas_call | solution.py:275
  (72 shorter events, 5.8 us)
Async XLA Ops:
  1.0 23.6 %collective-permute-start = (bf16[2,32,768]{2,1,0:T(8,128)(2,1)S(1)}, bf16[2,32,768]{2,1,0:T(8,128)(2,1)S(1)}, u32[]{:S(2)}, u32[]{:S(2)}) collective-permute-start(bf16[2,32,768]{2,1,0:T(8,128)(2,1)S(1)} %get-tuple-element.34), channel_id=1, source_target_pairs={{0,1},{1,2},{2,3},{3,0},{4,5},{5,6},{6,7},{7,4},{8,9},{9,10},{10,1... | collective-permute-start | bytes 294920 | tf_op jit(solution)/shard_map/ppermute | solution.py:297
  2.6 22.1 %collective-permute-start.1 = (bf16[2,32,768]{2,1,0:T(8,128)(2,1)S(1)}, bf16[2,32,768]{2,1,0:T(8,128)(2,1)S(1)}, u32[]{:S(2)}, u32[]{:S(2)}) collective-permute-start(bf16[2,32,768]{2,1,0:T(8,128)(2,1)S(1)} %get-tuple-element.34), channel_id=1, source_target_pairs={{0,2},{1,3},{2,0},{3,1},{4,6},{5,7},{6,4},{7,5},{8,10},{9,11},{10,... | collective-permute-start | bytes 294920 | tf_op jit(solution)/shard_map/ppermute | solution.py:297
  3.8 20.9 %collective-permute-start.2 = (bf16[2,32,768]{2,1,0:T(8,128)(2,1)S(1)}, bf16[2,32,768]{2,1,0:T(8,128)(2,1)S(1)}, u32[]{:S(2)}, u32[]{:S(2)}) collective-permute-start(bf16[2,32,768]{2,1,0:T(8,128)(2,1)S(1)} %get-tuple-element.34), channel_id=1, source_target_pairs={{0,3},{1,0},{2,1},{3,2},{4,7},{5,4},{6,5},{7,6},{8,11},{9,8},{10,9... | collective-permute-start | bytes 294920 | tf_op jit(solution)/shard_map/ppermute | solution.py:297
  5.6 26.8 %collective-permute-start.3 = (bf16[2,32,768]{2,1,0:T(8,128)(2,1)S(1)}, bf16[2,32,768]{2,1,0:T(8,128)(2,1)S(1)}, u32[]{:S(2)}, u32[]{:S(2)}) collective-permute-start(bf16[2,32,768]{2,1,0:T(8,128)(2,1)S(1)} %get-tuple-element.33), channel_id=1, source_target_pairs={{0,1},{1,2},{2,3},{3,0},{4,5},{5,6},{6,7},{7,4},{8,9},{9,10},{10,1... | collective-permute-start | bytes 294920 | tf_op jit(solution)/shard_map/ppermute | solution.py:297
  5.8 26.6 %collective-permute-start.4 = (bf16[2,32,768]{2,1,0:T(8,128)(2,1)S(1)}, bf16[2,32,768]{2,1,0:T(8,128)(2,1)S(1)}, u32[]{:S(2)}, u32[]{:S(2)}) collective-permute-start(bf16[2,32,768]{2,1,0:T(8,128)(2,1)S(1)} %get-tuple-element.33), channel_id=1, source_target_pairs={{0,2},{1,3},{2,0},{3,1},{4,6},{5,7},{6,4},{7,5},{8,10},{9,11},{10,... | collective-permute-start | bytes 294920 | tf_op jit(solution)/shard_map/ppermute | solution.py:297
  9.9 2.8 %copy-start = (bf16[2,768,2048]{2,1,0:T(8,128)(2,1)S(1)}, bf16[2,768,2048]{2,1,0:T(8,128)(2,1)}, u32[]{:S(2)}) copy-start(bf16[2,768,2048]{2,1,0:T(8,128)(2,1)} %x_ref.5) | copy-start | bytes 18874372
  12.6 0.9 copy-start.6
  14.5 9.9 %copy-start.11 = (bf16[2,2,32,768]{3,2,1,0:T(8,128)(2,1)S(1)}, bf16[2,2,32,768]{3,2,1,0:T(8,128)(2,1)}, u32[]{:S(2)}) copy-start(bf16[2,2,32,768]{3,2,1,0:T(8,128)(2,1)} %param.9) | copy-start | bytes 589828
  14.5 9.9 %copy-start.12 = (f32[32]{0:T(128)S(1)}, f32[32]{0:T(128)}, u32[]{:S(2)}) copy-start(f32[32]{0:T(128)} %param.12) | copy-start | bytes 388
  21.7 2.7 %copy-start.1 = (bf16[2,768,2048]{2,1,0:T(8,128)(2,1)}, bf16[2,768,2048]{2,1,0:T(8,128)(2,1)S(1)}, u32[]{:S(2)}) copy-start(bf16[2,768,2048]{2,1,0:T(8,128)(2,1)S(1)} %get-tuple-element.17.contrib_ref) | copy-start | bytes 18874372
  24.6 11.2 %collective-permute-start.5 = (bf16[2,32,768]{2,1,0:T(8,128)(2,1)S(1)}, bf16[2,32,768]{2,1,0:T(8,128)(2,1)S(1)}, u32[]{:S(2)}, u32[]{:S(2)}) collective-permute-start(bf16[2,32,768]{2,1,0:T(8,128)(2,1)S(1)} %get-tuple-element.33), channel_id=1, source_target_pairs={{0,3},{1,0},{2,1},{3,2},{4,7},{5,4},{6,5},{7,6},{8,11},{9,8},{10,9... | collective-permute-start | bytes 294920 | tf_op jit(solution)/shard_map/ppermute | solution.py:297
  24.7 2.8 %copy-start.2 = (bf16[2,768,2048]{2,1,0:T(8,128)(2,1)S(1)}, bf16[2,768,2048]{2,1,0:T(8,128)(2,1)}, u32[]{:S(2)}) copy-start(bf16[2,768,2048]{2,1,0:T(8,128)(2,1)} %copy-done.1) | copy-start | bytes 18874372
  27.5 2.8 %copy-start.3 = (bf16[2,768,2048]{2,1,0:T(8,128)(2,1)S(1)}, bf16[2,768,2048]{2,1,0:T(8,128)(2,1)}, u32[]{:S(2)}) copy-start(bf16[2,768,2048]{2,1,0:T(8,128)(2,1)} %copy-done.1) | copy-start | bytes 18874372
  29.0 3.5 %collective-permute-start.6 = (bf16[128,2048]{1,0:T(8,128)(2,1)S(1)}, bf16[128,2048]{1,0:T(8,128)(2,1)S(1)}, u32[]{:S(2)}, u32[]{:S(2)}) collective-permute-start(bf16[128,2048]{1,0:T(8,128)(2,1)S(1)} %own_end_state.2), channel_id=1, source_target_pairs={{0,4},{1,5},{2,6},{3,7},{16,20},{17,21},{18,22},{19,23}} | collective-permute-start | bytes 1572872 | tf_op jit(solution)/shard_map/ppermute | solution.py:328
  30.3 21.9 %slice-start = ((s8[6291456]{0:T(1024)(128)(4,1)}), s8[4194304]{0:T(1024)(128)(4,1)S(1)}, s32[]{:S(2)}) async-start(s8[6291456]{0:T(1024)(128)(4,1)} %bitcast.51), calls=%async_computation | async-start | bytes 8388608
  31.7 2.4 %collective-permute-start.9 = (bf16[128,2048]{1,0:T(8,128)(2,1)S(1)}, bf16[128,2048]{1,0:T(8,128)(2,1)S(1)}, u32[]{:S(2)}, u32[]{:S(2)}) collective-permute-start(bf16[128,2048]{1,0:T(8,128)(2,1)S(1)} %own_end_state.3), channel_id=1, source_target_pairs={{0,4},{1,5},{2,6},{3,7},{16,20},{17,21},{18,22},{19,23}} | collective-permute-start | bytes 1572872 | tf_op jit(solution)/shard_map/ppermute | solution.py:328
  32.5 19.7 %slice-start.1 = ((s8[6291456]{0:T(1024)(128)(4,1)}), s8[2097152]{0:T(1024)(128)(4,1)S(1)}, s32[]{:S(2)}) async-start(s8[6291456]{0:T(1024)(128)(4,1)} %bitcast.51), calls=%async_computation.1 | async-start | bytes 4194304
  32.7 10.6 %collective-permute-start.7 = (bf16[128,2048]{1,0:T(8,128)(2,1)S(1)}, bf16[128,2048]{1,0:T(8,128)(2,1)S(1)}, u32[]{:S(2)}, u32[]{:S(2)}) collective-permute-start(bf16[128,2048]{1,0:T(8,128)(2,1)S(1)} %fusion), channel_id=1, source_target_pairs={{4,8},{5,9},{6,10},{7,11},{20,24},{21,25},{22,26},{23,27}} | collective-permute-start | bytes 1572872 | tf_op jit(solution)/shard_map/ppermute | solution.py:328
  34.3 17.9 %copy-start.7 = (f32[2,32,768]{2,1,0:T(8,128)S(1)}, f32[2,32,768]{2,1,0:T(8,128)}, u32[]{:S(2)}) copy-start(f32[2,32,768]{2,1,0:T(8,128)} %step_ref.5) | copy-start | bytes 589828
  34.3 17.9 %copy-start.9 = (f32[2,32,768]{2,1,0:T(8,128)S(1)}, f32[2,32,768]{2,1,0:T(8,128)}, u32[]{:S(2)}) copy-start(f32[2,32,768]{2,1,0:T(8,128)} %decay_ref.5) | copy-start | bytes 589828
  34.3 14.6 %collective-permute-start.10 = (bf16[128,2048]{1,0:T(8,128)(2,1)S(1)}, bf16[128,2048]{1,0:T(8,128)(2,1)S(1)}, u32[]{:S(2)}, u32[]{:S(2)}) collective-permute-start(bf16[128,2048]{1,0:T(8,128)(2,1)S(1)} %fusion.2), channel_id=1, source_target_pairs={{4,8},{5,9},{6,10},{7,11},{20,24},{21,25},{22,26},{23,27}} | collective-permute-start | bytes 1572872 | tf_op jit(solution)/shard_map/ppermute | solution.py:328
  43.6 37.6 %collective-permute-start.8 = (bf16[128,2048]{1,0:T(8,128)(2,1)S(1)}, bf16[128,2048]{1,0:T(8,128)(2,1)S(1)}, u32[]{:S(2)}, u32[]{:S(2)}) collective-permute-start(bf16[128,2048]{1,0:T(8,128)(2,1)S(1)} %get-tuple-element.27), channel_id=1, source_target_pairs={{8,12},{9,13},{10,14},{11,15},{24,28},{25,29},{26,30},{27,31}} | collective-permute-start | bytes 1572872 | tf_op jit(solution)/shard_map/ppermute | solution.py:328
  50.0 40.1 %collective-permute-start.11 = (bf16[128,2048]{1,0:T(8,128)(2,1)}, bf16[128,2048]{1,0:T(8,128)(2,1)}, u32[]{:S(2)}, u32[]{:S(2)}) collective-permute-start(bf16[128,2048]{1,0:T(8,128)(2,1)} %get-tuple-element.25), channel_id=1, source_target_pairs={{8,12},{9,13},{10,14},{11,15},{24,28},{25,29},{26,30},{27,31}} | collective-permute-start | bytes 1572872 | tf_op jit(solution)/shard_map/ppermute | solution.py:328
  65.9 1.7 %copy-start.4 = (bf16[768,2048]{1,0:T(8,128)(2,1)}, bf16[768,2048]{1,0:T(8,128)(2,1)S(1)}, u32[]{:S(2)}) copy-start(bf16[768,2048]{1,0:T(8,128)(2,1)S(1)} %get-tuple-element.16.factor_ref) | copy-start | bytes 9437188
  81.4 1.9 %copy-start.5 = (bf16[768,2048]{1,0:T(8,128)(2,1)S(1)}, bf16[768,2048]{1,0:T(8,128)(2,1)}, u32[]{:S(2)}) copy-start(bf16[768,2048]{1,0:T(8,128)(2,1)} %copy-done.4) | copy-start | bytes 9437188
  86.3 13.1 %collective-permute-start.12 = (f32[6,1,128]{2,1,0:T(1,128)S(1)}, f32[6,1,128]{2,1,0:T(1,128)S(1)}, u32[]{:S(2)}, u32[]{:S(2)}) collective-permute-start(f32[6,1,128]{2,1,0:T(1,128)S(1)} %get-tuple-element.23), channel_id=1, source_target_pairs={{0,1},{1,2},{2,3},{3,0},{4,5},{5,6},{6,7},{7,4},{8,9},{9,10},{10,1... | collective-permute-start | bytes 9224 | tf_op jit(solution)/shard_map/ppermute | solution.py:297
  88.3 11.1 %collective-permute-start.13 = (f32[6,1,128]{2,1,0:T(1,128)S(1)}, f32[6,1,128]{2,1,0:T(1,128)S(1)}, u32[]{:S(2)}, u32[]{:S(2)}) collective-permute-start(f32[6,1,128]{2,1,0:T(1,128)S(1)} %get-tuple-element.23), channel_id=1, source_target_pairs={{0,2},{1,3},{2,0},{3,1},{4,6},{5,7},{6,4},{7,5},{8,10},{9,11},{10,... | collective-permute-start | bytes 9224 | tf_op jit(solution)/shard_map/ppermute | solution.py:297
  90.1 9.3 %collective-permute-start.14 = (f32[6,1,128]{2,1,0:T(1,128)S(1)}, f32[6,1,128]{2,1,0:T(1,128)S(1)}, u32[]{:S(2)}, u32[]{:S(2)}) collective-permute-start(f32[6,1,128]{2,1,0:T(1,128)S(1)} %get-tuple-element.23), channel_id=1, source_target_pairs={{0,3},{1,0},{2,1},{3,2},{4,7},{5,4},{6,5},{7,6},{8,11},{9,8},{10,9... | collective-permute-start | bytes 9224 | tf_op jit(solution)/shard_map/ppermute | solution.py:297
  91.3 11.8 %copy-start.10 = (f32[2048]{0:T(1024)S(1)}, f32[2048]{0:T(1024)}, u32[]{:S(2)}) copy-start(f32[2048]{0:T(1024)} %param.13) | copy-start | bytes 24580
  94.4 5.1 %collective-permute-start.15 = (f32[6,1,128]{2,1,0:T(1,128)S(1)}, f32[6,1,128]{2,1,0:T(1,128)S(1)}, u32[]{:S(2)}, u32[]{:S(2)}) collective-permute-start(f32[6,1,128]{2,1,0:T(1,128)S(1)} %get-tuple-element.24), channel_id=1, source_target_pairs={{0,1},{1,2},{2,3},{3,0},{4,5},{5,6},{6,7},{7,4},{8,9},{9,10},{10,1... | collective-permute-start | bytes 9224 | tf_op jit(solution)/shard_map/ppermute | solution.py:297
  96.5 4.5 %collective-permute-start.16 = (f32[6,1,128]{2,1,0:T(1,128)S(1)}, f32[6,1,128]{2,1,0:T(1,128)S(1)}, u32[]{:S(2)}, u32[]{:S(2)}) collective-permute-start(f32[6,1,128]{2,1,0:T(1,128)S(1)} %get-tuple-element.24), channel_id=1, source_target_pairs={{0,2},{1,3},{2,0},{3,1},{4,6},{5,7},{6,4},{7,5},{8,10},{9,11},{10,... | collective-permute-start | bytes 9224 | tf_op jit(solution)/shard_map/ppermute | solution.py:297
  99.4 3.6 %collective-permute-start.17 = (f32[6,1,128]{2,1,0:T(1,128)S(1)}, f32[6,1,128]{2,1,0:T(1,128)S(1)}, u32[]{:S(2)}, u32[]{:S(2)}) collective-permute-start(f32[6,1,128]{2,1,0:T(1,128)S(1)} %get-tuple-element.24), channel_id=1, source_target_pairs={{0,3},{1,0},{2,1},{3,2},{4,7},{5,4},{6,5},{7,6},{8,11},{9,8},{10,9... | collective-permute-start | bytes 9224 | tf_op jit(solution)/shard_map/ppermute | solution.py:297
  (1 other events, 0.9 us)

commit v2 on v1

v2 whole, which is shorter than its diff:
```python
import functools

import jax
import jax.numpy as jnp
import numpy as np
from jax import lax
from jax.experimental import pallas as pl
from jax.experimental.pallas import tpu as pltpu
from jax.sharding import PartitionSpec as P

SPAN = 128
HALF = 256
F32 = jnp.float32
BF16 = jnp.bfloat16
VMEM_LIMIT = 20 * 1024 * 1024
PARAMS = pltpu.CompilerParams(vmem_limit_bytes=VMEM_LIMIT)
ENTER, LEAVE, FIRST, REST, TOTAL = range(5)


def mm(a, b):
    return jnp.dot(a, b, preferred_element_type=F32)


def exact_dot(a, b):
    return jnp.dot(a, b, precision=lax.Precision.HIGHEST, preferred_element_type=F32)


def iotas(shape):
    return (
        lax.broadcasted_iota(jnp.int32, shape, 0),
        lax.broadcasted_iota(jnp.int32, shape, 1),
    )


def two_parts(v):
    high = v.astype(BF16).astype(F32)
    return [high, v - high]


def upright(parts):
    return jnp.concatenate(parts, axis=0).T.astype(BF16)


def tables_kernel(step_ref, decay_ref, spread_ref, scale_ref, both_ref, rows_ref):
    seqs, heads, length = decay_ref.shape
    blocks = length // SPAN
    at, lane = iotas((length, SPAN))
    kind, block = lane // blocks, lane % blocks
    first, mid, end = block * SPAN, block * SPAN + SPAN // 2, block * SPAN + SPAN
    chosen = (
        ((kind == ENTER) & (at >= first) & (at < mid))
        | ((kind == LEAVE) & (at >= mid) & (at < end))
        | ((kind == FIRST) & (at < mid))
        | ((kind == REST) & (at >= first))
        | (kind == TOTAL)
    )
    chosen = jnp.where(chosen, 1.0, 0.0).astype(F32)
    row, col = iotas((SPAN, SPAN))
    until = jnp.where(row <= col, 1.0, 0.0).astype(F32)
    for s in range(seqs):
        exponent = exact_dot(decay_ref[s], chosen)
        per_block = upright(two_parts(jnp.exp(exponent)))
        rows_ref[s] = mm(per_block, spread_ref[...])[: rows_ref.shape[1]]
        for k in range(blocks):
            sl = slice(k * SPAN, (k + 1) * SPAN)
            step = step_ref[s, :, sl]
            summed = exact_dot(decay_ref[s, :, sl], until)
            middle = exponent[:, ENTER * blocks + k:ENTER * blocks + k + 1]
            rest = exponent[:, REST * blocks + k:REST * blocks + k + 1]
            scale = step * jnp.exp(rest - summed)
            rise = jnp.exp(summed - middle)
            fall = step * jnp.exp(middle - summed)
            scale_ref[s, sl, :] = upright(two_parts(scale))
            both_ref[s, sl, :] = upright(two_parts(rise) + two_parts(fall))


def tables(step_size, log_decay, spread):
    seqs, heads, length = log_decay.shape
    channels = spread.shape[1]
    return pl.pallas_call(
        tables_kernel,
        out_shape=[
            jax.ShapeDtypeStruct((seqs, length, 2 * heads), BF16),
            jax.ShapeDtypeStruct((seqs, length, 4 * heads), BF16),
            jax.ShapeDtypeStruct((seqs, 32, channels), F32),
        ],
        compiler_params=PARAMS,
        name="tables",
    )(step_size, log_decay, spread)


def contrib_kernel(x_ref, scale_ref, spread_ref, contrib_ref):
    length, width = x_ref.shape[1:]
    for k in range(length // SPAN):
        rows = slice(k * SPAN, (k + 1) * SPAN)
        scale = scale_ref[0, rows, :]
        for lo in range(0, width, HALF):
            sl = slice(lo, lo + HALF)
            wide = mm(scale, spread_ref[:, sl]).astype(BF16)
            contrib_ref[0, rows, sl] = x_ref[0, rows, sl] * wide


def contributions(features, scale, spread):
    seqs, length, channels = features.shape
    width = min(512, channels)
    tile = pl.BlockSpec((1, length, width), lambda s, j: (s, 0, j))
    return pl.pallas_call(
        contrib_kernel,
        grid=(seqs, channels // width),
        in_specs=[
            tile,
            pl.BlockSpec((1,) + scale.shape[1:], lambda s, j: (s, 0, 0)),
            pl.BlockSpec((spread.shape[0], width), lambda s, j: (0, j)),
        ],
        out_specs=tile,
        out_shape=jax.ShapeDtypeStruct(features.shape, BF16),
        compiler_params=PARAMS,
        cost_estimate=pl.CostEstimate(
            flops=2 * seqs * length * channels * 64,
            bytes_accessed=4 * seqs * length * channels,
            transcendentals=0,
        ),
        name="contributions",
    )(features, scale, spread)


def state_kernel(b_ref, contrib_ref, state_ref):
    state_ref[...] = mm(b_ref[...], contrib_ref[0]).astype(BF16)


def end_state(b, contrib, seq):
    states, length = b.shape
    channels = contrib.shape[2]
    width = min(512, channels)
    return pl.pallas_call(
        state_kernel,
        grid=(channels // width,),
        in_specs=[
            pl.BlockSpec((states, length), lambda j: (0, 0)),
            pl.BlockSpec((1, length, width), lambda j: (seq, 0, j)),
        ],
        out_specs=pl.BlockSpec((states, width), lambda j: (0, j)),
        out_shape=jax.ShapeDtypeStruct((states, channels), BF16),
        compiler_params=PARAMS,
        cost_estimate=pl.CostEstimate(
            flops=2 * length * channels * states,
            bytes_accessed=2 * length * channels,
            transcendentals=0,
        ),
        name="own_end_state",
    )(b, contrib)


def local_kernel(
    x_ref, gate_ref, b_ref, c_ref, both_ref, rise_ref, fall_ref, rows_ref, skip_ref,
    own_ref, factor_ref, left,
):
    length, width = x_ref.shape[1:]
    blocks = length // SPAN

    @pl.when(pl.program_id(0) == 0)
    def _():
        row, col = iotas((SPAN, SPAN))
        for k in range(blocks):
            sl = slice(k * SPAN, (k + 1) * SPAN)
            c_t = c_ref[:, sl].T
            affinity = mm(c_t, b_ref[:, sl])
            left[k, :, :SPAN] = jnp.where(row >= col, affinity, 0.0).astype(BF16)
            left[k, :, SPAN:] = c_t

    halves = [slice(lo, lo + HALF) for lo in range(0, width, HALF)]
    states = [None] * len(halves)
    for k in range(blocks):
        rows = slice(k * SPAN, (k + 1) * SPAN)
        both = both_ref[0, rows, :]

        def row_of(kind, sl):
            at = kind * blocks + k
            return rows_ref[0, at:at + 1, sl]

        for number, sl in enumerate(halves):
            x = x_ref[0, rows, sl]
            weighted = x * mm(both, fall_ref[:, sl]).astype(BF16)
            if k == 0:
                mixed = mm(left[k, :, :SPAN], weighted)
            else:
                entering = row_of(ENTER, sl) * states[number]
                mixed = mm(
                    left[k], jnp.concatenate([weighted, entering.astype(BF16)], axis=0)
                )
            if k < blocks - 1:
                added = mm(b_ref[:, rows], weighted)
                if k > 0:
                    added = added + entering
                states[number] = row_of(LEAVE, sl) * added
            half = 0.5 * gate_ref[0, rows, sl].astype(F32)
            gate = (half * jnp.tanh(half) + half).astype(BF16)
            lift = mm(both, rise_ref[:, sl]).astype(BF16) * gate
            skip = skip_ref[:, sl] * x * gate
            own_ref[rows, sl] = lift * mixed.astype(BF16) + skip
            factor_ref[rows, sl] = lift * row_of(FIRST, sl).astype(BF16)


def local_terms(features, gate_in, b, c, both, rise, fall, rows, skip_row, seq):
    _, length, channels = features.shape
    states = b.shape[0]
    width = min(512, channels)
    tile = pl.BlockSpec((1, length, width), lambda j: (seq, 0, j))
    whole = pl.BlockSpec((states, length), lambda j: (0, 0))
    column = lambda a: pl.BlockSpec((a.shape[0], width), lambda j: (0, j))
    out = pl.BlockSpec((length, width), lambda j: (0, j))
    return pl.pallas_call(
        local_kernel,
        grid=(channels // width,),
        in_specs=[
            tile, tile, whole, whole,
            pl.BlockSpec((1,) + both.shape[1:], lambda j: (seq, 0, 0)),
            column(rise), column(fall),
            pl.BlockSpec((1, rows.shape[1], width), lambda j: (seq, 0, j)),
            column(skip_row),
        ],
        out_specs=[out, out],
        out_shape=[jax.ShapeDtypeStruct((length, channels), BF16)] * 2,
        scratch_shapes=[pltpu.VMEM((length // SPAN, SPAN, SPAN + states), BF16)],
        compiler_params=PARAMS,
        cost_estimate=pl.CostEstimate(
            flops=2 * length * channels * 512,
            bytes_accessed=8 * length * channels,
            transcendentals=length * channels,
        ),
        name="local_terms",
    )(features, gate_in, b, c, both, rise, fall, rows, skip_row)


def joined_kernel(own_ref, factor_ref, c_ref, incoming_ref, gated_ref, square_ref):
    length, channels = own_ref.shape
    c_t = c_ref[...].T
    ones = jnp.ones((HALF, 128), BF16)
    squares = jnp.zeros((length, 128), F32)
    for lo in range(0, channels, HALF):
        sl = slice(lo, lo + HALF)
        carried = mm(c_t, incoming_ref[:, sl]).astype(BF16)
        gated = own_ref[:, sl] + factor_ref[:, sl] * carried
        gated_ref[:, sl] = gated
        squares = squares + mm(gated * gated, ones)
    for at in range(0, length, SPAN):
        square_ref[at // SPAN] = squares[at:at + SPAN].T[:1]


def joined(own, factor, c, incoming):
    length, channels = own.shape
    states = c.shape[0]
    blocks = length // SPAN
    tall = 2 * SPAN if blocks % 2 == 0 else SPAN
    tile = pl.BlockSpec((tall, channels), lambda k: (k, 0))
    return pl.pallas_call(
        joined_kernel,
        grid=(length // tall,),
        in_specs=[
            tile, tile,
            pl.BlockSpec((states, tall), lambda k: (0, k)),
            pl.BlockSpec((states, channels), lambda k: (0, 0)),
        ],
        out_specs=[tile, pl.BlockSpec((tall // SPAN, 1, SPAN), lambda k: (k, 0, 0))],
        out_shape=[
            jax.ShapeDtypeStruct((length, channels), BF16),
            jax.ShapeDtypeStruct((blocks, 1, SPAN), F32),
        ],
        compiler_params=PARAMS,
        cost_estimate=pl.CostEstimate(
            flops=2 * length * channels * states,
            bytes_accessed=6 * length * channels,
            transcendentals=0,
        ),
        name="joined",
    )(own, factor, c, incoming)


def norm_kernel(all_channels, gated_ref, square_ref, gain_ref, *refs):
    out_ref = refs[-1]
    tall, channels = gated_ref.shape
    for k in range(tall // SPAN):
        rows = slice(k * SPAN, (k + 1) * SPAN)
        total = jnp.sum(square_ref[:, k, 0], axis=0, keepdims=True)
        inverse = lax.rsqrt(total / all_channels + 1e-05)
        column = jnp.broadcast_to(inverse, (128, SPAN)).T
        for lo in range(0, channels, 128):
            sl = slice(lo, lo + 128)
            out_ref[0, rows, sl] = (
                gated_ref[rows, sl].astype(F32) * column * gain_ref[:, sl]
            ).astype(BF16)


def normed(gated, squares, gain_row, all_channels, seq, seqs, before):
    length, channels = gated.shape
    shards, blocks = squares.shape[:2]
    tall = 2 * SPAN if blocks % 2 == 0 else SPAN
    operands = [gated, squares, gain_row]
    in_specs = [
        pl.BlockSpec((tall, channels), lambda k: (k, 0)),
        pl.BlockSpec((shards, tall // SPAN, 1, SPAN), lambda k: (0, k, 0, 0)),
        pl.BlockSpec(gain_row.shape, lambda k: (0, 0)),
    ]
    if before is not None:
        operands.append(before)
        in_specs.append(pl.BlockSpec(memory_space=pl.ANY))
    return pl.pallas_call(
        functools.partial(norm_kernel, all_channels),
        grid=(length // tall,),
        in_specs=in_specs,
        out_specs=pl.BlockSpec((1, tall, channels), lambda k: (seq, k, 0)),
        out_shape=jax.ShapeDtypeStruct((seqs, length, channels), BF16),
        input_output_aliases={} if before is None else {3: 0},
        compiler_params=PARAMS,
        cost_estimate=pl.CostEstimate(
            flops=2 * length * channels,
            bytes_accessed=4 * length * channels,
            transcendentals=0,
        ),
        name="normed",
    )(*operands)


def from_all(shard, axis):
    devices = lax.axis_size(axis)
    return [shard] + [
        lax.ppermute(shard, axis, [(i, (i + by) % devices) for i in range(devices)])
        for by in range(1, devices)
    ]


def body(features, gate_in, state_proj, step_size, log_decay, skip_gain, norm_gain):
    seqs, length, channels = features.shape
    heads = step_size.shape[1]
    head_dim = channels // heads
    features = pltpu.with_memory_space_constraint(features, pltpu.HBM)
    gate_in = pltpu.with_memory_space_constraint(gate_in, pltpu.HBM)
    one = np.repeat(np.eye(heads, dtype=np.float32), head_dim, axis=1)
    pair = np.concatenate([one, one], axis=0)
    none = np.zeros_like(pair)
    spread = jnp.asarray(pair, BF16)
    rise = jnp.asarray(np.concatenate([pair, none], axis=0), BF16)
    fall = jnp.asarray(np.concatenate([none, pair], axis=0), BF16)
    skip_row = jnp.repeat(skip_gain.astype(BF16), head_dim)[None, :]
    gain_row = norm_gain[None, :]

    b = [jnp.concatenate(p, axis=0) for p in zip(*[
        [piece[s] for s in range(seqs)] for piece in from_all(state_proj[0], "head")
    ])]
    c = [jnp.concatenate(p, axis=0) for p in zip(*[
        [piece[s] for s in range(seqs)] for piece in from_all(state_proj[1], "head")
    ])]
    scale, both, rows = tables(step_size, log_decay, spread)
    total_at = TOTAL * (length // SPAN)
    total = [rows[s, total_at:total_at + 1] for s in range(seqs)]
    contrib = contributions(features, scale, spread)
    own_state = [end_state(b[s], contrib, s) for s in range(seqs)]
    locals_ = [
        local_terms(features, gate_in, b[s], c[s], both, rise, fall, rows, skip_row, s)
        for s in range(seqs)
    ]
    sent = list(own_state)
    incoming = [None] * seqs
    devices = lax.axis_size("ctx")
    for turn in range(devices - 1):
        for s in range(seqs):
            received = lax.ppermute(sent[s], "ctx", [(turn, turn + 1)])
            incoming[s] = received if incoming[s] is None else incoming[s] + received
            sent[s] = (
                own_state[s].astype(F32) + total[s] * incoming[s].astype(F32)
            ).astype(BF16)
    pairs = [joined(*locals_[s], c[s], incoming[s]) for s in range(seqs)]
    out = None
    for s in range(seqs):
        squares = jnp.stack(from_all(pairs[s][1], "head"))
        out = normed(
            pairs[s][0], squares, gain_row, channels * lax.axis_size("head"), s, seqs, out
        )
    return out


def solution(mesh):
    in_specs = (
        P("groups", "ctx", "head"),
        P("groups", "ctx", "head"),
        P(None, "groups", "head", "ctx"),
        P("groups", "head", "ctx"),
        P("groups", "head", "ctx"),
        P("head"),
        P("head"),
    )
    out_specs = P("groups", "ctx", "head")
    return jax.shard_map(body, mesh=mesh, in_specs=in_specs, out_specs=out_specs, check_vma=False)
```

time: 110 us -> 97.9 us (0.89)
  the two profiles are of different devices: /device:TPU:14 before, /device:TPU:2 now
where the time goes in v2:
time: 97.9 us; the launch traced here: 97.3 us
  Pallas kernels  48 us (49%)
  starting transfers between devices  22.5 us (23%)
  waiting for transfers between devices  18.6 us (19%)
  local copies, waits for them, and re-layouts  5.84 us (6%)
  other arithmetic  1.97 us (2%)
    pallas_call x2, Pallas kernels, local_terms(): pl.pallas_call(local_kernel, grid=(channels // width,), in_specs=[tile, t...  24.6 us
    ppermute x12, starting transfers between devices, from_all(): lax.ppermute(shard, axis, [(i, (i + by) % devices) for i in range(devices)])  15.7 us
    ppermute x6, waiting for transfers between devices, body(): received = lax.ppermute(sent[s], 'ctx', [(turn, turn + 1)])  11.5 us
    ppermute x12, waiting for transfers between devices, from_all(): lax.ppermute(shard, axis, [(i, (i + by) % devices) for i in range(devices)])  7.09 us
    pallas_call x1, Pallas kernels, contributions(): pl.pallas_call(contrib_kernel, grid=(seqs, channels // width), in_specs=[...  6.78 us
    ppermute x6, starting transfers between devices, body(): received = lax.ppermute(sent[s], 'ctx', [(turn, turn + 1)])  6.75 us
    pallas_call x2, Pallas kernels, joined(): pl.pallas_call(joined_kernel, grid=(length // tall,), in_specs=[tile, til...  5.84 us
    pallas_call x2, Pallas kernels, normed(): pl.pallas_call(functools.partial(norm_kernel, all_channels), grid=(length...  5.39 us
  transfers between devices with their start and end apart: 18, of which 4 were waited for; matrix products, arithmetic and copies ran while one was open for 3% of the time, Pallas kernels for 47%

profile of v2, /device:TPU:2, one launch (start us, length us, event | category | flops | bytes accessed | tf_op | source)
XLA Modules:
  0.0 97.3 jit_solution(11127652770158513501)
XLA Ops:
  0.0 1.0 slice_bitcast_fusion
  1.0 3.7 %collective-permute-start.5 = (bf16[2,32,768]{2,1,0:T(8,128)(2,1)S(1)}, bf16[2,32,768]{2,1,0:T(8,128)(2,1)S(1)}, u32[]{:S(2)}, u32[]{:S(2)}) collective-permute-start(bf16[2,32,768]{2,1,0:T(8,128)(2,1)S(1)} %get-tuple-element.37), channel_id=1, source_target_pairs={{0,3},{1,0},{2,1},{3,2},{4,7},{5,4},{6,5},{7,6},{8,11},{9,8},{10,9... | collective-permute-start | bytes 294920 | tf_op jit(solution)/shard_map/ppermute | solution.py:327
  4.6 1.0 %collective-permute-start.3 = (bf16[2,32,768]{2,1,0:T(8,128)(2,1)S(1)}, bf16[2,32,768]{2,1,0:T(8,128)(2,1)S(1)}, u32[]{:S(2)}, u32[]{:S(2)}) collective-permute-start(bf16[2,32,768]{2,1,0:T(8,128)(2,1)S(1)} %get-tuple-element.37), channel_id=1, source_target_pairs={{0,1},{1,2},{2,3},{3,0},{4,5},{5,6},{6,7},{7,4},{8,9},{9,10},{10,1... | collective-permute-start | bytes 294920 | tf_op jit(solution)/shard_map/ppermute | solution.py:327
  5.6 2.8 %collective-permute-start.2 = (bf16[2,32,768]{2,1,0:T(8,128)(2,1)S(1)}, bf16[2,32,768]{2,1,0:T(8,128)(2,1)S(1)}, u32[]{:S(2)}, u32[]{:S(2)}) collective-permute-start(bf16[2,32,768]{2,1,0:T(8,128)(2,1)S(1)} %get-tuple-element.38), channel_id=1, source_target_pairs={{0,3},{1,0},{2,1},{3,2},{4,7},{5,4},{6,5},{7,6},{8,11},{9,8},{10,9... | collective-permute-start | bytes 294920 | tf_op jit(solution)/shard_map/ppermute | solution.py:327
  8.4 1.1 %collective-permute-start.1 = (bf16[2,32,768]{2,1,0:T(8,128)(2,1)S(1)}, bf16[2,32,768]{2,1,0:T(8,128)(2,1)S(1)}, u32[]{:S(2)}, u32[]{:S(2)}) collective-permute-start(bf16[2,32,768]{2,1,0:T(8,128)(2,1)S(1)} %get-tuple-element.38), channel_id=1, source_target_pairs={{0,2},{1,3},{2,0},{3,1},{4,6},{5,7},{6,4},{7,5},{8,10},{9,11},{10,... | collective-permute-start | bytes 294920 | tf_op jit(solution)/shard_map/ppermute | solution.py:327
  9.6 0.9 copy-done.2
  10.5 0.9 copy-done.4
  11.4 0.9 copy-done.5
  12.4 2.5 %tables.1 = (bf16[2,768,64]{2,1,0:T(8,128)(2,1)S(1)}, bf16[2,768,128]{2,1,0:T(8,128)(2,1)S(1)}, f32[2,32,2048]{2,1,0:T(8,128)S(1)}) custom-call(f32[2,32,768]{2,1,0:T(8,128)S(1)} %copy-done.4, f32[2,32,768]{2,1,0:T(8,128)S(1)} %copy-done.5, bf16[64,2048]{1,0:T(8,128)(2,1)S(1)} %copy-done.2), custom_call_target="tpu_custom_call" | custom-call | tf_op jit(solution)/shard_map/tables/pallas_call | solution.py:80
  14.9 0.9 slice_bitcast_fusion.14
  16.6 0.9 copy-done.3
  17.6 6.8 %contributions.1.contrib_ref = bf16[2,768,2048]{2,1,0:T(8,128)(2,1)S(1)} custom-call(bf16[2,768,2048]{2,1,0:T(8,128)(2,1)} %x_ref.5, bf16[2,768,64]{2,1,0:T(8,128)(2,1)S(1)} %get-tuple-element.20.scale_ref, bf16[64,2048]{1,0:T(8,128)(2,1)S(1)} %copy-done.3), custom_call_target="tpu_custom_call" | custom-call | flops 402653184 | bytes 12582912 | tf_op jit(solution)/shard_map/contributions/pallas_call | solution.py:107
  24.5 6.4 %collective-permute-done = bf16[2,32,768]{2,1,0:T(8,128)(2,1)S(1)} collective-permute-done((bf16[2,32,768]{2,1,0:T(8,128)(2,1)S(1)}, bf16[2,32,768]{2,1,0:T(8,128)(2,1)S(1)}, u32[]{:S(2)}, u32[]{:S(2)}) %collective-permute-start) | collective-permute-done | bytes 98336 | tf_op jit(solution)/shard_map/ppermute | solution.py:327
  30.9 1.4 %own_end_state.2 = bf16[128,2048]{1,0:T(8,128)(2,1)S(1)} custom-call(bf16[128,768]{1,0:T(8,128)(2,1)S(1)} %pad_maximum_fusion.b_ref, bf16[2,768,2048]{2,1,0:T(8,128)(2,1)S(1)} %contributions.1.contrib_ref), custom_call_target="tpu_custom_call" | custom-call | flops 402653184 | bytes 3145728 | tf_op jit(solution)/shard_map/own_end_state/pallas_call | solution.py:135
  32.3 0.7 collective-permute-start.6
  33.0 1.4 %own_end_state.3 = bf16[128,2048]{1,0:T(8,128)(2,1)S(1)} custom-call(bf16[128,768]{1,0:T(8,128)(2,1)S(1)} %pad_maximum_fusion.2.b_ref, bf16[2,768,2048]{2,1,0:T(8,128)(2,1)S(1)} %contributions.1.contrib_ref), custom_call_target="tpu_custom_call" | custom-call | flops 402653184 | bytes 3145728 | tf_op jit(solution)/shard_map/own_end_state/pallas_call | solution.py:135
  35.4 1.3 %collective-permute-start.7 = (bf16[128,2048]{1,0:T(8,128)(2,1)S(1)}, bf16[128,2048]{1,0:T(8,128)(2,1)S(1)}, u32[]{:S(2)}, u32[]{:S(2)}) collective-permute-start(bf16[128,2048]{1,0:T(8,128)(2,1)S(1)} %fusion), channel_id=1, source_target_pairs={{4,8},{5,9},{6,10},{7,11},{20,24},{21,25},{22,26},{23,27}} | collective-permute-start | bytes 1572872 | tf_op jit(solution)/shard_map/ppermute | solution.py:367
  36.9 1.4 %collective-permute-start.13 = (bf16[128,2048]{1,0:T(8,128)(2,1)S(1)}, bf16[128,2048]{1,0:T(8,128)(2,1)S(1)}, u32[]{:S(2)}, u32[]{:S(2)}) collective-permute-start(bf16[128,2048]{1,0:T(8,128)(2,1)S(1)} %fusion.2), channel_id=1, source_target_pairs={{4,8},{5,9},{6,10},{7,11},{20,24},{21,25},{22,26},{23,27}} | collective-permute-start | bytes 1572872 | tf_op jit(solution)/shard_map/ppermute | solution.py:367
  38.4 7.5 %collective-permute-done.7 = bf16[128,2048]{1,0:T(8,128)(2,1)S(1)} collective-permute-done((bf16[128,2048]{1,0:T(8,128)(2,1)S(1)}, bf16[128,2048]{1,0:T(8,128)(2,1)S(1)}, u32[]{:S(2)}, u32[]{:S(2)}) %collective-permute-start.7) | collective-permute-done | bytes 524320 | tf_op jit(solution)/shard_map/ppermute | solution.py:367
  46.2 1.3 %collective-permute-start.8 = (bf16[128,2048]{1,0:T(8,128)(2,1)S(1)}, bf16[128,2048]{1,0:T(8,128)(2,1)S(1)}, u32[]{:S(2)}, u32[]{:S(2)}) collective-permute-start(bf16[128,2048]{1,0:T(8,128)(2,1)S(1)} %get-tuple-element.29), channel_id=1, source_target_pairs={{8,12},{9,13},{10,14},{11,15},{24,28},{25,29},{26,30},{27,31}} | collective-permute-start | bytes 1572872 | tf_op jit(solution)/shard_map/ppermute | solution.py:367
  47.6 4.0 %collective-permute-done.13 = bf16[128,2048]{1,0:T(8,128)(2,1)S(1)} collective-permute-done((bf16[128,2048]{1,0:T(8,128)(2,1)S(1)}, bf16[128,2048]{1,0:T(8,128)(2,1)S(1)}, u32[]{:S(2)}, u32[]{:S(2)}) %collective-permute-start.13) | collective-permute-done | bytes 524320 | tf_op jit(solution)/shard_map/ppermute | solution.py:367
  51.9 1.3 %collective-permute-start.14 = (bf16[128,2048]{1,0:T(8,128)(2,1)S(1)}, bf16[128,2048]{1,0:T(8,128)(2,1)S(1)}, u32[]{:S(2)}, u32[]{:S(2)}) collective-permute-start(bf16[128,2048]{1,0:T(8,128)(2,1)S(1)} %get-tuple-element.27), channel_id=1, source_target_pairs={{8,12},{9,13},{10,14},{11,15},{24,28},{25,29},{26,30},{27,31}} | collective-permute-start | bytes 1572872 | tf_op jit(solution)/shard_map/ppermute | solution.py:367
  53.2 12.3 %local_terms.2 = (bf16[768,2048]{1,0:T(8,128)(2,1)S(1)}, bf16[768,2048]{1,0:T(8,128)(2,1)S(1)}) custom-call(bf16[2,768,2048]{2,1,0:T(8,128)(2,1)} %x_ref.5, bf16[2,768,2048]{2,1,0:T(8,128)(2,1)} %gate_ref.3, bf16[128,768]{1,0:T(8,128)(2,1)S(1)} %pad_maximum_fusion.b_ref, bf16[128,768]{1,0:T(8,128)(2,1)S(1)} %pad_maximum_fusion.1.c_ref, ...), custom_call_target="tpu_custom_call" | custom-call | flops 1610612736 | bytes 12582912 | tf_op jit(solution)/shard_map/local_terms/pallas_call | solution.py:212
  65.6 12.3 %local_terms.3 = (bf16[768,2048]{1,0:T(8,128)(2,1)S(1)}, bf16[768,2048]{1,0:T(8,128)(2,1)S(1)}) custom-call(bf16[2,768,2048]{2,1,0:T(8,128)(2,1)} %x_ref.5, bf16[2,768,2048]{2,1,0:T(8,128)(2,1)} %gate_ref.3, bf16[128,768]{1,0:T(8,128)(2,1)S(1)} %pad_maximum_fusion.2.b_ref, bf16[128,768]{1,0:T(8,128)(2,1)S(1)} %pad_maximum_fusion.3.c_ref, ...), custom_call_target="tpu_custom_call" | custom-call | flops 1610612736 | bytes 12582912 | tf_op jit(solution)/shard_map/local_terms/pallas_call | solution.py:212
  78.1 2.9 %joined.3 = (bf16[768,2048]{1,0:T(8,128)(2,1)S(1)}, f32[6,1,128]{2,1,0:T(1,128)S(1)}) custom-call(bf16[768,2048]{1,0:T(8,128)(2,1)S(1)} %get-tuple-element.23.own_ref, bf16[768,2048]{1,0:T(8,128)(2,1)S(1)} %get-tuple-element.24.factor_ref, bf16[128,768]{1,0:T(8,128)(2,1)S(1)} %pad_maximum_fusion.3.c_ref, bf16[128,2048]{1,0:T(8,128)(2,1)S(1)} %add.31.incoming_ref), custom_call_target="tpu_custom_call" | custom-call | flops 402653184 | bytes 9437184 | tf_op jit(solution)/shard_map/joined/pallas_call | solution.py:256
  81.1 1.9 %collective-permute-start.15 = (f32[6,1,128]{2,1,0:T(1,128)S(1)}, f32[6,1,128]{2,1,0:T(1,128)S(1)}, u32[]{:S(2)}, u32[]{:S(2)}) collective-permute-start(f32[6,1,128]{2,1,0:T(1,128)S(1)} %get-tuple-element.26), channel_id=1, source_target_pairs={{0,1},{1,2},{2,3},{3,0},{4,5},{5,6},{6,7},{7,4},{8,9},{9,10},{10,1... | collective-permute-start | bytes 9224 | tf_op jit(solution)/shard_map/ppermute | solution.py:327
  83.2 2.9 %joined.2 = (bf16[768,2048]{1,0:T(8,128)(2,1)S(1)}, f32[6,1,128]{2,1,0:T(1,128)S(1)}) custom-call(bf16[768,2048]{1,0:T(8,128)(2,1)S(1)} %get-tuple-element.18.own_ref, bf16[768,2048]{1,0:T(8,128)(2,1)S(1)} %get-tuple-element.19.factor_ref, bf16[128,768]{1,0:T(8,128)(2,1)S(1)} %pad_maximum_fusion.1.c_ref, bf16[128,2048]{1,0:T(8,128)(2,1)S(1)} %add.27.incoming_ref), custom_call_target="tpu_custom_call" | custom-call | flops 402653184 | bytes 9437184 | tf_op jit(solution)/shard_map/joined/pallas_call | solution.py:256
  86.2 2.4 %collective-permute-start.11 = (f32[6,1,128]{2,1,0:T(1,128)S(1)}, f32[6,1,128]{2,1,0:T(1,128)S(1)}, u32[]{:S(2)}, u32[]{:S(2)}) collective-permute-start(f32[6,1,128]{2,1,0:T(1,128)S(1)} %get-tuple-element.22), channel_id=1, source_target_pairs={{0,3},{1,0},{2,1},{3,2},{4,7},{5,4},{6,5},{7,6},{8,11},{9,8},{10,9... | collective-permute-start | bytes 9224 | tf_op jit(solution)/shard_map/ppermute | solution.py:327
  89.2 1.9 %collective-permute-start.9 = (f32[6,1,128]{2,1,0:T(1,128)S(1)}, f32[6,1,128]{2,1,0:T(1,128)S(1)}, u32[]{:S(2)}, u32[]{:S(2)}) collective-permute-start(f32[6,1,128]{2,1,0:T(1,128)S(1)} %get-tuple-element.22), channel_id=1, source_target_pairs={{0,1},{1,2},{2,3},{3,0},{4,5},{5,6},{6,7},{7,4},{8,9},{9,10},{10,1... | collective-permute-start | bytes 9224 | tf_op jit(solution)/shard_map/ppermute | solution.py:327
  91.2 2.7 %normed.2.refs_0_ = bf16[2,768,2048]{2,1,0:T(8,128)(2,1)} custom-call(bf16[768,2048]{1,0:T(8,128)(2,1)S(1)} %get-tuple-element.25.gated_ref, f32[4,6,1,128]{3,2,1,0:T(1,128)S(1)} %pad_maximum_fusion.5.square_ref, f32[1,2048]{1,0:T(1,128)S(1)} %bitcast.47), custom_call_target="tpu_custom_call" | custom-call | flops 3145728 | bytes 6291456 | tf_op jit(solution)/shard_map/normed/pallas_call | solution.py:307
  93.9 0.7 collective-permute-done.9
  94.6 2.7 %normed.3 = bf16[2,768,2048]{2,1,0:T(8,128)(2,1)} custom-call(bf16[768,2048]{1,0:T(8,128)(2,1)S(1)} %get-tuple-element.21.gated_ref, f32[4,6,1,128]{3,2,1,0:T(1,128)S(1)} %pad_maximum_fusion.4.square_ref, f32[1,2048]{1,0:T(1,128)S(1)} %bitcast.48, bf16[2,768,2048]{2,1,0:T(8,128)(2,1)} %normed.2.refs_0_), custom_call_target="tpu_custom_call", output_to_operand_aliasing={{}: (3, {})} | custom-call | flops 3145728 | bytes 6291456 | tf_op jit(solution)/shard_map/normed/pallas_call | solution.py:307
  (52 shorter events, 3.8 us)
Async XLA Ops:
  1.0 34.2 %collective-permute-start.5 = (bf16[2,32,768]{2,1,0:T(8,128)(2,1)S(1)}, bf16[2,32,768]{2,1,0:T(8,128)(2,1)S(1)}, u32[]{:S(2)}, u32[]{:S(2)}) collective-permute-start(bf16[2,32,768]{2,1,0:T(8,128)(2,1)S(1)} %get-tuple-element.37), channel_id=1, source_target_pairs={{0,3},{1,0},{2,1},{3,2},{4,7},{5,4},{6,5},{7,6},{8,11},{9,8},{10,9... | collective-permute-start | bytes 294920 | tf_op jit(solution)/shard_map/ppermute | solution.py:327
  4.6 30.6 %collective-permute-start.4 = (bf16[2,32,768]{2,1,0:T(8,128)(2,1)S(1)}, bf16[2,32,768]{2,1,0:T(8,128)(2,1)S(1)}, u32[]{:S(2)}, u32[]{:S(2)}) collective-permute-start(bf16[2,32,768]{2,1,0:T(8,128)(2,1)S(1)} %get-tuple-element.37), channel_id=1, source_target_pairs={{0,2},{1,3},{2,0},{3,1},{4,6},{5,7},{6,4},{7,5},{8,10},{9,11},{10,... | collective-permute-start | bytes 294920 | tf_op jit(solution)/shard_map/ppermute | solution.py:327
  4.6 33.7 %collective-permute-start.3 = (bf16[2,32,768]{2,1,0:T(8,128)(2,1)S(1)}, bf16[2,32,768]{2,1,0:T(8,128)(2,1)S(1)}, u32[]{:S(2)}, u32[]{:S(2)}) collective-permute-start(bf16[2,32,768]{2,1,0:T(8,128)(2,1)S(1)} %get-tuple-element.37), channel_id=1, source_target_pairs={{0,1},{1,2},{2,3},{3,0},{4,5},{5,6},{6,7},{7,4},{8,9},{9,10},{10,1... | collective-permute-start | bytes 294920 | tf_op jit(solution)/shard_map/ppermute | solution.py:327
  5.6 18.7 %collective-permute-start.2 = (bf16[2,32,768]{2,1,0:T(8,128)(2,1)S(1)}, bf16[2,32,768]{2,1,0:T(8,128)(2,1)S(1)}, u32[]{:S(2)}, u32[]{:S(2)}) collective-permute-start(bf16[2,32,768]{2,1,0:T(8,128)(2,1)S(1)} %get-tuple-element.38), channel_id=1, source_target_pairs={{0,3},{1,0},{2,1},{3,2},{4,7},{5,4},{6,5},{7,6},{8,11},{9,8},{10,9... | collective-permute-start | bytes 294920 | tf_op jit(solution)/shard_map/ppermute | solution.py:327
  8.4 16.0 %collective-permute-start.1 = (bf16[2,32,768]{2,1,0:T(8,128)(2,1)S(1)}, bf16[2,32,768]{2,1,0:T(8,128)(2,1)S(1)}, u32[]{:S(2)}, u32[]{:S(2)}) collective-permute-start(bf16[2,32,768]{2,1,0:T(8,128)(2,1)S(1)} %get-tuple-element.38), channel_id=1, source_target_pairs={{0,2},{1,3},{2,0},{3,1},{4,6},{5,7},{6,4},{7,5},{8,10},{9,11},{10,... | collective-permute-start | bytes 294920 | tf_op jit(solution)/shard_map/ppermute | solution.py:327
  9.6 0.9 copy-start.2
  10.5 0.9 copy-start.4
  11.4 0.9 copy-start.5
  16.6 1.0 copy-start.3
  24.4 6.5 %collective-permute-start = (bf16[2,32,768]{2,1,0:T(8,128)(2,1)S(1)}, bf16[2,32,768]{2,1,0:T(8,128)(2,1)S(1)}, u32[]{:S(2)}, u32[]{:S(2)}) collective-permute-start(bf16[2,32,768]{2,1,0:T(8,128)(2,1)S(1)} %get-tuple-element.38), channel_id=1, source_target_pairs={{0,1},{1,2},{2,3},{3,0},{4,5},{5,6},{6,7},{7,4},{8,9},{9,10},{10,1... | collective-permute-start | bytes 294920 | tf_op jit(solution)/shard_map/ppermute | solution.py:327
  32.3 2.9 %collective-permute-start.6 = (bf16[128,2048]{1,0:T(8,128)(2,1)S(1)}, bf16[128,2048]{1,0:T(8,128)(2,1)S(1)}, u32[]{:S(2)}, u32[]{:S(2)}) collective-permute-start(bf16[128,2048]{1,0:T(8,128)(2,1)S(1)} %own_end_state.2), channel_id=1, source_target_pairs={{0,4},{1,5},{2,6},{3,7},{16,20},{17,21},{18,22},{19,23}} | collective-permute-start | bytes 1572872 | tf_op jit(solution)/shard_map/ppermute | solution.py:367
  34.5 2.2 %collective-permute-start.12 = (bf16[128,2048]{1,0:T(8,128)(2,1)S(1)}, bf16[128,2048]{1,0:T(8,128)(2,1)S(1)}, u32[]{:S(2)}, u32[]{:S(2)}) collective-permute-start(bf16[128,2048]{1,0:T(8,128)(2,1)S(1)} %own_end_state.3), channel_id=1, source_target_pairs={{0,4},{1,5},{2,6},{3,7},{16,20},{17,21},{18,22},{19,23}} | collective-permute-start | bytes 1572872 | tf_op jit(solution)/shard_map/ppermute | solution.py:367
  35.4 10.5 %collective-permute-start.7 = (bf16[128,2048]{1,0:T(8,128)(2,1)S(1)}, bf16[128,2048]{1,0:T(8,128)(2,1)S(1)}, u32[]{:S(2)}, u32[]{:S(2)}) collective-permute-start(bf16[128,2048]{1,0:T(8,128)(2,1)S(1)} %fusion), channel_id=1, source_target_pairs={{4,8},{5,9},{6,10},{7,11},{20,24},{21,25},{22,26},{23,27}} | collective-permute-start | bytes 1572872 | tf_op jit(solution)/shard_map/ppermute | solution.py:367
  36.9 16.3 %copy-start = (bf16[128,2048]{1,0:T(8,128)(2,1)S(1)}, bf16[128,2048]{1,0:T(8,128)(2,1)}, u32[]{:S(2)}) copy-start(bf16[128,2048]{1,0:T(8,128)(2,1)} %constant.8.clone.fall_ref) | copy-start | bytes 1572868
  36.9 16.3 %copy-start.1 = (bf16[128,2048]{1,0:T(8,128)(2,1)S(1)}, bf16[128,2048]{1,0:T(8,128)(2,1)}, u32[]{:S(2)}) copy-start(bf16[128,2048]{1,0:T(8,128)(2,1)} %constant.7.clone.rise_ref) | copy-start | bytes 1572868
  36.9 14.6 %collective-permute-start.13 = (bf16[128,2048]{1,0:T(8,128)(2,1)S(1)}, bf16[128,2048]{1,0:T(8,128)(2,1)S(1)}, u32[]{:S(2)}, u32[]{:S(2)}) collective-permute-start(bf16[128,2048]{1,0:T(8,128)(2,1)S(1)} %fusion.2), channel_id=1, source_target_pairs={{4,8},{5,9},{6,10},{7,11},{20,24},{21,25},{22,26},{23,27}} | collective-permute-start | bytes 1572872 | tf_op jit(solution)/shard_map/ppermute | solution.py:367
  46.2 36.8 %collective-permute-start.8 = (bf16[128,2048]{1,0:T(8,128)(2,1)S(1)}, bf16[128,2048]{1,0:T(8,128)(2,1)S(1)}, u32[]{:S(2)}, u32[]{:S(2)}) collective-permute-start(bf16[128,2048]{1,0:T(8,128)(2,1)S(1)} %get-tuple-element.29), channel_id=1, source_target_pairs={{8,12},{9,13},{10,14},{11,15},{24,28},{25,29},{26,30},{27,31}} | collective-permute-start | bytes 1572872 | tf_op jit(solution)/shard_map/ppermute | solution.py:367
  51.9 26.1 %collective-permute-start.14 = (bf16[128,2048]{1,0:T(8,128)(2,1)S(1)}, bf16[128,2048]{1,0:T(8,128)(2,1)S(1)}, u32[]{:S(2)}, u32[]{:S(2)}) collective-permute-start(bf16[128,2048]{1,0:T(8,128)(2,1)S(1)} %get-tuple-element.27), channel_id=1, source_target_pairs={{8,12},{9,13},{10,14},{11,15},{24,28},{25,29},{26,30},{27,31}} | collective-permute-start | bytes 1572872 | tf_op jit(solution)/shard_map/ppermute | solution.py:367
  81.0 8.2 %collective-permute-start.17 = (f32[6,1,128]{2,1,0:T(1,128)S(1)}, f32[6,1,128]{2,1,0:T(1,128)S(1)}, u32[]{:S(2)}, u32[]{:S(2)}) collective-permute-start(f32[6,1,128]{2,1,0:T(1,128)S(1)} %get-tuple-element.26), channel_id=1, source_target_pairs={{0,3},{1,0},{2,1},{3,2},{4,7},{5,4},{6,5},{7,6},{8,11},{9,8},{10,9... | collective-permute-start | bytes 9224 | tf_op jit(solution)/shard_map/ppermute | solution.py:327
  81.0 10.1 %collective-permute-start.16 = (f32[6,1,128]{2,1,0:T(1,128)S(1)}, f32[6,1,128]{2,1,0:T(1,128)S(1)}, u32[]{:S(2)}, u32[]{:S(2)}) collective-permute-start(f32[6,1,128]{2,1,0:T(1,128)S(1)} %get-tuple-element.26), channel_id=1, source_target_pairs={{0,2},{1,3},{2,0},{3,1},{4,6},{5,7},{6,4},{7,5},{8,10},{9,11},{10,... | collective-permute-start | bytes 9224 | tf_op jit(solution)/shard_map/ppermute | solution.py:327
  81.1 10.0 %collective-permute-start.15 = (f32[6,1,128]{2,1,0:T(1,128)S(1)}, f32[6,1,128]{2,1,0:T(1,128)S(1)}, u32[]{:S(2)}, u32[]{:S(2)}) collective-permute-start(f32[6,1,128]{2,1,0:T(1,128)S(1)} %get-tuple-element.26), channel_id=1, source_target_pairs={{0,1},{1,2},{2,3},{3,0},{4,5},{5,6},{6,7},{7,4},{8,9},{9,10},{10,1... | collective-permute-start | bytes 9224 | tf_op jit(solution)/shard_map/ppermute | solution.py:327
  83.2 8.0 %copy-start.6 = (f32[2048]{0:T(1024)S(1)}, f32[2048]{0:T(1024)}, u32[]{:S(2)}) copy-start(f32[2048]{0:T(1024)} %param.16) | copy-start | bytes 24580
  86.2 7.7 %collective-permute-start.11 = (f32[6,1,128]{2,1,0:T(1,128)S(1)}, f32[6,1,128]{2,1,0:T(1,128)S(1)}, u32[]{:S(2)}, u32[]{:S(2)}) collective-permute-start(f32[6,1,128]{2,1,0:T(1,128)S(1)} %get-tuple-element.22), channel_id=1, source_target_pairs={{0,3},{1,0},{2,1},{3,2},{4,7},{5,4},{6,5},{7,6},{8,11},{9,8},{10,9... | collective-permute-start | bytes 9224 | tf_op jit(solution)/shard_map/ppermute | solution.py:327
  88.6 5.3 %collective-permute-start.10 = (f32[6,1,128]{2,1,0:T(1,128)S(1)}, f32[6,1,128]{2,1,0:T(1,128)S(1)}, u32[]{:S(2)}, u32[]{:S(2)}) collective-permute-start(f32[6,1,128]{2,1,0:T(1,128)S(1)} %get-tuple-element.22), channel_id=1, source_target_pairs={{0,2},{1,3},{2,0},{3,1},{4,6},{5,7},{6,4},{7,5},{8,10},{9,11},{10,... | collective-permute-start | bytes 9224 | tf_op jit(solution)/shard_map/ppermute | solution.py:327
  89.2 5.4 %collective-permute-start.9 = (f32[6,1,128]{2,1,0:T(1,128)S(1)}, f32[6,1,128]{2,1,0:T(1,128)S(1)}, u32[]{:S(2)}, u32[]{:S(2)}) collective-permute-start(f32[6,1,128]{2,1,0:T(1,128)S(1)} %get-tuple-element.22), channel_id=1, source_target_pairs={{0,1},{1,2},{2,3},{3,0},{4,5},{5,6},{6,7},{7,4},{8,9},{9,10},{10,1... | collective-permute-start | bytes 9224 | tf_op jit(solution)/shard_map/ppermute | solution.py:327

commit v3 on v2

v3 whole, which is shorter than its diff:
```python
import functools

import jax
import jax.numpy as jnp
import numpy as np
from jax import lax
from jax.experimental import pallas as pl
from jax.experimental.pallas import tpu as pltpu
from jax.sharding import PartitionSpec as P

SPAN = 128
HALF = 256
F32 = jnp.float32
BF16 = jnp.bfloat16
VMEM_LIMIT = 20 * 1024 * 1024
PARAMS = pltpu.CompilerParams(vmem_limit_bytes=VMEM_LIMIT)
ENTER, LEAVE, FIRST, REST, TOTAL = range(5)
ROWS = 32
WHOLE = pl.BlockSpec(memory_space=pltpu.VMEM)


def in_vmem(array):
    return pltpu.with_memory_space_constraint(array, pltpu.VMEM)


def in_hbm(array):
    return pltpu.with_memory_space_constraint(array, pltpu.HBM)


def mm(a, b):
    return jnp.dot(a, b, preferred_element_type=F32)


def exact_dot(a, b):
    return jnp.dot(a, b, precision=lax.Precision.HIGHEST, preferred_element_type=F32)


def iotas(shape):
    return (
        lax.broadcasted_iota(jnp.int32, shape, 0),
        lax.broadcasted_iota(jnp.int32, shape, 1),
    )


def two_parts(v):
    high = v.astype(BF16).astype(F32)
    return [high, v - high]


def upright(parts):
    return jnp.concatenate(parts, axis=0).T.astype(BF16)


def fill_tables(step_ref, decay_ref, skip_ref, spread_ref, scale_ref, both_ref, rows_ref):
    seqs, heads, length = decay_ref.shape
    blocks = length // SPAN
    at, lane = iotas((length, SPAN))
    kind, block = lane // blocks, lane % blocks
    first, mid, end = block * SPAN, block * SPAN + SPAN // 2, block * SPAN + SPAN
    chosen = (
        ((kind == ENTER) & (at >= first) & (at < mid))
        | ((kind == LEAVE) & (at >= mid) & (at < end))
        | ((kind == FIRST) & (at < mid))
        | ((kind == REST) & (at >= first))
        | (kind == TOTAL)
    )
    chosen = jnp.where(chosen, 1.0, 0.0).astype(F32)
    row, col = iotas((SPAN, SPAN))
    until = jnp.where(row <= col, 1.0, 0.0).astype(F32)
    spread = spread_ref[:heads, :]
    skip = jnp.broadcast_to(skip_ref[...], (8, heads))
    skip_row = sum(mm(part.astype(BF16), spread) for part in two_parts(skip))
    for s in range(seqs):
        exponent = exact_dot(decay_ref[s], chosen)
        per_block = upright(two_parts(jnp.exp(exponent)))
        rows_ref[s] = mm(per_block, spread_ref[...])[:ROWS]
        rows_ref[s, ROWS - 1:ROWS] = skip_row[:1]
        for k in range(blocks):
            sl = slice(k * SPAN, (k + 1) * SPAN)
            step = step_ref[s, :, sl]
            summed = exact_dot(decay_ref[s, :, sl], until)
            middle = exponent[:, ENTER * blocks + k:ENTER * blocks + k + 1]
            rest = exponent[:, REST * blocks + k:REST * blocks + k + 1]
            scale = step * jnp.exp(rest - summed)
            rise = jnp.exp(summed - middle)
            fall = step * jnp.exp(middle - summed)
            scale_ref[s, sl, :] = upright(two_parts(scale))
            both_ref[s, sl, :] = upright(two_parts(rise) + two_parts(fall))


def front_kernel(
    x_ref, step_ref, decay_ref, skip_ref, spread_ref, contrib_ref, both_ref, rows_ref, scale_ref
):
    seq, part = pl.program_id(0), pl.program_id(1)
    length, width = x_ref.shape[1:]

    @pl.when((seq == 0) & (part == 0))
    def _():
        fill_tables(step_ref, decay_ref, skip_ref, spread_ref, scale_ref, both_ref, rows_ref)

    scale = scale_ref[seq]
    for lo in range(0, width, HALF):
        at = pl.ds(pl.multiple_of(part * width + lo, HALF), HALF)
        wide = mm(scale, spread_ref[:, at]).astype(BF16)
        contrib_ref[seq, :, at] = x_ref[0, :, lo:lo + HALF] * wide


def front(features, step_size, log_decay, skip, spread):
    seqs, length, channels = features.shape
    heads = step_size.shape[1]
    width = min(512, channels)
    return pl.pallas_call(
        front_kernel,
        grid=(seqs, channels // width),
        in_specs=[
            pl.BlockSpec((1, length, width), lambda s, j: (s, 0, j)),
            WHOLE, WHOLE, WHOLE, WHOLE,
        ],
        out_specs=[WHOLE, WHOLE, WHOLE],
        out_shape=[
            pltpu.VMEM(features.shape, BF16),
            pltpu.VMEM((seqs, length, 4 * heads), BF16),
            pltpu.VMEM((seqs, ROWS, channels), F32),
        ],
        scratch_shapes=[pltpu.VMEM((seqs, length, 2 * heads), BF16)],
        compiler_params=PARAMS,
        cost_estimate=pl.CostEstimate(
            flops=2 * seqs * length * channels * 64,
            bytes_accessed=4 * seqs * length * channels,
            transcendentals=0,
        ),
        name="front",
    )(features, step_size, log_decay, skip, spread)


def state_kernel(seq, b_ref, contrib_ref, state_ref):
    channels = state_ref.shape[1]
    for lo in range(0, channels, HALF):
        sl = slice(lo, lo + HALF)
        state_ref[:, sl] = mm(b_ref[...], contrib_ref[seq, :, sl]).astype(BF16)


def end_state(b, contrib, seq):
    states, length = b.shape
    channels = contrib.shape[2]
    return pl.pallas_call(
        functools.partial(state_kernel, seq),
        in_specs=[WHOLE, WHOLE],
        out_specs=WHOLE,
        out_shape=pltpu.VMEM((states, channels), BF16),
        compiler_params=PARAMS,
        cost_estimate=pl.CostEstimate(
            flops=2 * length * channels * states,
            bytes_accessed=2 * length * channels,
            transcendentals=0,
        ),
        name="own_end_state",
    )(b, in_vmem(contrib))


def local_kernel(
    x_ref, gate_ref, b_ref, c_ref, both_ref, rise_ref, fall_ref, rows_ref,
    own_ref, factor_ref, left,
):
    length, width = x_ref.shape[1:]
    blocks = length // SPAN

    @pl.when(pl.program_id(0) == 0)
    def _():
        row, col = iotas((SPAN, SPAN))
        for k in range(blocks):
            sl = slice(k * SPAN, (k + 1) * SPAN)
            c_t = c_ref[:, sl].T
            affinity = mm(c_t, b_ref[:, sl])
            left[k, :SPAN, :SPAN] = jnp.where(row >= col, affinity, 0.0).astype(BF16)
            left[k, :SPAN, SPAN:] = c_t
            left[k, SPAN:, :SPAN] = b_ref[:, sl]
            left[k, SPAN:, SPAN:] = jnp.zeros_like(c_t)

    base = pl.program_id(0) * width
    halves = [slice(lo, lo + HALF) for lo in range(0, width, HALF)]
    places = [pl.ds(pl.multiple_of(base + lo, HALF), HALF) for lo in range(0, width, HALF)]
    both = both_ref[0]
    weighted, lift, skipped = [], [], []
    for sl in halves:
        x = x_ref[0, :, sl]
        weighted.append(x * mm(both, fall_ref[:, sl]).astype(BF16))
        half = 0.5 * gate_ref[0, :, sl].astype(F32)
        gate = (half * jnp.tanh(half) + half).astype(BF16)
        lift.append(mm(both, rise_ref[:, sl]).astype(BF16) * gate)
        skipped.append(rows_ref[0, ROWS - 1:ROWS, sl].astype(BF16) * x * gate)
    states = [None] * len(halves)
    for k in range(blocks):
        rows = slice(k * SPAN, (k + 1) * SPAN)

        def row_of(kind, sl):
            at = kind * blocks + k
            return rows_ref[0, at:at + 1, sl]

        for number, sl in enumerate(halves):
            here = weighted[number][rows]
            if k == 0:
                product = mm(left[k, :, :SPAN], here)
            else:
                entering = row_of(ENTER, sl) * states[number]
                right = jnp.concatenate([here, entering.astype(BF16)], axis=0)
                product = mm(left[k] if k < blocks - 1 else left[k, :SPAN], right)
            if k < blocks - 1:
                added = product[SPAN:]
                if k > 0:
                    added = added + entering
                states[number] = row_of(LEAVE, sl) * added
            rise = lift[number][rows]
            own_ref[rows, places[number]] = (
                rise * product[:SPAN].astype(BF16) + skipped[number][rows]
            )
            factor_ref[rows, places[number]] = rise * row_of(FIRST, sl).astype(BF16)


def local_terms(features, gate_in, b, c, both, rise, fall, rows, seq):
    _, length, channels = features.shape
    states = b.shape[0]
    width = min(512, channels)
    tile = pl.BlockSpec((1, length, width), lambda j: (seq, 0, j))
    column = pl.BlockSpec((rise.shape[0], width), lambda j: (0, j))
    return pl.pallas_call(
        local_kernel,
        grid=(channels // width,),
        in_specs=[
            tile, tile, WHOLE, WHOLE,
            pl.BlockSpec((1,) + both.shape[1:], lambda j: (seq, 0, 0)),
            column, column,
            pl.BlockSpec((1, ROWS, width), lambda j: (seq, 0, j)),
        ],
        out_specs=[WHOLE, WHOLE],
        out_shape=[pltpu.VMEM((length, channels), BF16)] * 2,
        scratch_shapes=[pltpu.VMEM((length // SPAN, SPAN + states, SPAN + states), BF16)],
        compiler_params=PARAMS,
        cost_estimate=pl.CostEstimate(
            flops=2 * length * channels * 512,
            bytes_accessed=8 * length * channels,
            transcendentals=length * channels,
        ),
        name="local_terms",
    )(features, gate_in, b, c, both, rise, fall, rows)


def joined_kernel(own_ref, factor_ref, c_ref, incoming_ref, gated_ref, square_ref):
    length, channels = own_ref.shape
    c_t = c_ref[...].T
    ones = jnp.ones((HALF, 128), BF16)
    squares = jnp.zeros((length, 128), F32)
    for lo in range(0, channels, HALF):
        sl = slice(lo, lo + HALF)
        carried = mm(c_t, incoming_ref[:, sl]).astype(BF16)
        gated = own_ref[:, sl] + factor_ref[:, sl] * carried
        gated_ref[:, sl] = gated
        squares = squares + mm(gated * gated, ones)
    for at in range(0, length, SPAN):
        square_ref[at // SPAN] = squares[at:at + SPAN].T[:1]


def joined(own, factor, c, incoming):
    length, channels = own.shape
    states = c.shape[0]
    blocks = length // SPAN
    return pl.pallas_call(
        joined_kernel,
        in_specs=[WHOLE] * 4,
        out_specs=[WHOLE] * 2,
        out_shape=[
            pltpu.VMEM((length, channels), BF16),
            pltpu.VMEM((blocks, 1, SPAN), F32),
        ],
        compiler_params=PARAMS,
        cost_estimate=pl.CostEstimate(
            flops=2 * length * channels * states,
            bytes_accessed=6 * length * channels,
            transcendentals=0,
        ),
        name="joined",
    )(in_vmem(own), in_vmem(factor), c, incoming)


def norm_kernel(all_channels, gated_ref, square_ref, gain_ref, *refs):
    out_ref = refs[-1]
    tall, channels = out_ref.shape[1:]
    base = pl.program_id(0) * tall
    for k in range(tall // SPAN):
        rows = slice(k * SPAN, (k + 1) * SPAN)
        place = pl.ds(pl.multiple_of(base + k * SPAN, SPAN), SPAN)
        total = jnp.sum(square_ref[:, k, 0], axis=0, keepdims=True)
        inverse = lax.rsqrt(total / all_channels + 1e-05)
        column = jnp.broadcast_to(inverse, (128, SPAN)).T
        for lo in range(0, channels, 128):
            sl = slice(lo, lo + 128)
            out_ref[0, rows, sl] = (
                gated_ref[place, sl].astype(F32) * column * gain_ref[:, sl]
            ).astype(BF16)


def normed(gated, squares, gain_row, all_channels, seq, seqs, before):
    length, channels = gated.shape
    shards, blocks = squares.shape[:2]
    tall = 2 * SPAN if blocks % 2 == 0 else SPAN
    operands = [in_vmem(gated), squares, gain_row]
    in_specs = [
        WHOLE,
        pl.BlockSpec((shards, tall // SPAN, 1, SPAN), lambda k: (0, k, 0, 0)),
        pl.BlockSpec(gain_row.shape, lambda k: (0, 0)),
    ]
    if before is not None:
        operands.append(before)
        in_specs.append(pl.BlockSpec(memory_space=pl.ANY))
    return pl.pallas_call(
        functools.partial(norm_kernel, all_channels),
        grid=(length // tall,),
        in_specs=in_specs,
        out_specs=pl.BlockSpec((1, tall, channels), lambda k: (seq, k, 0)),
        out_shape=jax.ShapeDtypeStruct((seqs, length, channels), BF16),
        input_output_aliases={} if before is None else {3: 0},
        compiler_params=PARAMS,
        cost_estimate=pl.CostEstimate(
            flops=2 * length * channels,
            bytes_accessed=4 * length * channels,
            transcendentals=0,
        ),
        name="normed",
    )(*operands)


def from_all(shard, axis):
    devices = lax.axis_size(axis)
    return [shard] + [
        lax.ppermute(shard, axis, [(i, (i + by) % devices) for i in range(devices)])
        for by in range(1, devices)
    ]


def body(features, gate_in, state_proj, step_size, log_decay, skip_gain, norm_gain):
    seqs, length, channels = features.shape
    heads = step_size.shape[1]
    head_dim = channels // heads
    one = np.repeat(np.eye(heads, dtype=np.float32), head_dim, axis=1)
    pair = np.concatenate([one, one], axis=0)
    none = np.zeros_like(pair)
    spread = jnp.asarray(pair, BF16)
    rise = jnp.asarray(np.concatenate([pair, none], axis=0), BF16)
    fall = jnp.asarray(np.concatenate([none, pair], axis=0), BF16)
    gain_row = norm_gain[None, :]

    def whole(pieces):
        return [jnp.concatenate([piece[s] for piece in pieces], axis=0) for s in range(seqs)]

    b_own, c_own = lax.optimization_barrier((state_proj[0], state_proj[1]))
    b = whole(from_all(b_own, "head"))
    contrib, both, rows = front(
        in_hbm(features), in_hbm(step_size), in_hbm(log_decay), skip_gain[None, :], in_hbm(spread)
    )
    c_own, contrib = lax.optimization_barrier((c_own, contrib))
    c = whole(from_all(c_own, "head"))
    own_state = [end_state(b[s], contrib, s) for s in range(seqs)]
    total_at = TOTAL * (length // SPAN)
    total = [rows[s, total_at:total_at + 1] for s in range(seqs)]
    devices = lax.axis_size("ctx")
    incoming = [None] * seqs
    sent = list(own_state)
    terms = [None] * seqs

    def pass_on(turn, s):
        return lax.ppermute(sent[s], "ctx", [(turn, turn + 1)])

    def take(received, s):
        incoming[s] = received if incoming[s] is None else incoming[s] + received
        sent[s] = (
            own_state[s].astype(F32) + total[s] * incoming[s].astype(F32)
        ).astype(BF16)

    for turn in range(devices - 1):
        received = [pass_on(turn, s) for s in range(seqs)]
        for s in range(seqs):
            if turn == 1:
                b[s], _ = lax.optimization_barrier((b[s], tuple(sent)))
                terms[s] = local_terms(
                    in_hbm(features), in_hbm(gate_in), b[s], c[s], both, rise, fall, rows, s
                )
                received[s], terms[s] = lax.optimization_barrier((received[s], terms[s]))
            take(received[s], s)
    out = None
    parts = [joined(*terms[s], c[s], incoming[s]) for s in range(seqs)]
    for s in range(seqs):
        squares = jnp.stack(from_all(parts[s][1], "head"))
        out = normed(
            parts[s][0], squares, gain_row, channels * lax.axis_size("head"), s, seqs, out
        )
    return out


def solution(mesh):
    in_specs = (
        P("groups", "ctx", "head"),
        P("groups", "ctx", "head"),
        P(None, "groups", "head", "ctx"),
        P("groups", "head", "ctx"),
        P("groups", "head", "ctx"),
        P("head"),
        P("head"),
    )
    out_specs = P("groups", "ctx", "head")
    return jax.shard_map(body, mesh=mesh, in_specs=in_specs, out_specs=out_specs, check_vma=False)
```

time: 97.9 us -> 70.2 us (0.72)
  the two profiles are of different devices: /device:TPU:2 before, /device:TPU:0 now
where the time goes in v3:
time: 70.2 us; the launch traced here: 69.2 us
  Pallas kernels  37.2 us (53%)
  starting transfers between devices  22.8 us (32%)
  waiting for transfers between devices  5.84 us (8%)
  local copies, waits for them, and re-layouts  1.71 us (2%)
  other arithmetic  1.29 us (2%)
    ppermute x12, starting transfers between devices, from_all(): lax.ppermute(shard, axis, [(i, (i + by) % devices) for i in range(devices)])  17.2 us
    pallas_call x2, Pallas kernels, local_terms(): pl.pallas_call(local_kernel, grid=(channels // width,), in_specs=[tile, t...  17 us
    pallas_call x1, Pallas kernels, front(): pl.pallas_call(front_kernel, grid=(seqs, channels // width), in_specs=[pl...  9.64 us
    ppermute x12, waiting for transfers between devices, from_all(): lax.ppermute(shard, axis, [(i, (i + by) % devices) for i in range(devices)])  5.82 us
    ppermute x6, starting transfers between devices, pass_on(): return lax.ppermute(sent[s], 'ctx', [(turn, turn + 1)])  5.55 us
    pallas_call x2, Pallas kernels, normed(): pl.pallas_call(functools.partial(norm_kernel, all_channels), grid=(length...  5.39 us
    pallas_call x2, Pallas kernels, joined(): pl.pallas_call(joined_kernel, in_specs=[WHOLE] * 4, out_specs=[WHOLE] * 2...  3.99 us
  transfers between devices with their start and end apart: 18, of which 2 were waited for; matrix products, arithmetic and copies ran while one was open for 2% of the time, Pallas kernels for 50%

profile of v3, /device:TPU:0, one launch (start us, length us, event | category | flops | bytes accessed | tf_op | source)
XLA Modules:
  0.0 69.2 jit_solution(3280841571910521618)
XLA Ops:
  0.0 1.0 %slice_bitcast_fusion = (bf16[2,32,768]{2,1,0:T(8,128)(2,1)S(1)}, bf16[2,32,768]{2,1,0:T(8,128)(2,1)S(1)}) fusion(bf16[2,2,32,768]{3,2,1,0:T(8,128)(2,1)} %param.12), kind=kLoop, calls=%fused_computation.12 | loop fusion | bytes 393216 | tf_op jit(solution)/shard_map/squeeze | solution.py:355
  1.0 5.1 %collective-permute-start.2 = (bf16[2,32,768]{2,1,0:T(8,128)(2,1)S(1)}, bf16[2,32,768]{2,1,0:T(8,128)(2,1)S(1)}, u32[]{:S(2)}, u32[]{:S(2)}) collective-permute-start(bf16[2,32,768]{2,1,0:T(8,128)(2,1)S(1)} %get-tuple-element.28), channel_id=1, source_target_pairs={{0,3},{1,0},{2,1},{3,2},{4,7},{5,4},{6,5},{7,6},{8,11},{9,8},{10,9... | collective-permute-start | bytes 294920 | tf_op jit(solution)/shard_map/ppermute | solution.py:335
  6.1 1.0 %collective-permute-start = (bf16[2,32,768]{2,1,0:T(8,128)(2,1)S(1)}, bf16[2,32,768]{2,1,0:T(8,128)(2,1)S(1)}, u32[]{:S(2)}, u32[]{:S(2)}) collective-permute-start(bf16[2,32,768]{2,1,0:T(8,128)(2,1)S(1)} %get-tuple-element.28), channel_id=1, source_target_pairs={{0,1},{1,2},{2,3},{3,0},{4,5},{5,6},{6,7},{7,4},{8,9},{9,10},{10,1... | collective-permute-start | bytes 294920 | tf_op jit(solution)/shard_map/ppermute | solution.py:335
  7.1 0.7 copy-done.3
  7.7 9.6 %front.1 = (bf16[2,768,2048]{2,1,0:T(8,128)(2,1)S(1)}, bf16[2,768,128]{2,1,0:T(8,128)(2,1)S(1)}, f32[2,32,2048]{2,1,0:T(8,128)S(1)}) custom-call(bf16[2,768,2048]{2,1,0:T(8,128)(2,1)} %x_ref.5, f32[2,32,768]{2,1,0:T(8,128)} %step_ref.1, f32[2,32,768]{2,1,0:T(8,128)} %decay_ref.1, f32[1,32]{1,0:T(1,128)S(1)} %bitcast.52, ...), custom_call_target="tpu_custom_call" | custom-call | flops 402653184 | bytes 12582912 | tf_op jit(solution)/shard_map/front/pallas_call | solution.py:112
  17.4 2.9 %collective-permute-start.9 = (bf16[2,32,768]{2,1,0:T(8,128)(2,1)S(1)}, bf16[2,32,768]{2,1,0:T(8,128)(2,1)S(1)}, u32[]{:S(2)}, u32[]{:S(2)}) collective-permute-start(bf16[2,32,768]{2,1,0:T(8,128)(2,1)S(1)} %get-tuple-element.34), channel_id=1, source_target_pairs={{0,3},{1,0},{2,1},{3,2},{4,7},{5,4},{6,5},{7,6},{8,11},{9,8},{10,9... | collective-permute-start | bytes 294920 | tf_op jit(solution)/shard_map/ppermute | solution.py:335
  20.2 1.1 %collective-permute-start.8 = (bf16[2,32,768]{2,1,0:T(8,128)(2,1)S(1)}, bf16[2,32,768]{2,1,0:T(8,128)(2,1)S(1)}, u32[]{:S(2)}, u32[]{:S(2)}) collective-permute-start(bf16[2,32,768]{2,1,0:T(8,128)(2,1)S(1)} %get-tuple-element.34), channel_id=1, source_target_pairs={{0,2},{1,3},{2,0},{3,1},{4,6},{5,7},{6,4},{7,5},{8,10},{9,11},{10,... | collective-permute-start | bytes 294920 | tf_op jit(solution)/shard_map/ppermute | solution.py:335
  21.6 0.6 own_end_state.2
  22.2 1.3 %collective-permute-start.3 = (bf16[128,2048]{1,0:T(8,128)(2,1)S(1)}, bf16[128,2048]{1,0:T(8,128)(2,1)S(1)}, u32[]{:S(2)}, u32[]{:S(2)}) collective-permute-start(bf16[128,2048]{1,0:T(8,128)(2,1)S(1)} %own_end_state.2), channel_id=1, source_target_pairs={{0,4},{1,5},{2,6},{3,7},{16,20},{17,21},{18,22},{19,23}} | collective-permute-start | bytes 1572872 | tf_op jit(solution)/shard_map/ppermute | solution.py:371
  23.5 0.6 own_end_state.3
  24.2 1.5 %collective-permute-start.5 = (bf16[128,2048]{1,0:T(8,128)(2,1)S(1)}, bf16[128,2048]{1,0:T(8,128)(2,1)S(1)}, u32[]{:S(2)}, u32[]{:S(2)}) collective-permute-start(bf16[128,2048]{1,0:T(8,128)(2,1)S(1)} %own_end_state.3), channel_id=1, source_target_pairs={{0,4},{1,5},{2,6},{3,7},{16,20},{17,21},{18,22},{19,23}} | collective-permute-start | bytes 1572872 | tf_op jit(solution)/shard_map/ppermute | solution.py:371
  25.7 3.9 %collective-permute-done.8 = bf16[2,32,768]{2,1,0:T(8,128)(2,1)S(1)} collective-permute-done((bf16[2,32,768]{2,1,0:T(8,128)(2,1)S(1)}, bf16[2,32,768]{2,1,0:T(8,128)(2,1)S(1)}, u32[]{:S(2)}, u32[]{:S(2)}) %collective-permute-start.8) | collective-permute-done | bytes 98336 | tf_op jit(solution)/shard_map/ppermute | solution.py:335
  29.6 0.2 fusion.2
  29.8 0.7 %collective-permute-start.6 = (bf16[128,2048]{1,0:T(8,128)(2,1)S(1)}, bf16[128,2048]{1,0:T(8,128)(2,1)S(1)}, u32[]{:S(2)}, u32[]{:S(2)}) collective-permute-start(bf16[128,2048]{1,0:T(8,128)(2,1)S(1)} %fusion.2), channel_id=1, source_target_pairs={{4,8},{5,9},{6,10},{7,11},{20,24},{21,25},{22,26},{23,27}} | collective-permute-start | bytes 1572872 | tf_op jit(solution)/shard_map/ppermute | solution.py:371
  30.5 0.2 fusion
  30.7 0.7 %collective-permute-start.4 = (bf16[128,2048]{1,0:T(8,128)(2,1)S(1)}, bf16[128,2048]{1,0:T(8,128)(2,1)S(1)}, u32[]{:S(2)}, u32[]{:S(2)}) collective-permute-start(bf16[128,2048]{1,0:T(8,128)(2,1)S(1)} %fusion), channel_id=1, source_target_pairs={{4,8},{5,9},{6,10},{7,11},{20,24},{21,25},{22,26},{23,27}} | collective-permute-start | bytes 1572872 | tf_op jit(solution)/shard_map/ppermute | solution.py:371
  31.4 8.5 %local_terms.2 = (bf16[768,2048]{1,0:T(8,128)(2,1)S(1)}, bf16[768,2048]{1,0:T(8,128)(2,1)S(1)}) custom-call(bf16[2,768,2048]{2,1,0:T(8,128)(2,1)} %x_ref.5, bf16[2,768,2048]{2,1,0:T(8,128)(2,1)} %gate_ref.3, bf16[128,768]{1,0:T(8,128)(2,1)S(1)} %pad_maximum_fusion.1.b_ref, bf16[128,768]{1,0:T(8,128)(2,1)S(1)} %get-tuple-element.75.c_ref, ...), custom_call_target="tpu_custom_call" | custom-call | flops 1610612736 | bytes 12582912 | tf_op jit(solution)/shard_map/local_terms/pallas_call | solution.py:226
  39.9 0.3 fusion.3
  40.2 0.7 %collective-permute-start.14 = (bf16[128,2048]{1,0:T(8,128)(2,1)S(1)}, bf16[128,2048]{1,0:T(8,128)(2,1)S(1)}, u32[]{:S(2)}, u32[]{:S(2)}) collective-permute-start(bf16[128,2048]{1,0:T(8,128)(2,1)S(1)} %get-tuple-element.53), channel_id=1, source_target_pairs={{8,12},{9,13},{10,14},{11,15},{24,28},{25,29},{26,30},{27,31}} | collective-permute-start | bytes 1572872 | tf_op jit(solution)/shard_map/ppermute | solution.py:371
  40.9 8.5 %local_terms.3 = (bf16[768,2048]{1,0:T(8,128)(2,1)S(1)}, bf16[768,2048]{1,0:T(8,128)(2,1)S(1)}) custom-call(bf16[2,768,2048]{2,1,0:T(8,128)(2,1)} %x_ref.5, bf16[2,768,2048]{2,1,0:T(8,128)(2,1)} %gate_ref.3, bf16[128,768]{1,0:T(8,128)(2,1)S(1)} %pad_maximum_fusion.b_ref, bf16[128,768]{1,0:T(8,128)(2,1)S(1)} %get-tuple-element.76.c_ref, ...), custom_call_target="tpu_custom_call" | custom-call | flops 1610612736 | bytes 12582912 | tf_op jit(solution)/shard_map/local_terms/pallas_call | solution.py:226
  49.5 0.3 fusion.1
  49.8 0.7 %collective-permute-start.10 = (bf16[128,2048]{1,0:T(8,128)(2,1)S(1)}, bf16[128,2048]{1,0:T(8,128)(2,1)S(1)}, u32[]{:S(2)}, u32[]{:S(2)}) collective-permute-start(bf16[128,2048]{1,0:T(8,128)(2,1)S(1)} %get-tuple-element.51), channel_id=1, source_target_pairs={{8,12},{9,13},{10,14},{11,15},{24,28},{25,29},{26,30},{27,31}} | collective-permute-start | bytes 1572872 | tf_op jit(solution)/shard_map/ppermute | solution.py:371
  50.6 2.0 %joined.3 = (bf16[768,2048]{1,0:T(8,128)(2,1)S(1)}, f32[6,1,128]{2,1,0:T(1,128)S(1)}) custom-call(bf16[768,2048]{1,0:T(8,128)(2,1)S(1)} %get-tuple-element.47.own_ref, bf16[768,2048]{1,0:T(8,128)(2,1)S(1)} %get-tuple-element.48.factor_ref, bf16[128,768]{1,0:T(8,128)(2,1)S(1)} %get-tuple-element.75.c_ref, bf16[128,2048]{1,0:T(8,128)(2,1)S(1)} %add.31.incoming_ref), custom_call_target="tpu_custom_call" | custom-call | flops 402653184 | bytes 9437184 | tf_op jit(solution)/shard_map/joined/pallas_call | solution.py:267
  52.6 1.3 %collective-permute-start.17 = (f32[6,1,128]{2,1,0:T(1,128)S(1)}, f32[6,1,128]{2,1,0:T(1,128)S(1)}, u32[]{:S(2)}, u32[]{:S(2)}) collective-permute-start(f32[6,1,128]{2,1,0:T(1,128)S(1)} %get-tuple-element.50), channel_id=1, source_target_pairs={{0,3},{1,0},{2,1},{3,2},{4,7},{5,4},{6,5},{7,6},{8,11},{9,8},{10,9... | collective-permute-start | bytes 9224 | tf_op jit(solution)/shard_map/ppermute | solution.py:335
  54.0 1.9 %collective-permute-start.15 = (f32[6,1,128]{2,1,0:T(1,128)S(1)}, f32[6,1,128]{2,1,0:T(1,128)S(1)}, u32[]{:S(2)}, u32[]{:S(2)}) collective-permute-start(f32[6,1,128]{2,1,0:T(1,128)S(1)} %get-tuple-element.50), channel_id=1, source_target_pairs={{0,1},{1,2},{2,3},{3,0},{4,5},{5,6},{6,7},{7,4},{8,9},{9,10},{10,1... | collective-permute-start | bytes 9224 | tf_op jit(solution)/shard_map/ppermute | solution.py:335
  56.1 2.0 %joined.2 = (bf16[768,2048]{1,0:T(8,128)(2,1)S(1)}, f32[6,1,128]{2,1,0:T(1,128)S(1)}) custom-call(bf16[768,2048]{1,0:T(8,128)(2,1)S(1)} %get-tuple-element.42.own_ref, bf16[768,2048]{1,0:T(8,128)(2,1)S(1)} %get-tuple-element.43.factor_ref, bf16[128,768]{1,0:T(8,128)(2,1)S(1)} %get-tuple-element.76.c_ref, bf16[128,2048]{1,0:T(8,128)(2,1)S(1)} %add.30.incoming_ref), custom_call_target="tpu_custom_call" | custom-call | flops 402653184 | bytes 9437184 | tf_op jit(solution)/shard_map/joined/pallas_call | solution.py:267
  58.1 1.9 %collective-permute-start.13 = (f32[6,1,128]{2,1,0:T(1,128)S(1)}, f32[6,1,128]{2,1,0:T(1,128)S(1)}, u32[]{:S(2)}, u32[]{:S(2)}) collective-permute-start(f32[6,1,128]{2,1,0:T(1,128)S(1)} %get-tuple-element.46), channel_id=1, source_target_pairs={{0,3},{1,0},{2,1},{3,2},{4,7},{5,4},{6,5},{7,6},{8,11},{9,8},{10,9... | collective-permute-start | bytes 9224 | tf_op jit(solution)/shard_map/ppermute | solution.py:335
  60.0 1.0 %collective-permute-start.12 = (f32[6,1,128]{2,1,0:T(1,128)S(1)}, f32[6,1,128]{2,1,0:T(1,128)S(1)}, u32[]{:S(2)}, u32[]{:S(2)}) collective-permute-start(f32[6,1,128]{2,1,0:T(1,128)S(1)} %get-tuple-element.46), channel_id=1, source_target_pairs={{0,2},{1,3},{2,0},{3,1},{4,6},{5,7},{6,4},{7,5},{8,10},{9,11},{10,... | collective-permute-start | bytes 9224 | tf_op jit(solution)/shard_map/ppermute | solution.py:335
  61.1 0.7 %collective-permute-start.11 = (f32[6,1,128]{2,1,0:T(1,128)S(1)}, f32[6,1,128]{2,1,0:T(1,128)S(1)}, u32[]{:S(2)}, u32[]{:S(2)}) collective-permute-start(f32[6,1,128]{2,1,0:T(1,128)S(1)} %get-tuple-element.46), channel_id=1, source_target_pairs={{0,1},{1,2},{2,3},{3,0},{4,5},{5,6},{6,7},{7,4},{8,9},{9,10},{10,1... | collective-permute-start | bytes 9224 | tf_op jit(solution)/shard_map/ppermute | solution.py:335
  61.8 2.7 %normed.2.refs_0_ = bf16[2,768,2048]{2,1,0:T(8,128)(2,1)} custom-call(bf16[768,2048]{1,0:T(8,128)(2,1)S(1)} %get-tuple-element.49.gated_ref, f32[4,6,1,128]{3,2,1,0:T(1,128)S(1)} %pad_maximum_fusion.5.square_ref, f32[1,2048]{1,0:T(1,128)S(1)} %bitcast.48), custom_call_target="tpu_custom_call" | custom-call | flops 3145728 | bytes 6291456 | tf_op jit(solution)/shard_map/normed/pallas_call | solution.py:315
  64.5 1.9 %collective-permute-done.11 = f32[6,1,128]{2,1,0:T(1,128)S(1)} collective-permute-done((f32[6,1,128]{2,1,0:T(1,128)S(1)}, f32[6,1,128]{2,1,0:T(1,128)S(1)}, u32[]{:S(2)}, u32[]{:S(2)}) %collective-permute-start.11) | collective-permute-done | bytes 3104 | tf_op jit(solution)/shard_map/ppermute | solution.py:335
  66.5 2.7 %normed.3 = bf16[2,768,2048]{2,1,0:T(8,128)(2,1)} custom-call(bf16[768,2048]{1,0:T(8,128)(2,1)S(1)} %get-tuple-element.45.gated_ref, f32[4,6,1,128]{3,2,1,0:T(1,128)S(1)} %pad_maximum_fusion.4.square_ref, f32[1,2048]{1,0:T(1,128)S(1)} %bitcast.49, bf16[2,768,2048]{2,1,0:T(8,128)(2,1)} %normed.2.refs_0_), custom_call_target="tpu_custom_call", output_to_operand_aliasing={{}: (3, {})} | custom-call | flops 3145728 | bytes 6291456 | tf_op jit(solution)/shard_map/normed/pallas_call | solution.py:315
  (42 shorter events, 0.6 us)
Async XLA Ops:
  1.0 20.5 %collective-permute-start.2 = (bf16[2,32,768]{2,1,0:T(8,128)(2,1)S(1)}, bf16[2,32,768]{2,1,0:T(8,128)(2,1)S(1)}, u32[]{:S(2)}, u32[]{:S(2)}) collective-permute-start(bf16[2,32,768]{2,1,0:T(8,128)(2,1)S(1)} %get-tuple-element.28), channel_id=1, source_target_pairs={{0,3},{1,0},{2,1},{3,2},{4,7},{5,4},{6,5},{7,6},{8,11},{9,8},{10,9... | collective-permute-start | bytes 294920 | tf_op jit(solution)/shard_map/ppermute | solution.py:335
  6.1 15.4 %collective-permute-start.1 = (bf16[2,32,768]{2,1,0:T(8,128)(2,1)S(1)}, bf16[2,32,768]{2,1,0:T(8,128)(2,1)S(1)}, u32[]{:S(2)}, u32[]{:S(2)}) collective-permute-start(bf16[2,32,768]{2,1,0:T(8,128)(2,1)S(1)} %get-tuple-element.28), channel_id=1, source_target_pairs={{0,2},{1,3},{2,0},{3,1},{4,6},{5,7},{6,4},{7,5},{8,10},{9,11},{10,... | collective-permute-start | bytes 294920 | tf_op jit(solution)/shard_map/ppermute | solution.py:335
  6.1 15.5 %collective-permute-start = (bf16[2,32,768]{2,1,0:T(8,128)(2,1)S(1)}, bf16[2,32,768]{2,1,0:T(8,128)(2,1)S(1)}, u32[]{:S(2)}, u32[]{:S(2)}) collective-permute-start(bf16[2,32,768]{2,1,0:T(8,128)(2,1)S(1)} %get-tuple-element.28), channel_id=1, source_target_pairs={{0,1},{1,2},{2,3},{3,0},{4,5},{5,6},{6,7},{7,4},{8,9},{9,10},{10,1... | collective-permute-start | bytes 294920 | tf_op jit(solution)/shard_map/ppermute | solution.py:335
  7.1 0.7 copy-start.3
  17.4 8.3 %collective-permute-start.9 = (bf16[2,32,768]{2,1,0:T(8,128)(2,1)S(1)}, bf16[2,32,768]{2,1,0:T(8,128)(2,1)S(1)}, u32[]{:S(2)}, u32[]{:S(2)}) collective-permute-start(bf16[2,32,768]{2,1,0:T(8,128)(2,1)S(1)} %get-tuple-element.34), channel_id=1, source_target_pairs={{0,3},{1,0},{2,1},{3,2},{4,7},{5,4},{6,5},{7,6},{8,11},{9,8},{10,9... | collective-permute-start | bytes 294920 | tf_op jit(solution)/shard_map/ppermute | solution.py:335
  20.2 9.3 %collective-permute-start.8 = (bf16[2,32,768]{2,1,0:T(8,128)(2,1)S(1)}, bf16[2,32,768]{2,1,0:T(8,128)(2,1)S(1)}, u32[]{:S(2)}, u32[]{:S(2)}) collective-permute-start(bf16[2,32,768]{2,1,0:T(8,128)(2,1)S(1)} %get-tuple-element.34), channel_id=1, source_target_pairs={{0,2},{1,3},{2,0},{3,1},{4,6},{5,7},{6,4},{7,5},{8,10},{9,11},{10,... | collective-permute-start | bytes 294920 | tf_op jit(solution)/shard_map/ppermute | solution.py:335
  21.4 8.1 %collective-permute-start.7 = (bf16[2,32,768]{2,1,0:T(8,128)(2,1)S(1)}, bf16[2,32,768]{2,1,0:T(8,128)(2,1)S(1)}, u32[]{:S(2)}, u32[]{:S(2)}) collective-permute-start(bf16[2,32,768]{2,1,0:T(8,128)(2,1)S(1)} %get-tuple-element.34), channel_id=1, source_target_pairs={{0,1},{1,2},{2,3},{3,0},{4,5},{5,6},{6,7},{7,4},{8,9},{9,10},{10,1... | collective-permute-start | bytes 294920 | tf_op jit(solution)/shard_map/ppermute | solution.py:335
  22.2 8.3 %collective-permute-start.3 = (bf16[128,2048]{1,0:T(8,128)(2,1)S(1)}, bf16[128,2048]{1,0:T(8,128)(2,1)S(1)}, u32[]{:S(2)}, u32[]{:S(2)}) collective-permute-start(bf16[128,2048]{1,0:T(8,128)(2,1)S(1)} %own_end_state.2), channel_id=1, source_target_pairs={{0,4},{1,5},{2,6},{3,7},{16,20},{17,21},{18,22},{19,23}} | collective-permute-start | bytes 1572872 | tf_op jit(solution)/shard_map/ppermute | solution.py:371
  24.1 7.2 %copy-start = (bf16[128,2048]{1,0:T(8,128)(2,1)S(1)}, bf16[128,2048]{1,0:T(8,128)(2,1)}, u32[]{:S(2)}) copy-start(bf16[128,2048]{1,0:T(8,128)(2,1)} %constant.8.clone.fall_ref) | copy-start | bytes 1572868
  24.2 7.2 %copy-start.1 = (bf16[128,2048]{1,0:T(8,128)(2,1)S(1)}, bf16[128,2048]{1,0:T(8,128)(2,1)}, u32[]{:S(2)}) copy-start(bf16[128,2048]{1,0:T(8,128)(2,1)} %constant.7.clone.rise_ref) | copy-start | bytes 1572868
  24.2 5.4 %collective-permute-start.5 = (bf16[128,2048]{1,0:T(8,128)(2,1)S(1)}, bf16[128,2048]{1,0:T(8,128)(2,1)S(1)}, u32[]{:S(2)}, u32[]{:S(2)}) collective-permute-start(bf16[128,2048]{1,0:T(8,128)(2,1)S(1)} %own_end_state.3), channel_id=1, source_target_pairs={{0,4},{1,5},{2,6},{3,7},{16,20},{17,21},{18,22},{19,23}} | collective-permute-start | bytes 1572872 | tf_op jit(solution)/shard_map/ppermute | solution.py:371
  29.8 10.1 %collective-permute-start.6 = (bf16[128,2048]{1,0:T(8,128)(2,1)S(1)}, bf16[128,2048]{1,0:T(8,128)(2,1)S(1)}, u32[]{:S(2)}, u32[]{:S(2)}) collective-permute-start(bf16[128,2048]{1,0:T(8,128)(2,1)S(1)} %fusion.2), channel_id=1, source_target_pairs={{4,8},{5,9},{6,10},{7,11},{20,24},{21,25},{22,26},{23,27}} | collective-permute-start | bytes 1572872 | tf_op jit(solution)/shard_map/ppermute | solution.py:371
  30.7 18.8 %collective-permute-start.4 = (bf16[128,2048]{1,0:T(8,128)(2,1)S(1)}, bf16[128,2048]{1,0:T(8,128)(2,1)S(1)}, u32[]{:S(2)}, u32[]{:S(2)}) collective-permute-start(bf16[128,2048]{1,0:T(8,128)(2,1)S(1)} %fusion), channel_id=1, source_target_pairs={{4,8},{5,9},{6,10},{7,11},{20,24},{21,25},{22,26},{23,27}} | collective-permute-start | bytes 1572872 | tf_op jit(solution)/shard_map/ppermute | solution.py:371
  40.2 10.3 %collective-permute-start.14 = (bf16[128,2048]{1,0:T(8,128)(2,1)S(1)}, bf16[128,2048]{1,0:T(8,128)(2,1)S(1)}, u32[]{:S(2)}, u32[]{:S(2)}) collective-permute-start(bf16[128,2048]{1,0:T(8,128)(2,1)S(1)} %get-tuple-element.53), channel_id=1, source_target_pairs={{8,12},{9,13},{10,14},{11,15},{24,28},{25,29},{26,30},{27,31}} | collective-permute-start | bytes 1572872 | tf_op jit(solution)/shard_map/ppermute | solution.py:371
  49.8 6.2 %collective-permute-start.10 = (bf16[128,2048]{1,0:T(8,128)(2,1)S(1)}, bf16[128,2048]{1,0:T(8,128)(2,1)S(1)}, u32[]{:S(2)}, u32[]{:S(2)}) collective-permute-start(bf16[128,2048]{1,0:T(8,128)(2,1)S(1)} %get-tuple-element.51), channel_id=1, source_target_pairs={{8,12},{9,13},{10,14},{11,15},{24,28},{25,29},{26,30},{27,31}} | collective-permute-start | bytes 1572872 | tf_op jit(solution)/shard_map/ppermute | solution.py:371
  52.6 8.5 %collective-permute-start.17 = (f32[6,1,128]{2,1,0:T(1,128)S(1)}, f32[6,1,128]{2,1,0:T(1,128)S(1)}, u32[]{:S(2)}, u32[]{:S(2)}) collective-permute-start(f32[6,1,128]{2,1,0:T(1,128)S(1)} %get-tuple-element.50), channel_id=1, source_target_pairs={{0,3},{1,0},{2,1},{3,2},{4,7},{5,4},{6,5},{7,6},{8,11},{9,8},{10,9... | collective-permute-start | bytes 9224 | tf_op jit(solution)/shard_map/ppermute | solution.py:335
  54.0 7.9 %collective-permute-start.16 = (f32[6,1,128]{2,1,0:T(1,128)S(1)}, f32[6,1,128]{2,1,0:T(1,128)S(1)}, u32[]{:S(2)}, u32[]{:S(2)}) collective-permute-start(f32[6,1,128]{2,1,0:T(1,128)S(1)} %get-tuple-element.50), channel_id=1, source_target_pairs={{0,2},{1,3},{2,0},{3,1},{4,6},{5,7},{6,4},{7,5},{8,10},{9,11},{10,... | collective-permute-start | bytes 9224 | tf_op jit(solution)/shard_map/ppermute | solution.py:335
  54.0 7.8 %collective-permute-start.15 = (f32[6,1,128]{2,1,0:T(1,128)S(1)}, f32[6,1,128]{2,1,0:T(1,128)S(1)}, u32[]{:S(2)}, u32[]{:S(2)}) collective-permute-start(f32[6,1,128]{2,1,0:T(1,128)S(1)} %get-tuple-element.50), channel_id=1, source_target_pairs={{0,1},{1,2},{2,3},{3,0},{4,5},{5,6},{6,7},{7,4},{8,9},{9,10},{10,1... | collective-permute-start | bytes 9224 | tf_op jit(solution)/shard_map/ppermute | solution.py:335
  56.1 5.7 %copy-start.2 = (f32[2048]{0:T(1024)S(1)}, f32[2048]{0:T(1024)}, u32[]{:S(2)}) copy-start(f32[2048]{0:T(1024)} %param.16) | copy-start | bytes 24580
  58.1 6.4 %collective-permute-start.13 = (f32[6,1,128]{2,1,0:T(1,128)S(1)}, f32[6,1,128]{2,1,0:T(1,128)S(1)}, u32[]{:S(2)}, u32[]{:S(2)}) collective-permute-start(f32[6,1,128]{2,1,0:T(1,128)S(1)} %get-tuple-element.46), channel_id=1, source_target_pairs={{0,3},{1,0},{2,1},{3,2},{4,7},{5,4},{6,5},{7,6},{8,11},{9,8},{10,9... | collective-permute-start | bytes 9224 | tf_op jit(solution)/shard_map/ppermute | solution.py:335
  60.0 4.5 %collective-permute-start.12 = (f32[6,1,128]{2,1,0:T(1,128)S(1)}, f32[6,1,128]{2,1,0:T(1,128)S(1)}, u32[]{:S(2)}, u32[]{:S(2)}) collective-permute-start(f32[6,1,128]{2,1,0:T(1,128)S(1)} %get-tuple-element.46), channel_id=1, source_target_pairs={{0,2},{1,3},{2,0},{3,1},{4,6},{5,7},{6,4},{7,5},{8,10},{9,11},{10,... | collective-permute-start | bytes 9224 | tf_op jit(solution)/shard_map/ppermute | solution.py:335
  61.1 5.4 %collective-permute-start.11 = (f32[6,1,128]{2,1,0:T(1,128)S(1)}, f32[6,1,128]{2,1,0:T(1,128)S(1)}, u32[]{:S(2)}, u32[]{:S(2)}) collective-permute-start(f32[6,1,128]{2,1,0:T(1,128)S(1)} %get-tuple-element.46), channel_id=1, source_target_pairs={{0,1},{1,2},{2,3},{3,0},{4,5},{5,6},{6,7},{7,4},{8,9},{9,10},{10,1... | collective-permute-start | bytes 9224 | tf_op jit(solution)/shard_map/ppermute | solution.py:335

commit v4 on v3

v4 whole, which is shorter than its diff:
```python
import functools

import jax
import jax.numpy as jnp
import numpy as np
from jax import lax
from jax.experimental import pallas as pl
from jax.experimental.pallas import tpu as pltpu
from jax.sharding import PartitionSpec as P

SPAN = 128
HALF = 256
F32 = jnp.float32
BF16 = jnp.bfloat16
VMEM_LIMIT = 20 * 1024 * 1024
PARAMS = pltpu.CompilerParams(vmem_limit_bytes=VMEM_LIMIT)
ENTER, LEAVE, FIRST, TOTAL = range(4)
ROWS = 32
WHOLE = pl.BlockSpec(memory_space=pltpu.VMEM)
ANYWHERE = pl.BlockSpec(memory_space=pl.ANY)


def in_vmem(array):
    return pltpu.with_memory_space_constraint(array, pltpu.VMEM)


def in_hbm(array):
    return pltpu.with_memory_space_constraint(array, pltpu.HBM)


def mm(a, b):
    return jnp.dot(a, b, preferred_element_type=F32)


def exact_dot(a, b):
    return jnp.dot(a, b, precision=lax.Precision.HIGHEST, preferred_element_type=F32)


def iotas(shape):
    return (
        lax.broadcasted_iota(jnp.int32, shape, 0),
        lax.broadcasted_iota(jnp.int32, shape, 1),
    )


def two_parts(v):
    high = v.astype(BF16).astype(F32)
    return [high, v - high]


def upright(parts):
    return jnp.concatenate(parts, axis=0).T.astype(BF16)


def fill_tables(step_ref, decay_ref, skip_ref, spread, both_ref, rows_ref):
    seqs, heads, length = decay_ref.shape
    blocks = length // SPAN
    at, lane = iotas((length, SPAN))
    kind, block = lane // blocks, lane % blocks
    first, mid, end = block * SPAN, block * SPAN + SPAN // 2, block * SPAN + SPAN
    chosen = (
        ((kind == ENTER) & (at >= first) & (at < mid))
        | ((kind == LEAVE) & (at >= mid) & (at < end))
        | ((kind == FIRST) & (at < mid))
        | (kind == TOTAL)
    )
    chosen = jnp.where(chosen, 1.0, 0.0).astype(F32)
    row, col = iotas((SPAN, SPAN))
    until = jnp.where(row <= col, 1.0, 0.0).astype(F32)
    skip = jnp.broadcast_to(skip_ref[...], (8, heads))
    skip_row = sum(mm(part.astype(BF16), spread[:heads]) for part in two_parts(skip))
    for s in range(seqs):
        exponent = exact_dot(decay_ref[s], chosen)
        per_block = upright(two_parts(jnp.exp(exponent)))
        rows_ref[s] = mm(per_block, spread)[:ROWS]
        rows_ref[s, ROWS - 1:ROWS] = skip_row[:1]
        for k in range(blocks):
            sl = slice(k * SPAN, (k + 1) * SPAN)
            summed = exact_dot(decay_ref[s, :, sl], until)
            middle = exponent[:, ENTER * blocks + k:ENTER * blocks + k + 1]
            rise = jnp.exp(summed - middle)
            fall = step_ref[s, :, sl] * jnp.exp(middle - summed)
            both_ref[s, sl, :] = upright(two_parts(rise) + two_parts(fall))


def front_kernel(
    x_hbm, step_ref, decay_ref, skip_ref, bands_hbm,
    x_ref, weighted_ref, both_ref, rows_ref, bands, sems,
):
    seqs, length, channels = x_ref.shape
    blocks = length // SPAN
    heads = decay_ref.shape[1]
    band_copy = pltpu.make_async_copy(bands_hbm, bands, sems.at[seqs * blocks])
    band_copy.start()
    copies = []
    for s in range(seqs):
        for k in range(blocks):
            place = (s, pl.ds(k * SPAN, SPAN))
            copies.append(
                pltpu.make_async_copy(x_hbm.at[place], x_ref.at[place], sems.at[s * blocks + k])
            )
            copies[-1].start()
    band_copy.wait()
    fill_tables(
        step_ref, decay_ref, skip_ref, bands[2 * heads:4 * heads], both_ref, rows_ref
    )
    for s in range(seqs):
        for k in range(blocks):
            rows = slice(k * SPAN, (k + 1) * SPAN)
            copies[s * blocks + k].wait()
            both = both_ref[s, rows]
            for lo in range(0, channels, HALF):
                sl = slice(lo, lo + HALF)
                wide = mm(both, bands[:4 * heads, sl]).astype(BF16)
                weighted_ref[s, rows, sl] = x_ref[s, rows, sl] * wide


def front(features, step_size, log_decay, skip, bands):
    seqs, length, channels = features.shape
    heads = step_size.shape[1]
    return pl.pallas_call(
        front_kernel,
        in_specs=[ANYWHERE, WHOLE, WHOLE, WHOLE, ANYWHERE],
        out_specs=[WHOLE] * 4,
        out_shape=[
            pltpu.VMEM(features.shape, BF16),
            pltpu.VMEM(features.shape, BF16),
            pltpu.VMEM((seqs, length, 4 * heads), BF16),
            pltpu.VMEM((seqs, ROWS, channels), F32),
        ],
        scratch_shapes=[
            pltpu.VMEM(bands.shape, BF16),
            pltpu.SemaphoreType.DMA((seqs * (length // SPAN) + 1,)),
        ],
        compiler_params=PARAMS,
        cost_estimate=pl.CostEstimate(
            flops=2 * seqs * length * channels * 64,
            bytes_accessed=4 * seqs * length * channels,
            transcendentals=0,
        ),
        name="front",
    )(features, step_size, log_decay, skip, bands)


def state_kernel(seq, b_ref, weighted_ref, rows_ref, entering_ref, state_ref):
    length = weighted_ref.shape[1]
    channels = state_ref.shape[1]
    blocks = length // SPAN
    for lo in range(0, channels, HALF):
        sl = slice(lo, lo + HALF)
        state = None
        for k in range(blocks):
            rows = slice(k * SPAN, (k + 1) * SPAN)
            added = mm(b_ref[:, rows], weighted_ref[seq, rows, sl])
            if k > 0:
                at = ENTER * blocks + k
                entering = rows_ref[seq, at:at + 1, sl] * state
                entering_ref[k - 1, :, sl] = entering.astype(BF16)
                added = added + entering
            at = LEAVE * blocks + k
            state = rows_ref[seq, at:at + 1, sl] * added
        state_ref[:, sl] = state.astype(BF16)


def end_state(b, weighted, rows, seq):
    states, length = b.shape
    channels = weighted.shape[2]
    return pl.pallas_call(
        functools.partial(state_kernel, seq),
        in_specs=[WHOLE] * 3,
        out_specs=[WHOLE] * 2,
        out_shape=[
            pltpu.VMEM((length // SPAN - 1, states, channels), BF16),
            pltpu.VMEM((states, channels), BF16),
        ],
        compiler_params=PARAMS,
        cost_estimate=pl.CostEstimate(
            flops=2 * length * channels * states,
            bytes_accessed=2 * length * channels,
            transcendentals=0,
        ),
        name="own_states",
    )(b, in_vmem(weighted), in_vmem(rows))


def local_kernel(
    seq, gate_hbm, x_ref, weighted_ref, entering_ref, b_ref, c_ref, both_ref, bands_ref, rows_ref,
    own_ref, factor_ref, gates, sems,
):
    length, channels = own_ref.shape
    blocks = length // SPAN
    heads4 = both_ref.shape[2]
    copies = []
    for k in range(blocks):
        rows = pl.ds(k * SPAN, SPAN)
        copies.append(
            pltpu.make_async_copy(gate_hbm.at[seq, rows], gates.at[rows], sems.at[k])
        )
        copies[-1].start()
    row, col = iotas((SPAN, SPAN))
    for k in range(blocks):
        rows = slice(k * SPAN, (k + 1) * SPAN)
        c_t = c_ref[:, rows].T
        affinity = mm(c_t, b_ref[:, rows])
        left = jnp.where(row >= col, affinity, 0.0).astype(BF16)
        if k > 0:
            left = jnp.concatenate([left, c_t], axis=1)
        both = both_ref[seq, rows]
        copies[k].wait()
        at = FIRST * blocks + k
        for lo in range(0, channels, HALF):
            sl = slice(lo, lo + HALF)
            right = weighted_ref[seq, rows, sl]
            if k > 0:
                right = jnp.concatenate([right, entering_ref[k - 1, :, sl]], axis=0)
            mixed = mm(left, right).astype(BF16)
            half = 0.5 * gates[rows, sl].astype(F32)
            gate = (half * jnp.tanh(half) + half).astype(BF16)
            rise = mm(both, bands_ref[heads4 // 2:heads4 // 2 + heads4, sl]).astype(BF16) * gate
            skip = rows_ref[seq, ROWS - 1:ROWS, sl].astype(BF16) * x_ref[seq, rows, sl]
            own_ref[rows, sl] = rise * mixed + skip * gate
            factor_ref[rows, sl] = rise * rows_ref[seq, at:at + 1, sl].astype(BF16)


def local_terms(gate_in, x, weighted, entering, b, c, both, bands, rows, seq):
    _, length, channels = gate_in.shape
    return pl.pallas_call(
        functools.partial(local_kernel, seq),
        in_specs=[ANYWHERE] + [WHOLE] * 8,
        out_specs=[WHOLE, WHOLE],
        out_shape=[pltpu.VMEM((length, channels), BF16)] * 2,
        scratch_shapes=[
            pltpu.VMEM((length, channels), BF16),
            pltpu.SemaphoreType.DMA((length // SPAN,)),
        ],
        compiler_params=PARAMS,
        cost_estimate=pl.CostEstimate(
            flops=2 * length * channels * 512,
            bytes_accessed=8 * length * channels,
            transcendentals=length * channels,
        ),
        name="local_terms",
    )(
        gate_in, in_vmem(x), in_vmem(weighted), in_vmem(entering), b, c, in_vmem(both), bands,
        in_vmem(rows),
    )


def joined_kernel(own_ref, factor_ref, c_ref, incoming_ref, gated_ref, square_ref):
    length, channels = own_ref.shape
    for at in range(0, length, SPAN):
        rows = slice(at, at + SPAN)
        c_t = c_ref[:, rows].T
        squares = jnp.zeros((SPAN, 128), F32)
        for lo in range(0, channels, HALF):
            sl = slice(lo, lo + HALF)
            carried = mm(c_t, incoming_ref[:, sl]).astype(BF16)
            gated = own_ref[rows, sl] + factor_ref[rows, sl] * carried
            gated_ref[rows, sl] = gated
            power = gated * gated
            pair = sum(power[:, left:left + 128] for left in range(0, HALF, 128))
            squares = squares + pair.astype(F32)
        square_ref[at // SPAN] = jnp.sum(squares.T, axis=0, keepdims=True)


def joined(own, factor, c, incoming):
    length, channels = own.shape
    states = c.shape[0]
    blocks = length // SPAN
    return pl.pallas_call(
        joined_kernel,
        in_specs=[WHOLE] * 4,
        out_specs=[WHOLE] * 2,
        out_shape=[
            pltpu.VMEM((length, channels), BF16),
            pltpu.VMEM((blocks, 1, SPAN), F32),
        ],
        compiler_params=PARAMS,
        cost_estimate=pl.CostEstimate(
            flops=2 * length * channels * states,
            bytes_accessed=6 * length * channels,
            transcendentals=0,
        ),
        name="joined",
    )(in_vmem(own), in_vmem(factor), c, incoming)


def norm_kernel(all_channels, seq, gated_ref, square_ref, gain_ref, *refs):
    out_hbm, staged, sems = refs[-3:]
    length, channels = gated_ref.shape
    copies = []
    for k in range(length // SPAN):
        rows = slice(k * SPAN, (k + 1) * SPAN)
        total = jnp.sum(square_ref[:, k, 0], axis=0, keepdims=True)
        inverse = lax.rsqrt(total / all_channels + 1e-05)
        column = jnp.broadcast_to(inverse, (128, SPAN)).T
        for lo in range(0, channels, 128):
            sl = slice(lo, lo + 128)
            staged[rows, sl] = (
                gated_ref[rows, sl].astype(F32) * column * gain_ref[:, sl]
            ).astype(BF16)
        place = pl.ds(k * SPAN, SPAN)
        copies.append(
            pltpu.make_async_copy(staged.at[place], out_hbm.at[seq, place], sems.at[k])
        )
        copies[-1].start()
    for copy in copies:
        copy.wait()


def normed(gated, squares, gain_row, all_channels, seq, seqs, before):
    length, channels = gated.shape
    operands = [in_vmem(gated), squares, gain_row]
    in_specs = [WHOLE] * 3
    if before is not None:
        operands.append(before)
        in_specs.append(ANYWHERE)
    return pl.pallas_call(
        functools.partial(norm_kernel, all_channels, seq),
        in_specs=in_specs,
        out_specs=ANYWHERE,
        out_shape=jax.ShapeDtypeStruct((seqs, length, channels), BF16),
        input_output_aliases={} if before is None else {3: 0},
        scratch_shapes=[
            pltpu.VMEM((length, channels), BF16),
            pltpu.SemaphoreType.DMA((length // SPAN,)),
        ],
        compiler_params=PARAMS,
        cost_estimate=pl.CostEstimate(
            flops=2 * length * channels,
            bytes_accessed=4 * length * channels,
            transcendentals=0,
        ),
        name="normed",
    )(*operands)


def from_all(shard, axis):
    devices = lax.axis_size(axis)
    return [shard] + [
        lax.ppermute(shard, axis, [(i, (i + by) % devices) for i in range(devices)])
        for by in range(1, devices)
    ]


def at_once(shard, axis):
    devices = lax.axis_size(axis)
    return lax.all_to_all(jnp.broadcast_to(shard, (devices,) + shard.shape), axis, 0, 0)


def body(features, gate_in, state_proj, step_size, log_decay, skip_gain, norm_gain):
    seqs, length, channels = features.shape
    heads = step_size.shape[1]
    pair = np.repeat(np.concatenate([np.eye(heads)] * 2), channels // heads, axis=1)
    bands = jnp.asarray(np.concatenate([0 * pair, pair, 0 * pair]), BF16)
    gain_row = norm_gain[None, :]

    def whole(pieces):
        return [jnp.concatenate([piece[s] for piece in pieces], axis=0) for s in range(seqs)]

    b_own, c_own = lax.optimization_barrier((state_proj[0], state_proj[1]))
    b = whole(from_all(b_own, "head"))
    x, weighted, both, rows = front(
        in_hbm(features), in_hbm(step_size), in_hbm(log_decay), in_hbm(skip_gain[None, :]),
        in_hbm(bands),
    )
    c_own, weighted = lax.optimization_barrier((c_own, weighted))
    c = from_all(c_own, "head")
    entering, sent = zip(*[end_state(b[s], weighted, rows, s) for s in range(seqs)])
    own_state, sent = list(sent), list(sent)
    total_at = TOTAL * (length // SPAN)
    total = [rows[s, total_at:total_at + 1] for s in range(seqs)]
    devices = lax.axis_size("ctx")
    incoming = [None] * seqs
    terms = [None] * seqs

    def pass_on(turn, s):
        return lax.ppermute(sent[s], "ctx", [(turn, turn + 1)])

    def take(received, s):
        incoming[s] = received if incoming[s] is None else incoming[s] + received
        sent[s] = (
            own_state[s].astype(F32) + total[s] * incoming[s].astype(F32)
        ).astype(BF16)
        if s > 0:
            sent[s], _ = lax.optimization_barrier((sent[s], sent[s - 1]))

    for turn in range(devices - 1):
        received = [pass_on(turn, s) for s in range(seqs)]
        if turn == 1:
            c, _ = lax.optimization_barrier((c, tuple(sent)))
            c = whole(c)
        for s in range(seqs):
            if turn == 1:
                if s > 0:
                    c[s], _ = lax.optimization_barrier((c[s], sent[s - 1]))
                terms[s] = local_terms(
                    in_hbm(gate_in), x, weighted, entering[s], b[s], c[s], both, bands, rows, s
                )
                received[s], terms[s] = lax.optimization_barrier((received[s], terms[s]))
            take(received[s], s)
    out = None
    parts = [joined(*terms[s], c[s], incoming[s]) for s in range(seqs)]
    for s in range(seqs):
        squares = at_once(parts[s][1], "head")
        out = normed(
            parts[s][0], squares, gain_row, channels * lax.axis_size("head"), s, seqs, out
        )
    return out


def solution(mesh):
    in_specs = (
        P("groups", "ctx", "head"),
        P("groups", "ctx", "head"),
        P(None, "groups", "head", "ctx"),
        P("groups", "head", "ctx"),
        P("groups", "head", "ctx"),
        P("head"),
        P("head"),
    )
    out_specs = P("groups", "ctx", "head")
    return jax.shard_map(body, mesh=mesh, in_specs=in_specs, out_specs=out_specs, check_vma=False)
```

time: 70.2 us -> 67.6 us (0.963)
  Pallas kernels: 37.2 us -> 26.4 us
  local copies, waits for them, and re-layouts: 1.71 us -> 9.63 us
  waiting for transfers between devices: 5.84 us -> 3.59 us
  starting transfers between devices: 22.8 us -> 25 us
    pallas_call x7, Pallas kernels: 33.2 us -> 23.4 us  [the longest x2 9.28 us: local_terms(): pl.pallas_call(functools.partial(local_kernel, seq), in_specs=[ANYWHERE]...]
    all_to_all x0 -> x2, starting transfers between devices: none -> 8.37 us  [at_once(): lax.all_to_all(jnp.broadcast_to(shard, (devices,) + shard.shape), axis, 0...]
    unnamed x8 -> x18, local copies, waits for them, and re-layouts: 0.67 us -> 7.38 us
    ppermute x12 -> x6, starting transfers between devices: 17.2 us -> 10.9 us  [from_all(): lax.ppermute(shard, axis, [(i, (i + by) % devices) for i in range(devices)])]
    ppermute x12 -> x6, waiting for transfers between devices: 5.82 us -> 1.15 us  [from_all(): lax.ppermute(shard, axis, [(i, (i + by) % devices) for i in range(devices)])]
    all_to_all x0 -> x2, waiting for transfers between devices: none -> 1.84 us  [at_once(): lax.all_to_all(jnp.broadcast_to(shard, (devices,) + shard.shape), axis, 0...]
    broadcast_in_dim x0 -> x2, local copies, waits for them, and re-layouts: none -> 1.21 us  [at_once(): jnp.broadcast_to(shard, (devices,) + shard.shape)]
    pallas_call x2, Pallas kernels: 3.99 us -> 2.98 us  [joined(): pl.pallas_call(joined_kernel, in_specs=[WHOLE] * 4, out_specs=[WHOLE] * 2...]
  transfers between devices with their start and end apart: 18 -> 14, of which waited for: 2 -> 4; matrix products, arithmetic and copies ran while one was open for 2% -> 3% of each run, Pallas kernels for 50% -> 35%
where the time goes in v4:
time: 67.6 us; the launch traced here: 66.4 us
  Pallas kernels  26.4 us (39%)
  starting transfers between devices  25 us (37%)
  local copies, waits for them, and re-layouts  9.63 us (14%)
  waiting for transfers between devices  3.59 us (5%)
  other arithmetic  1.25 us (2%)
    ppermute x6, starting transfers between devices, from_all(): lax.ppermute(shard, axis, [(i, (i + by) % devices) for i in range(devices)])  10.9 us
    pallas_call x2, Pallas kernels, local_terms(): pl.pallas_call(functools.partial(local_kernel, seq), in_specs=[ANYWHERE]...  9.28 us
    all_to_all x2, starting transfers between devices, at_once(): lax.all_to_all(jnp.broadcast_to(shard, (devices,) + shard.shape), axis, 0...  8.37 us
    pallas_call x1, Pallas kernels, front(): pl.pallas_call(front_kernel, in_specs=[ANYWHERE, WHOLE, WHOLE, WHOLE, ANY...  8.01 us
    unnamed x18, local copies, waits for them, and re-layouts  7.38 us
    ppermute x6, starting transfers between devices, pass_on(): return lax.ppermute(sent[s], 'ctx', [(turn, turn + 1)])  5.73 us
    pallas_call x2, Pallas kernels, normed(): pl.pallas_call(functools.partial(norm_kernel, all_channels, seq), in_spec...  4.06 us
    pallas_call x2, Pallas kernels, joined(): pl.pallas_call(joined_kernel, in_specs=[WHOLE] * 4, out_specs=[WHOLE] * 2...  2.98 us
  transfers between devices with their start and end apart: 14, of which 4 were waited for; matrix products, arithmetic and copies ran while one was open for 3% of the time, Pallas kernels for 35%

profile of v4, /device:TPU:0, one launch (start us, length us, event | category | flops | bytes accessed | tf_op | source)
XLA Modules:
  0.0 66.4 jit_solution(15411341381080694951)
XLA Ops:
  0.0 1.0 %slice_bitcast_fusion = (bf16[2,32,768]{2,1,0:T(8,128)(2,1)S(1)}, bf16[2,32,768]{2,1,0:T(8,128)(2,1)S(1)}) fusion(bf16[2,2,32,768]{3,2,1,0:T(8,128)(2,1)} %param.10), kind=kLoop, calls=%fused_computation.12 | loop fusion | bytes 393216 | tf_op jit(solution)/shard_map/squeeze | solution.py:361
  1.0 3.1 %collective-permute-start = (bf16[2,32,768]{2,1,0:T(8,128)(2,1)S(1)}, bf16[2,32,768]{2,1,0:T(8,128)(2,1)S(1)}, u32[]{:S(2)}, u32[]{:S(2)}) collective-permute-start(bf16[2,32,768]{2,1,0:T(8,128)(2,1)S(1)} %get-tuple-element.38), channel_id=1, source_target_pairs={{0,1},{1,2},{2,3},{3,0},{4,5},{5,6},{6,7},{7,4},{8,9},{9,10},{10,1... | collective-permute-start | bytes 294920 | tf_op jit(solution)/shard_map/ppermute | solution.py:341
  4.0 2.6 %collective-permute-start.1 = (bf16[2,32,768]{2,1,0:T(8,128)(2,1)S(1)}, bf16[2,32,768]{2,1,0:T(8,128)(2,1)S(1)}, u32[]{:S(2)}, u32[]{:S(2)}) collective-permute-start(bf16[2,32,768]{2,1,0:T(8,128)(2,1)S(1)} %get-tuple-element.38), channel_id=1, source_target_pairs={{0,2},{1,3},{2,0},{3,1},{4,6},{5,7},{6,4},{7,5},{8,10},{9,11},{10,... | collective-permute-start | bytes 294920 | tf_op jit(solution)/shard_map/ppermute | solution.py:341
  6.6 1.3 %collective-permute-start.2 = (bf16[2,32,768]{2,1,0:T(8,128)(2,1)S(1)}, bf16[2,32,768]{2,1,0:T(8,128)(2,1)S(1)}, u32[]{:S(2)}, u32[]{:S(2)}) collective-permute-start(bf16[2,32,768]{2,1,0:T(8,128)(2,1)S(1)} %get-tuple-element.38), channel_id=1, source_target_pairs={{0,3},{1,0},{2,1},{3,2},{4,7},{5,4},{6,5},{7,6},{8,11},{9,8},{10,9... | collective-permute-start | bytes 294920 | tf_op jit(solution)/shard_map/ppermute | solution.py:341
  8.0 8.0 %front.1 = (bf16[2,768,2048]{2,1,0:T(8,128)(2,1)S(1)}, bf16[2,768,2048]{2,1,0:T(8,128)(2,1)S(1)}, bf16[2,768,128]{2,1,0:T(8,128)(2,1)S(1)}, f32[2,32,2048]{2,1,0:T(8,128)S(1)}) custom-call(bf16[2,768,2048]{2,1,0:T(8,128)(2,1)} %x_hbm.1, f32[2,32,768]{2,1,0:T(8,128)} %step_ref.1, f32[2,32,768]{2,1,0:T(8,128)} %decay_ref.1, f32[1,32]{1,0:T(1,128)} %bitcast.54, ...), custom_call_target="tpu_custom_call" | custom-call | flops 402653184 | bytes 12582912 | tf_op jit(solution)/shard_map/front/pallas_call | solution.py:121
  16.1 1.0 %own_states.3 = (bf16[5,128,2048]{2,1,0:T(8,128)(2,1)S(1)}, bf16[128,2048]{1,0:T(8,128)(2,1)S(1)}) custom-call(bf16[128,768]{1,0:T(8,128)(2,1)S(1)} %get-tuple-element.96.b_ref, bf16[2,768,2048]{2,1,0:T(8,128)(2,1)S(1)} %get-tuple-element.41.weighted_ref, f32[2,32,2048]{2,1,0:T(8,128)S(1)} %get-tuple-element.42.rows_ref), custom_call_target="tpu_custom_call" | custom-call | flops 402653184 | bytes 3145728 | tf_op jit(solution)/shard_map/own_states/pallas_call | solution.py:168
  17.2 1.3 %collective-permute-start.4 = (bf16[128,2048]{1,0:T(8,128)(2,1)S(1)}, bf16[128,2048]{1,0:T(8,128)(2,1)S(1)}, u32[]{:S(2)}, u32[]{:S(2)}) collective-permute-start(bf16[128,2048]{1,0:T(8,128)(2,1)S(1)} %get-tuple-element.44), channel_id=1, source_target_pairs={{0,4},{1,5},{2,6},{3,7},{16,20},{17,21},{18,22},{19,23}} | collective-permute-start | bytes 1572872 | tf_op jit(solution)/shard_map/ppermute | solution.py:378
  18.5 0.7 %collective-permute-start.6 = (bf16[2,32,768]{2,1,0:T(8,128)(2,1)S(1)}, bf16[2,32,768]{2,1,0:T(8,128)(2,1)S(1)}, u32[]{:S(2)}, u32[]{:S(2)}) collective-permute-start(bf16[2,32,768]{2,1,0:T(8,128)(2,1)S(1)} %get-tuple-element.49), channel_id=1, source_target_pairs={{0,1},{1,2},{2,3},{3,0},{4,5},{5,6},{6,7},{7,4},{8,9},{9,10},{10,1... | collective-permute-start | bytes 294920 | tf_op jit(solution)/shard_map/ppermute | solution.py:341
  19.2 0.7 %collective-permute-start.7 = (bf16[2,32,768]{2,1,0:T(8,128)(2,1)S(1)}, bf16[2,32,768]{2,1,0:T(8,128)(2,1)S(1)}, u32[]{:S(2)}, u32[]{:S(2)}) collective-permute-start(bf16[2,32,768]{2,1,0:T(8,128)(2,1)S(1)} %get-tuple-element.49), channel_id=1, source_target_pairs={{0,2},{1,3},{2,0},{3,1},{4,6},{5,7},{6,4},{7,5},{8,10},{9,11},{10,... | collective-permute-start | bytes 294920 | tf_op jit(solution)/shard_map/ppermute | solution.py:341
  19.9 2.5 %collective-permute-start.8 = (bf16[2,32,768]{2,1,0:T(8,128)(2,1)S(1)}, bf16[2,32,768]{2,1,0:T(8,128)(2,1)S(1)}, u32[]{:S(2)}, u32[]{:S(2)}) collective-permute-start(bf16[2,32,768]{2,1,0:T(8,128)(2,1)S(1)} %get-tuple-element.49), channel_id=1, source_target_pairs={{0,3},{1,0},{2,1},{3,2},{4,7},{5,4},{6,5},{7,6},{8,11},{9,8},{10,9... | collective-permute-start | bytes 294920 | tf_op jit(solution)/shard_map/ppermute | solution.py:341
  22.4 1.0 %own_states.2 = (bf16[5,128,2048]{2,1,0:T(8,128)(2,1)S(1)}, bf16[128,2048]{1,0:T(8,128)(2,1)S(1)}) custom-call(bf16[128,768]{1,0:T(8,128)(2,1)S(1)} %get-tuple-element.95.b_ref, bf16[2,768,2048]{2,1,0:T(8,128)(2,1)S(1)} %get-tuple-element.41.weighted_ref, f32[2,32,2048]{2,1,0:T(8,128)S(1)} %get-tuple-element.42.rows_ref), custom_call_target="tpu_custom_call" | custom-call | flops 402653184 | bytes 3145728 | tf_op jit(solution)/shard_map/own_states/pallas_call | solution.py:168
  23.4 1.5 %collective-permute-start.3 = (bf16[128,2048]{1,0:T(8,128)(2,1)S(1)}, bf16[128,2048]{1,0:T(8,128)(2,1)S(1)}, u32[]{:S(2)}, u32[]{:S(2)}) collective-permute-start(bf16[128,2048]{1,0:T(8,128)(2,1)S(1)} %get-tuple-element.43), channel_id=1, source_target_pairs={{0,4},{1,5},{2,6},{3,7},{16,20},{17,21},{18,22},{19,23}} | collective-permute-start | bytes 1572872 | tf_op jit(solution)/shard_map/ppermute | solution.py:378
  25.1 0.7 %collective-permute-start.9 = (bf16[128,2048]{1,0:T(8,128)(2,1)S(1)}, bf16[128,2048]{1,0:T(8,128)(2,1)S(1)}, u32[]{:S(2)}, u32[]{:S(2)}) collective-permute-start(bf16[128,2048]{1,0:T(8,128)(2,1)S(1)} %fusion.2), channel_id=1, source_target_pairs={{4,8},{5,9},{6,10},{7,11},{20,24},{21,25},{22,26},{23,27}} | collective-permute-start | bytes 1572872 | tf_op jit(solution)/shard_map/ppermute | solution.py:378
  26.5 0.7 %collective-permute-start.5 = (bf16[128,2048]{1,0:T(8,128)(2,1)S(1)}, bf16[128,2048]{1,0:T(8,128)(2,1)S(1)}, u32[]{:S(2)}, u32[]{:S(2)}) collective-permute-start(bf16[128,2048]{1,0:T(8,128)(2,1)S(1)} %fusion), channel_id=1, source_target_pairs={{4,8},{5,9},{6,10},{7,11},{20,24},{21,25},{22,26},{23,27}} | collective-permute-start | bytes 1572872 | tf_op jit(solution)/shard_map/ppermute | solution.py:378
  27.2 1.1 %collective-permute-done.7 = bf16[2,32,768]{2,1,0:T(8,128)(2,1)S(1)} collective-permute-done((bf16[2,32,768]{2,1,0:T(8,128)(2,1)S(1)}, bf16[2,32,768]{2,1,0:T(8,128)(2,1)S(1)}, u32[]{:S(2)}, u32[]{:S(2)}) %collective-permute-start.7) | collective-permute-done | bytes 98336 | tf_op jit(solution)/shard_map/ppermute | solution.py:341
  28.5 4.6 %local_terms.2 = (bf16[768,2048]{1,0:T(8,128)(2,1)S(1)}, bf16[768,2048]{1,0:T(8,128)(2,1)S(1)}) custom-call(bf16[2,768,2048]{2,1,0:T(8,128)(2,1)} %gate_hbm.3, bf16[2,768,2048]{2,1,0:T(8,128)(2,1)S(1)} %get-tuple-element.46.x_ref, bf16[2,768,2048]{2,1,0:T(8,128)(2,1)S(1)} %get-tuple-element.41.weighted_ref, ...), custom_call_target="tpu_custom_call" | custom-call | flops 1610612736 | bytes 12582912 | tf_op jit(solution)/shard_map/local_terms/pallas_call | solution.py:227
  33.5 0.9 %collective-permute-start.11 = (bf16[128,2048]{1,0:T(8,128)(2,1)S(1)}, bf16[128,2048]{1,0:T(8,128)(2,1)S(1)}, u32[]{:S(2)}, u32[]{:S(2)}) collective-permute-start(bf16[128,2048]{1,0:T(8,128)(2,1)S(1)} %get-tuple-element.73), channel_id=1, source_target_pairs={{8,12},{9,13},{10,14},{11,15},{24,28},{25,29},{26,30},{27,31}} | collective-permute-start | bytes 1572872 | tf_op jit(solution)/shard_map/ppermute | solution.py:378
  34.4 4.6 %local_terms.3 = (bf16[768,2048]{1,0:T(8,128)(2,1)S(1)}, bf16[768,2048]{1,0:T(8,128)(2,1)S(1)}) custom-call(bf16[2,768,2048]{2,1,0:T(8,128)(2,1)} %gate_hbm.3, bf16[2,768,2048]{2,1,0:T(8,128)(2,1)S(1)} %get-tuple-element.46.x_ref, bf16[2,768,2048]{2,1,0:T(8,128)(2,1)S(1)} %get-tuple-element.41.weighted_ref, ...), custom_call_target="tpu_custom_call" | custom-call | flops 1610612736 | bytes 12582912 | tf_op jit(solution)/shard_map/local_terms/pallas_call | solution.py:227
  39.4 0.7 %collective-permute-start.10 = (bf16[128,2048]{1,0:T(8,128)(2,1)S(1)}, bf16[128,2048]{1,0:T(8,128)(2,1)S(1)}, u32[]{:S(2)}, u32[]{:S(2)}) collective-permute-start(bf16[128,2048]{1,0:T(8,128)(2,1)S(1)} %get-tuple-element.64), channel_id=1, source_target_pairs={{8,12},{9,13},{10,14},{11,15},{24,28},{25,29},{26,30},{27,31}} | collective-permute-start | bytes 1572872 | tf_op jit(solution)/shard_map/ppermute | solution.py:378
  40.2 1.5 %joined.3 = (bf16[768,2048]{1,0:T(8,128)(2,1)S(1)}, f32[6,1,128]{2,1,0:T(1,128)S(1)}) custom-call(bf16[768,2048]{1,0:T(8,128)(2,1)S(1)} %get-tuple-element.67.own_ref, bf16[768,2048]{1,0:T(8,128)(2,1)S(1)} %get-tuple-element.68.factor_ref, bf16[128,768]{1,0:T(8,128)(2,1)S(1)} %pad_maximum_fusion.3.c_ref, bf16[128,2048]{1,0:T(8,128)(2,1)S(1)} %add.31.incoming_ref), custom_call_target="tpu_custom_call" | custom-call | flops 402653184 | bytes 9437184 | tf_op jit(solution)/shard_map/joined/pallas_call | solution.py:270
  41.8 1.6 %copy-done.5 = bf16[768,2048]{1,0:T(8,128)(2,1)} copy-done((bf16[768,2048]{1,0:T(8,128)(2,1)}, bf16[768,2048]{1,0:T(8,128)(2,1)S(1)}, u32[]{:S(2)}) %copy-start.5) | copy-done | bytes 3145752
  43.4 0.6 broadcast_in_dim.15
  44.0 3.5 %all-to-all-start.1 = ((f32[4,6,1,128]{3,2,1,0:T(1,128)}), f32[4,6,1,128]{3,2,1,0:T(1,128)S(1)}, u32[]{:S(2)}, u32[]{:S(2)}) async-start(f32[4,6,1,128]{3,2,1,0:T(1,128)} %broadcast_in_dim.15), calls=%async_computation.1 | async-start | bytes 24576 | tf_op jit(solution)/shard_map/all_to_all | solution.py:348
  47.6 1.9 %copy-done.2 = bf16[768,2048]{1,0:T(8,128)(2,1)S(1)} copy-done((bf16[768,2048]{1,0:T(8,128)(2,1)S(1)}, bf16[768,2048]{1,0:T(8,128)(2,1)}, u32[]{:S(2)}) %copy-start.2) | copy-done | bytes 3145752
  49.5 1.9 %copy-done.4 = bf16[768,2048]{1,0:T(8,128)(2,1)S(1)} copy-done((bf16[768,2048]{1,0:T(8,128)(2,1)S(1)}, bf16[768,2048]{1,0:T(8,128)(2,1)}, u32[]{:S(2)}) %copy-start.4) | copy-done | bytes 3145752
  51.4 1.5 %joined.2 = (bf16[768,2048]{1,0:T(8,128)(2,1)S(1)}, f32[6,1,128]{2,1,0:T(1,128)S(1)}) custom-call(bf16[768,2048]{1,0:T(8,128)(2,1)S(1)} %copy-done.2, bf16[768,2048]{1,0:T(8,128)(2,1)S(1)} %copy-done.4, bf16[128,768]{1,0:T(8,128)(2,1)S(1)} %pad_maximum_fusion.2.c_ref, bf16[128,2048]{1,0:T(8,128)(2,1)S(1)} %add.30.incoming_ref), custom_call_target="tpu_custom_call" | custom-call | flops 402653184 | bytes 9437184 | tf_op jit(solution)/shard_map/joined/pallas_call | solution.py:270
  53.1 0.6 broadcast_in_dim.13
  53.7 4.9 %all-to-all-start = ((f32[4,6,1,128]{3,2,1,0:T(1,128)}), f32[4,6,1,128]{3,2,1,0:T(1,128)S(1)}, u32[]{:S(2)}, u32[]{:S(2)}) async-start(f32[4,6,1,128]{3,2,1,0:T(1,128)} %broadcast_in_dim.13), calls=%async_computation | async-start | bytes 24576 | tf_op jit(solution)/shard_map/all_to_all | solution.py:348
  58.6 1.9 %copy-done.6 = bf16[768,2048]{1,0:T(8,128)(2,1)S(1)} copy-done((bf16[768,2048]{1,0:T(8,128)(2,1)S(1)}, bf16[768,2048]{1,0:T(8,128)(2,1)}, u32[]{:S(2)}) %copy-start.6) | copy-done | bytes 3145752
  60.5 2.0 %normed.2.refs_0_ = bf16[2,768,2048]{2,1,0:T(8,128)(2,1)} custom-call(bf16[768,2048]{1,0:T(8,128)(2,1)S(1)} %copy-done.6, f32[4,6,1,128]{3,2,1,0:T(1,128)S(1)} %all-to-all-done.1.square_ref, f32[1,2048]{1,0:T(1,128)S(1)} %bitcast.46), custom_call_target="tpu_custom_call" | custom-call | flops 3145728 | bytes 6291456 | tf_op jit(solution)/shard_map/normed/pallas_call | solution.py:318
  62.5 1.7 %all-to-all-done.square_ref = f32[4,6,1,128]{3,2,1,0:T(1,128)S(1)} async-done(((f32[4,6,1,128]{3,2,1,0:T(1,128)}), f32[4,6,1,128]{3,2,1,0:T(1,128)S(1)}, u32[]{:S(2)}, u32[]{:S(2)}) %all-to-all-start) | async-done | bytes 12320 | tf_op jit(solution)/shard_map/all_to_all | solution.py:348
  64.2 2.0 %normed.3 = bf16[2,768,2048]{2,1,0:T(8,128)(2,1)} custom-call(bf16[768,2048]{1,0:T(8,128)(2,1)S(1)} %get-tuple-element.65.gated_ref, f32[4,6,1,128]{3,2,1,0:T(1,128)S(1)} %all-to-all-done.square_ref, f32[1,2048]{1,0:T(1,128)S(1)} %bitcast.47, bf16[2,768,2048]{2,1,0:T(8,128)(2,1)} %normed.2.refs_0_), custom_call_target="tpu_custom_call", output_to_operand_aliasing={{}: (3, {})} | custom-call | flops 3145728 | bytes 6291456 | tf_op jit(solution)/shard_map/normed/pallas_call | solution.py:318
  (44 shorter events, 2.2 us)
Async XLA Ops:
  1.0 15.0 %collective-permute-start = (bf16[2,32,768]{2,1,0:T(8,128)(2,1)S(1)}, bf16[2,32,768]{2,1,0:T(8,128)(2,1)S(1)}, u32[]{:S(2)}, u32[]{:S(2)}) collective-permute-start(bf16[2,32,768]{2,1,0:T(8,128)(2,1)S(1)} %get-tuple-element.38), channel_id=1, source_target_pairs={{0,1},{1,2},{2,3},{3,0},{4,5},{5,6},{6,7},{7,4},{8,9},{9,10},{10,1... | collective-permute-start | bytes 294920 | tf_op jit(solution)/shard_map/ppermute | solution.py:341
  4.0 12.0 %collective-permute-start.1 = (bf16[2,32,768]{2,1,0:T(8,128)(2,1)S(1)}, bf16[2,32,768]{2,1,0:T(8,128)(2,1)S(1)}, u32[]{:S(2)}, u32[]{:S(2)}) collective-permute-start(bf16[2,32,768]{2,1,0:T(8,128)(2,1)S(1)} %get-tuple-element.38), channel_id=1, source_target_pairs={{0,2},{1,3},{2,0},{3,1},{4,6},{5,7},{6,4},{7,5},{8,10},{9,11},{10,... | collective-permute-start | bytes 294920 | tf_op jit(solution)/shard_map/ppermute | solution.py:341
  6.6 9.4 %collective-permute-start.2 = (bf16[2,32,768]{2,1,0:T(8,128)(2,1)S(1)}, bf16[2,32,768]{2,1,0:T(8,128)(2,1)S(1)}, u32[]{:S(2)}, u32[]{:S(2)}) collective-permute-start(bf16[2,32,768]{2,1,0:T(8,128)(2,1)S(1)} %get-tuple-element.38), channel_id=1, source_target_pairs={{0,3},{1,0},{2,1},{3,2},{4,7},{5,4},{6,5},{7,6},{8,11},{9,8},{10,9... | collective-permute-start | bytes 294920 | tf_op jit(solution)/shard_map/ppermute | solution.py:341
  17.2 7.8 %collective-permute-start.4 = (bf16[128,2048]{1,0:T(8,128)(2,1)S(1)}, bf16[128,2048]{1,0:T(8,128)(2,1)S(1)}, u32[]{:S(2)}, u32[]{:S(2)}) collective-permute-start(bf16[128,2048]{1,0:T(8,128)(2,1)S(1)} %get-tuple-element.44), channel_id=1, source_target_pairs={{0,4},{1,5},{2,6},{3,7},{16,20},{17,21},{18,22},{19,23}} | collective-permute-start | bytes 1572872 | tf_op jit(solution)/shard_map/ppermute | solution.py:378
  18.5 8.8 %collective-permute-start.6 = (bf16[2,32,768]{2,1,0:T(8,128)(2,1)S(1)}, bf16[2,32,768]{2,1,0:T(8,128)(2,1)S(1)}, u32[]{:S(2)}, u32[]{:S(2)}) collective-permute-start(bf16[2,32,768]{2,1,0:T(8,128)(2,1)S(1)} %get-tuple-element.49), channel_id=1, source_target_pairs={{0,1},{1,2},{2,3},{3,0},{4,5},{5,6},{6,7},{7,4},{8,9},{9,10},{10,1... | collective-permute-start | bytes 294920 | tf_op jit(solution)/shard_map/ppermute | solution.py:341
  19.2 9.2 %collective-permute-start.7 = (bf16[2,32,768]{2,1,0:T(8,128)(2,1)S(1)}, bf16[2,32,768]{2,1,0:T(8,128)(2,1)S(1)}, u32[]{:S(2)}, u32[]{:S(2)}) collective-permute-start(bf16[2,32,768]{2,1,0:T(8,128)(2,1)S(1)} %get-tuple-element.49), channel_id=1, source_target_pairs={{0,2},{1,3},{2,0},{3,1},{4,6},{5,7},{6,4},{7,5},{8,10},{9,11},{10,... | collective-permute-start | bytes 294920 | tf_op jit(solution)/shard_map/ppermute | solution.py:341
  19.9 8.5 %collective-permute-start.8 = (bf16[2,32,768]{2,1,0:T(8,128)(2,1)S(1)}, bf16[2,32,768]{2,1,0:T(8,128)(2,1)S(1)}, u32[]{:S(2)}, u32[]{:S(2)}) collective-permute-start(bf16[2,32,768]{2,1,0:T(8,128)(2,1)S(1)} %get-tuple-element.49), channel_id=1, source_target_pairs={{0,3},{1,0},{2,1},{3,2},{4,7},{5,4},{6,5},{7,6},{8,11},{9,8},{10,9... | collective-permute-start | bytes 294920 | tf_op jit(solution)/shard_map/ppermute | solution.py:341
  23.4 5.1 %copy-start = (bf16[192,2048]{1,0:T(8,128)(2,1)S(1)}, bf16[192,2048]{1,0:T(8,128)(2,1)}, u32[]{:S(2)}) copy-start(bf16[192,2048]{1,0:T(8,128)(2,1)} %constant.2.clone.bands_hbm.bands_ref) | copy-start | bytes 2359300
  23.4 2.9 %collective-permute-start.3 = (bf16[128,2048]{1,0:T(8,128)(2,1)S(1)}, bf16[128,2048]{1,0:T(8,128)(2,1)S(1)}, u32[]{:S(2)}, u32[]{:S(2)}) collective-permute-start(bf16[128,2048]{1,0:T(8,128)(2,1)S(1)} %get-tuple-element.43), channel_id=1, source_target_pairs={{0,4},{1,5},{2,6},{3,7},{16,20},{17,21},{18,22},{19,23}} | collective-permute-start | bytes 1572872 | tf_op jit(solution)/shard_map/ppermute | solution.py:378
  25.1 8.1 %collective-permute-start.9 = (bf16[128,2048]{1,0:T(8,128)(2,1)S(1)}, bf16[128,2048]{1,0:T(8,128)(2,1)S(1)}, u32[]{:S(2)}, u32[]{:S(2)}) collective-permute-start(bf16[128,2048]{1,0:T(8,128)(2,1)S(1)} %fusion.2), channel_id=1, source_target_pairs={{4,8},{5,9},{6,10},{7,11},{20,24},{21,25},{22,26},{23,27}} | collective-permute-start | bytes 1572872 | tf_op jit(solution)/shard_map/ppermute | solution.py:378
  26.5 12.5 %collective-permute-start.5 = (bf16[128,2048]{1,0:T(8,128)(2,1)S(1)}, bf16[128,2048]{1,0:T(8,128)(2,1)S(1)}, u32[]{:S(2)}, u32[]{:S(2)}) collective-permute-start(bf16[128,2048]{1,0:T(8,128)(2,1)S(1)} %fusion), channel_id=1, source_target_pairs={{4,8},{5,9},{6,10},{7,11},{20,24},{21,25},{22,26},{23,27}} | collective-permute-start | bytes 1572872 | tf_op jit(solution)/shard_map/ppermute | solution.py:378
  33.5 6.6 %collective-permute-start.11 = (bf16[128,2048]{1,0:T(8,128)(2,1)S(1)}, bf16[128,2048]{1,0:T(8,128)(2,1)S(1)}, u32[]{:S(2)}, u32[]{:S(2)}) collective-permute-start(bf16[128,2048]{1,0:T(8,128)(2,1)S(1)} %get-tuple-element.73), channel_id=1, source_target_pairs={{8,12},{9,13},{10,14},{11,15},{24,28},{25,29},{26,30},{27,31}} | collective-permute-start | bytes 1572872 | tf_op jit(solution)/shard_map/ppermute | solution.py:378
  39.0 2.7 %copy-start.1 = (bf16[768,2048]{1,0:T(8,128)(2,1)}, bf16[768,2048]{1,0:T(8,128)(2,1)S(1)}, u32[]{:S(2)}) copy-start(bf16[768,2048]{1,0:T(8,128)(2,1)S(1)} %get-tuple-element.61.own_ref) | copy-start | bytes 9437188
  39.0 2.7 %copy-start.3 = (bf16[768,2048]{1,0:T(8,128)(2,1)}, bf16[768,2048]{1,0:T(8,128)(2,1)S(1)}, u32[]{:S(2)}) copy-start(bf16[768,2048]{1,0:T(8,128)(2,1)S(1)} %get-tuple-element.62.factor_ref) | copy-start | bytes 9437188
  39.4 8.1 %collective-permute-start.10 = (bf16[128,2048]{1,0:T(8,128)(2,1)S(1)}, bf16[128,2048]{1,0:T(8,128)(2,1)S(1)}, u32[]{:S(2)}, u32[]{:S(2)}) collective-permute-start(bf16[128,2048]{1,0:T(8,128)(2,1)S(1)} %get-tuple-element.64), channel_id=1, source_target_pairs={{8,12},{9,13},{10,14},{11,15},{24,28},{25,29},{26,30},{27,31}} | collective-permute-start | bytes 1572872 | tf_op jit(solution)/shard_map/ppermute | solution.py:378
  41.8 1.6 %copy-start.5 = (bf16[768,2048]{1,0:T(8,128)(2,1)}, bf16[768,2048]{1,0:T(8,128)(2,1)S(1)}, u32[]{:S(2)}) copy-start(bf16[768,2048]{1,0:T(8,128)(2,1)S(1)} %get-tuple-element.69.gated_ref) | copy-start | bytes 9437188
  44.0 9.1 %all-to-all-start.1 = ((f32[4,6,1,128]{3,2,1,0:T(1,128)}), f32[4,6,1,128]{3,2,1,0:T(1,128)S(1)}, u32[]{:S(2)}, u32[]{:S(2)}) async-start(f32[4,6,1,128]{3,2,1,0:T(1,128)} %broadcast_in_dim.15), calls=%async_computation.1 | async-start | bytes 24576 | tf_op jit(solution)/shard_map/all_to_all | solution.py:348
  47.6 1.9 %copy-start.2 = (bf16[768,2048]{1,0:T(8,128)(2,1)S(1)}, bf16[768,2048]{1,0:T(8,128)(2,1)}, u32[]{:S(2)}) copy-start(bf16[768,2048]{1,0:T(8,128)(2,1)} %copy-done.1) | copy-start | bytes 9437188
  49.5 1.9 %copy-start.4 = (bf16[768,2048]{1,0:T(8,128)(2,1)S(1)}, bf16[768,2048]{1,0:T(8,128)(2,1)}, u32[]{:S(2)}) copy-start(bf16[768,2048]{1,0:T(8,128)(2,1)} %copy-done.3) | copy-start | bytes 9437188
  51.4 7.2 %copy-start.7 = (f32[2048]{0:T(1024)S(1)}, f32[2048]{0:T(1024)}, u32[]{:S(2)}) copy-start(f32[2048]{0:T(1024)} %param.14) | copy-start | bytes 24580
  53.7 10.5 %all-to-all-start = ((f32[4,6,1,128]{3,2,1,0:T(1,128)}), f32[4,6,1,128]{3,2,1,0:T(1,128)S(1)}, u32[]{:S(2)}, u32[]{:S(2)}) async-start(f32[4,6,1,128]{3,2,1,0:T(1,128)} %broadcast_in_dim.13), calls=%async_computation | async-start | bytes 24576 | tf_op jit(solution)/shard_map/all_to_all | solution.py:348
  58.6 1.9 %copy-start.6 = (bf16[768,2048]{1,0:T(8,128)(2,1)S(1)}, bf16[768,2048]{1,0:T(8,128)(2,1)}, u32[]{:S(2)}) copy-start(bf16[768,2048]{1,0:T(8,128)(2,1)} %copy-done.5) | copy-start | bytes 9437188

commit v5 on v4

v5 whole, which is shorter than its diff:
```python
import functools

import jax
import jax.numpy as jnp
import numpy as np
from jax import lax
from jax.experimental import pallas as pl
from jax.experimental.pallas import tpu as pltpu
from jax.sharding import PartitionSpec as P

SPAN = 128
HALF = 256
F32 = jnp.float32
BF16 = jnp.bfloat16
VMEM_LIMIT = 12 * 1024 * 1024
PARAMS = pltpu.CompilerParams(vmem_limit_bytes=VMEM_LIMIT)
ENTER, LEAVE, FIRST, TOTAL = range(4)
ROWS = 32
WHOLE = pl.BlockSpec(memory_space=pltpu.VMEM)
ANYWHERE = pl.BlockSpec(memory_space=pl.ANY)


def in_vmem(array):
    return pltpu.with_memory_space_constraint(array, pltpu.VMEM)


def in_hbm(array):
    return pltpu.with_memory_space_constraint(array, pltpu.HBM)


def mm(a, b):
    return jnp.dot(a, b, preferred_element_type=F32)


def exact_dot(a, b):
    return jnp.dot(a, b, precision=lax.Precision.HIGHEST, preferred_element_type=F32)


def iotas(shape):
    return (
        lax.broadcasted_iota(jnp.int32, shape, 0),
        lax.broadcasted_iota(jnp.int32, shape, 1),
    )


def two_parts(v):
    high = v.astype(BF16).astype(F32)
    return [high, v - high]


def upright(parts):
    return jnp.concatenate(parts, axis=0).T.astype(BF16)


def fill_tables(step_ref, decay_ref, skip_ref, spread, both_ref, rows_ref):
    seqs, heads, length = decay_ref.shape
    blocks = length // SPAN
    at, lane = iotas((length, SPAN))
    kind, block = lane // blocks, lane % blocks
    first, mid, end = block * SPAN, block * SPAN + SPAN // 2, block * SPAN + SPAN
    chosen = (
        ((kind == ENTER) & (at >= first) & (at < mid))
        | ((kind == LEAVE) & (at >= mid) & (at < end))
        | ((kind == FIRST) & (at < mid))
        | (kind == TOTAL)
    )
    chosen = jnp.where(chosen, 1.0, 0.0).astype(F32)
    row, col = iotas((SPAN, SPAN))
    until = jnp.where(row <= col, 1.0, 0.0).astype(F32)
    skip = jnp.broadcast_to(skip_ref[...], (8, heads))
    skip_row = sum(mm(part.astype(BF16), spread[:heads]) for part in two_parts(skip))
    for s in range(seqs):
        exponent = exact_dot(decay_ref[s], chosen)
        per_block = upright(two_parts(jnp.exp(exponent)))
        rows_ref[s] = mm(per_block, spread)[:ROWS]
        rows_ref[s, ROWS - 1:ROWS] = skip_row[:1]
        for k in range(blocks):
            sl = slice(k * SPAN, (k + 1) * SPAN)
            summed = exact_dot(decay_ref[s, :, sl], until)
            middle = exponent[:, ENTER * blocks + k:ENTER * blocks + k + 1]
            rise = jnp.exp(summed - middle)
            fall = step_ref[s, :, sl] * jnp.exp(middle - summed)
            both_ref[s, sl, :] = upright(two_parts(rise) + two_parts(fall))


def front_kernel(
    x_ref, step_ref, decay_ref, skip_ref, bands_ref, weighted_ref, both_ref, rows_ref
):
    seqs, length, channels = x_ref.shape
    heads = decay_ref.shape[1]
    fill_tables(
        step_ref, decay_ref, skip_ref, bands_ref[2 * heads:4 * heads], both_ref, rows_ref
    )
    for s in range(seqs):
        for k in range(length // SPAN):
            rows = slice(k * SPAN, (k + 1) * SPAN)
            both = both_ref[s, rows]
            for lo in range(0, channels, HALF):
                sl = slice(lo, lo + HALF)
                wide = mm(both, bands_ref[:4 * heads, sl]).astype(BF16)
                weighted_ref[s, rows, sl] = x_ref[s, rows, sl] * wide


def front(features, step_size, log_decay, skip, bands):
    seqs, length, channels = features.shape
    heads = step_size.shape[1]
    return pl.pallas_call(
        front_kernel,
        in_specs=[WHOLE] * 5,
        out_specs=[WHOLE] * 3,
        out_shape=[
            pltpu.VMEM(features.shape, BF16),
            pltpu.VMEM((seqs, length, 4 * heads), BF16),
            pltpu.VMEM((seqs, ROWS, channels), F32),
        ],
        compiler_params=PARAMS,
        cost_estimate=pl.CostEstimate(
            flops=2 * seqs * length * channels * 64,
            bytes_accessed=4 * seqs * length * channels,
            transcendentals=0,
        ),
        name="front",
    )(in_vmem(features), step_size, log_decay, skip, bands)


def state_kernel(b_ref, weighted_ref, rows_ref, entering_ref, state_ref):
    seqs, length, channels = weighted_ref.shape
    blocks = length // SPAN
    for s in range(seqs):
        for lo in range(0, channels, HALF):
            sl = slice(lo, lo + HALF)
            state = None
            for k in range(blocks):
                rows = slice(k * SPAN, (k + 1) * SPAN)
                added = mm(b_ref[s, :, rows], weighted_ref[s, rows, sl])
                if k > 0:
                    at = ENTER * blocks + k
                    entering = rows_ref[s, at:at + 1, sl] * state
                    entering_ref[s, k - 1, :, sl] = entering.astype(BF16)
                    added = added + entering
                at = LEAVE * blocks + k
                state = rows_ref[s, at:at + 1, sl] * added
            state_ref[s, :, sl] = state.astype(BF16)


def own_states(b, weighted, rows):
    seqs, states, length = b.shape
    channels = weighted.shape[2]
    return pl.pallas_call(
        state_kernel,
        in_specs=[WHOLE] * 3,
        out_specs=[WHOLE] * 2,
        out_shape=[
            pltpu.VMEM((seqs, length // SPAN - 1, states, channels), BF16),
            pltpu.VMEM((seqs, states, channels), BF16),
        ],
        compiler_params=PARAMS,
        cost_estimate=pl.CostEstimate(
            flops=2 * seqs * length * channels * states,
            bytes_accessed=2 * seqs * length * channels,
            transcendentals=0,
        ),
        name="own_states",
    )(b, in_vmem(weighted), in_vmem(rows))


def local_kernel(
    gate_ref, x_ref, weighted_ref, entering_ref, b_ref, c_ref, both_ref, bands_ref, rows_ref,
    own_ref, factor_ref,
):
    seqs, length, channels = own_ref.shape
    blocks = length // SPAN
    heads4 = both_ref.shape[2]
    row, col = iotas((SPAN, SPAN))
    for s in range(seqs):
        for k in range(blocks):
            rows = slice(k * SPAN, (k + 1) * SPAN)
            c_t = c_ref[s, :, rows].T
            affinity = mm(c_t, b_ref[s, :, rows])
            left = jnp.where(row >= col, affinity, 0.0).astype(BF16)
            if k > 0:
                left = jnp.concatenate([left, c_t], axis=1)
            both = both_ref[s, rows]
            at = FIRST * blocks + k
            for lo in range(0, channels, HALF):
                sl = slice(lo, lo + HALF)
                right = weighted_ref[s, rows, sl]
                if k > 0:
                    right = jnp.concatenate([right, entering_ref[s, k - 1, :, sl]], axis=0)
                mixed = mm(left, right).astype(BF16)
                half = 0.5 * gate_ref[s, rows, sl].astype(F32)
                gate = (half * jnp.tanh(half) + half).astype(BF16)
                wide = mm(both, bands_ref[heads4 // 2:heads4 // 2 + heads4, sl])
                rise = wide.astype(BF16) * gate
                skip = rows_ref[s, ROWS - 1:ROWS, sl].astype(BF16) * x_ref[s, rows, sl]
                own_ref[s, rows, sl] = rise * mixed + skip * gate
                factor_ref[s, rows, sl] = rise * rows_ref[s, at:at + 1, sl].astype(BF16)


def local_terms(gate_in, x, weighted, entering, b, c, both, bands, rows):
    seqs, length, channels = gate_in.shape
    return pl.pallas_call(
        local_kernel,
        in_specs=[WHOLE] * 9,
        out_specs=[WHOLE, WHOLE],
        out_shape=[pltpu.VMEM(gate_in.shape, BF16)] * 2,
        compiler_params=PARAMS,
        cost_estimate=pl.CostEstimate(
            flops=2 * seqs * length * channels * 512,
            bytes_accessed=8 * seqs * length * channels,
            transcendentals=seqs * length * channels,
        ),
        name="local_terms",
    )(
        in_vmem(gate_in), in_vmem(x), in_vmem(weighted), in_vmem(entering), b, c, in_vmem(both),
        bands, in_vmem(rows),
    )


def joined_kernel(own_ref, factor_ref, c_ref, *refs):
    gated_ref, square_ref = refs[-2:]
    seqs, length, channels = own_ref.shape
    blocks = length // SPAN
    for s in range(seqs):
        for k in range(blocks):
            rows = slice(k * SPAN, (k + 1) * SPAN)
            c_t = c_ref[s, :, rows].T
            squares = jnp.zeros((SPAN, 128), F32)
            for lo in range(0, channels, HALF):
                sl = slice(lo, lo + HALF)
                carried = mm(c_t, refs[s][:, sl]).astype(BF16)
                gated = own_ref[s, rows, sl] + factor_ref[s, rows, sl] * carried
                gated_ref[s, rows, sl] = gated
                power = gated * gated
                pair = sum(power[:, left:left + 128] for left in range(0, HALF, 128))
                squares = squares + pair.astype(F32)
            square_ref[s * blocks + k] = jnp.sum(squares.T, axis=0, keepdims=True)


def joined(own, factor, c, incoming):
    seqs, length, channels = own.shape
    states = c.shape[1]
    return pl.pallas_call(
        joined_kernel,
        in_specs=[WHOLE] * (3 + seqs),
        out_specs=[WHOLE] * 2,
        out_shape=[
            pltpu.VMEM(own.shape, BF16),
            pltpu.VMEM((seqs * (length // SPAN), 1, SPAN), F32),
        ],
        input_output_aliases={0: 0},
        compiler_params=PARAMS,
        cost_estimate=pl.CostEstimate(
            flops=2 * seqs * length * channels * states,
            bytes_accessed=6 * seqs * length * channels,
            transcendentals=0,
        ),
        name="joined",
    )(in_vmem(own), in_vmem(factor), c, *incoming)


def norm_kernel(all_channels, gated_ref, square_ref, gain_ref, out_hbm, staged, sems):
    seqs, length, channels = gated_ref.shape
    blocks = length // SPAN
    copies = []
    for s in range(seqs):
        for k in range(blocks):
            at = s * blocks + k
            rows = slice(k * SPAN, (k + 1) * SPAN)
            total = jnp.sum(square_ref[:, at, 0], axis=0, keepdims=True)
            inverse = lax.rsqrt(total / all_channels + 1e-05)
            column = jnp.broadcast_to(inverse, (128, SPAN)).T
            for lo in range(0, channels, 128):
                sl = slice(lo, lo + 128)
                staged[s, rows, sl] = (
                    gated_ref[s, rows, sl].astype(F32) * column * gain_ref[:, sl]
                ).astype(BF16)
            place = (s, pl.ds(k * SPAN, SPAN))
            copies.append(
                pltpu.make_async_copy(staged.at[place], out_hbm.at[place], sems.at[at])
            )
            copies[-1].start()
    for copy in copies:
        copy.wait()


def normed(gated, squares, gain_row, all_channels):
    seqs, length, channels = gated.shape
    return pl.pallas_call(
        functools.partial(norm_kernel, all_channels),
        in_specs=[WHOLE] * 3,
        out_specs=ANYWHERE,
        out_shape=jax.ShapeDtypeStruct(gated.shape, BF16),
        scratch_shapes=[
            pltpu.VMEM(gated.shape, BF16),
            pltpu.SemaphoreType.DMA((seqs * (length // SPAN),)),
        ],
        compiler_params=PARAMS,
        cost_estimate=pl.CostEstimate(
            flops=2 * seqs * length * channels,
            bytes_accessed=4 * seqs * length * channels,
            transcendentals=0,
        ),
        name="normed",
    )(in_vmem(gated), squares, gain_row)


def from_all(shard, axis):
    devices = lax.axis_size(axis)
    return [shard] + [
        lax.ppermute(shard, axis, [(i, (i + by) % devices) for i in range(devices)])
        for by in range(1, devices)
    ]


def as_parts(row):
    high = row.astype(BF16)
    low = (row - high.astype(F32)).astype(BF16)
    return jnp.concatenate([high, low, jnp.zeros((14, row.shape[1]), BF16)], axis=0)


def body(features, gate_in, state_proj, step_size, log_decay, skip_gain, norm_gain):
    seqs, length, channels = features.shape
    heads = step_size.shape[1]
    pair = np.repeat(np.concatenate([np.eye(heads)] * 2), channels // heads, axis=1)
    bands = jnp.asarray(np.concatenate([0 * pair, pair, 0 * pair]), BF16)
    b_own, c_own = lax.optimization_barrier((state_proj[0], state_proj[1]))
    c = from_all(c_own, "head")
    b = jnp.concatenate(from_all(b_own, "head"), axis=1)
    states = b.shape[1]
    weighted, both, rows = front(
        features, in_hbm(step_size), in_hbm(log_decay), in_hbm(skip_gain[None, :]), in_hbm(bands)
    )
    entering, ends = own_states(b, weighted, rows)

    place = lax.axis_index("ctx")
    even = place % 2 == 0
    devices = lax.axis_size("ctx")
    swap = [(i, i ^ 1) for i in range(devices)]
    total_at = TOTAL * (length // SPAN)
    decay = [rows[s, total_at:total_at + 1] for s in range(seqs)]
    other = lax.ppermute(
        jnp.concatenate([
            jnp.where(even, ends[1], ends[0]),
            as_parts(jnp.where(even, decay[1], decay[0])),
        ]),
        "ctx", swap,
    )
    end_other = other[:states].astype(F32)
    decay_other = other[states:states + 1].astype(F32) + other[states + 1:states + 2].astype(F32)
    end_first = ends[0].astype(F32)
    past = jnp.where(
        even,
        end_other + decay_other * end_first,
        ends[1].astype(F32) + decay[1] * end_other,
    )
    decay_past = decay_other * jnp.where(even, decay[0], decay[1])
    entered = None
    for hop in range(0, devices - 2, 2):
        sent = past if entered is None else past + decay_past * entered.astype(F32)
        got = lax.ppermute(sent.astype(BF16), "ctx", [(hop, hop + 2), (hop + 1, hop + 3)])
        if entered is None:
            c, _ = lax.optimization_barrier((c, sent))
            c = jnp.concatenate(c, axis=1)
            terms = local_terms(
                gate_in, features, weighted, entering, b, c, both, in_hbm(bands), rows
            )
            got, terms = lax.optimization_barrier((got, terms))
        entered = got if entered is None else entered + got
    entered32 = entered.astype(F32)
    shared = lax.ppermute(
        jnp.where(even, end_first + decay[0] * entered32, entered32).astype(BF16), "ctx", swap
    )
    incoming = [
        jnp.where(even, entered, shared),
        jnp.where(even, shared, (end_other + decay_other * entered32).astype(BF16)),
    ]
    gated, squares = joined(*terms, c, incoming)
    squares = jnp.stack(from_all(squares, "head"))
    return normed(gated, squares, norm_gain[None, :], channels * lax.axis_size("head"))


def solution(mesh):
    in_specs = (
        P("groups", "ctx", "head"),
        P("groups", "ctx", "head"),
        P(None, "groups", "head", "ctx"),
        P("groups", "head", "ctx"),
        P("groups", "head", "ctx"),
        P("head"),
        P("head"),
    )
    out_specs = P("groups", "ctx", "head")
    return jax.shard_map(body, mesh=mesh, in_specs=in_specs, out_specs=out_specs, check_vma=False)
```

time: 67.6 us -> 55.6 us (0.82); the launches traced: 66.4 us -> 55.4 us
  starting transfers between devices: 25 us -> 17.1 us
  waiting for transfers between devices: 3.59 us -> 10.9 us
  local copies, waits for them, and re-layouts: 9.63 us -> 3.93 us
  Pallas kernels: 26.4 us -> 21.9 us
    all_to_all x2 -> x0, starting transfers between devices: 8.37 us -> none  [at_once(): lax.all_to_all(jnp.broadcast_to(shard, (devices,) + shard.shape), axis, 0...]
    ppermute x6 -> x9, waiting for transfers between devices: 1.15 us -> 8.95 us  [from_all(): lax.ppermute(shard, axis, [(i, (i + by) % devices) for i in range(devices)])]
    unnamed x18 -> x16, local copies, waits for them, and re-layouts: 7.38 us -> 2.86 us
    pallas_call x9 -> x5, Pallas kernels: 26.4 us -> 21.9 us  [the longest x1 7.86 us: local_terms(): pl.pallas_call(local_kernel, in_specs=[WHOLE] * 9, out_specs=[WHOLE, WHOL...]
    ppermute x6 -> x9, starting transfers between devices: 10.9 us -> 13.4 us  [from_all(): lax.ppermute(shard, axis, [(i, (i + by) % devices) for i in range(devices)])]
    ppermute x6 -> x3, starting transfers between devices: 5.73 us -> 3.74 us  [the longest x1 3.6 us: body(): lax.ppermute(sent.astype(BF16), 'ctx', [(hop, hop + 2), (hop + 1, hop + 3)])]
    all_to_all x2 -> x0, waiting for transfers between devices: 1.84 us -> none  [at_once(): lax.all_to_all(jnp.broadcast_to(shard, (devices,) + shard.shape), axis, 0...]
    ppermute x6 -> x3, waiting for transfers between devices: 0.59 us -> 1.9 us  [the longest x1 1.9 us: body(): lax.ppermute(jnp.where(even, end_first + decay[0] * entered32, entered32)...]
  transfers between devices with their start and end apart: 14 -> 12, of which waited for: 4 -> 5; matrix products, arithmetic and copies ran while one was open for 3% -> 1% of each run, Pallas kernels for 35% -> 24%
where the time goes in v5:
time: 55.6 us; the launch traced here: 55.4 us
  Pallas kernels  21.9 us (39%)
  starting transfers between devices  17.1 us (31%)
  waiting for transfers between devices  10.9 us (20%)
  local copies, waits for them, and re-layouts  3.93 us (7%)
  other arithmetic  1.14 us (2%)
    ppermute x9, starting transfers between devices, from_all(): lax.ppermute(shard, axis, [(i, (i + by) % devices) for i in range(devices)])  13.4 us
    ppermute x9, waiting for transfers between devices, from_all(): lax.ppermute(shard, axis, [(i, (i + by) % devices) for i in range(devices)])  8.95 us
    pallas_call x1, Pallas kernels, local_terms(): pl.pallas_call(local_kernel, in_specs=[WHOLE] * 9, out_specs=[WHOLE, WHOL...  7.86 us
    pallas_call x1, Pallas kernels, front(): pl.pallas_call(front_kernel, in_specs=[WHOLE] * 5, out_specs=[WHOLE] * 3,...  5.19 us
    pallas_call x1, Pallas kernels, joined(): pl.pallas_call(joined_kernel, in_specs=[WHOLE] * (3 + seqs), out_specs=[W...  3.81 us
    ppermute x1, starting transfers between devices, body(): lax.ppermute(sent.astype(BF16), 'ctx', [(hop, hop + 2), (hop + 1, hop + 3)])  3.6 us
    pallas_call x1, Pallas kernels, normed(): pl.pallas_call(functools.partial(norm_kernel, all_channels), in_specs=[WH...  3.1 us
    unnamed x16, local copies, waits for them, and re-layouts  2.86 us
  transfers between devices with their start and end apart: 12, of which 5 were waited for; matrix products, arithmetic and copies ran while one was open for 1% of the time, Pallas kernels for 24%

profile of v5, /device:TPU:0, one launch (start us, length us, event | category | flops | bytes accessed | tf_op | source)
XLA Modules:
  0.0 55.4 jit_solution(1637955259068131487)
XLA Ops:
  0.0 1.0 %slice_bitcast_fusion = (bf16[2,32,768]{2,1,0:T(8,128)(2,1)S(1)}, bf16[2,32,768]{2,1,0:T(8,128)(2,1)S(1)}) fusion(bf16[2,2,32,768]{3,2,1,0:T(8,128)(2,1)} %param.10), kind=kLoop, calls=%fused_computation.16 | loop fusion | bytes 393216 | tf_op jit(solution)/shard_map/squeeze | solution.py:327
  1.0 5.1 %collective-permute-start.2 = (bf16[2,32,768]{2,1,0:T(8,128)(2,1)S(1)}, bf16[2,32,768]{2,1,0:T(8,128)(2,1)S(1)}, u32[]{:S(2)}, u32[]{:S(2)}) collective-permute-start(bf16[2,32,768]{2,1,0:T(8,128)(2,1)S(1)} %get-tuple-element.23), channel_id=1, source_target_pairs={{0,3},{1,0},{2,1},{3,2},{4,7},{5,4},{6,5},{7,6},{8,11},{9,8},{10,9... | collective-permute-start | bytes 294920 | tf_op jit(solution)/shard_map/ppermute | solution.py:311
  6.1 1.0 %collective-permute-start = (bf16[2,32,768]{2,1,0:T(8,128)(2,1)S(1)}, bf16[2,32,768]{2,1,0:T(8,128)(2,1)S(1)}, u32[]{:S(2)}, u32[]{:S(2)}) collective-permute-start(bf16[2,32,768]{2,1,0:T(8,128)(2,1)S(1)} %get-tuple-element.23), channel_id=1, source_target_pairs={{0,1},{1,2},{2,3},{3,0},{4,5},{5,6},{6,7},{7,4},{8,9},{9,10},{10,1... | collective-permute-start | bytes 294920 | tf_op jit(solution)/shard_map/ppermute | solution.py:311
  7.1 2.8 %copy-done = bf16[2,768,2048]{2,1,0:T(8,128)(2,1)S(1)} copy-done((bf16[2,768,2048]{2,1,0:T(8,128)(2,1)S(1)}, bf16[2,768,2048]{2,1,0:T(8,128)(2,1)}, u32[]{:S(2)}) %copy-start) | copy-done | bytes 6291480
  9.9 5.2 %front.1 = (bf16[2,768,2048]{2,1,0:T(8,128)(2,1)S(1)}, bf16[2,768,128]{2,1,0:T(8,128)(2,1)S(1)}, f32[2,32,2048]{2,1,0:T(8,128)S(1)}) custom-call(bf16[2,768,2048]{2,1,0:T(8,128)(2,1)S(1)} %copy-done, f32[2,32,768]{2,1,0:T(8,128)} %step_ref.1, f32[2,32,768]{2,1,0:T(8,128)} %decay_ref.1, f32[1,32]{1,0:T(1,128)} %bitcast.39, ...), custom_call_target="tpu_custom_call" | custom-call | flops 402653184 | bytes 12582912 | tf_op jit(solution)/shard_map/front/pallas_call | solution.py:107
  15.1 0.1 pad.7.clone
  15.3 0.0 collective-permute-done.2
  15.3 0.0 slice-start
  15.3 0.0 copy-start.1
  15.3 1.9 %own_states.1 = (bf16[2,5,128,2048]{3,2,1,0:T(8,128)(2,1)S(1)}, bf16[2,128,2048]{2,1,0:T(8,128)(2,1)S(1)}) custom-call(bf16[2,128,768]{2,1,0:T(8,128)(2,1)S(1)} %constant_dynamic-update-slice_fusion.b_ref, bf16[2,768,2048]{2,1,0:T(8,128)(2,1)S(1)} %get-tuple-element.24.weighted_ref, f32[2,32,2048]{2,1,0:T(8,128)S(1)} %get-tuple-element.25.rows_ref), custom_call_target="tpu_custom_call" | custom-call | flops 805306368 | bytes 6291456 | tf_op jit(solution)/shard_map/own_states/pallas_call | solution.py:149
  17.3 0.1 select_bitcast_fusion
  17.3 0.2 maximum_maximum_fusion
  17.5 0.1 collective-permute-start.3
  17.6 2.9 %collective-permute-start.7 = (bf16[2,32,768]{2,1,0:T(8,128)(2,1)S(1)}, bf16[2,32,768]{2,1,0:T(8,128)(2,1)S(1)}, u32[]{:S(2)}, u32[]{:S(2)}) collective-permute-start(bf16[2,32,768]{2,1,0:T(8,128)(2,1)S(1)} %get-tuple-element.29), channel_id=1, source_target_pairs={{0,3},{1,0},{2,1},{3,2},{4,7},{5,4},{6,5},{7,6},{8,11},{9,8},{10,9... | collective-permute-start | bytes 294920 | tf_op jit(solution)/shard_map/ppermute | solution.py:311
  20.4 1.1 %collective-permute-start.6 = (bf16[2,32,768]{2,1,0:T(8,128)(2,1)S(1)}, bf16[2,32,768]{2,1,0:T(8,128)(2,1)S(1)}, u32[]{:S(2)}, u32[]{:S(2)}) collective-permute-start(bf16[2,32,768]{2,1,0:T(8,128)(2,1)S(1)} %get-tuple-element.29), channel_id=1, source_target_pairs={{0,2},{1,3},{2,0},{3,1},{4,6},{5,7},{6,4},{7,5},{8,10},{9,11},{10,... | collective-permute-start | bytes 294920 | tf_op jit(solution)/shard_map/ppermute | solution.py:311
  21.6 0.3 fusion
  21.9 3.6 %collective-permute-start.4 = (bf16[128,2048]{1,0:T(8,128)(2,1)S(1)}, bf16[128,2048]{1,0:T(8,128)(2,1)S(1)}, u32[]{:S(2)}, u32[]{:S(2)}) collective-permute-start(bf16[128,2048]{1,0:T(8,128)(2,1)S(1)} %fusion), channel_id=1, source_target_pairs={{0,8},{4,12},{1,9},{5,13},{2,10},{6,14},{3,11},{7,15},{16,24},{20,... | collective-permute-start | bytes 1572872 | tf_op jit(solution)/shard_map/ppermute | solution.py:361
  25.5 5.5 %collective-permute-done.6 = bf16[2,32,768]{2,1,0:T(8,128)(2,1)S(1)} collective-permute-done((bf16[2,32,768]{2,1,0:T(8,128)(2,1)S(1)}, bf16[2,32,768]{2,1,0:T(8,128)(2,1)S(1)}, u32[]{:S(2)}, u32[]{:S(2)}) %collective-permute-start.6) | collective-permute-done | bytes 98336 | tf_op jit(solution)/shard_map/ppermute | solution.py:311
  31.1 7.9 %local_terms.1 = (bf16[2,768,2048]{2,1,0:T(8,128)(2,1)S(1)}, bf16[2,768,2048]{2,1,0:T(8,128)(2,1)S(1)}) custom-call(bf16[2,768,2048]{2,1,0:T(8,128)(2,1)S(1)} %copy-done.1, bf16[2,768,2048]{2,1,0:T(8,128)(2,1)S(1)} %bitcast.29, bf16[2,768,2048]{2,1,0:T(8,128)(2,1)S(1)} %get-tuple-element.24.weighted_ref, ...), custom_call_target="tpu_custom_call" | custom-call | flops 3221225472 | bytes 25165824 | tf_op jit(solution)/shard_map/local_terms/pallas_call | solution.py:202
  39.0 0.2 fusion.3
  39.2 0.1 collective-permute-start.8
  39.3 1.9 %collective-permute-done.8 = bf16[128,2048]{1,0:T(8,128)(2,1)S(1)} collective-permute-done((bf16[128,2048]{1,0:T(8,128)(2,1)S(1)}, bf16[128,2048]{1,0:T(8,128)(2,1)S(1)}, u32[]{:S(2)}, u32[]{:S(2)}) %collective-permute-start.8) | collective-permute-done | bytes 524320 | tf_op jit(solution)/shard_map/ppermute | solution.py:371
  41.2 0.3 fusion.4
  41.5 0.0 copy-start.2
  41.5 3.8 %joined.1 = (bf16[2,768,2048]{2,1,0:T(8,128)(2,1)S(1)}, f32[12,1,128]{2,1,0:T(1,128)S(1)}) custom-call(bf16[2,768,2048]{2,1,0:T(8,128)(2,1)S(1)} %get-tuple-element.36.own_ref, bf16[2,768,2048]{2,1,0:T(8,128)(2,1)S(1)} %get-tuple-element.37.factor_ref, ...), custom_call_target="tpu_custom_call", output_to_operand_aliasing={{0}: (0, {})} | custom-call | flops 805306368 | bytes 18874368 | tf_op jit(solution)/shard_map/joined/pallas_call | solution.py:243
  45.3 1.1 %collective-permute-start.11 = (f32[12,1,128]{2,1,0:T(1,128)S(1)}, f32[12,1,128]{2,1,0:T(1,128)S(1)}, u32[]{:S(2)}, u32[]{:S(2)}) collective-permute-start(f32[12,1,128]{2,1,0:T(1,128)S(1)} %get-tuple-element.40), channel_id=1, source_target_pairs={{0,3},{1,0},{2,1},{3,2},{4,7},{5,4},{6,5},{7,6},{8,11},{9,8},{10,9... | collective-permute-start | bytes 18440 | tf_op jit(solution)/shard_map/ppermute | solution.py:311
  46.5 0.2 collective-permute-start.10
  46.6 1.9 %collective-permute-start.9 = (f32[12,1,128]{2,1,0:T(1,128)S(1)}, f32[12,1,128]{2,1,0:T(1,128)S(1)}, u32[]{:S(2)}, u32[]{:S(2)}) collective-permute-start(f32[12,1,128]{2,1,0:T(1,128)S(1)} %get-tuple-element.40), channel_id=1, source_target_pairs={{0,1},{1,2},{2,3},{3,0},{4,5},{5,6},{6,7},{7,4},{8,9},{9,10},{10,1... | collective-permute-start | bytes 18440 | tf_op jit(solution)/shard_map/ppermute | solution.py:311
  48.6 0.4 collective-permute-done.11
  49.0 2.0 %collective-permute-done.10 = f32[12,1,128]{2,1,0:T(1,128)S(1)} collective-permute-done((f32[12,1,128]{2,1,0:T(1,128)S(1)}, f32[12,1,128]{2,1,0:T(1,128)S(1)}, u32[]{:S(2)}, u32[]{:S(2)}) %collective-permute-start.10) | collective-permute-done | bytes 6176 | tf_op jit(solution)/shard_map/ppermute | solution.py:311
  51.0 1.0 %collective-permute-done.9 = f32[12,1,128]{2,1,0:T(1,128)S(1)} collective-permute-done((f32[12,1,128]{2,1,0:T(1,128)S(1)}, f32[12,1,128]{2,1,0:T(1,128)S(1)}, u32[]{:S(2)}, u32[]{:S(2)}) %collective-permute-start.9) | collective-permute-done | bytes 6176 | tf_op jit(solution)/shard_map/ppermute | solution.py:311
  52.1 3.1 %normed.1 = bf16[2,768,2048]{2,1,0:T(8,128)(2,1)} custom-call(bf16[2,768,2048]{2,1,0:T(8,128)(2,1)S(1)} %get-tuple-element.39.gated_ref, f32[4,12,1,128]{3,2,1,0:T(1,128)S(1)} %pad_maximum_fusion.square_ref, f32[1,2048]{1,0:T(1,128)S(1)} %bitcast.30), custom_call_target="tpu_custom_call" | custom-call | flops 6291456 | bytes 12582912 | tf_op jit(solution)/shard_map/normed/pallas_call | solution.py:289
  (29 shorter events, 0.2 us)
Async XLA Ops:
  1.0 14.3 %collective-permute-start.2 = (bf16[2,32,768]{2,1,0:T(8,128)(2,1)S(1)}, bf16[2,32,768]{2,1,0:T(8,128)(2,1)S(1)}, u32[]{:S(2)}, u32[]{:S(2)}) collective-permute-start(bf16[2,32,768]{2,1,0:T(8,128)(2,1)S(1)} %get-tuple-element.23), channel_id=1, source_target_pairs={{0,3},{1,0},{2,1},{3,2},{4,7},{5,4},{6,5},{7,6},{8,11},{9,8},{10,9... | collective-permute-start | bytes 294920 | tf_op jit(solution)/shard_map/ppermute | solution.py:311
  6.1 9.2 %collective-permute-start.1 = (bf16[2,32,768]{2,1,0:T(8,128)(2,1)S(1)}, bf16[2,32,768]{2,1,0:T(8,128)(2,1)S(1)}, u32[]{:S(2)}, u32[]{:S(2)}) collective-permute-start(bf16[2,32,768]{2,1,0:T(8,128)(2,1)S(1)} %get-tuple-element.23), channel_id=1, source_target_pairs={{0,2},{1,3},{2,0},{3,1},{4,6},{5,7},{6,4},{7,5},{8,10},{9,11},{10,... | collective-permute-start | bytes 294920 | tf_op jit(solution)/shard_map/ppermute | solution.py:311
  6.1 9.1 %collective-permute-start = (bf16[2,32,768]{2,1,0:T(8,128)(2,1)S(1)}, bf16[2,32,768]{2,1,0:T(8,128)(2,1)S(1)}, u32[]{:S(2)}, u32[]{:S(2)}) collective-permute-start(bf16[2,32,768]{2,1,0:T(8,128)(2,1)S(1)} %get-tuple-element.23), channel_id=1, source_target_pairs={{0,1},{1,2},{2,3},{3,0},{4,5},{5,6},{6,7},{7,4},{8,9},{9,10},{10,1... | collective-permute-start | bytes 294920 | tf_op jit(solution)/shard_map/ppermute | solution.py:311
  7.1 2.8 %copy-start = (bf16[2,768,2048]{2,1,0:T(8,128)(2,1)S(1)}, bf16[2,768,2048]{2,1,0:T(8,128)(2,1)}, u32[]{:S(2)}) copy-start(bf16[2,768,2048]{2,1,0:T(8,128)(2,1)} %x_ref.3) | copy-start | bytes 18874372
  15.3 15.8 %slice-start = ((s8[6291456]{0:T(1024)(128)(4,1)}), s8[4194304]{0:T(1024)(128)(4,1)S(1)}, s32[]{:S(2)}) async-start(s8[6291456]{0:T(1024)(128)(4,1)} %bitcast.28), calls=%async_computation | async-start | bytes 8388608
  15.3 15.8 %slice-start.1 = ((s8[6291456]{0:T(1024)(128)(4,1)}), s8[2097152]{0:T(1024)(128)(4,1)S(1)}, s32[]{:S(2)}) async-start(s8[6291456]{0:T(1024)(128)(4,1)} %bitcast.28), calls=%async_computation.1 | async-start | bytes 4194304
  15.3 15.8 %copy-start.1 = (bf16[2,768,2048]{2,1,0:T(8,128)(2,1)S(1)}, bf16[2,768,2048]{2,1,0:T(8,128)(2,1)}, u32[]{:S(2)}) copy-start(bf16[2,768,2048]{2,1,0:T(8,128)(2,1)} %gate_ref.1) | copy-start | bytes 18874372
  17.5 4.1 %collective-permute-start.3 = (bf16[144,2048]{1,0:T(8,128)(2,1)S(1)}, bf16[144,2048]{1,0:T(8,128)(2,1)S(1)}, u32[]{:S(2)}, u32[]{:S(2)}) collective-permute-start(bf16[144,2048]{1,0:T(8,128)(2,1)S(1)} %maximum_maximum_fusion), channel_id=1, source_target_pairs={{0,4},{4,0},{8,12},{12,8},{1,5},{5,1},{9,13},{13,9},{2,6},{6,2},{1... | collective-permute-start | bytes 1769480 | tf_op jit(solution)/shard_map/ppermute | solution.py:342
  17.6 8.0 %collective-permute-start.7 = (bf16[2,32,768]{2,1,0:T(8,128)(2,1)S(1)}, bf16[2,32,768]{2,1,0:T(8,128)(2,1)S(1)}, u32[]{:S(2)}, u32[]{:S(2)}) collective-permute-start(bf16[2,32,768]{2,1,0:T(8,128)(2,1)S(1)} %get-tuple-element.29), channel_id=1, source_target_pairs={{0,3},{1,0},{2,1},{3,2},{4,7},{5,4},{6,5},{7,6},{8,11},{9,8},{10,9... | collective-permute-start | bytes 294920 | tf_op jit(solution)/shard_map/ppermute | solution.py:311
  20.4 10.6 %collective-permute-start.6 = (bf16[2,32,768]{2,1,0:T(8,128)(2,1)S(1)}, bf16[2,32,768]{2,1,0:T(8,128)(2,1)S(1)}, u32[]{:S(2)}, u32[]{:S(2)}) collective-permute-start(bf16[2,32,768]{2,1,0:T(8,128)(2,1)S(1)} %get-tuple-element.29), channel_id=1, source_target_pairs={{0,2},{1,3},{2,0},{3,1},{4,6},{5,7},{6,4},{7,5},{8,10},{9,11},{10,... | collective-permute-start | bytes 294920 | tf_op jit(solution)/shard_map/ppermute | solution.py:311
  21.6 9.4 %collective-permute-start.5 = (bf16[2,32,768]{2,1,0:T(8,128)(2,1)S(1)}, bf16[2,32,768]{2,1,0:T(8,128)(2,1)S(1)}, u32[]{:S(2)}, u32[]{:S(2)}) collective-permute-start(bf16[2,32,768]{2,1,0:T(8,128)(2,1)S(1)} %get-tuple-element.29), channel_id=1, source_target_pairs={{0,1},{1,2},{2,3},{3,0},{4,5},{5,6},{6,7},{7,4},{8,9},{9,10},{10,1... | collective-permute-start | bytes 294920 | tf_op jit(solution)/shard_map/ppermute | solution.py:311
  21.9 17.0 %collective-permute-start.4 = (bf16[128,2048]{1,0:T(8,128)(2,1)S(1)}, bf16[128,2048]{1,0:T(8,128)(2,1)S(1)}, u32[]{:S(2)}, u32[]{:S(2)}) collective-permute-start(bf16[128,2048]{1,0:T(8,128)(2,1)S(1)} %fusion), channel_id=1, source_target_pairs={{0,8},{4,12},{1,9},{5,13},{2,10},{6,14},{3,11},{7,15},{16,24},{20,... | collective-permute-start | bytes 1572872 | tf_op jit(solution)/shard_map/ppermute | solution.py:361
  39.2 2.0 %collective-permute-start.8 = (bf16[128,2048]{1,0:T(8,128)(2,1)S(1)}, bf16[128,2048]{1,0:T(8,128)(2,1)S(1)}, u32[]{:S(2)}, u32[]{:S(2)}) collective-permute-start(bf16[128,2048]{1,0:T(8,128)(2,1)S(1)} %fusion.3), channel_id=1, source_target_pairs={{0,4},{4,0},{8,12},{12,8},{1,5},{5,1},{9,13},{13,9},{2,6},{6,2},{1... | collective-permute-start | bytes 1572872 | tf_op jit(solution)/shard_map/ppermute | solution.py:371
  41.5 10.6 %copy-start.2 = (f32[2048]{0:T(1024)S(1)}, f32[2048]{0:T(1024)}, u32[]{:S(2)}) copy-start(f32[2048]{0:T(1024)} %param.14) | copy-start | bytes 24580
  45.3 3.7 %collective-permute-start.11 = (f32[12,1,128]{2,1,0:T(1,128)S(1)}, f32[12,1,128]{2,1,0:T(1,128)S(1)}, u32[]{:S(2)}, u32[]{:S(2)}) collective-permute-start(f32[12,1,128]{2,1,0:T(1,128)S(1)} %get-tuple-element.40), channel_id=1, source_target_pairs={{0,3},{1,0},{2,1},{3,2},{4,7},{5,4},{6,5},{7,6},{8,11},{9,8},{10,9... | collective-permute-start | bytes 18440 | tf_op jit(solution)/shard_map/ppermute | solution.py:311
  46.5 4.6 %collective-permute-start.10 = (f32[12,1,128]{2,1,0:T(1,128)S(1)}, f32[12,1,128]{2,1,0:T(1,128)S(1)}, u32[]{:S(2)}, u32[]{:S(2)}) collective-permute-start(f32[12,1,128]{2,1,0:T(1,128)S(1)} %get-tuple-element.40), channel_id=1, source_target_pairs={{0,2},{1,3},{2,0},{3,1},{4,6},{5,7},{6,4},{7,5},{8,10},{9,11},{10,... | collective-permute-start | bytes 18440 | tf_op jit(solution)/shard_map/ppermute | solution.py:311
  46.6 5.4 %collective-permute-start.9 = (f32[12,1,128]{2,1,0:T(1,128)S(1)}, f32[12,1,128]{2,1,0:T(1,128)S(1)}, u32[]{:S(2)}, u32[]{:S(2)}) collective-permute-start(f32[12,1,128]{2,1,0:T(1,128)S(1)} %get-tuple-element.40), channel_id=1, source_target_pairs={{0,1},{1,2},{2,3},{3,0},{4,5},{5,6},{6,7},{7,4},{8,9},{9,10},{10,1... | collective-permute-start | bytes 18440 | tf_op jit(solution)/shard_map/ppermute | solution.py:311

commit v6 on v5

v6 whole, which is shorter than its diff:
```python
import functools

import jax
import jax.numpy as jnp
import numpy as np
from jax import lax
from jax.experimental import pallas as pl
from jax.experimental.pallas import tpu as pltpu
from jax.sharding import PartitionSpec as P

SPAN = 128
HALF = 256
F32 = jnp.float32
BF16 = jnp.bfloat16
VMEM_LIMIT = 12 * 1024 * 1024
PARAMS = pltpu.CompilerParams(vmem_limit_bytes=VMEM_LIMIT)
ENTER, LEAVE, FIRST, TOTAL = range(4)
ROWS = 32
WHOLE = pl.BlockSpec(memory_space=pltpu.VMEM)
ANYWHERE = pl.BlockSpec(memory_space=pl.ANY)


def in_vmem(array):
    return pltpu.with_memory_space_constraint(array, pltpu.VMEM)


def in_hbm(array):
    return pltpu.with_memory_space_constraint(array, pltpu.HBM)


def mm(a, b):
    return jnp.dot(a, b, preferred_element_type=F32)


def mm_nt(a, b):
    return lax.dot_general(a, b, (((1,), (1,)), ((), ())), preferred_element_type=F32)


def iotas(shape):
    return (
        lax.broadcasted_iota(jnp.int32, shape, 0),
        lax.broadcasted_iota(jnp.int32, shape, 1),
    )


def three_parts(v):
    high = v.astype(BF16)
    rest = v - high.astype(F32)
    mid = rest.astype(BF16)
    return [high, mid, (rest - mid.astype(F32)).astype(BF16)]


def fill_tables(step_ref, decay_ref, skip_ref, sums_ref, rise_band, both_ref, rows_ref):
    seqs, heads, length = decay_ref.shape
    blocks = length // SPAN
    _, lane = iotas((SPAN, 4 * heads))
    rising = lane < 2 * heads
    is_high = (lane < heads) | ((lane >= 2 * heads) & (lane < 3 * heads))
    until = sums_ref[:SPAN]
    same = sums_ref[SPAN:]

    def parts_of(v):
        high = v.astype(BF16).astype(F32)
        return jnp.where(is_high[:v.shape[0]], high, v - high).astype(BF16)

    skip = jnp.concatenate([skip_ref[...]] * 4, axis=1)
    for s in range(seqs):
        decays = three_parts(jnp.concatenate([decay_ref[s]] * 4, axis=0))
        steps = three_parts(jnp.concatenate([step_ref[s]] * 4, axis=0))
        enter, leave, first = [], [], []
        before = jnp.zeros((1, 4 * heads), F32)
        for k in range(blocks):
            sl = slice(k * SPAN, (k + 1) * SPAN)
            summed = mm_nt(until, jnp.concatenate([p[:, sl] for p in decays], axis=1))
            step = mm_nt(same, jnp.concatenate([p[:, sl] for p in steps], axis=1))
            middle = summed[SPAN // 2 - 1:SPAN // 2]
            last = summed[SPAN - 1:]
            above = summed - middle
            factor = jnp.exp(jnp.where(rising, above, -above))
            both_ref[s, sl, :] = parts_of(jnp.where(rising, factor, step * factor))
            enter.append(jnp.exp(middle))
            leave.append(jnp.exp(last - middle))
            first.append(jnp.exp(middle + before))
            before = before + last
        table = enter + leave + first + [jnp.exp(before)]
        table = table + [jnp.zeros_like(before)] * (ROWS - 1 - len(table)) + [skip]
        rows_ref[s] = mm(parts_of(jnp.concatenate(table, axis=0)), rise_band)


def front_kernel(
    x_hbm, step_hbm, decay_hbm, skip_ref, sums_ref, bands_hbm,
    x_ref, weighted_ref, both_ref, rows_ref, step, decay, bands, sems,
):
    seqs, length, channels = x_ref.shape
    heads = decay.shape[1]
    blocks = length // SPAN
    small = [
        pltpu.make_async_copy(source, target, sems.at[seqs * blocks + i])
        for i, (source, target) in enumerate(
            [(decay_hbm, decay), (step_hbm, step), (bands_hbm, bands)]
        )
    ]
    for copy in small:
        copy.start()
    copies = []
    for s in range(seqs):
        for k in range(blocks):
            place = (s, pl.ds(k * SPAN, SPAN))
            copies.append(
                pltpu.make_async_copy(x_hbm.at[place], x_ref.at[place], sems.at[s * blocks + k])
            )
            copies[-1].start(priority=k % 2)
    for copy in small:
        copy.wait()
    fill_tables(
        step, decay, skip_ref, sums_ref, bands[2 * heads:], both_ref, rows_ref
    )
    for s in range(seqs):
        for k in range(blocks):
            rows = slice(k * SPAN, (k + 1) * SPAN)
            copies[s * blocks + k].wait()
            both = both_ref[s, rows]
            for lo in range(0, channels, HALF):
                sl = slice(lo, lo + HALF)
                wide = mm(both, bands[:4 * heads, sl]).astype(BF16)
                weighted_ref[s, rows, sl] = x_ref[s, rows, sl] * wide


def front(features, step_size, log_decay, skip, sums, bands):
    seqs, length, channels = features.shape
    heads = step_size.shape[1]
    return pl.pallas_call(
        front_kernel,
        in_specs=[ANYWHERE, ANYWHERE, ANYWHERE, WHOLE, WHOLE, ANYWHERE],
        out_specs=[WHOLE] * 4,
        out_shape=[
            pltpu.VMEM(features.shape, BF16),
            pltpu.VMEM(features.shape, BF16),
            pltpu.VMEM((seqs, length, 4 * heads), BF16),
            pltpu.VMEM((seqs, ROWS, channels), F32),
        ],
        scratch_shapes=[
            pltpu.VMEM(step_size.shape, F32),
            pltpu.VMEM(log_decay.shape, F32),
            pltpu.VMEM(bands.shape, BF16),
            pltpu.SemaphoreType.DMA((seqs * (length // SPAN) + 3,)),
        ],
        compiler_params=PARAMS,
        cost_estimate=pl.CostEstimate(
            flops=2 * seqs * length * channels * 64,
            bytes_accessed=4 * seqs * length * channels,
            transcendentals=0,
        ),
        name="front",
    )(
        in_hbm(features), in_hbm(step_size), in_hbm(log_decay), in_hbm(skip), in_hbm(sums),
        in_hbm(bands),
    )


def state_kernel(b_ref, weighted_ref, rows_ref, entering_ref, state_ref):
    seqs, length, channels = weighted_ref.shape
    blocks = length // SPAN
    for s in range(seqs):
        for lo in range(0, channels, HALF):
            sl = slice(lo, lo + HALF)
            state = None
            for k in range(blocks):
                rows = slice(k * SPAN, (k + 1) * SPAN)
                added = mm(b_ref[s, :, rows], weighted_ref[s, rows, sl])
                if k > 0:
                    at = ENTER * blocks + k
                    entering = rows_ref[s, at:at + 1, sl] * state
                    entering_ref[s, k - 1, :, sl] = entering.astype(BF16)
                    added = added + entering
                at = LEAVE * blocks + k
                state = rows_ref[s, at:at + 1, sl] * added
            state_ref[s, :, sl] = state.astype(BF16)


def own_states(b, weighted, rows):
    seqs, states, length = b.shape
    channels = weighted.shape[2]
    return pl.pallas_call(
        state_kernel,
        in_specs=[WHOLE] * 3,
        out_specs=[WHOLE] * 2,
        out_shape=[
            pltpu.VMEM((seqs, length // SPAN - 1, states, channels), BF16),
            pltpu.VMEM((seqs, states, channels), BF16),
        ],
        compiler_params=PARAMS,
        cost_estimate=pl.CostEstimate(
            flops=2 * seqs * length * channels * states,
            bytes_accessed=2 * seqs * length * channels,
            transcendentals=0,
        ),
        name="own_states",
    )(b, in_vmem(weighted), in_vmem(rows))


def gate_kernel(gate_ref, x_ref, both_ref, band_ref, rows_ref, lift_ref, skipped_ref):
    seqs, length, channels = lift_ref.shape
    for s in range(seqs):
        for k in range(length // SPAN):
            rows = slice(k * SPAN, (k + 1) * SPAN)
            both = both_ref[s, rows]
            for lo in range(0, channels, HALF):
                sl = slice(lo, lo + HALF)
                half = 0.5 * gate_ref[s, rows, sl].astype(F32)
                gate = (half * jnp.tanh(half) + half).astype(BF16)
                lift_ref[s, rows, sl] = mm(both, band_ref[:, sl]).astype(BF16) * gate
                skip = rows_ref[s, ROWS - 1:ROWS, sl].astype(BF16) * x_ref[s, rows, sl]
                skipped_ref[s, rows, sl] = skip * gate


def gates(gate_in, x, both, band, rows):
    seqs, length, channels = gate_in.shape
    return pl.pallas_call(
        gate_kernel,
        in_specs=[WHOLE] * 5,
        out_specs=[WHOLE, WHOLE],
        out_shape=[pltpu.VMEM(gate_in.shape, BF16)] * 2,
        compiler_params=PARAMS,
        cost_estimate=pl.CostEstimate(
            flops=2 * seqs * length * channels * 256,
            bytes_accessed=8 * seqs * length * channels,
            transcendentals=seqs * length * channels,
        ),
        name="gates",
    )(in_vmem(gate_in), in_vmem(x), in_vmem(both), band, in_vmem(rows))


def final_kernel(
    weighted_ref, entering_ref, lift_ref, skipped_ref, b_ref, c_ref, rows_ref, *refs
):
    gated_ref, square_ref = refs[-2:]
    seqs, length, channels = lift_ref.shape
    blocks = length // SPAN
    row, col = iotas((SPAN, SPAN))
    for s in range(seqs):
        for k in range(blocks):
            rows = slice(k * SPAN, (k + 1) * SPAN)
            c_t = c_ref[s, :, rows].T
            affinity = mm(c_t, b_ref[s, :, rows])
            masked = jnp.where(row >= col, affinity, 0.0).astype(BF16)
            left = jnp.concatenate([masked, c_t], axis=1)
            squares = jnp.zeros((SPAN, 128), F32)
            at = FIRST * blocks + k
            for lo in range(0, channels, HALF):
                sl = slice(lo, lo + HALF)
                entering = rows_ref[s, at:at + 1, sl].astype(BF16) * refs[s][:, sl]
                if k > 0:
                    entering = entering + entering_ref[s, k - 1, :, sl]
                right = jnp.concatenate([weighted_ref[s, rows, sl], entering], axis=0)
                mixed = mm(left, right).astype(BF16)
                gated = lift_ref[s, rows, sl] * mixed + skipped_ref[s, rows, sl]
                gated_ref[s, rows, sl] = gated
                power = gated * gated
                pair = sum(power[:, left_:left_ + 128] for left_ in range(0, HALF, 128))
                squares = squares + pair.astype(F32)
            square_ref[s * blocks + k] = jnp.sum(squares.T, axis=0, keepdims=True)


def final(weighted, entering, lift, skipped, b, c, rows, incoming):
    seqs, length, channels = lift.shape
    states = c.shape[1]
    return pl.pallas_call(
        final_kernel,
        in_specs=[WHOLE] * (7 + seqs),
        out_specs=[WHOLE] * 2,
        out_shape=[
            pltpu.VMEM(lift.shape, BF16),
            pltpu.VMEM((seqs * (length // SPAN), 1, SPAN), F32),
        ],
        compiler_params=PARAMS,
        cost_estimate=pl.CostEstimate(
            flops=4 * seqs * length * channels * states,
            bytes_accessed=6 * seqs * length * channels,
            transcendentals=0,
        ),
        name="final",
    )(
        in_vmem(weighted), in_vmem(entering), in_vmem(lift), in_vmem(skipped), b, c,
        in_vmem(rows), *incoming,
    )


def norm_kernel(all_channels, gated_ref, square_ref, gain_ref, out_hbm, staged, sems):
    seqs, length, channels = gated_ref.shape
    blocks = length // SPAN
    copies = []
    for s in range(seqs):
        for k in range(blocks):
            at = s * blocks + k
            rows = slice(k * SPAN, (k + 1) * SPAN)
            total = jnp.sum(square_ref[:, at, 0], axis=0, keepdims=True)
            inverse = lax.rsqrt(total / all_channels + 1e-05)
            column = jnp.broadcast_to(inverse, (128, SPAN)).T
            for lo in range(0, channels, 128):
                sl = slice(lo, lo + 128)
                staged[s, rows, sl] = (
                    gated_ref[s, rows, sl].astype(F32) * column * gain_ref[:, sl]
                ).astype(BF16)
            place = (s, pl.ds(k * SPAN, SPAN))
            copies.append(
                pltpu.make_async_copy(staged.at[place], out_hbm.at[place], sems.at[at])
            )
            copies[-1].start(priority=k % 2)
    for copy in copies:
        copy.wait()


def normed(gated, squares, gain_row, all_channels):
    seqs, length, channels = gated.shape
    return pl.pallas_call(
        functools.partial(norm_kernel, all_channels),
        in_specs=[WHOLE] * 3,
        out_specs=ANYWHERE,
        out_shape=jax.ShapeDtypeStruct(gated.shape, BF16),
        scratch_shapes=[
            pltpu.VMEM(gated.shape, BF16),
            pltpu.SemaphoreType.DMA((seqs * (length // SPAN),)),
        ],
        compiler_params=PARAMS,
        cost_estimate=pl.CostEstimate(
            flops=2 * seqs * length * channels,
            bytes_accessed=4 * seqs * length * channels,
            transcendentals=0,
        ),
        name="normed",
    )(in_vmem(gated), squares, gain_row)


def from_all(shard, axis):
    devices = lax.axis_size(axis)
    return [shard] + [
        lax.ppermute(shard, axis, [(i, (i + by) % devices) for i in range(devices)])
        for by in range(1, devices)
    ]


def as_parts(row):
    high = row.astype(BF16)
    low = (row - high.astype(F32)).astype(BF16)
    return jnp.concatenate([high, low, jnp.zeros((14, row.shape[1]), BF16)], axis=0)


def body(features, gate_in, state_proj, step_size, log_decay, skip_gain, norm_gain):
    seqs, length, channels = features.shape
    heads = step_size.shape[1]
    pair = np.repeat(np.concatenate([np.eye(heads)] * 2), channels // heads, axis=1)
    bands = jnp.asarray(np.concatenate([0 * pair, pair, 0 * pair]), BF16)
    rise_band = jnp.asarray(np.concatenate([pair, 0 * pair]), BF16)
    until = np.tril(np.ones((SPAN, SPAN)))
    sums = jnp.asarray(np.concatenate([np.tile(until, 3), np.tile(np.eye(SPAN), 3)]), BF16)
    b_own, c_own = lax.optimization_barrier((state_proj[0], state_proj[1]))
    b = jnp.concatenate(from_all(b_own, "head"), axis=1)
    states = b.shape[1]
    x, weighted, both, rows = front(
        features, step_size, log_decay, skip_gain[None, :], sums, bands
    )
    entering, ends = own_states(b, weighted, rows)

    place = lax.axis_index("ctx")
    even = place % 2 == 0
    devices = lax.axis_size("ctx")
    swap = [(i, i ^ 1) for i in range(devices)]
    total_at = TOTAL * (length // SPAN)
    decay = [rows[s, total_at:total_at + 1] for s in range(seqs)]
    other = lax.ppermute(
        jnp.concatenate([
            jnp.where(even, ends[1], ends[0]),
            as_parts(jnp.where(even, decay[1], decay[0])),
        ]),
        "ctx", swap,
    )
    end_other = other[:states].astype(F32)
    decay_other = other[states:states + 1].astype(F32) + other[states + 1:states + 2].astype(F32)
    end_first = ends[0].astype(F32)
    past = jnp.where(
        even,
        end_other + decay_other * end_first,
        ends[1].astype(F32) + decay[1] * end_other,
    )
    decay_past = decay_other * jnp.where(even, decay[0], decay[1])
    entered = None
    for hop in range(0, devices - 2, 2):
        sent = past if entered is None else past + decay_past * entered.astype(F32)
        got = lax.ppermute(sent.astype(BF16), "ctx", [(hop, hop + 2), (hop + 1, hop + 3)])
        if entered is None:
            c_own, x, _ = lax.optimization_barrier((c_own, x, sent))
            c = from_all(c_own, "head")
            terms = gates(gate_in, x, both, rise_band, rows)
            got, terms, c = lax.optimization_barrier((got, terms, c))
            c = jnp.concatenate(c, axis=1)
        entered = got if entered is None else entered + got
    entered32 = entered.astype(F32)
    shared = lax.ppermute(
        jnp.where(even, end_first + decay[0] * entered32, entered32).astype(BF16), "ctx", swap
    )
    incoming = [
        jnp.where(even, entered, shared),
        jnp.where(even, shared, (end_other + decay_other * entered32).astype(BF16)),
    ]
    gated, squares = final(weighted, entering, *terms, b, c, rows, incoming)
    squares = lax.all_gather(squares, "head")
    return normed(gated, squares, norm_gain[None, :], channels * lax.axis_size("head"))


def solution(mesh):
    in_specs = (
        P("groups", "ctx", "head"),
        P("groups", "ctx", "head"),
        P(None, "groups", "head", "ctx"),
        P("groups", "head", "ctx"),
        P("groups", "head", "ctx"),
        P("head"),
        P("head"),
    )
    out_specs = P("groups", "ctx", "head")
    return jax.shard_map(body, mesh=mesh, in_specs=in_specs, out_specs=out_specs, check_vma=False)
```

time: 55.6 us -> 61.5 us (1.11)
  blocking collectives: 0 us -> 13.1 us
  waiting for transfers between devices: 10.9 us -> 3.84 us
  local copies, waits for them, and re-layouts: 3.93 us -> 6.59 us
  starting transfers between devices: 17.1 us -> 14.5 us
    all_gather x0 -> x1, blocking collectives: none -> 13.1 us  [body(): squares = lax.all_gather(squares, 'head')]
    ppermute x9 -> x6, waiting for transfers between devices: 8.95 us -> 0.02 us  [from_all(): lax.ppermute(shard, axis, [(i, (i + by) % devices) for i in range(devices)])]
    unnamed x16 -> x15, local copies, waits for them, and re-layouts: 2.86 us -> 5.53 us
    ppermute x9 -> x6, starting transfers between devices: 13.4 us -> 10.9 us  [from_all(): lax.ppermute(shard, axis, [(i, (i + by) % devices) for i in range(devices)])]
    ppermute x1, waiting for transfers between devices: 0.01 us -> 1.97 us  [body(): lax.ppermute(jnp.concatenate([jnp.where(even, ends[1], ends[0]), as_parts...]
  transfers between devices with their start and end apart: 12 -> 9, of which waited for: 5 -> 2; matrix products, arithmetic and copies ran while one was open for 1% -> 0% of each run, Pallas kernels for 24% -> 20%
where the time goes in v6:
time: 61.5 us; the launch traced here: 61.3 us
  Pallas kernels  21.8 us (35%)
  starting transfers between devices  14.5 us (24%)
  blocking collectives  13.1 us (21%)
  local copies, waits for them, and re-layouts  6.59 us (11%)
  waiting for transfers between devices  3.84 us (6%)
  other arithmetic  1.12 us (2%)
    all_gather x1, blocking collectives, body(): squares = lax.all_gather(squares, 'head')  13.1 us
    ppermute x6, starting transfers between devices, from_all(): lax.ppermute(shard, axis, [(i, (i + by) % devices) for i in range(devices)])  10.9 us
    pallas_call x1, Pallas kernels, front(): pl.pallas_call(front_kernel, in_specs=[ANYWHERE, ANYWHERE, ANYWHERE, WHOL...  7.37 us
    unnamed x15, local copies, waits for them, and re-layouts  5.53 us
    pallas_call x1, Pallas kernels, gates(): pl.pallas_call(gate_kernel, in_specs=[WHOLE] * 5, out_specs=[WHOLE, WHOLE...  5.02 us
    pallas_call x1, Pallas kernels, final(): pl.pallas_call(final_kernel, in_specs=[WHOLE] * (7 + seqs), out_specs=[WH...  4.25 us
    ppermute x1, starting transfers between devices, body(): lax.ppermute(sent.astype(BF16), 'ctx', [(hop, hop + 2), (hop + 1, hop + 3)])  3.43 us
    pallas_call x1, Pallas kernels, normed(): pl.pallas_call(functools.partial(norm_kernel, all_channels), in_specs=[WH...  3.07 us
  transfers between devices with their start and end apart: 9, of which 2 were waited for; matrix products, arithmetic and copies ran while one was open for 0% of the time, Pallas kernels for 20%

profile of v6, /device:TPU:0, one launch (start us, length us, event | category | flops | bytes accessed | tf_op | source)
XLA Modules:
  0.0 61.3 jit_solution(16543646212429908975)
XLA Ops:
  0.0 1.0 %slice_bitcast_fusion = (bf16[2,32,768]{2,1,0:T(8,128)(2,1)S(1)}, bf16[2,32,768]{2,1,0:T(8,128)(2,1)S(1)}) fusion(bf16[2,2,32,768]{3,2,1,0:T(8,128)(2,1)} %param.12), kind=kLoop, calls=%fused_computation.17 | loop fusion | bytes 393216 | tf_op jit(solution)/shard_map/squeeze | solution.py:357
  1.0 3.1 %collective-permute-start = (bf16[2,32,768]{2,1,0:T(8,128)(2,1)S(1)}, bf16[2,32,768]{2,1,0:T(8,128)(2,1)S(1)}, u32[]{:S(2)}, u32[]{:S(2)}) collective-permute-start(bf16[2,32,768]{2,1,0:T(8,128)(2,1)S(1)} %get-tuple-element.27), channel_id=1, source_target_pairs={{0,1},{1,2},{2,3},{3,0},{4,5},{5,6},{6,7},{7,4},{8,9},{9,10},{10,1... | collective-permute-start | bytes 294920 | tf_op jit(solution)/shard_map/ppermute | solution.py:338
  4.0 2.6 %collective-permute-start.1 = (bf16[2,32,768]{2,1,0:T(8,128)(2,1)S(1)}, bf16[2,32,768]{2,1,0:T(8,128)(2,1)S(1)}, u32[]{:S(2)}, u32[]{:S(2)}) collective-permute-start(bf16[2,32,768]{2,1,0:T(8,128)(2,1)S(1)} %get-tuple-element.27), channel_id=1, source_target_pairs={{0,2},{1,3},{2,0},{3,1},{4,6},{5,7},{6,4},{7,5},{8,10},{9,11},{10,... | collective-permute-start | bytes 294920 | tf_op jit(solution)/shard_map/ppermute | solution.py:338
  6.6 1.3 %collective-permute-start.2 = (bf16[2,32,768]{2,1,0:T(8,128)(2,1)S(1)}, bf16[2,32,768]{2,1,0:T(8,128)(2,1)S(1)}, u32[]{:S(2)}, u32[]{:S(2)}) collective-permute-start(bf16[2,32,768]{2,1,0:T(8,128)(2,1)S(1)} %get-tuple-element.27), channel_id=1, source_target_pairs={{0,3},{1,0},{2,1},{3,2},{4,7},{5,4},{6,5},{7,6},{8,11},{9,8},{10,9... | collective-permute-start | bytes 294920 | tf_op jit(solution)/shard_map/ppermute | solution.py:338
  8.0 7.4 %front.1 = (bf16[2,768,2048]{2,1,0:T(8,128)(2,1)S(1)}, bf16[2,768,2048]{2,1,0:T(8,128)(2,1)S(1)}, bf16[2,768,128]{2,1,0:T(8,128)(2,1)S(1)}, f32[2,32,2048]{2,1,0:T(8,128)S(1)}) custom-call(bf16[2,768,2048]{2,1,0:T(8,128)(2,1)} %x_hbm.1, f32[2,32,768]{2,1,0:T(8,128)} %step_hbm.1, f32[2,32,768]{2,1,0:T(8,128)} %decay_hbm.1, f32[1,32]{1,0:T(1,128)} %bitcast.33, ...), custom_call_target="tpu_custom_call" | custom-call | flops 402653184 | bytes 12582912 | tf_op jit(solution)/shard_map/front/pallas_call | solution.py:132
  15.4 0.1 pad.7.clone
  15.5 0.0 collective-permute-done
  15.5 0.0 slice-start
  15.5 0.0 copy-start.2
  15.6 0.0 slice-start.1
  15.6 2.0 %own_states.1 = (bf16[2,5,128,2048]{3,2,1,0:T(8,128)(2,1)S(1)}, bf16[2,128,2048]{2,1,0:T(8,128)(2,1)S(1)}) custom-call(bf16[2,128,768]{2,1,0:T(8,128)(2,1)S(1)} %constant_dynamic-update-slice_fusion.b_ref, bf16[2,768,2048]{2,1,0:T(8,128)(2,1)S(1)} %get-tuple-element.26.weighted_ref, f32[2,32,2048]{2,1,0:T(8,128)S(1)} %get-tuple-element.28.rows_ref), custom_call_target="tpu_custom_call" | custom-call | flops 805306368 | bytes 6291456 | tf_op jit(solution)/shard_map/own_states/pallas_call | solution.py:184
  17.7 0.1 select_bitcast_fusion
  17.7 0.2 maximum_maximum_fusion
  17.9 0.1 collective-permute-start.3
  18.0 2.0 %collective-permute-done.3 = bf16[144,2048]{1,0:T(8,128)(2,1)S(1)} collective-permute-done((bf16[144,2048]{1,0:T(8,128)(2,1)S(1)}, bf16[144,2048]{1,0:T(8,128)(2,1)S(1)}, u32[]{:S(2)}, u32[]{:S(2)}) %collective-permute-start.3) | collective-permute-done | bytes 589856 | tf_op jit(solution)/shard_map/ppermute | solution.py:371
  20.0 0.3 fusion
  20.3 3.4 %collective-permute-start.4 = (bf16[128,2048]{1,0:T(8,128)(2,1)S(1)}, bf16[128,2048]{1,0:T(8,128)(2,1)S(1)}, u32[]{:S(2)}, u32[]{:S(2)}) collective-permute-start(bf16[128,2048]{1,0:T(8,128)(2,1)S(1)} %fusion), channel_id=1, source_target_pairs={{0,8},{4,12},{1,9},{5,13},{2,10},{6,14},{3,11},{7,15},{16,24},{20,... | collective-permute-start | bytes 1572872 | tf_op jit(solution)/shard_map/ppermute | solution.py:390
  23.7 0.7 %collective-permute-start.5 = (bf16[2,32,768]{2,1,0:T(8,128)(2,1)S(1)}, bf16[2,32,768]{2,1,0:T(8,128)(2,1)S(1)}, u32[]{:S(2)}, u32[]{:S(2)}) collective-permute-start(bf16[2,32,768]{2,1,0:T(8,128)(2,1)S(1)} %get-tuple-element.40), channel_id=1, source_target_pairs={{0,1},{1,2},{2,3},{3,0},{4,5},{5,6},{6,7},{7,4},{8,9},{9,10},{10,1... | collective-permute-start | bytes 294920 | tf_op jit(solution)/shard_map/ppermute | solution.py:338
  24.5 1.2 %collective-permute-start.6 = (bf16[2,32,768]{2,1,0:T(8,128)(2,1)S(1)}, bf16[2,32,768]{2,1,0:T(8,128)(2,1)S(1)}, u32[]{:S(2)}, u32[]{:S(2)}) collective-permute-start(bf16[2,32,768]{2,1,0:T(8,128)(2,1)S(1)} %get-tuple-element.40), channel_id=1, source_target_pairs={{0,2},{1,3},{2,0},{3,1},{4,6},{5,7},{6,4},{7,5},{8,10},{9,11},{10,... | collective-permute-start | bytes 294920 | tf_op jit(solution)/shard_map/ppermute | solution.py:338
  25.6 2.0 %collective-permute-start.7 = (bf16[2,32,768]{2,1,0:T(8,128)(2,1)S(1)}, bf16[2,32,768]{2,1,0:T(8,128)(2,1)S(1)}, u32[]{:S(2)}, u32[]{:S(2)}) collective-permute-start(bf16[2,32,768]{2,1,0:T(8,128)(2,1)S(1)} %get-tuple-element.40), channel_id=1, source_target_pairs={{0,3},{1,0},{2,1},{3,2},{4,7},{5,4},{6,5},{7,6},{8,11},{9,8},{10,9... | collective-permute-start | bytes 294920 | tf_op jit(solution)/shard_map/ppermute | solution.py:338
  27.6 5.0 %gates.1 = (bf16[2,768,2048]{2,1,0:T(8,128)(2,1)S(1)}, bf16[2,768,2048]{2,1,0:T(8,128)(2,1)S(1)}) custom-call(bf16[2,768,2048]{2,1,0:T(8,128)(2,1)S(1)} %bitcast.26, bf16[2,768,2048]{2,1,0:T(8,128)(2,1)S(1)} %get-tuple-element.33.x_ref, bf16[2,768,128]{2,1,0:T(8,128)(2,1)S(1)} %get-tuple-element.34.both_ref, bf16[128,2048]{1,0:T(8,128)(2,1)S(1)} %copy-done.2, ...), custom_call_target="tpu_custom_call" | custom-call | flops 1610612736 | bytes 25165824 | tf_op jit(solution)/shard_map/gates/pallas_call | solution.py:219
  32.7 0.0 copy-start
  32.7 2.7 %copy-done = bf16[2,768,2048]{2,1,0:T(8,128)(2,1)} copy-done((bf16[2,768,2048]{2,1,0:T(8,128)(2,1)}, bf16[2,768,2048]{2,1,0:T(8,128)(2,1)S(1)}, u32[]{:S(2)}) %copy-start) | copy-done | bytes 6291480
  35.4 0.2 fusion.3
  35.6 0.1 collective-permute-start.8
  35.7 1.9 %collective-permute-done.8 = bf16[128,2048]{1,0:T(8,128)(2,1)S(1)} collective-permute-done((bf16[128,2048]{1,0:T(8,128)(2,1)S(1)}, bf16[128,2048]{1,0:T(8,128)(2,1)S(1)}, u32[]{:S(2)}, u32[]{:S(2)}) %collective-permute-start.8) | collective-permute-done | bytes 524320 | tf_op jit(solution)/shard_map/ppermute | solution.py:399
  37.6 0.3 fusion.4
  37.9 0.0 copy-start.1
  37.9 2.8 %copy-done.1 = bf16[2,768,2048]{2,1,0:T(8,128)(2,1)S(1)} copy-done((bf16[2,768,2048]{2,1,0:T(8,128)(2,1)S(1)}, bf16[2,768,2048]{2,1,0:T(8,128)(2,1)}, u32[]{:S(2)}) %copy-start.1) | copy-done | bytes 6291480
  40.7 4.2 %final.1 = (bf16[2,768,2048]{2,1,0:T(8,128)(2,1)S(1)}, f32[12,1,128]{2,1,0:T(1,128)S(1)}) custom-call(bf16[2,768,2048]{2,1,0:T(8,128)(2,1)S(1)} %get-tuple-element.26.weighted_ref, bf16[2,5,128,2048]{3,2,1,0:T(8,128)(2,1)S(1)} %get-tuple-element.29.entering_ref, bf16[2,768,2048]{2,1,0:T(8,128)(2,1)S(1)} %copy-done.1, ...), custom_call_target="tpu_custom_call" | custom-call | flops 1610612736 | bytes 18874368 | tf_op jit(solution)/shard_map/final/pallas_call | solution.py:268
  44.9 13.1 %all-gather = f32[48,1,128]{2,1,0:T(1,128)S(1)} all-gather(f32[12,1,128]{2,1,0:T(1,128)S(1)} %get-tuple-element.46), channel_id=2, replica_groups=mesh['groups'=2,'ctx'=4,'head'=4] {'head'}, dimensions={0}, use_global_device_ids=true | all-gather | bytes 30720 | tf_op jit(solution)/shard_map/all_gather | solution.py:407
  58.1 3.1 %normed.1 = bf16[2,768,2048]{2,1,0:T(8,128)(2,1)} custom-call(bf16[2,768,2048]{2,1,0:T(8,128)(2,1)S(1)} %get-tuple-element.45.gated_ref, f32[4,12,1,128]{3,2,1,0:T(1,128)S(1)} %bitcast.27, f32[1,2048]{1,0:T(1,128)S(1)} %bitcast.28), custom_call_target="tpu_custom_call" | custom-call | flops 6291456 | bytes 12582912 | tf_op jit(solution)/shard_map/normed/pallas_call | solution.py:316
  (22 shorter events, 0.2 us)
Async XLA Ops:
  1.0 14.6 %collective-permute-start = (bf16[2,32,768]{2,1,0:T(8,128)(2,1)S(1)}, bf16[2,32,768]{2,1,0:T(8,128)(2,1)S(1)}, u32[]{:S(2)}, u32[]{:S(2)}) collective-permute-start(bf16[2,32,768]{2,1,0:T(8,128)(2,1)S(1)} %get-tuple-element.27), channel_id=1, source_target_pairs={{0,1},{1,2},{2,3},{3,0},{4,5},{5,6},{6,7},{7,4},{8,9},{9,10},{10,1... | collective-permute-start | bytes 294920 | tf_op jit(solution)/shard_map/ppermute | solution.py:338
  4.0 11.5 %collective-permute-start.1 = (bf16[2,32,768]{2,1,0:T(8,128)(2,1)S(1)}, bf16[2,32,768]{2,1,0:T(8,128)(2,1)S(1)}, u32[]{:S(2)}, u32[]{:S(2)}) collective-permute-start(bf16[2,32,768]{2,1,0:T(8,128)(2,1)S(1)} %get-tuple-element.27), channel_id=1, source_target_pairs={{0,2},{1,3},{2,0},{3,1},{4,6},{5,7},{6,4},{7,5},{8,10},{9,11},{10,... | collective-permute-start | bytes 294920 | tf_op jit(solution)/shard_map/ppermute | solution.py:338
  6.6 9.0 %collective-permute-start.2 = (bf16[2,32,768]{2,1,0:T(8,128)(2,1)S(1)}, bf16[2,32,768]{2,1,0:T(8,128)(2,1)S(1)}, u32[]{:S(2)}, u32[]{:S(2)}) collective-permute-start(bf16[2,32,768]{2,1,0:T(8,128)(2,1)S(1)} %get-tuple-element.27), channel_id=1, source_target_pairs={{0,3},{1,0},{2,1},{3,2},{4,7},{5,4},{6,5},{7,6},{8,11},{9,8},{10,9... | collective-permute-start | bytes 294920 | tf_op jit(solution)/shard_map/ppermute | solution.py:338
  15.5 12.1 %slice-start = ((s8[6291456]{0:T(1024)(128)(4,1)}), s8[4194304]{0:T(1024)(128)(4,1)S(1)}, s32[]{:S(2)}) async-start(s8[6291456]{0:T(1024)(128)(4,1)} %bitcast.25), calls=%async_computation | async-start | bytes 8388608
  15.5 12.1 %copy-start.2 = (bf16[128,2048]{1,0:T(8,128)(2,1)S(1)}, bf16[128,2048]{1,0:T(8,128)(2,1)}, u32[]{:S(2)}) copy-start(bf16[128,2048]{1,0:T(8,128)(2,1)} %constant.28.clone.band_ref) | copy-start | bytes 1572868
  15.6 12.0 %slice-start.1 = ((s8[6291456]{0:T(1024)(128)(4,1)}), s8[2097152]{0:T(1024)(128)(4,1)S(1)}, s32[]{:S(2)}) async-start(s8[6291456]{0:T(1024)(128)(4,1)} %bitcast.25), calls=%async_computation.1 | async-start | bytes 4194304
  17.9 2.1 %collective-permute-start.3 = (bf16[144,2048]{1,0:T(8,128)(2,1)S(1)}, bf16[144,2048]{1,0:T(8,128)(2,1)S(1)}, u32[]{:S(2)}, u32[]{:S(2)}) collective-permute-start(bf16[144,2048]{1,0:T(8,128)(2,1)S(1)} %maximum_maximum_fusion), channel_id=1, source_target_pairs={{0,4},{4,0},{8,12},{12,8},{1,5},{5,1},{9,13},{13,9},{2,6},{6,2},{1... | collective-permute-start | bytes 1769480 | tf_op jit(solution)/shard_map/ppermute | solution.py:371
  20.3 15.1 %collective-permute-start.4 = (bf16[128,2048]{1,0:T(8,128)(2,1)S(1)}, bf16[128,2048]{1,0:T(8,128)(2,1)S(1)}, u32[]{:S(2)}, u32[]{:S(2)}) collective-permute-start(bf16[128,2048]{1,0:T(8,128)(2,1)S(1)} %fusion), channel_id=1, source_target_pairs={{0,8},{4,12},{1,9},{5,13},{2,10},{6,14},{3,11},{7,15},{16,24},{20,... | collective-permute-start | bytes 1572872 | tf_op jit(solution)/shard_map/ppermute | solution.py:390
  23.7 11.6 %collective-permute-start.5 = (bf16[2,32,768]{2,1,0:T(8,128)(2,1)S(1)}, bf16[2,32,768]{2,1,0:T(8,128)(2,1)S(1)}, u32[]{:S(2)}, u32[]{:S(2)}) collective-permute-start(bf16[2,32,768]{2,1,0:T(8,128)(2,1)S(1)} %get-tuple-element.40), channel_id=1, source_target_pairs={{0,1},{1,2},{2,3},{3,0},{4,5},{5,6},{6,7},{7,4},{8,9},{9,10},{10,1... | collective-permute-start | bytes 294920 | tf_op jit(solution)/shard_map/ppermute | solution.py:338
  24.5 10.9 %collective-permute-start.6 = (bf16[2,32,768]{2,1,0:T(8,128)(2,1)S(1)}, bf16[2,32,768]{2,1,0:T(8,128)(2,1)S(1)}, u32[]{:S(2)}, u32[]{:S(2)}) collective-permute-start(bf16[2,32,768]{2,1,0:T(8,128)(2,1)S(1)} %get-tuple-element.40), channel_id=1, source_target_pairs={{0,2},{1,3},{2,0},{3,1},{4,6},{5,7},{6,4},{7,5},{8,10},{9,11},{10,... | collective-permute-start | bytes 294920 | tf_op jit(solution)/shard_map/ppermute | solution.py:338
  25.6 9.8 %collective-permute-start.7 = (bf16[2,32,768]{2,1,0:T(8,128)(2,1)S(1)}, bf16[2,32,768]{2,1,0:T(8,128)(2,1)S(1)}, u32[]{:S(2)}, u32[]{:S(2)}) collective-permute-start(bf16[2,32,768]{2,1,0:T(8,128)(2,1)S(1)} %get-tuple-element.40), channel_id=1, source_target_pairs={{0,3},{1,0},{2,1},{3,2},{4,7},{5,4},{6,5},{7,6},{8,11},{9,8},{10,9... | collective-permute-start | bytes 294920 | tf_op jit(solution)/shard_map/ppermute | solution.py:338
  32.7 2.7 %copy-start = (bf16[2,768,2048]{2,1,0:T(8,128)(2,1)}, bf16[2,768,2048]{2,1,0:T(8,128)(2,1)S(1)}, u32[]{:S(2)}) copy-start(bf16[2,768,2048]{2,1,0:T(8,128)(2,1)S(1)} %get-tuple-element.38.lift_ref) | copy-start | bytes 18874372
  35.6 2.0 %collective-permute-start.8 = (bf16[128,2048]{1,0:T(8,128)(2,1)S(1)}, bf16[128,2048]{1,0:T(8,128)(2,1)S(1)}, u32[]{:S(2)}, u32[]{:S(2)}) collective-permute-start(bf16[128,2048]{1,0:T(8,128)(2,1)S(1)} %fusion.3), channel_id=1, source_target_pairs={{0,4},{4,0},{8,12},{12,8},{1,5},{5,1},{9,13},{13,9},{2,6},{6,2},{1... | collective-permute-start | bytes 1572872 | tf_op jit(solution)/shard_map/ppermute | solution.py:399
  37.9 2.8 %copy-start.1 = (bf16[2,768,2048]{2,1,0:T(8,128)(2,1)S(1)}, bf16[2,768,2048]{2,1,0:T(8,128)(2,1)}, u32[]{:S(2)}) copy-start(bf16[2,768,2048]{2,1,0:T(8,128)(2,1)} %copy-done) | copy-start | bytes 18874372
  40.7 17.4 %copy-start.3 = (f32[2048]{0:T(1024)S(1)}, f32[2048]{0:T(1024)}, u32[]{:S(2)}) copy-start(f32[2048]{0:T(1024)} %param.16) | copy-start | bytes 24580

commit v7 on v6

--- a/solution.py
+++ b/solution.py
@@ -12,8 +12,9 @@
 HALF = 256
 F32 = jnp.float32
 BF16 = jnp.bfloat16
-VMEM_LIMIT = 12 * 1024 * 1024
-PARAMS = pltpu.CompilerParams(vmem_limit_bytes=VMEM_LIMIT)
+MIB = 1024 * 1024
+PARAMS = pltpu.CompilerParams(vmem_limit_bytes=4 * MIB)
+STAGING_PARAMS = pltpu.CompilerParams(vmem_limit_bytes=10 * MIB)
 ENTER, LEAVE, FIRST, TOTAL = range(4)
 ROWS = 32
 WHOLE = pl.BlockSpec(memory_space=pltpu.VMEM)
@@ -87,75 +88,57 @@
         rows_ref[s] = mm(parts_of(jnp.concatenate(table, axis=0)), rise_band)
 
 
-def front_kernel(
-    x_hbm, step_hbm, decay_hbm, skip_ref, sums_ref, bands_hbm,
-    x_ref, weighted_ref, both_ref, rows_ref, step, decay, bands, sems,
+def tables_kernel(
+    step_ref, decay_ref, skip_ref, sums_ref, band_ref, both_ref, rows_ref
 ):
+    fill_tables(step_ref, decay_ref, skip_ref, sums_ref, band_ref[...], both_ref, rows_ref)
+
+
+def tables(step_size, log_decay, skip, sums, band):
+    seqs, heads, length = log_decay.shape
+    return pl.pallas_call(
+        tables_kernel,
+        in_specs=[WHOLE] * 5,
+        out_specs=[WHOLE] * 2,
+        out_shape=[
+            pltpu.VMEM((seqs, length, 4 * heads), BF16),
+            pltpu.VMEM((seqs, ROWS, band.shape[1]), F32),
+        ],
+        compiler_params=PARAMS,
+        cost_estimate=pl.CostEstimate(
+            flops=10 ** 9, bytes_accessed=10 ** 7, transcendentals=0
+        ),
+        name="tables",
+    )(in_hbm(step_size), in_hbm(log_decay), in_hbm(skip), in_hbm(sums), in_hbm(band))
+
+
+def weight_kernel(x_ref, both_ref, band_ref, weighted_ref):
     seqs, length, channels = x_ref.shape
-    heads = decay.shape[1]
-    blocks = length // SPAN
-    small = [
-        pltpu.make_async_copy(source, target, sems.at[seqs * blocks + i])
-        for i, (source, target) in enumerate(
-            [(decay_hbm, decay), (step_hbm, step), (bands_hbm, bands)]
-        )
-    ]
-    for copy in small:
-        copy.start()
-    copies = []
-    for s in range(seqs):
-        for k in range(blocks):
-            place = (s, pl.ds(k * SPAN, SPAN))
-            copies.append(
-                pltpu.make_async_copy(x_hbm.at[place], x_ref.at[place], sems.at[s * blocks + k])
-            )
-            copies[-1].start(priority=k % 2)
-    for copy in small:
-        copy.wait()
-    fill_tables(
-        step, decay, skip_ref, sums_ref, bands[2 * heads:], both_ref, rows_ref
-    )
-    for s in range(seqs):
-        for k in range(blocks):
+    for s in range(seqs):
+        for k in range(length // SPAN):
             rows = slice(k * SPAN, (k + 1) * SPAN)
-            copies[s * blocks + k].wait()
             both = both_ref[s, rows]
             for lo in range(0, channels, HALF):
                 sl = slice(lo, lo + HALF)
-                wide = mm(both, bands[:4 * heads, sl]).astype(BF16)
+                wide = mm(both, band_ref[:, sl]).astype(BF16)
                 weighted_ref[s, rows, sl] = x_ref[s, rows, sl] * wide
 
 
-def front(features, step_size, log_decay, skip, sums, bands):
-    seqs, length, channels = features.shape
-    heads = step_size.shape[1]
-    return pl.pallas_call(
-        front_kernel,
-        in_specs=[ANYWHERE, ANYWHERE, ANYWHERE, WHOLE, WHOLE, ANYWHERE],
-        out_specs=[WHOLE] * 4,
-        out_shape=[
-            pltpu.VMEM(features.shape, BF16),
-            pltpu.VMEM(features.shape, BF16),
-            pltpu.VMEM((seqs, length, 4 * heads), BF16),
-            pltpu.VMEM((seqs, ROWS, channels), F32),
-        ],
-        scratch_shapes=[
-            pltpu.VMEM(step_size.shape, F32),
-            pltpu.VMEM(log_decay.shape, F32),
-            pltpu.VMEM(bands.shape, BF16),
-            pltpu.SemaphoreType.DMA((seqs * (length // SPAN) + 3,)),
-        ],
-        compiler_params=PARAMS,
-        cost_estimate=pl.CostEstimate(
-            flops=2 * seqs * length * channels * 64,
+def weigh(x, both, band):
+    seqs, length, channels = x.shape
+    return pl.pallas_call(
+        weight_kernel,
+        in_specs=[WHOLE] * 3,
+        out_specs=WHOLE,
+        out_shape=pltpu.VMEM(x.shape, BF16),
+        compiler_params=PARAMS,
+        cost_estimate=pl.CostEstimate(
+            flops=2 * seqs * length * channels * 256,
             bytes_accessed=4 * seqs * length * channels,
             transcendentals=0,
         ),
-        name="front",
-    )(
-        in_hbm(features), in_hbm(step_size), in_hbm(log_decay), in_hbm(skip), in_hbm(sums),
-        in_hbm(bands),
-    )
+        name="weigh",
+    )(in_vmem(x), in_vmem(both), band)
 
 
 def state_kernel(b_ref, weighted_ref, rows_ref, entering_ref, state_ref):
@@ -231,27 +214,54 @@
     )(in_vmem(gate_in), in_vmem(x), in_vmem(both), band, in_vmem(rows))
 
 
+def left_kernel(b_ref, c_ref, left_ref):
+    seqs, states, length = b_ref.shape
+    row, col = iotas((SPAN, SPAN))
+    for s in range(seqs):
+        for k in range(length // SPAN):
+            rows = slice(k * SPAN, (k + 1) * SPAN)
+            c_t = c_ref[s, :, rows].T
+            affinity = mm(c_t, b_ref[s, :, rows])
+            left_ref[s, rows, :SPAN] = jnp.where(row >= col, affinity, 0.0).astype(BF16)
+            left_ref[s, rows, SPAN:] = c_t
+
+
+def left_of(b, c):
+    seqs, states, length = b.shape
+    return pl.pallas_call(
+        left_kernel,
+        in_specs=[WHOLE] * 2,
+        out_specs=WHOLE,
+        out_shape=pltpu.VMEM((seqs, length, SPAN + states), BF16),
+        compiler_params=PARAMS,
+        cost_estimate=pl.CostEstimate(
+            flops=2 * seqs * length * SPAN * states,
+            bytes_accessed=8 * seqs * length * SPAN,
+            transcendentals=0,
+        ),
+        name="left",
+    )(b, c)
+
+
 def final_kernel(
-    weighted_ref, entering_ref, lift_ref, skipped_ref, b_ref, c_ref, rows_ref, *refs
+    weighted_ref, near_ref, far_ref, lift_ref, skipped_ref, left_ref, rows_ref, *refs
 ):
     gated_ref, square_ref = refs[-2:]
     seqs, length, channels = lift_ref.shape
     blocks = length // SPAN
-    row, col = iotas((SPAN, SPAN))
     for s in range(seqs):
         for k in range(blocks):
             rows = slice(k * SPAN, (k + 1) * SPAN)
-            c_t = c_ref[s, :, rows].T
-            affinity = mm(c_t, b_ref[s, :, rows])
-            masked = jnp.where(row >= col, affinity, 0.0).astype(BF16)
-            left = jnp.concatenate([masked, c_t], axis=1)
+            left = left_ref[s, rows]
             squares = jnp.zeros((SPAN, 128), F32)
             at = FIRST * blocks + k
             for lo in range(0, channels, HALF):
                 sl = slice(lo, lo + HALF)
                 entering = rows_ref[s, at:at + 1, sl].astype(BF16) * refs[s][:, sl]
                 if k > 0:
-                    entering = entering + entering_ref[s, k - 1, :, sl]
+                    entering = entering + jnp.concatenate(
+                        [near_ref[s, k - 1, :, sl], far_ref[s, k - 1, :, sl]], axis=0
+                    )
                 right = jnp.concatenate([weighted_ref[s, rows, sl], entering], axis=0)
                 mixed = mm(left, right).astype(BF16)
                 gated = lift_ref[s, rows, sl] * mixed + skipped_ref[s, rows, sl]
@@ -259,30 +269,34 @@
                 power = gated * gated
                 pair = sum(power[:, left_:left_ + 128] for left_ in range(0, HALF, 128))
                 squares = squares + pair.astype(F32)
-            square_ref[s * blocks + k] = jnp.sum(squares.T, axis=0, keepdims=True)
-
-
-def final(weighted, entering, lift, skipped, b, c, rows, incoming):
+            at = s * blocks + k
+            square_ref[at:at + 1] = jnp.sum(squares.T, axis=0, keepdims=True)
+    unused = square_ref.shape[0] - seqs * blocks
+    if unused:
+        square_ref[seqs * blocks:] = jnp.zeros((unused, SPAN), F32)
+
+
+def final(weighted, near, far, lift, skipped, left, rows, incoming):
     seqs, length, channels = lift.shape
-    states = c.shape[1]
+    positions = -(-seqs * length // SPAN // 8) * 8
     return pl.pallas_call(
         final_kernel,
         in_specs=[WHOLE] * (7 + seqs),
         out_specs=[WHOLE] * 2,
         out_shape=[
             pltpu.VMEM(lift.shape, BF16),
-            pltpu.VMEM((seqs * (length // SPAN), 1, SPAN), F32),
+            pltpu.VMEM((positions, SPAN), F32),
         ],
         compiler_params=PARAMS,
         cost_estimate=pl.CostEstimate(
-            flops=4 * seqs * length * channels * states,
+            flops=4 * seqs * length * channels * SPAN,
             bytes_accessed=6 * seqs * length * channels,
             transcendentals=0,
         ),
         name="final",
     )(
-        in_vmem(weighted), in_vmem(entering), in_vmem(lift), in_vmem(skipped), b, c,
-        in_vmem(rows), *incoming,
+        in_vmem(weighted), in_vmem(near), in_vmem(far), in_vmem(lift), in_vmem(skipped),
+        in_vmem(left), in_vmem(rows), *incoming,
     )
 
 
@@ -294,7 +308,7 @@
         for k in range(blocks):
             at = s * blocks + k
             rows = slice(k * SPAN, (k + 1) * SPAN)
-            total = jnp.sum(square_ref[:, at, 0], axis=0, keepdims=True)
+            total = jnp.sum(square_ref[:, at], axis=0, keepdims=True)
             inverse = lax.rsqrt(total / all_channels + 1e-05)
             column = jnp.broadcast_to(inverse, (128, SPAN)).T
             for lo in range(0, channels, 128):
@@ -322,7 +336,7 @@
             pltpu.VMEM(gated.shape, BF16),
             pltpu.SemaphoreType.DMA((seqs * (length // SPAN),)),
         ],
-        compiler_params=PARAMS,
+        compiler_params=STAGING_PARAMS,
         cost_estimate=pl.CostEstimate(
             flops=2 * seqs * length * channels,
             bytes_accessed=4 * seqs * length * channels,
@@ -350,17 +364,14 @@
     seqs, length, channels = features.shape
     heads = step_size.shape[1]
     pair = np.repeat(np.concatenate([np.eye(heads)] * 2), channels // heads, axis=1)
-    bands = jnp.asarray(np.concatenate([0 * pair, pair, 0 * pair]), BF16)
     rise_band = jnp.asarray(np.concatenate([pair, 0 * pair]), BF16)
+    fall_band = jnp.asarray(np.concatenate([0 * pair, pair]), BF16)
     until = np.tril(np.ones((SPAN, SPAN)))
     sums = jnp.asarray(np.concatenate([np.tile(until, 3), np.tile(np.eye(SPAN), 3)]), BF16)
     b_own, c_own = lax.optimization_barrier((state_proj[0], state_proj[1]))
-    b = jnp.concatenate(from_all(b_own, "head"), axis=1)
-    states = b.shape[1]
-    x, weighted, both, rows = front(
-        features, step_size, log_decay, skip_gain[None, :], sums, bands
-    )
-    entering, ends = own_states(b, weighted, rows)
+    b_far = from_all(b_own, "head")[1:]
+    both, rows = tables(step_size, log_decay, skip_gain[None, :], sums, rise_band)
+    weighted = weigh(features, both, fall_band)
 
     place = lax.axis_index("ctx")
     even = place % 2 == 0
@@ -368,43 +379,63 @@
     swap = [(i, i ^ 1) for i in range(devices)]
     total_at = TOTAL * (length // SPAN)
     decay = [rows[s, total_at:total_at + 1] for s in range(seqs)]
+
+    def past_chip(ends, other, decay_other):
+        return jnp.where(
+            even,
+            other + decay_other * ends[0].astype(F32),
+            ends[1].astype(F32) + decay[1] * other,
+        )
+
+    def across(past, entered, hop):
+        sent = past if entered is None else past + decay_past * entered.astype(F32)
+        sent = sent.astype(BF16)
+        return sent, lax.ppermute(sent, "ctx", [(hop, hop + 2), (hop + 1, hop + 3)])
+
+    near, near_ends = own_states(b_own, weighted, rows)
+    own_rows = b_own.shape[1]
     other = lax.ppermute(
         jnp.concatenate([
-            jnp.where(even, ends[1], ends[0]),
+            jnp.where(even, near_ends[1], near_ends[0]),
             as_parts(jnp.where(even, decay[1], decay[0])),
         ]),
         "ctx", swap,
     )
-    end_other = other[:states].astype(F32)
-    decay_other = other[states:states + 1].astype(F32) + other[states + 1:states + 2].astype(F32)
-    end_first = ends[0].astype(F32)
-    past = jnp.where(
-        even,
-        end_other + decay_other * end_first,
-        ends[1].astype(F32) + decay[1] * end_other,
+    near_other = other[:own_rows].astype(F32)
+    decay_other = (
+        other[own_rows:own_rows + 1].astype(F32) + other[own_rows + 1:own_rows + 2].astype(F32)
     )
     decay_past = decay_other * jnp.where(even, decay[0], decay[1])
-    entered = None
-    for hop in range(0, devices - 2, 2):
-        sent = past if entered is None else past + decay_past * entered.astype(F32)
-        got = lax.ppermute(sent.astype(BF16), "ctx", [(hop, hop + 2), (hop + 1, hop + 3)])
-        if entered is None:
-            c_own, x, _ = lax.optimization_barrier((c_own, x, sent))
-            c = from_all(c_own, "head")
-            terms = gates(gate_in, x, both, rise_band, rows)
-            got, terms, c = lax.optimization_barrier((got, terms, c))
-            c = jnp.concatenate(c, axis=1)
-        entered = got if entered is None else entered + got
+    near_past = past_chip(near_ends, near_other, decay_other)
+    near_sent, near_got = across(near_past, None, 0)
+    b_far, _ = lax.optimization_barrier((b_far, near_sent))
+    b_far = jnp.concatenate(b_far, axis=1)
+    far, far_ends = own_states(b_far, weighted, rows)
+    far_other = lax.ppermute(jnp.where(even, far_ends[1], far_ends[0]), "ctx", swap).astype(F32)
+    far_past = past_chip(far_ends, far_other, decay_other)
+    far_sent, far_got = across(far_past, None, 0)
+    c_own, features, _ = lax.optimization_barrier((c_own, features, far_sent))
+    c = from_all(c_own, "head")
+    terms = gates(gate_in, features, both, rise_band, rows)
+    c, terms = lax.optimization_barrier((c, terms))
+    left = left_of(jnp.concatenate([b_own, b_far], axis=1), jnp.concatenate(c, axis=1))
+    near_got, far_got, left = lax.optimization_barrier((near_got, far_got, left))
+    for hop in range(2, devices - 2, 2):
+        near_got = near_got + across(near_past, near_got, hop)[1]
+        far_got = far_got + across(far_past, far_got, hop)[1]
+    entered = jnp.concatenate([near_got, far_got])
     entered32 = entered.astype(F32)
+    ends = [jnp.concatenate([near_ends[s], far_ends[s]]).astype(F32) for s in range(seqs)]
     shared = lax.ppermute(
-        jnp.where(even, end_first + decay[0] * entered32, entered32).astype(BF16), "ctx", swap
-    )
+        jnp.where(even, ends[0] + decay[0] * entered32, entered32).astype(BF16), "ctx", swap
+    )
+    end_other = jnp.concatenate([near_other, far_other])
     incoming = [
         jnp.where(even, entered, shared),
         jnp.where(even, shared, (end_other + decay_other * entered32).astype(BF16)),
     ]
-    gated, squares = final(weighted, entering, *terms, b, c, rows, incoming)
-    squares = lax.all_gather(squares, "head")
+    gated, squares = final(weighted, near, far, *terms, left, rows, incoming)
+    squares = jnp.stack(from_all(squares, "head"))
     return normed(gated, squares, norm_gain[None, :], channels * lax.axis_size("head"))
 
 

time: 61.5 us -> 58.8 us (0.956)
  blocking collectives: 13.1 us -> 0 us
  waiting for transfers between devices: 3.84 us -> 12.3 us
  starting transfers between devices: 14.5 us -> 18.6 us
  Pallas kernels: 21.8 us -> 20.3 us
  local copies, waits for them, and re-layouts: 6.59 us -> 5.63 us
    all_gather x1 -> x0, blocking collectives: 13.1 us -> none  [body(): squares = lax.all_gather(squares, 'head')]
    ppermute x6 -> x9, waiting for transfers between devices: 0.02 us -> 7.44 us  [from_all(): lax.ppermute(shard, axis, [(i, (i + by) % devices) for i in range(devices)])]
    pallas_call x1 -> x3, Pallas kernels: 7.37 us -> 4.9 us  [the longest x1 2.82 us: tables(): pl.pallas_call(tables_kernel, in_specs=[WHOLE] * 5, out_specs=[WHOLE] * 2...]
    ppermute x6 -> x9, starting transfers between devices: 10.9 us -> 13.4 us  [from_all(): lax.ppermute(shard, axis, [(i, (i + by) % devices) for i in range(devices)])]
    unnamed x15 -> x19, local copies, waits for them, and re-layouts: 5.53 us -> 3.88 us
    ppermute x3 -> x5, starting transfers between devices: 3.57 us -> 5.19 us  [the longest x2 4.98 us: across(): lax.ppermute(sent, 'ctx', [(hop, hop + 2), (hop + 1, hop + 3)])]
    ppermute x3 -> x5, waiting for transfers between devices: 3.83 us -> 4.86 us  [the longest x1 1.8 us: body(): lax.ppermute(jnp.where(even, ends[0] + decay[0] * entered32, entered32).a...]
    squeeze x1, local copies, waits for them, and re-layouts: 0.95 us -> 1.59 us  [body(): b_own, c_own = lax.optimization_barrier((state_proj[0], state_proj[1]))]
  transfers between devices with their start and end apart: 9 -> 14, of which waited for: 2 -> 7; matrix products, arithmetic and copies ran while one was open for 0% -> 1% of each run, Pallas kernels for 20% -> 22%
where the time goes in v7:
time: 58.8 us; the launch traced here: 58.5 us
  Pallas kernels  20.3 us (35%)
  starting transfers between devices  18.6 us (32%)
  waiting for transfers between devices  12.3 us (21%)
  local copies, waits for them, and re-layouts  5.63 us (10%)
  other arithmetic  1.15 us (2%)
    ppermute x9, starting transfers between devices, from_all(): lax.ppermute(shard, axis, [(i, (i + by) % devices) for i in range(devices)])  13.4 us
    ppermute x9, waiting for transfers between devices, from_all(): lax.ppermute(shard, axis, [(i, (i + by) % devices) for i in range(devices)])  7.44 us
    pallas_call x1, Pallas kernels, gates(): pl.pallas_call(gate_kernel, in_specs=[WHOLE] * 5, out_specs=[WHOLE, WHOLE...  5.12 us
    ppermute x2, starting transfers between devices, across(): lax.ppermute(sent, 'ctx', [(hop, hop + 2), (hop + 1, hop + 3)])  4.98 us
    pallas_call x1, Pallas kernels, final(): pl.pallas_call(final_kernel, in_specs=[WHOLE] * (7 + seqs), out_specs=[WH...  4.65 us
    unnamed x19, local copies, waits for them, and re-layouts  3.88 us
    pallas_call x1, Pallas kernels, normed(): pl.pallas_call(functools.partial(norm_kernel, all_channels), in_specs=[WH...  3.08 us
    pallas_call x1, Pallas kernels, tables(): pl.pallas_call(tables_kernel, in_specs=[WHOLE] * 5, out_specs=[WHOLE] * 2...  2.82 us
  transfers between devices with their start and end apart: 14, of which 7 were waited for; matrix products, arithmetic and copies ran while one was open for 1% of the time, Pallas kernels for 22%

profile of v7, /device:TPU:0, one launch (start us, length us, event | category | flops | bytes accessed | tf_op | source)
XLA Modules:
  0.0 58.5 jit_solution(13695839284218967495)
XLA Ops:
  0.0 1.6 %slice_bitcast_fusion.2 = (bf16[2,32,768]{2,1,0:T(8,128)(2,1)}, bf16[2,32,768]{2,1,0:T(8,128)(2,1)S(1)}) fusion(bf16[2,2,32,768]{3,2,1,0:T(8,128)(2,1)} %param.12), kind=kLoop, calls=%fused_computation.20 | loop fusion | bytes 393216 | tf_op jit(solution)/shard_map/squeeze | solution.py:371
  1.6 5.0 %collective-permute-start.2 = (bf16[2,32,768]{2,1,0:T(8,128)(2,1)S(1)}, bf16[2,32,768]{2,1,0:T(8,128)(2,1)S(1)}, u32[]{:S(2)}, u32[]{:S(2)}) collective-permute-start(bf16[2,32,768]{2,1,0:T(8,128)(2,1)S(1)} %get-tuple-element.32.b_ref), channel_id=1, source_target_pairs={{0,3},{1,0},{2,1},{3,2},{4,7},{5,4},{6,5},{7,6},{8,11},{9,8},{10,9... | collective-permute-start | bytes 294920 | tf_op jit(solution)/shard_map/ppermute | solution.py:352
  6.6 1.0 %collective-permute-start = (bf16[2,32,768]{2,1,0:T(8,128)(2,1)S(1)}, bf16[2,32,768]{2,1,0:T(8,128)(2,1)S(1)}, u32[]{:S(2)}, u32[]{:S(2)}) collective-permute-start(bf16[2,32,768]{2,1,0:T(8,128)(2,1)S(1)} %get-tuple-element.32.b_ref), channel_id=1, source_target_pairs={{0,1},{1,2},{2,3},{3,0},{4,5},{5,6},{6,7},{7,4},{8,9},{9,10},{10,1... | collective-permute-start | bytes 294920 | tf_op jit(solution)/shard_map/ppermute | solution.py:352
  7.7 2.8 %tables.1 = (bf16[2,768,128]{2,1,0:T(8,128)(2,1)S(1)}, f32[2,32,2048]{2,1,0:T(8,128)S(1)}) custom-call(f32[2,32,768]{2,1,0:T(8,128)} %step_ref.1, f32[2,32,768]{2,1,0:T(8,128)} %decay_ref.1, f32[1,32]{1,0:T(1,128)} %bitcast.52, bf16[256,384]{1,0:T(8,128)(2,1)} %constant.29.clone.sums_ref, bf16[128,2048]{1,0:T(8,128)(2,1)} %constant.27.clone.band_ref), custom_call_target="tpu_custom_call" | custom-call | flops 1000000000 | bytes 10000000 | tf_op jit(solution)/shard_map/tables/pallas_call | solution.py:99
  10.6 2.8 %copy-done = bf16[2,768,2048]{2,1,0:T(8,128)(2,1)S(1)} copy-done((bf16[2,768,2048]{2,1,0:T(8,128)(2,1)S(1)}, bf16[2,768,2048]{2,1,0:T(8,128)(2,1)}, u32[]{:S(2)}) %copy-start) | copy-done | bytes 6291480
  13.3 1.0 %copy-done.1 = bf16[128,2048]{1,0:T(8,128)(2,1)S(1)} copy-done((bf16[128,2048]{1,0:T(8,128)(2,1)S(1)}, bf16[128,2048]{1,0:T(8,128)(2,1)}, u32[]{:S(2)}) %copy-start.1) | copy-done | bytes 524312
  14.4 1.8 %weigh.1.weighted_ref = bf16[2,768,2048]{2,1,0:T(8,128)(2,1)S(1)} custom-call(bf16[2,768,2048]{2,1,0:T(8,128)(2,1)S(1)} %copy-done, bf16[2,768,128]{2,1,0:T(8,128)(2,1)S(1)} %get-tuple-element.31.both_ref, bf16[128,2048]{1,0:T(8,128)(2,1)S(1)} %copy-done.1), custom_call_target="tpu_custom_call" | custom-call | flops 1610612736 | bytes 12582912 | tf_op jit(solution)/shard_map/weigh/pallas_call | solution.py:129
  16.2 1.0 %own_states.2 = (bf16[2,5,32,2048]{3,2,1,0:T(8,128)(2,1)S(1)}, bf16[2,32,2048]{2,1,0:T(8,128)(2,1)S(1)}) custom-call(bf16[2,32,768]{2,1,0:T(8,128)(2,1)S(1)} %get-tuple-element.32.b_ref, bf16[2,768,2048]{2,1,0:T(8,128)(2,1)S(1)} %weigh.1.weighted_ref, f32[2,32,2048]{2,1,0:T(8,128)S(1)} %get-tuple-element.33.rows_ref), custom_call_target="tpu_custom_call" | custom-call | flops 201326592 | bytes 6291456 | tf_op jit(solution)/shard_map/own_states/pallas_call | solution.py:167
  17.3 0.1 maximum_maximum_fusion
  17.5 1.4 %collective-permute-done.3 = bf16[48,2048]{1,0:T(8,128)(2,1)S(1)} collective-permute-done((bf16[48,2048]{1,0:T(8,128)(2,1)S(1)}, bf16[48,2048]{1,0:T(8,128)(2,1)S(1)}, u32[]{:S(2)}, u32[]{:S(2)}) %collective-permute-start.3) | collective-permute-done | bytes 196640 | tf_op jit(solution)/shard_map/ppermute | solution.py:397
  18.9 0.1 select_convert_fusion.1
  19.0 3.7 %collective-permute-start.8 = (bf16[32,2048]{1,0:T(8,128)(2,1)S(1)}, bf16[32,2048]{1,0:T(8,128)(2,1)S(1)}, u32[]{:S(2)}, u32[]{:S(2)}) collective-permute-start(bf16[32,2048]{1,0:T(8,128)(2,1)S(1)} %select_convert_fusion.1), channel_id=1, source_target_pairs={{0,8},{4,12},{1,9},{5,13},{2,10},{6,14},{3,11},{7,15},{16,24},{20,... | collective-permute-start | bytes 393224 | tf_op jit(solution)/shard_map/ppermute | solution.py:393
  22.8 1.6 %own_states.3 = (bf16[2,5,96,2048]{3,2,1,0:T(8,128)(2,1)S(1)}, bf16[2,96,2048]{2,1,0:T(8,128)(2,1)S(1)}) custom-call(bf16[2,96,768]{2,1,0:T(8,128)(2,1)S(1)} %pad_maximum_fusion.2.b_ref, bf16[2,768,2048]{2,1,0:T(8,128)(2,1)S(1)} %weigh.1.weighted_ref, f32[2,32,2048]{2,1,0:T(8,128)S(1)} %get-tuple-element.33.rows_ref), custom_call_target="tpu_custom_call" | custom-call | flops 603979776 | bytes 6291456 | tf_op jit(solution)/shard_map/own_states/pallas_call | solution.py:167
  24.5 1.7 %collective-permute-done.4 = bf16[96,2048]{1,0:T(8,128)(2,1)S(1)} collective-permute-done((bf16[96,2048]{1,0:T(8,128)(2,1)S(1)}, bf16[96,2048]{1,0:T(8,128)(2,1)S(1)}, u32[]{:S(2)}, u32[]{:S(2)}) %collective-permute-start.4) | collective-permute-done | bytes 393248 | tf_op jit(solution)/shard_map/ppermute | solution.py:414
  26.2 0.2 select_convert_fusion
  26.4 1.3 %collective-permute-start.9 = (bf16[96,2048]{1,0:T(8,128)(2,1)S(1)}, bf16[96,2048]{1,0:T(8,128)(2,1)S(1)}, u32[]{:S(2)}, u32[]{:S(2)}) collective-permute-start(bf16[96,2048]{1,0:T(8,128)(2,1)S(1)} %select_convert_fusion), channel_id=1, source_target_pairs={{0,8},{4,12},{1,9},{5,13},{2,10},{6,14},{3,11},{7,15},{16,24},{20,... | collective-permute-start | bytes 1179656 | tf_op jit(solution)/shard_map/ppermute | solution.py:393
  27.8 2.9 %collective-permute-start.7 = (bf16[2,32,768]{2,1,0:T(8,128)(2,1)S(1)}, bf16[2,32,768]{2,1,0:T(8,128)(2,1)S(1)}, u32[]{:S(2)}, u32[]{:S(2)}) collective-permute-start(bf16[2,32,768]{2,1,0:T(8,128)(2,1)S(1)} %copy-done.4), channel_id=1, source_target_pairs={{0,3},{1,0},{2,1},{3,2},{4,7},{5,4},{6,5},{7,6},{8,11},{9,8},{10,9... | collective-permute-start | bytes 294920 | tf_op jit(solution)/shard_map/ppermute | solution.py:352
  30.7 1.1 %collective-permute-start.6 = (bf16[2,32,768]{2,1,0:T(8,128)(2,1)S(1)}, bf16[2,32,768]{2,1,0:T(8,128)(2,1)S(1)}, u32[]{:S(2)}, u32[]{:S(2)}) collective-permute-start(bf16[2,32,768]{2,1,0:T(8,128)(2,1)S(1)} %copy-done.4), channel_id=1, source_target_pairs={{0,2},{1,3},{2,0},{3,1},{4,6},{5,7},{6,4},{7,5},{8,10},{9,11},{10,... | collective-permute-start | bytes 294920 | tf_op jit(solution)/shard_map/ppermute | solution.py:352
  31.9 5.1 %gates.1 = (bf16[2,768,2048]{2,1,0:T(8,128)(2,1)S(1)}, bf16[2,768,2048]{2,1,0:T(8,128)(2,1)S(1)}) custom-call(bf16[2,768,2048]{2,1,0:T(8,128)(2,1)S(1)} %bitcast.40, bf16[2,768,2048]{2,1,0:T(8,128)(2,1)S(1)} %bitcast.38, bf16[2,768,128]{2,1,0:T(8,128)(2,1)S(1)} %get-tuple-element.31.both_ref, bf16[128,2048]{1,0:T(8,128)(2,1)S(1)} %copy-done.2, ...), custom_call_target="tpu_custom_call" | custom-call | flops 1610612736 | bytes 25165824 | tf_op jit(solution)/shard_map/gates/pallas_call | solution.py:202
  37.0 3.9 %collective-permute-done.6 = bf16[2,32,768]{2,1,0:T(8,128)(2,1)S(1)} collective-permute-done((bf16[2,32,768]{2,1,0:T(8,128)(2,1)S(1)}, bf16[2,32,768]{2,1,0:T(8,128)(2,1)S(1)}, u32[]{:S(2)}, u32[]{:S(2)}) %collective-permute-start.6) | collective-permute-done | bytes 98336 | tf_op jit(solution)/shard_map/ppermute | solution.py:352
  41.0 0.3 left.1.left_ref
  41.3 0.2 fusion.1
  41.7 1.8 %collective-permute-done.10 = bf16[128,2048]{1,0:T(8,128)(2,1)S(1)} collective-permute-done((bf16[128,2048]{1,0:T(8,128)(2,1)S(1)}, bf16[128,2048]{1,0:T(8,128)(2,1)S(1)}, u32[]{:S(2)}, u32[]{:S(2)}) %collective-permute-start.10) | collective-permute-done | bytes 524320 | tf_op jit(solution)/shard_map/ppermute | solution.py:429
  43.5 0.3 fusion.4
  43.8 4.7 %final.1 = (bf16[2,768,2048]{2,1,0:T(8,128)(2,1)S(1)}, f32[16,128]{1,0:T(8,128)S(1)}) custom-call(bf16[2,768,2048]{2,1,0:T(8,128)(2,1)S(1)} %weigh.1.weighted_ref, bf16[2,5,32,2048]{3,2,1,0:T(8,128)(2,1)S(1)} %get-tuple-element.34.near_ref, bf16[2,5,96,2048]{3,2,1,0:T(8,128)(2,1)S(1)} %get-tuple-element.39.far_ref, ...), custom_call_target="tpu_custom_call" | custom-call | flops 1610612736 | bytes 18874368 | tf_op jit(solution)/shard_map/final/pallas_call | solution.py:282
  48.5 0.8 %collective-permute-start.13 = (f32[16,128]{1,0:T(8,128)S(1)}, f32[16,128]{1,0:T(8,128)S(1)}, u32[]{:S(2)}, u32[]{:S(2)}) collective-permute-start(f32[16,128]{1,0:T(8,128)S(1)} %get-tuple-element.56), channel_id=1, source_target_pairs={{0,3},{1,0},{2,1},{3,2},{4,7},{5,4},{6,5},{7,6},{8,11},{9,8},{10,9... | collective-permute-start | bytes 24584 | tf_op jit(solution)/shard_map/ppermute | solution.py:352
  49.2 0.6 %collective-permute-start.12 = (f32[16,128]{1,0:T(8,128)S(1)}, f32[16,128]{1,0:T(8,128)S(1)}, u32[]{:S(2)}, u32[]{:S(2)}) collective-permute-start(f32[16,128]{1,0:T(8,128)S(1)} %get-tuple-element.56), channel_id=1, source_target_pairs={{0,2},{1,3},{2,0},{3,1},{4,6},{5,7},{6,4},{7,5},{8,10},{9,11},{10,... | collective-permute-start | bytes 24584 | tf_op jit(solution)/shard_map/ppermute | solution.py:352
  49.8 1.9 %collective-permute-start.11 = (f32[16,128]{1,0:T(8,128)S(1)}, f32[16,128]{1,0:T(8,128)S(1)}, u32[]{:S(2)}, u32[]{:S(2)}) collective-permute-start(f32[16,128]{1,0:T(8,128)S(1)} %get-tuple-element.56), channel_id=1, source_target_pairs={{0,1},{1,2},{2,3},{3,0},{4,5},{5,6},{6,7},{7,4},{8,9},{9,10},{10,1... | collective-permute-start | bytes 24584 | tf_op jit(solution)/shard_map/ppermute | solution.py:352
  51.7 0.4 collective-permute-done.13
  52.2 1.6 %collective-permute-done.12 = f32[16,128]{1,0:T(8,128)S(1)} collective-permute-done((f32[16,128]{1,0:T(8,128)S(1)}, f32[16,128]{1,0:T(8,128)S(1)}, u32[]{:S(2)}, u32[]{:S(2)}) %collective-permute-start.12) | collective-permute-done | bytes 8224 | tf_op jit(solution)/shard_map/ppermute | solution.py:352
  53.8 1.5 %collective-permute-done.11 = f32[16,128]{1,0:T(8,128)S(1)} collective-permute-done((f32[16,128]{1,0:T(8,128)S(1)}, f32[16,128]{1,0:T(8,128)S(1)}, u32[]{:S(2)}, u32[]{:S(2)}) %collective-permute-start.11) | collective-permute-done | bytes 8224 | tf_op jit(solution)/shard_map/ppermute | solution.py:352
  55.3 3.1 %normed.1 = bf16[2,768,2048]{2,1,0:T(8,128)(2,1)} custom-call(bf16[2,768,2048]{2,1,0:T(8,128)(2,1)S(1)} %get-tuple-element.55.gated_ref, f32[4,16,128]{2,1,0:T(8,128)S(1)} %pad_maximum_fusion.3.square_ref, f32[1,2048]{1,0:T(1,128)S(1)} %bitcast.42), custom_call_target="tpu_custom_call" | custom-call | flops 6291456 | bytes 12582912 | tf_op jit(solution)/shard_map/normed/pallas_call | solution.py:330
  (48 shorter events, 0.8 us)
Async XLA Ops:
  1.6 21.1 %collective-permute-start.2 = (bf16[2,32,768]{2,1,0:T(8,128)(2,1)S(1)}, bf16[2,32,768]{2,1,0:T(8,128)(2,1)S(1)}, u32[]{:S(2)}, u32[]{:S(2)}) collective-permute-start(bf16[2,32,768]{2,1,0:T(8,128)(2,1)S(1)} %get-tuple-element.32.b_ref), channel_id=1, source_target_pairs={{0,3},{1,0},{2,1},{3,2},{4,7},{5,4},{6,5},{7,6},{8,11},{9,8},{10,9... | collective-permute-start | bytes 294920 | tf_op jit(solution)/shard_map/ppermute | solution.py:352
  6.6 16.1 %collective-permute-start.1 = (bf16[2,32,768]{2,1,0:T(8,128)(2,1)S(1)}, bf16[2,32,768]{2,1,0:T(8,128)(2,1)S(1)}, u32[]{:S(2)}, u32[]{:S(2)}) collective-permute-start(bf16[2,32,768]{2,1,0:T(8,128)(2,1)S(1)} %get-tuple-element.32.b_ref), channel_id=1, source_target_pairs={{0,2},{1,3},{2,0},{3,1},{4,6},{5,7},{6,4},{7,5},{8,10},{9,11},{10,... | collective-permute-start | bytes 294920 | tf_op jit(solution)/shard_map/ppermute | solution.py:352
  6.6 16.1 %collective-permute-start = (bf16[2,32,768]{2,1,0:T(8,128)(2,1)S(1)}, bf16[2,32,768]{2,1,0:T(8,128)(2,1)S(1)}, u32[]{:S(2)}, u32[]{:S(2)}) collective-permute-start(bf16[2,32,768]{2,1,0:T(8,128)(2,1)S(1)} %get-tuple-element.32.b_ref), channel_id=1, source_target_pairs={{0,1},{1,2},{2,3},{3,0},{4,5},{5,6},{6,7},{7,4},{8,9},{9,10},{10,1... | collective-permute-start | bytes 294920 | tf_op jit(solution)/shard_map/ppermute | solution.py:352
  10.5 2.8 %copy-start = (bf16[2,768,2048]{2,1,0:T(8,128)(2,1)S(1)}, bf16[2,768,2048]{2,1,0:T(8,128)(2,1)}, u32[]{:S(2)}) copy-start(bf16[2,768,2048]{2,1,0:T(8,128)(2,1)} %x_ref.2) | copy-start | bytes 18874372
  13.3 1.0 %copy-start.1 = (bf16[128,2048]{1,0:T(8,128)(2,1)S(1)}, bf16[128,2048]{1,0:T(8,128)(2,1)}, u32[]{:S(2)}) copy-start(bf16[128,2048]{1,0:T(8,128)(2,1)} %constant.28.clone.band_ref) | copy-start | bytes 1572868
  14.4 17.5 %slice-start.2 = ((s8[6291456]{0:T(1024)(128)(4,1)}), s8[4194304]{0:T(1024)(128)(4,1)S(1)}, s32[]{:S(2)}) async-start(s8[6291456]{0:T(1024)(128)(4,1)} %bitcast.39), calls=%async_computation.2 | async-start | bytes 8388608
  16.2 15.7 %slice-start.3 = ((s8[6291456]{0:T(1024)(128)(4,1)}), s8[2097152]{0:T(1024)(128)(4,1)S(1)}, s32[]{:S(2)}) async-start(s8[6291456]{0:T(1024)(128)(4,1)} %bitcast.39), calls=%async_computation.3 | async-start | bytes 4194304
  17.4 1.5 %collective-permute-start.3 = (bf16[48,2048]{1,0:T(8,128)(2,1)S(1)}, bf16[48,2048]{1,0:T(8,128)(2,1)S(1)}, u32[]{:S(2)}, u32[]{:S(2)}) collective-permute-start(bf16[48,2048]{1,0:T(8,128)(2,1)S(1)} %maximum_maximum_fusion), channel_id=1, source_target_pairs={{0,4},{4,0},{8,12},{12,8},{1,5},{5,1},{9,13},{13,9},{2,6},{6,2},{1... | collective-permute-start | bytes 589832 | tf_op jit(solution)/shard_map/ppermute | solution.py:397
  18.9 8.9 %copy-start.4 = (bf16[2,32,768]{2,1,0:T(8,128)(2,1)S(1)}, bf16[2,32,768]{2,1,0:T(8,128)(2,1)}, u32[]{:S(2)}) copy-start(bf16[2,32,768]{2,1,0:T(8,128)(2,1)} %get-tuple-element.48) | copy-start | bytes 294916
  18.9 12.9 %slice-start = ((s8[6291456]{0:T(1024)(128)(4,1)}), s8[4194304]{0:T(1024)(128)(4,1)S(1)}, s32[]{:S(2)}) async-start(s8[6291456]{0:T(1024)(128)(4,1)} %bitcast.37), calls=%async_computation | async-start | bytes 8388608
  18.9 12.9 %copy-start.2 = (bf16[128,2048]{1,0:T(8,128)(2,1)S(1)}, bf16[128,2048]{1,0:T(8,128)(2,1)}, u32[]{:S(2)}) copy-start(bf16[128,2048]{1,0:T(8,128)(2,1)} %constant.27.clone.band_ref) | copy-start | bytes 1572868
  19.0 22.2 %collective-permute-start.8 = (bf16[32,2048]{1,0:T(8,128)(2,1)S(1)}, bf16[32,2048]{1,0:T(8,128)(2,1)S(1)}, u32[]{:S(2)}, u32[]{:S(2)}) collective-permute-start(bf16[32,2048]{1,0:T(8,128)(2,1)S(1)} %select_convert_fusion.1), channel_id=1, source_target_pairs={{0,8},{4,12},{1,9},{5,13},{2,10},{6,14},{3,11},{7,15},{16,24},{20,... | collective-permute-start | bytes 393224 | tf_op jit(solution)/shard_map/ppermute | solution.py:393
  22.8 9.1 %slice-start.1 = ((s8[6291456]{0:T(1024)(128)(4,1)}), s8[2097152]{0:T(1024)(128)(4,1)S(1)}, s32[]{:S(2)}) async-start(s8[6291456]{0:T(1024)(128)(4,1)} %bitcast.37), calls=%async_computation.1 | async-start | bytes 4194304
  24.4 1.8 %collective-permute-start.4 = (bf16[96,2048]{1,0:T(8,128)(2,1)S(1)}, bf16[96,2048]{1,0:T(8,128)(2,1)S(1)}, u32[]{:S(2)}, u32[]{:S(2)}) collective-permute-start(bf16[96,2048]{1,0:T(8,128)(2,1)S(1)} %bitcast_select_fusion), channel_id=1, source_target_pairs={{0,4},{4,0},{8,12},{12,8},{1,5},{5,1},{9,13},{13,9},{2,6},{6,2},{1... | collective-permute-start | bytes 1179656 | tf_op jit(solution)/shard_map/ppermute | solution.py:414
  26.4 14.8 %collective-permute-start.9 = (bf16[96,2048]{1,0:T(8,128)(2,1)S(1)}, bf16[96,2048]{1,0:T(8,128)(2,1)S(1)}, u32[]{:S(2)}, u32[]{:S(2)}) collective-permute-start(bf16[96,2048]{1,0:T(8,128)(2,1)S(1)} %select_convert_fusion), channel_id=1, source_target_pairs={{0,8},{4,12},{1,9},{5,13},{2,10},{6,14},{3,11},{7,15},{16,24},{20,... | collective-permute-start | bytes 1179656 | tf_op jit(solution)/shard_map/ppermute | solution.py:393
  27.8 9.2 %collective-permute-start.7 = (bf16[2,32,768]{2,1,0:T(8,128)(2,1)S(1)}, bf16[2,32,768]{2,1,0:T(8,128)(2,1)S(1)}, u32[]{:S(2)}, u32[]{:S(2)}) collective-permute-start(bf16[2,32,768]{2,1,0:T(8,128)(2,1)S(1)} %copy-done.4), channel_id=1, source_target_pairs={{0,3},{1,0},{2,1},{3,2},{4,7},{5,4},{6,5},{7,6},{8,11},{9,8},{10,9... | collective-permute-start | bytes 294920 | tf_op jit(solution)/shard_map/ppermute | solution.py:352
  30.7 10.3 %collective-permute-start.6 = (bf16[2,32,768]{2,1,0:T(8,128)(2,1)S(1)}, bf16[2,32,768]{2,1,0:T(8,128)(2,1)S(1)}, u32[]{:S(2)}, u32[]{:S(2)}) collective-permute-start(bf16[2,32,768]{2,1,0:T(8,128)(2,1)S(1)} %copy-done.4), channel_id=1, source_target_pairs={{0,2},{1,3},{2,0},{3,1},{4,6},{5,7},{6,4},{7,5},{8,10},{9,11},{10,... | collective-permute-start | bytes 294920 | tf_op jit(solution)/shard_map/ppermute | solution.py:352
  31.8 9.1 %collective-permute-start.5 = (bf16[2,32,768]{2,1,0:T(8,128)(2,1)S(1)}, bf16[2,32,768]{2,1,0:T(8,128)(2,1)S(1)}, u32[]{:S(2)}, u32[]{:S(2)}) collective-permute-start(bf16[2,32,768]{2,1,0:T(8,128)(2,1)S(1)} %copy-done.4), channel_id=1, source_target_pairs={{0,1},{1,2},{2,3},{3,0},{4,5},{5,6},{6,7},{7,4},{8,9},{9,10},{10,1... | collective-permute-start | bytes 294920 | tf_op jit(solution)/shard_map/ppermute | solution.py:352
  41.6 2.0 %collective-permute-start.10 = (bf16[128,2048]{1,0:T(8,128)(2,1)S(1)}, bf16[128,2048]{1,0:T(8,128)(2,1)S(1)}, u32[]{:S(2)}, u32[]{:S(2)}) collective-permute-start(bf16[128,2048]{1,0:T(8,128)(2,1)S(1)} %fusion.1), channel_id=1, source_target_pairs={{0,4},{4,0},{8,12},{12,8},{1,5},{5,1},{9,13},{13,9},{2,6},{6,2},{1... | collective-permute-start | bytes 1572872 | tf_op jit(solution)/shard_map/ppermute | solution.py:429
  43.8 11.5 %copy-start.3 = (f32[2048]{0:T(1024)S(1)}, f32[2048]{0:T(1024)}, u32[]{:S(2)}) copy-start(f32[2048]{0:T(1024)} %param.16) | copy-start | bytes 24580
  48.5 3.7 %collective-permute-start.13 = (f32[16,128]{1,0:T(8,128)S(1)}, f32[16,128]{1,0:T(8,128)S(1)}, u32[]{:S(2)}, u32[]{:S(2)}) collective-permute-start(f32[16,128]{1,0:T(8,128)S(1)} %get-tuple-element.56), channel_id=1, source_target_pairs={{0,3},{1,0},{2,1},{3,2},{4,7},{5,4},{6,5},{7,6},{8,11},{9,8},{10,9... | collective-permute-start | bytes 24584 | tf_op jit(solution)/shard_map/ppermute | solution.py:352
  49.2 4.5 %collective-permute-start.12 = (f32[16,128]{1,0:T(8,128)S(1)}, f32[16,128]{1,0:T(8,128)S(1)}, u32[]{:S(2)}, u32[]{:S(2)}) collective-permute-start(f32[16,128]{1,0:T(8,128)S(1)} %get-tuple-element.56), channel_id=1, source_target_pairs={{0,2},{1,3},{2,0},{3,1},{4,6},{5,7},{6,4},{7,5},{8,10},{9,11},{10,... | collective-permute-start | bytes 24584 | tf_op jit(solution)/shard_map/ppermute | solution.py:352
  49.8 5.4 %collective-permute-start.11 = (f32[16,128]{1,0:T(8,128)S(1)}, f32[16,128]{1,0:T(8,128)S(1)}, u32[]{:S(2)}, u32[]{:S(2)}) collective-permute-start(f32[16,128]{1,0:T(8,128)S(1)} %get-tuple-element.56), channel_id=1, source_target_pairs={{0,1},{1,2},{2,3},{3,0},{4,5},{5,6},{6,7},{7,4},{8,9},{9,10},{10,1... | collective-permute-start | bytes 24584 | tf_op jit(solution)/shard_map/ppermute | solution.py:352

commit v8 on v7

v8 whole, which is shorter than its diff:
```python
import functools

import jax
import jax.numpy as jnp
import numpy as np
from jax import lax
from jax.experimental import pallas as pl
from jax.experimental.pallas import tpu as pltpu
from jax.sharding import PartitionSpec as P

SPAN = 128
HALF = 256
F32 = jnp.float32
BF16 = jnp.bfloat16
MIB = 1024 * 1024
PARAMS = pltpu.CompilerParams(vmem_limit_bytes=4 * MIB)
COST = pl.CostEstimate(flops=1000, bytes_accessed=1000, transcendentals=0)
STAGING_PARAMS = pltpu.CompilerParams(vmem_limit_bytes=10 * MIB)
ENTER, LEAVE, FIRST, TOTAL = range(4)
ROWS = 32
WHOLE = pl.BlockSpec(memory_space=pltpu.VMEM)
ANYWHERE = pl.BlockSpec(memory_space=pl.ANY)


def in_vmem(array):
    return pltpu.with_memory_space_constraint(array, pltpu.VMEM)


def in_hbm(array):
    return pltpu.with_memory_space_constraint(array, pltpu.HBM)


def mm(a, b):
    return jnp.dot(a, b, preferred_element_type=F32)


def mm_nt(a, b):
    return lax.dot_general(a, b, (((1,), (1,)), ((), ())), preferred_element_type=F32)


def iotas(shape):
    return (
        lax.broadcasted_iota(jnp.int32, shape, 0),
        lax.broadcasted_iota(jnp.int32, shape, 1),
    )


def two_parts(v):
    high = v.astype(BF16)
    return [high, (v - high.astype(F32)).astype(BF16)]


def fill_tables(step_ref, decay_ref, skip_ref, sums_ref, rise_band, both_ref, rows_ref):
    seqs, heads, length = decay_ref.shape
    blocks = length // SPAN
    _, lane = iotas((SPAN, 4 * heads))
    rising = lane < 2 * heads
    is_high = (lane < heads) | ((lane >= 2 * heads) & (lane < 3 * heads))
    until = sums_ref[:SPAN]
    same = sums_ref[SPAN:]

    def parts_of(v):
        high = v.astype(BF16).astype(F32)
        return jnp.where(is_high[:v.shape[0]], high, v - high).astype(BF16)

    skip = jnp.concatenate([skip_ref[...]] * 4, axis=1)
    for s in range(seqs):
        decays = two_parts(jnp.concatenate([decay_ref[s]] * 4, axis=0))
        steps = two_parts(jnp.concatenate([step_ref[s]] * 4, axis=0))
        enter, leave, first = [], [], []
        before = jnp.zeros((1, 4 * heads), F32)
        for k in range(blocks):
            sl = slice(k * SPAN, (k + 1) * SPAN)
            summed = mm_nt(until, jnp.concatenate([p[:, sl] for p in decays], axis=1))
            step = mm_nt(same, jnp.concatenate([p[:, sl] for p in steps], axis=1))
            middle = summed[SPAN // 2 - 1:SPAN // 2]
            last = summed[SPAN - 1:]
            above = summed - middle
            factor = jnp.exp(jnp.where(rising, above, -above))
            both_ref[s, sl, :] = parts_of(jnp.where(rising, factor, step * factor))
            enter.append(jnp.exp(middle))
            leave.append(jnp.exp(last - middle))
            first.append(jnp.exp(middle + before))
            before = before + last
        table = enter + leave + first + [jnp.exp(before)]
        table = table + [jnp.zeros_like(before)] * (ROWS - 1 - len(table)) + [skip]
        rows_ref[s] = mm(parts_of(jnp.concatenate(table, axis=0)), rise_band)


def front_kernel(
    x_hbm, step_hbm, decay_hbm, skip_hbm, sums_hbm, bands_hbm,
    x_ref, weighted_ref, both_ref, rows_ref, bands, step, decay, skip, sums, sems,
):
    seqs, length, channels = x_ref.shape
    heads = decay.shape[1]
    pairs = [(decay_hbm, decay), (step_hbm, step), (sums_hbm, sums), (skip_hbm, skip)]
    pairs += [(x_hbm.at[s], x_ref.at[s]) for s in range(seqs)] + [(bands_hbm, bands)]
    copies = [
        pltpu.make_async_copy(source, target, sems.at[i])
        for i, (source, target) in enumerate(pairs)
    ]
    for copy in copies:
        copy.start()
    for copy in copies[:4] + copies[-1:]:
        copy.wait()
    fill_tables(step, decay, skip, sums, bands[2 * heads:], both_ref, rows_ref)
    for s in range(seqs):
        copies[4 + s].wait()
        for k in range(length // SPAN):
            rows = slice(k * SPAN, (k + 1) * SPAN)
            both = both_ref[s, rows]
            for lo in range(0, channels, HALF):
                sl = slice(lo, lo + HALF)
                wide = mm(both, bands[:4 * heads, sl]).astype(BF16)
                weighted_ref[s, rows, sl] = x_ref[s, rows, sl] * wide


def front(features, step_size, log_decay, skip, sums, bands):
    seqs, length, channels = features.shape
    heads = step_size.shape[1]
    operands = [features, step_size, log_decay, skip, sums, bands]
    return pl.pallas_call(
        front_kernel,
        in_specs=[ANYWHERE] * 6,
        out_specs=[WHOLE] * 5,
        out_shape=[
            pltpu.VMEM(features.shape, BF16),
            pltpu.VMEM(features.shape, BF16),
            pltpu.VMEM((seqs, length, 4 * heads), BF16),
            pltpu.VMEM((seqs, ROWS, channels), F32),
            pltpu.VMEM(bands.shape, BF16),
        ],
        scratch_shapes=[
            pltpu.VMEM(step_size.shape, F32),
            pltpu.VMEM(log_decay.shape, F32),
            pltpu.VMEM(skip.shape, F32),
            pltpu.VMEM(sums.shape, BF16),
            pltpu.SemaphoreType.DMA((seqs + 5,)),
        ],
        compiler_params=PARAMS,
        cost_estimate=COST,
        name="front",
    )(*[in_hbm(operand) for operand in operands])


def state_kernel(b_ref, weighted_ref, rows_ref, entering_ref, state_ref):
    seqs, length, channels = weighted_ref.shape
    blocks = length // SPAN
    for s in range(seqs):
        for lo in range(0, channels, HALF):
            sl = slice(lo, lo + HALF)
            state = None
            for k in range(blocks):
                rows = slice(k * SPAN, (k + 1) * SPAN)
                added = mm(b_ref[s, :, rows], weighted_ref[s, rows, sl])
                if k > 0:
                    at = ENTER * blocks + k
                    entering = rows_ref[s, at:at + 1, sl] * state
                    entering_ref[s, k - 1, :, sl] = entering.astype(BF16)
                    added = added + entering
                at = LEAVE * blocks + k
                state = rows_ref[s, at:at + 1, sl] * added
            state_ref[s, :, sl] = state.astype(BF16)


def own_states(b, weighted, rows):
    seqs, states, length = b.shape
    channels = weighted.shape[2]
    return pl.pallas_call(
        state_kernel,
        in_specs=[WHOLE] * 3,
        out_specs=[WHOLE] * 2,
        out_shape=[
            pltpu.VMEM((seqs, length // SPAN - 1, states, channels), BF16),
            pltpu.VMEM((seqs, states, channels), BF16),
        ],
        compiler_params=PARAMS,
        cost_estimate=COST,
        name="own_states",
    )(b, in_vmem(weighted), in_vmem(rows))


def gate_kernel(seq, gate_ref, x_ref, both_ref, bands_ref, rows_ref, lift_ref, skipped_ref):
    length, channels = lift_ref.shape
    heads4 = both_ref.shape[2]
    band = slice(heads4 // 2, heads4 // 2 + heads4)
    for k in range(length // SPAN):
        rows = slice(k * SPAN, (k + 1) * SPAN)
        both = both_ref[seq, rows]
        for lo in range(0, channels, HALF):
            sl = slice(lo, lo + HALF)
            half = 0.5 * gate_ref[seq, rows, sl].astype(F32)
            gate = (half * jnp.tanh(half) + half).astype(BF16)
            lift_ref[rows, sl] = mm(both, bands_ref[band, sl]).astype(BF16) * gate
            skip = rows_ref[seq, ROWS - 1:ROWS, sl].astype(BF16) * x_ref[seq, rows, sl]
            skipped_ref[rows, sl] = skip * gate


def gates(gate_in, x, both, bands, rows, seq):
    _, length, channels = gate_in.shape
    return pl.pallas_call(
        functools.partial(gate_kernel, seq),
        in_specs=[WHOLE] * 5,
        out_specs=[WHOLE, WHOLE],
        out_shape=[pltpu.VMEM((length, channels), BF16)] * 2,
        compiler_params=PARAMS,
        cost_estimate=COST,
        name="gates",
    )(in_vmem(gate_in), in_vmem(x), in_vmem(both), in_vmem(bands), in_vmem(rows))


def local_kernel(
    seq, weighted_ref, near_ref, far_ref, lift_ref, skipped_ref, b_ref, c_ref, rows_ref,
    own_ref, factor_ref, c_t_ref,
):
    length, channels = own_ref.shape
    blocks = length // SPAN
    row, col = iotas((SPAN, SPAN))
    for k in range(blocks):
        rows = slice(k * SPAN, (k + 1) * SPAN)
        c_t = c_ref[seq, :, rows].T
        c_t_ref[rows] = c_t
        affinity = mm(c_t, b_ref[seq, :, rows])
        left = jnp.where(row >= col, affinity, 0.0).astype(BF16)
        if k > 0:
            left = jnp.concatenate([left, c_t], axis=1)
        at = FIRST * blocks + k
        for lo in range(0, channels, HALF):
            sl = slice(lo, lo + HALF)
            right = weighted_ref[seq, rows, sl]
            if k > 0:
                right = jnp.concatenate(
                    [right, near_ref[seq, k - 1, :, sl], far_ref[seq, k - 1, :, sl]], axis=0
                )
            lift = lift_ref[rows, sl]
            own_ref[rows, sl] = lift * mm(left, right).astype(BF16) + skipped_ref[rows, sl]
            factor_ref[rows, sl] = lift * rows_ref[seq, at:at + 1, sl].astype(BF16)


def local_terms(weighted, near, far, lift, skipped, b, c, rows, seq):
    length, channels = lift.shape
    states = b.shape[1]
    return pl.pallas_call(
        functools.partial(local_kernel, seq),
        in_specs=[WHOLE] * 8,
        out_specs=[WHOLE] * 3,
        out_shape=[
            pltpu.VMEM(lift.shape, BF16),
            pltpu.VMEM(lift.shape, BF16),
            pltpu.VMEM((length, states), BF16),
        ],
        compiler_params=PARAMS,
        cost_estimate=COST,
        name="local_terms",
    )(
        in_vmem(weighted), in_vmem(near), in_vmem(far), in_vmem(lift), in_vmem(skipped), b, c,
        in_vmem(rows),
    )


def joined_kernel(seqs, *refs):
    gated_ref, square_ref = refs[-2:]
    length, channels = refs[0].shape
    blocks = length // SPAN
    for s in range(seqs):
        own_ref, factor_ref, c_t_ref, incoming_ref = refs[4 * s:4 * s + 4]
        for k in range(blocks):
            rows = slice(k * SPAN, (k + 1) * SPAN)
            c_t = c_t_ref[rows]
            squares = jnp.zeros((SPAN, 128), F32)
            for lo in range(0, channels, HALF):
                sl = slice(lo, lo + HALF)
                carried = mm(c_t, incoming_ref[:, sl]).astype(BF16)
                gated = own_ref[rows, sl] + factor_ref[rows, sl] * carried
                gated_ref[s, rows, sl] = gated
                power = gated * gated
                pair = sum(power[:, left:left + 128] for left in range(0, HALF, 128))
                squares = squares + pair.astype(F32)
            at = s * blocks + k
            square_ref[at:at + 1] = jnp.sum(squares.T, axis=0, keepdims=True)
    unused = square_ref.shape[0] - seqs * blocks
    if unused:
        square_ref[seqs * blocks:] = jnp.zeros((unused, SPAN), F32)


def joined(terms, incoming):
    seqs = len(terms)
    length, channels = terms[0][0].shape
    states = terms[0][2].shape[1]
    operands = []
    for s in range(seqs):
        operands += [in_vmem(term) for term in terms[s]] + [incoming[s]]
    return pl.pallas_call(
        functools.partial(joined_kernel, seqs),
        in_specs=[WHOLE] * len(operands),
        out_specs=[WHOLE] * 2,
        out_shape=[
            pltpu.VMEM((seqs, length, channels), BF16),
            pltpu.VMEM((-(-seqs * length // SPAN // 8) * 8, SPAN), F32),
        ],
        compiler_params=PARAMS,
        cost_estimate=COST,
        name="joined",
    )(*operands)


def norm_kernel(all_channels, gated_ref, square_ref, gain_ref, out_hbm, staged, sems):
    seqs, length, channels = gated_ref.shape
    blocks = length // SPAN
    copies = []
    for s in range(seqs):
        for k in range(blocks):
            at = s * blocks + k
            rows = slice(k * SPAN, (k + 1) * SPAN)
            total = jnp.sum(square_ref[:, at], axis=0, keepdims=True)
            inverse = lax.rsqrt(total / all_channels + 1e-05)
            column = jnp.broadcast_to(inverse, (128, SPAN)).T
            for lo in range(0, channels, 128):
                sl = slice(lo, lo + 128)
                staged[s, rows, sl] = (
                    gated_ref[s, rows, sl].astype(F32) * column * gain_ref[:, sl]
                ).astype(BF16)
            place = (s, pl.ds(k * SPAN, SPAN))
            copies.append(
                pltpu.make_async_copy(staged.at[place], out_hbm.at[place], sems.at[at])
            )
            copies[-1].start(priority=k % 2)
    for copy in copies:
        copy.wait()


def normed(gated, squares, gain_row, all_channels):
    seqs, length, channels = gated.shape
    return pl.pallas_call(
        functools.partial(norm_kernel, all_channels),
        in_specs=[WHOLE] * 3,
        out_specs=ANYWHERE,
        out_shape=jax.ShapeDtypeStruct(gated.shape, BF16),
        scratch_shapes=[
            pltpu.VMEM(gated.shape, BF16),
            pltpu.SemaphoreType.DMA((seqs * (length // SPAN),)),
        ],
        compiler_params=STAGING_PARAMS,
        cost_estimate=COST,
        name="normed",
    )(in_vmem(gated), squares, gain_row)


def from_all(shard, axis):
    devices = lax.axis_size(axis)
    paired = devices & (devices - 1) == 0
    return [shard] + [
        lax.ppermute(
            shard, axis, [(i, i ^ by if paired else (i + by) % devices) for i in range(devices)]
        )
        for by in range(1, devices)
    ]


def as_parts(row):
    high = row.astype(BF16)
    low = (row - high.astype(F32)).astype(BF16)
    return jnp.concatenate([high, low, jnp.zeros((14, row.shape[1]), BF16)], axis=0)


def body(features, gate_in, state_proj, step_size, log_decay, skip_gain, norm_gain):
    seqs, length, channels = features.shape
    heads = step_size.shape[1]
    pair = np.repeat(np.concatenate([np.eye(heads)] * 2), channels // heads, axis=1)
    bands = jnp.asarray(np.concatenate([0 * pair, pair, 0 * pair]), BF16)
    until = np.tril(np.ones((SPAN, SPAN)))
    sums = jnp.asarray(np.concatenate([np.tile(until, 2), np.tile(np.eye(SPAN), 2)]), BF16)
    b_own, c_own = lax.optimization_barrier((state_proj[0], state_proj[1]))
    b_far = from_all(b_own, "head")[1:]
    x, weighted, both, rows, bands = front(
        features, step_size, log_decay, skip_gain[None, :], sums, bands
    )

    place = lax.axis_index("ctx")
    even = place % 2 == 0
    devices = lax.axis_size("ctx")
    swap = [(i, i ^ 1) for i in range(devices)]
    total_at = TOTAL * (length // SPAN)
    decay = [rows[s, total_at:total_at + 1] for s in range(seqs)]

    def past_chip(ends, other, decay_other):
        return jnp.where(
            even,
            other + decay_other * ends[0].astype(F32),
            ends[1].astype(F32) + decay[1] * other,
        )

    def across(past, entered, hop):
        sent = past if entered is None else past + decay_past * entered.astype(F32)
        sent = sent.astype(BF16)
        return sent, lax.ppermute(sent, "ctx", [(hop, hop + 2), (hop + 1, hop + 3)])

    near, near_ends = own_states(b_own, weighted, rows)
    own_rows = b_own.shape[1]
    other = lax.ppermute(
        jnp.concatenate([
            jnp.where(even, near_ends[1], near_ends[0]),
            as_parts(jnp.where(even, decay[1], decay[0])),
        ]),
        "ctx", swap,
    )
    gated_by = [None] * seqs
    gate_x, _ = lax.optimization_barrier((x, near_ends))
    gated_by[0] = gates(gate_in, gate_x, both, bands, rows, 0)
    b_far, gated_by[0] = lax.optimization_barrier((b_far, gated_by[0]))
    b_far = jnp.concatenate(b_far, axis=1)
    far, far_ends = own_states(b_far, weighted, rows)
    far_other = lax.ppermute(jnp.where(even, far_ends[1], far_ends[0]), "ctx", swap).astype(F32)
    other, _ = lax.optimization_barrier((other, far_ends))
    near_other = other[:own_rows].astype(F32)
    decay_other = (
        other[own_rows:own_rows + 1].astype(F32) + other[own_rows + 1:own_rows + 2].astype(F32)
    )
    decay_past = decay_other * jnp.where(even, decay[0], decay[1])
    near_past = past_chip(near_ends, near_other, decay_other)
    near_sent, near_got = across(near_past, None, 0)
    far_other, _ = lax.optimization_barrier((far_other, near_sent))
    far_past = past_chip(far_ends, far_other, decay_other)
    far_sent, far_got = across(far_past, None, 0)
    c_own, gate_x, _ = lax.optimization_barrier((c_own, x, far_sent))
    c = from_all(c_own, "head")
    for s in range(1, seqs):
        gated_by[s] = gates(gate_in, gate_x, both, bands, rows, s)
    c, gated_by = lax.optimization_barrier((c, gated_by))
    c = jnp.concatenate(c, axis=1)
    b = jnp.concatenate([b_own, b_far], axis=1)
    terms = [local_terms(weighted, near, far, *gated_by[s], b, c, rows, s) for s in range(seqs)]
    near_got, far_got, terms = lax.optimization_barrier((near_got, far_got, terms))
    for hop in range(2, devices - 2, 2):
        near_got = near_got + across(near_past, near_got, hop)[1]
        far_got = far_got + across(far_past, far_got, hop)[1]
    entered = jnp.concatenate([near_got, far_got])
    entered32 = entered.astype(F32)
    ends = [jnp.concatenate([near_ends[s], far_ends[s]]).astype(F32) for s in range(seqs)]
    shared = lax.ppermute(
        jnp.where(even, ends[0] + decay[0] * entered32, entered32).astype(BF16), "ctx", swap
    )
    end_other = jnp.concatenate([near_other, far_other])
    incoming = [
        jnp.where(even, entered, shared),
        jnp.where(even, shared, (end_other + decay_other * entered32).astype(BF16)),
    ]
    gated, squares = joined(terms, incoming)
    squares = jnp.stack(from_all(squares, "head"))
    return normed(gated, squares, norm_gain[None, :], channels * lax.axis_size("head"))


def solution(mesh):
    in_specs = (
        P("groups", "ctx", "head"),
        P("groups", "ctx", "head"),
        P(None, "groups", "head", "ctx"),
        P("groups", "head", "ctx"),
        P("groups", "head", "ctx"),
        P("head"),
        P("head"),
    )
    out_specs = P("groups", "ctx", "head")
    return jax.shard_map(body, mesh=mesh, in_specs=in_specs, out_specs=out_specs, check_vma=False)
```

time: 58.8 us -> 57 us (0.969)
  local copies, waits for them, and re-layouts: 5.63 us -> 1.45 us
  Pallas kernels: 20.3 us -> 23.6 us
  waiting for transfers between devices: 12.3 us -> 9.96 us
  starting transfers between devices: 18.6 us -> 20.2 us
    ppermute x9, waiting for transfers between devices: 7.44 us -> 3.85 us  [from_all(): lax.ppermute(shard, axis, [(i, i ^ by if paired else (i + by) % devices)...]
    unnamed x19 -> x13, local copies, waits for them, and re-layouts: 3.88 us -> 0.32 us
    pallas_call x5 -> x6, Pallas kernels: 14.7 us -> 17.9 us  [the longest x1 6.43 us: front(): pl.pallas_call(front_kernel, in_specs=[ANYWHERE] * 6, out_specs=[WHOLE] *...]
    ppermute x2, waiting for transfers between devices: 0.01 us -> 2.9 us  [across(): lax.ppermute(sent, 'ctx', [(hop, hop + 2), (hop + 1, hop + 3)])]
    ppermute x1, waiting for transfers between devices: 1.39 us -> 0.01 us  [body(): lax.ppermute(jnp.concatenate([jnp.where(even, near_ends[1], near_ends[0])...]
    ppermute x9, starting transfers between devices: 13.4 us -> 14.7 us  [from_all(): lax.ppermute(shard, axis, [(i, i ^ by if paired else (i + by) % devices)...]
    squeeze x1, local copies, waits for them, and re-layouts: 1.59 us -> 0.95 us  [body(): b_own, c_own = lax.optimization_barrier((state_proj[0], state_proj[1]))]
  transfers between devices with their start and end apart: 14 -> 14, of which waited for: 7 -> 6; matrix products, arithmetic and copies ran while one was open for 1% -> 1% of each run, Pallas kernels for 22% -> 31%
where the time goes in v8:
time: 57 us; the launch traced here: 56.7 us
  Pallas kernels  23.6 us (41%)
  starting transfers between devices  20.2 us (35%)
  waiting for transfers between devices  9.96 us (17%)
  local copies, waits for them, and re-layouts  1.45 us (3%)
  other arithmetic  1.11 us (2%)
    ppermute x9, starting transfers between devices, from_all(): lax.ppermute(shard, axis, [(i, i ^ by if paired else (i + by) % devices)...  14.7 us
    pallas_call x1, Pallas kernels, front(): pl.pallas_call(front_kernel, in_specs=[ANYWHERE] * 6, out_specs=[WHOLE] *...  6.43 us
    ppermute x2, starting transfers between devices, across(): lax.ppermute(sent, 'ctx', [(hop, hop + 2), (hop + 1, hop + 3)])  5.04 us
    pallas_call x2, Pallas kernels, gates(): pl.pallas_call(functools.partial(gate_kernel, seq), in_specs=[WHOLE] * 5,...  4.85 us
    ppermute x9, waiting for transfers between devices, from_all(): lax.ppermute(shard, axis, [(i, i ^ by if paired else (i + by) % devices)...  3.85 us
    pallas_call x2, Pallas kernels, local_terms(): pl.pallas_call(functools.partial(local_kernel, seq), in_specs=[WHOLE] * 8...  3.73 us
    pallas_call x1, Pallas kernels, normed(): pl.pallas_call(functools.partial(norm_kernel, all_channels), in_specs=[WH...  3.09 us
    pallas_call x1, Pallas kernels, joined(): pl.pallas_call(functools.partial(joined_kernel, seqs), in_specs=[WHOLE] *...  2.93 us
  transfers between devices with their start and end apart: 14, of which 6 were waited for; matrix products, arithmetic and copies ran while one was open for 1% of the time, Pallas kernels for 31%

profile of v8, /device:TPU:0, one launch (start us, length us, event | category | flops | bytes accessed | tf_op | source)
XLA Modules:
  0.0 56.7 jit_solution(7790362888152378307)
XLA Ops:
  0.0 1.0 %slice_bitcast_fusion.2 = (bf16[2,32,768]{2,1,0:T(8,128)(2,1)S(1)}, bf16[2,32,768]{2,1,0:T(8,128)(2,1)S(1)}) fusion(bf16[2,2,32,768]{3,2,1,0:T(8,128)(2,1)} %param.11), kind=kLoop, calls=%fused_computation.18 | loop fusion | bytes 393216 | tf_op jit(solution)/shard_map/squeeze | solution.py:373
  1.0 5.1 %collective-permute-start.3 = (bf16[2,32,768]{2,1,0:T(8,128)(2,1)S(1)}, bf16[2,32,768]{2,1,0:T(8,128)(2,1)S(1)}, u32[]{:S(2)}, u32[]{:S(2)}) collective-permute-start(bf16[2,32,768]{2,1,0:T(8,128)(2,1)S(1)} %get-tuple-element.54.b_ref), channel_id=1, source_target_pairs={{0,3},{1,2},{2,1},{3,0},{4,7},{5,6},{6,5},{7,4},{8,11},{9,10},{10,... | collective-permute-start | bytes 294920 | tf_op jit(solution)/shard_map/ppermute | solution.py:353
  6.1 0.6 %collective-permute-start.1 = (bf16[2,32,768]{2,1,0:T(8,128)(2,1)S(1)}, bf16[2,32,768]{2,1,0:T(8,128)(2,1)S(1)}, u32[]{:S(2)}, u32[]{:S(2)}) collective-permute-start(bf16[2,32,768]{2,1,0:T(8,128)(2,1)S(1)} %get-tuple-element.54.b_ref), channel_id=1, source_target_pairs={{0,1},{1,0},{2,3},{3,2},{4,5},{5,4},{6,7},{7,6},{8,9},{9,8},{10,11... | collective-permute-start | bytes 294920 | tf_op jit(solution)/shard_map/ppermute | solution.py:353
  6.7 6.4 %front.1 = (bf16[2,768,2048]{2,1,0:T(8,128)(2,1)S(1)}, bf16[2,768,2048]{2,1,0:T(8,128)(2,1)S(1)}, bf16[2,768,128]{2,1,0:T(8,128)(2,1)S(1)}, f32[2,32,2048]{2,1,0:T(8,128)S(1)}, bf16[192,2048]{1,0:T(8,128)(2,1)S(1)}) custom-call(bf16[2,768,2048]{2,1,0:T(8,128)(2,1)} %x_hbm.1, f32[2,32,768]{2,1,0:T(8,128)} %step_hbm.1, f32[2,32,768]{2,1,0:T(8,128)} %decay_hbm.1, ...), custom_call_target="tpu_custom_call" | custom-call | flops 1000 | bytes 1000 | tf_op jit(solution)/shard_map/front/pallas_call | solution.py:122
  13.2 1.0 %own_states.2 = (bf16[2,5,32,2048]{3,2,1,0:T(8,128)(2,1)S(1)}, bf16[2,32,2048]{2,1,0:T(8,128)(2,1)S(1)}) custom-call(bf16[2,32,768]{2,1,0:T(8,128)(2,1)S(1)} %get-tuple-element.54.b_ref, bf16[2,768,2048]{2,1,0:T(8,128)(2,1)S(1)} %get-tuple-element.55.weighted_ref, f32[2,32,2048]{2,1,0:T(8,128)S(1)} %get-tuple-element.56.rows_ref), custom_call_target="tpu_custom_call" | custom-call | flops 1000 | bytes 1000 | tf_op jit(solution)/shard_map/own_states/pallas_call | solution.py:169
  14.2 0.1 pad.14.clone
  14.3 0.1 maximum_maximum_fusion
  14.6 0.2 slice-done.1
  14.8 2.4 %gates.2 = (bf16[768,2048]{1,0:T(8,128)(2,1)S(1)}, bf16[768,2048]{1,0:T(8,128)(2,1)S(1)}) custom-call(bf16[2,768,2048]{2,1,0:T(8,128)(2,1)S(1)} %bitcast.38, bf16[2,768,2048]{2,1,0:T(8,128)(2,1)S(1)} %get-tuple-element.76.x_ref, bf16[2,768,128]{2,1,0:T(8,128)(2,1)S(1)} %get-tuple-element.60.both_ref, bf16[192,2048]{1,0:T(8,128)(2,1)S(1)} %get-tuple-element.61.bands_ref, ...), custom_call_target="tpu_custom_call" | custom-call | flops 1000 | bytes 1000 | tf_op jit(solution)/shard_map/gates/pallas_call | solution.py:201
  17.3 1.5 %own_states.3 = (bf16[2,5,96,2048]{3,2,1,0:T(8,128)(2,1)S(1)}, bf16[2,96,2048]{2,1,0:T(8,128)(2,1)S(1)}) custom-call(bf16[2,96,768]{2,1,0:T(8,128)(2,1)S(1)} %pad_maximum_fusion.b_ref, bf16[2,768,2048]{2,1,0:T(8,128)(2,1)S(1)} %get-tuple-element.55.weighted_ref, f32[2,32,2048]{2,1,0:T(8,128)S(1)} %get-tuple-element.56.rows_ref), custom_call_target="tpu_custom_call" | custom-call | flops 1000 | bytes 1000 | tf_op jit(solution)/shard_map/own_states/pallas_call | solution.py:169
  19.0 0.3 collective-permute-start.5
  19.3 0.1 select_convert_fusion.1
  19.4 1.3 %collective-permute-done.5 = bf16[96,2048]{1,0:T(8,128)(2,1)S(1)} collective-permute-done((bf16[96,2048]{1,0:T(8,128)(2,1)S(1)}, bf16[96,2048]{1,0:T(8,128)(2,1)S(1)}, u32[]{:S(2)}, u32[]{:S(2)}) %collective-permute-start.5) | collective-permute-done | bytes 393248 | tf_op jit(solution)/shard_map/ppermute | solution.py:413
  20.8 0.2 select_convert_fusion
  21.0 3.8 %collective-permute-start.9 = (bf16[2,32,768]{2,1,0:T(8,128)(2,1)S(1)}, bf16[2,32,768]{2,1,0:T(8,128)(2,1)S(1)}, u32[]{:S(2)}, u32[]{:S(2)}) collective-permute-start(bf16[2,32,768]{2,1,0:T(8,128)(2,1)S(1)} %get-tuple-element.81), channel_id=1, source_target_pairs={{0,3},{1,2},{2,1},{3,0},{4,7},{5,6},{6,5},{7,4},{8,11},{9,10},{10,... | collective-permute-start | bytes 294920 | tf_op jit(solution)/shard_map/ppermute | solution.py:353
  24.9 0.6 %collective-permute-start.7 = (bf16[2,32,768]{2,1,0:T(8,128)(2,1)S(1)}, bf16[2,32,768]{2,1,0:T(8,128)(2,1)S(1)}, u32[]{:S(2)}, u32[]{:S(2)}) collective-permute-start(bf16[2,32,768]{2,1,0:T(8,128)(2,1)S(1)} %get-tuple-element.81), channel_id=1, source_target_pairs={{0,1},{1,0},{2,3},{3,2},{4,5},{5,4},{6,7},{7,6},{8,9},{9,8},{10,11... | collective-permute-start | bytes 294920 | tf_op jit(solution)/shard_map/ppermute | solution.py:353
  25.5 3.5 %collective-permute-start.4 = (bf16[32,2048]{1,0:T(8,128)(2,1)S(1)}, bf16[32,2048]{1,0:T(8,128)(2,1)S(1)}, u32[]{:S(2)}, u32[]{:S(2)}) collective-permute-start(bf16[32,2048]{1,0:T(8,128)(2,1)S(1)} %select_convert_fusion.1), channel_id=1, source_target_pairs={{0,8},{4,12},{1,9},{5,13},{2,10},{6,14},{3,11},{7,15},{16,24},{20,... | collective-permute-start | bytes 393224 | tf_op jit(solution)/shard_map/ppermute | solution.py:396
  29.1 1.5 %collective-permute-start.6 = (bf16[96,2048]{1,0:T(8,128)(2,1)S(1)}, bf16[96,2048]{1,0:T(8,128)(2,1)S(1)}, u32[]{:S(2)}, u32[]{:S(2)}) collective-permute-start(bf16[96,2048]{1,0:T(8,128)(2,1)S(1)} %select_convert_fusion), channel_id=1, source_target_pairs={{0,8},{4,12},{1,9},{5,13},{2,10},{6,14},{3,11},{7,15},{16,24},{20,... | collective-permute-start | bytes 1179656 | tf_op jit(solution)/shard_map/ppermute | solution.py:396
  30.6 2.4 %gates.3 = (bf16[768,2048]{1,0:T(8,128)(2,1)S(1)}, bf16[768,2048]{1,0:T(8,128)(2,1)S(1)}) custom-call(bf16[2,768,2048]{2,1,0:T(8,128)(2,1)S(1)} %bitcast.38, bf16[2,768,2048]{2,1,0:T(8,128)(2,1)S(1)} %get-tuple-element.76.x_ref, bf16[2,768,128]{2,1,0:T(8,128)(2,1)S(1)} %get-tuple-element.60.both_ref, bf16[192,2048]{1,0:T(8,128)(2,1)S(1)} %get-tuple-element.61.bands_ref, ...), custom_call_target="tpu_custom_call" | custom-call | flops 1000 | bytes 1000 | tf_op jit(solution)/shard_map/gates/pallas_call | solution.py:201
  33.0 0.2 collective-permute-done.8
  33.3 1.9 %local_terms.3 = (bf16[768,2048]{1,0:T(8,128)(2,1)S(1)}, bf16[768,2048]{1,0:T(8,128)(2,1)S(1)}, bf16[768,128]{1,0:T(8,128)(2,1)S(1)}) custom-call(bf16[2,768,2048]{2,1,0:T(8,128)(2,1)S(1)} %get-tuple-element.55.weighted_ref, bf16[2,5,32,2048]{3,2,1,0:T(8,128)(2,1)S(1)} %get-tuple-element.70.near_ref, bf16[2,5,96,2048]{3,2,1,0:T(8,128)(2,1)S(1)} %get-tuple-element.71.far_ref, ...), custom_call_target="tpu_custom_call" | custom-call | flops 1000 | bytes 1000 | tf_op jit(solution)/shard_map/local_terms/pallas_call | solution.py:243
  35.2 1.9 %local_terms.2 = (bf16[768,2048]{1,0:T(8,128)(2,1)S(1)}, bf16[768,2048]{1,0:T(8,128)(2,1)S(1)}, bf16[768,128]{1,0:T(8,128)(2,1)S(1)}) custom-call(bf16[2,768,2048]{2,1,0:T(8,128)(2,1)S(1)} %get-tuple-element.55.weighted_ref, bf16[2,5,32,2048]{3,2,1,0:T(8,128)(2,1)S(1)} %get-tuple-element.70.near_ref, bf16[2,5,96,2048]{3,2,1,0:T(8,128)(2,1)S(1)} %get-tuple-element.71.far_ref, ...), custom_call_target="tpu_custom_call" | custom-call | flops 1000 | bytes 1000 | tf_op jit(solution)/shard_map/local_terms/pallas_call | solution.py:243
  37.0 2.9 %collective-permute-done.6 = bf16[96,2048]{1,0:T(8,128)(2,1)S(1)} collective-permute-done((bf16[96,2048]{1,0:T(8,128)(2,1)S(1)}, bf16[96,2048]{1,0:T(8,128)(2,1)S(1)}, u32[]{:S(2)}, u32[]{:S(2)}) %collective-permute-start.6) | collective-permute-done | bytes 393248 | tf_op jit(solution)/shard_map/ppermute | solution.py:396
  40.0 0.2 fusion.1
  40.3 1.9 %collective-permute-done.10 = bf16[128,2048]{1,0:T(8,128)(2,1)S(1)} collective-permute-done((bf16[128,2048]{1,0:T(8,128)(2,1)S(1)}, bf16[128,2048]{1,0:T(8,128)(2,1)S(1)}, u32[]{:S(2)}, u32[]{:S(2)}) %collective-permute-start.10) | collective-permute-done | bytes 524320 | tf_op jit(solution)/shard_map/ppermute | solution.py:440
  42.2 0.3 fusion.4
  42.5 2.9 %joined.1 = (bf16[2,768,2048]{2,1,0:T(8,128)(2,1)S(1)}, f32[16,128]{1,0:T(8,128)S(1)}) custom-call(bf16[768,2048]{1,0:T(8,128)(2,1)S(1)} %get-tuple-element.93.refs_0_, bf16[768,2048]{1,0:T(8,128)(2,1)S(1)} %get-tuple-element.94.refs_1_, bf16[768,128]{1,0:T(8,128)(2,1)S(1)} %get-tuple-element.95.refs_2_, bf16[128,2048]{1,0:T(8,128)(2,1)S(1)} %get-tuple-element.104.refs_3_, ...), custom_call_target="tpu_custom_call" | custom-call | flops 1000 | bytes 1000 | tf_op jit(solution)/shard_map/joined/pallas_call | solution.py:293
  45.4 3.5 %collective-permute-start.13 = (f32[16,128]{1,0:T(8,128)S(1)}, f32[16,128]{1,0:T(8,128)S(1)}, u32[]{:S(2)}, u32[]{:S(2)}) collective-permute-start(f32[16,128]{1,0:T(8,128)S(1)} %get-tuple-element.102), channel_id=1, source_target_pairs={{0,3},{1,2},{2,1},{3,0},{4,7},{5,6},{6,5},{7,4},{8,11},{9,10},{10,... | collective-permute-start | bytes 24584 | tf_op jit(solution)/shard_map/ppermute | solution.py:353
  48.9 0.9 %collective-permute-start.11 = (f32[16,128]{1,0:T(8,128)S(1)}, f32[16,128]{1,0:T(8,128)S(1)}, u32[]{:S(2)}, u32[]{:S(2)}) collective-permute-start(f32[16,128]{1,0:T(8,128)S(1)} %get-tuple-element.102), channel_id=1, source_target_pairs={{0,1},{1,0},{2,3},{3,2},{4,5},{5,4},{6,7},{7,6},{8,9},{9,8},{10,11... | collective-permute-start | bytes 24584 | tf_op jit(solution)/shard_map/ppermute | solution.py:353
  49.9 1.1 %collective-permute-done.13 = f32[16,128]{1,0:T(8,128)S(1)} collective-permute-done((f32[16,128]{1,0:T(8,128)S(1)}, f32[16,128]{1,0:T(8,128)S(1)}, u32[]{:S(2)}, u32[]{:S(2)}) %collective-permute-start.13) | collective-permute-done | bytes 8224 | tf_op jit(solution)/shard_map/ppermute | solution.py:353
  50.9 2.6 %collective-permute-done.12 = f32[16,128]{1,0:T(8,128)S(1)} collective-permute-done((f32[16,128]{1,0:T(8,128)S(1)}, f32[16,128]{1,0:T(8,128)S(1)}, u32[]{:S(2)}, u32[]{:S(2)}) %collective-permute-start.12) | collective-permute-done | bytes 8224 | tf_op jit(solution)/shard_map/ppermute | solution.py:353
  53.5 3.1 %normed.1 = bf16[2,768,2048]{2,1,0:T(8,128)(2,1)} custom-call(bf16[2,768,2048]{2,1,0:T(8,128)(2,1)S(1)} %get-tuple-element.101.gated_ref, f32[4,16,128]{2,1,0:T(8,128)S(1)} %pad_maximum_fusion.1.square_ref, f32[1,2048]{1,0:T(1,128)S(1)} %bitcast.40), custom_call_target="tpu_custom_call" | custom-call | flops 1000 | bytes 1000 | tf_op jit(solution)/shard_map/normed/pallas_call | solution.py:334
  (41 shorter events, 0.6 us)
Async XLA Ops:
  1.0 16.3 %collective-permute-start.3 = (bf16[2,32,768]{2,1,0:T(8,128)(2,1)S(1)}, bf16[2,32,768]{2,1,0:T(8,128)(2,1)S(1)}, u32[]{:S(2)}, u32[]{:S(2)}) collective-permute-start(bf16[2,32,768]{2,1,0:T(8,128)(2,1)S(1)} %get-tuple-element.54.b_ref), channel_id=1, source_target_pairs={{0,3},{1,2},{2,1},{3,0},{4,7},{5,6},{6,5},{7,4},{8,11},{9,10},{10,... | collective-permute-start | bytes 294920 | tf_op jit(solution)/shard_map/ppermute | solution.py:353
  6.1 11.2 %collective-permute-start.2 = (bf16[2,32,768]{2,1,0:T(8,128)(2,1)S(1)}, bf16[2,32,768]{2,1,0:T(8,128)(2,1)S(1)}, u32[]{:S(2)}, u32[]{:S(2)}) collective-permute-start(bf16[2,32,768]{2,1,0:T(8,128)(2,1)S(1)} %get-tuple-element.54.b_ref), channel_id=1, source_target_pairs={{0,2},{1,3},{2,0},{3,1},{4,6},{5,7},{6,4},{7,5},{8,10},{9,11},{10,... | collective-permute-start | bytes 294920 | tf_op jit(solution)/shard_map/ppermute | solution.py:353
  6.1 11.2 %collective-permute-start.1 = (bf16[2,32,768]{2,1,0:T(8,128)(2,1)S(1)}, bf16[2,32,768]{2,1,0:T(8,128)(2,1)S(1)}, u32[]{:S(2)}, u32[]{:S(2)}) collective-permute-start(bf16[2,32,768]{2,1,0:T(8,128)(2,1)S(1)} %get-tuple-element.54.b_ref), channel_id=1, source_target_pairs={{0,1},{1,0},{2,3},{3,2},{4,5},{5,4},{6,7},{7,6},{8,9},{9,8},{10,11... | collective-permute-start | bytes 294920 | tf_op jit(solution)/shard_map/ppermute | solution.py:353
  6.7 7.8 %slice-start = ((s8[6291456]{0:T(1024)(128)(4,1)}), s8[4194304]{0:T(1024)(128)(4,1)S(1)}, s32[]{:S(2)}) async-start(s8[6291456]{0:T(1024)(128)(4,1)} %bitcast.37), calls=%async_computation | async-start | bytes 8388608
  13.2 1.6 %slice-start.1 = ((s8[6291456]{0:T(1024)(128)(4,1)}), s8[2097152]{0:T(1024)(128)(4,1)S(1)}, s32[]{:S(2)}) async-start(s8[6291456]{0:T(1024)(128)(4,1)} %bitcast.37), calls=%async_computation.1 | async-start | bytes 4194304
  14.4 4.9 %collective-permute-start = (bf16[48,2048]{1,0:T(8,128)(2,1)S(1)}, bf16[48,2048]{1,0:T(8,128)(2,1)S(1)}, u32[]{:S(2)}, u32[]{:S(2)}) collective-permute-start(bf16[48,2048]{1,0:T(8,128)(2,1)S(1)} %maximum_maximum_fusion), channel_id=1, source_target_pairs={{0,4},{4,0},{8,12},{12,8},{1,5},{5,1},{9,13},{13,9},{2,6},{6,2},{1... | collective-permute-start | bytes 589832 | tf_op jit(solution)/shard_map/ppermute | solution.py:400
  19.0 1.8 %collective-permute-start.5 = (bf16[96,2048]{1,0:T(8,128)(2,1)S(1)}, bf16[96,2048]{1,0:T(8,128)(2,1)S(1)}, u32[]{:S(2)}, u32[]{:S(2)}) collective-permute-start(bf16[96,2048]{1,0:T(8,128)(2,1)S(1)} %bitcast_select_fusion), channel_id=1, source_target_pairs={{0,4},{4,0},{8,12},{12,8},{1,5},{5,1},{9,13},{13,9},{2,6},{6,2},{1... | collective-permute-start | bytes 1179656 | tf_op jit(solution)/shard_map/ppermute | solution.py:413
  21.0 12.0 %collective-permute-start.9 = (bf16[2,32,768]{2,1,0:T(8,128)(2,1)S(1)}, bf16[2,32,768]{2,1,0:T(8,128)(2,1)S(1)}, u32[]{:S(2)}, u32[]{:S(2)}) collective-permute-start(bf16[2,32,768]{2,1,0:T(8,128)(2,1)S(1)} %get-tuple-element.81), channel_id=1, source_target_pairs={{0,3},{1,2},{2,1},{3,0},{4,7},{5,6},{6,5},{7,4},{8,11},{9,10},{10,... | collective-permute-start | bytes 294920 | tf_op jit(solution)/shard_map/ppermute | solution.py:353
  24.9 8.4 %collective-permute-start.8 = (bf16[2,32,768]{2,1,0:T(8,128)(2,1)S(1)}, bf16[2,32,768]{2,1,0:T(8,128)(2,1)S(1)}, u32[]{:S(2)}, u32[]{:S(2)}) collective-permute-start(bf16[2,32,768]{2,1,0:T(8,128)(2,1)S(1)} %get-tuple-element.81), channel_id=1, source_target_pairs={{0,2},{1,3},{2,0},{3,1},{4,6},{5,7},{6,4},{7,5},{8,10},{9,11},{10,... | collective-permute-start | bytes 294920 | tf_op jit(solution)/shard_map/ppermute | solution.py:353
  24.9 8.4 %collective-permute-start.7 = (bf16[2,32,768]{2,1,0:T(8,128)(2,1)S(1)}, bf16[2,32,768]{2,1,0:T(8,128)(2,1)S(1)}, u32[]{:S(2)}, u32[]{:S(2)}) collective-permute-start(bf16[2,32,768]{2,1,0:T(8,128)(2,1)S(1)} %get-tuple-element.81), channel_id=1, source_target_pairs={{0,1},{1,0},{2,3},{3,2},{4,5},{5,4},{6,7},{7,6},{8,9},{9,8},{10,11... | collective-permute-start | bytes 294920 | tf_op jit(solution)/shard_map/ppermute | solution.py:353
  25.5 11.5 %collective-permute-start.4 = (bf16[32,2048]{1,0:T(8,128)(2,1)S(1)}, bf16[32,2048]{1,0:T(8,128)(2,1)S(1)}, u32[]{:S(2)}, u32[]{:S(2)}) collective-permute-start(bf16[32,2048]{1,0:T(8,128)(2,1)S(1)} %select_convert_fusion.1), channel_id=1, source_target_pairs={{0,8},{4,12},{1,9},{5,13},{2,10},{6,14},{3,11},{7,15},{16,24},{20,... | collective-permute-start | bytes 393224 | tf_op jit(solution)/shard_map/ppermute | solution.py:396
  29.1 10.9 %collective-permute-start.6 = (bf16[96,2048]{1,0:T(8,128)(2,1)S(1)}, bf16[96,2048]{1,0:T(8,128)(2,1)S(1)}, u32[]{:S(2)}, u32[]{:S(2)}) collective-permute-start(bf16[96,2048]{1,0:T(8,128)(2,1)S(1)} %select_convert_fusion), channel_id=1, source_target_pairs={{0,8},{4,12},{1,9},{5,13},{2,10},{6,14},{3,11},{7,15},{16,24},{20,... | collective-permute-start | bytes 1179656 | tf_op jit(solution)/shard_map/ppermute | solution.py:396
  40.2 2.0 %collective-permute-start.10 = (bf16[128,2048]{1,0:T(8,128)(2,1)S(1)}, bf16[128,2048]{1,0:T(8,128)(2,1)S(1)}, u32[]{:S(2)}, u32[]{:S(2)}) collective-permute-start(bf16[128,2048]{1,0:T(8,128)(2,1)S(1)} %fusion.1), channel_id=1, source_target_pairs={{0,4},{4,0},{8,12},{12,8},{1,5},{5,1},{9,13},{13,9},{2,6},{6,2},{1... | collective-permute-start | bytes 1572872 | tf_op jit(solution)/shard_map/ppermute | solution.py:440
  42.5 11.0 %copy-start = (f32[2048]{0:T(1024)S(1)}, f32[2048]{0:T(1024)}, u32[]{:S(2)}) copy-start(f32[2048]{0:T(1024)} %param.15) | copy-start | bytes 24580
  45.4 5.5 %collective-permute-start.13 = (f32[16,128]{1,0:T(8,128)S(1)}, f32[16,128]{1,0:T(8,128)S(1)}, u32[]{:S(2)}, u32[]{:S(2)}) collective-permute-start(f32[16,128]{1,0:T(8,128)S(1)} %get-tuple-element.102), channel_id=1, source_target_pairs={{0,3},{1,2},{2,1},{3,0},{4,7},{5,6},{6,5},{7,4},{8,11},{9,10},{10,... | collective-permute-start | bytes 24584 | tf_op jit(solution)/shard_map/ppermute | solution.py:353
  48.9 4.5 %collective-permute-start.12 = (f32[16,128]{1,0:T(8,128)S(1)}, f32[16,128]{1,0:T(8,128)S(1)}, u32[]{:S(2)}, u32[]{:S(2)}) collective-permute-start(f32[16,128]{1,0:T(8,128)S(1)} %get-tuple-element.102), channel_id=1, source_target_pairs={{0,2},{1,3},{2,0},{3,1},{4,6},{5,7},{6,4},{7,5},{8,10},{9,11},{10,... | collective-permute-start | bytes 24584 | tf_op jit(solution)/shard_map/ppermute | solution.py:353
  48.9 4.5 %collective-permute-start.11 = (f32[16,128]{1,0:T(8,128)S(1)}, f32[16,128]{1,0:T(8,128)S(1)}, u32[]{:S(2)}, u32[]{:S(2)}) collective-permute-start(f32[16,128]{1,0:T(8,128)S(1)} %get-tuple-element.102), channel_id=1, source_target_pairs={{0,1},{1,0},{2,3},{3,2},{4,5},{5,4},{6,7},{7,6},{8,9},{9,8},{10,11... | collective-permute-start | bytes 24584 | tf_op jit(solution)/shard_map/ppermute | solution.py:353

commit v9 on v8

v9 whole, which is shorter than its diff:
```python
import functools

import jax
import jax.numpy as jnp
import numpy as np
from jax import lax
from jax.experimental import pallas as pl
from jax.experimental.pallas import tpu as pltpu
from jax.sharding import PartitionSpec as P

SPAN = 128
HALF = 256
F32 = jnp.float32
BF16 = jnp.bfloat16
MIB = 1024 * 1024
PARAMS = pltpu.CompilerParams(vmem_limit_bytes=4 * MIB)
COST = pl.CostEstimate(flops=1000, bytes_accessed=1000, transcendentals=0)
GATES_COST = pl.CostEstimate(flops=2 * 10**9, bytes_accessed=25 * 10**6, transcendentals=3 * 10**6)
LEFT_COST = pl.CostEstimate(flops=5 * 10**7, bytes_accessed=16 * 10**5, transcendentals=0)
STAGING_PARAMS = pltpu.CompilerParams(vmem_limit_bytes=10 * MIB)
ENTER, LEAVE, FIRST, TOTAL = range(4)
ROWS = 32
WHOLE = pl.BlockSpec(memory_space=pltpu.VMEM)
ANYWHERE = pl.BlockSpec(memory_space=pl.ANY)


def in_vmem(array):
    return pltpu.with_memory_space_constraint(array, pltpu.VMEM)


def in_hbm(array):
    return pltpu.with_memory_space_constraint(array, pltpu.HBM)


def mm(a, b):
    return jnp.dot(a, b, preferred_element_type=F32)


def mm_nt(a, b):
    return lax.dot_general(a, b, (((1,), (1,)), ((), ())), preferred_element_type=F32)


def iotas(shape):
    return (
        lax.broadcasted_iota(jnp.int32, shape, 0),
        lax.broadcasted_iota(jnp.int32, shape, 1),
    )


def two_parts(v):
    high = v.astype(BF16)
    return [high, (v - high.astype(F32)).astype(BF16)]


def fill_tables(step_ref, decay_ref, skip_ref, sums_ref, rise_band, both_ref, rows_ref):
    seqs, heads, length = decay_ref.shape
    blocks = length // SPAN
    _, lane = iotas((SPAN, 4 * heads))
    rising = lane < 2 * heads
    is_high = (lane < heads) | ((lane >= 2 * heads) & (lane < 3 * heads))
    until = sums_ref[:SPAN]
    same = sums_ref[SPAN:]

    def parts_of(v):
        high = v.astype(BF16).astype(F32)
        return jnp.where(is_high[:v.shape[0]], high, v - high).astype(BF16)

    skip = jnp.concatenate([skip_ref[...]] * 4, axis=1)
    for s in range(seqs):
        decays = two_parts(jnp.concatenate([decay_ref[s]] * 4, axis=0))
        steps = two_parts(jnp.concatenate([step_ref[s]] * 4, axis=0))
        enter, leave, first = [], [], []
        before = jnp.zeros((1, 4 * heads), F32)
        for k in range(blocks):
            sl = slice(k * SPAN, (k + 1) * SPAN)
            summed = mm_nt(until, jnp.concatenate([p[:, sl] for p in decays], axis=1))
            step = mm_nt(same, jnp.concatenate([p[:, sl] for p in steps], axis=1))
            middle = summed[SPAN // 2 - 1:SPAN // 2]
            last = summed[SPAN - 1:]
            above = summed - middle
            factor = jnp.exp(jnp.where(rising, above, -above))
            both_ref[s, sl, :] = parts_of(jnp.where(rising, factor, step * factor))
            enter.append(jnp.exp(middle))
            leave.append(jnp.exp(last - middle))
            first.append(jnp.exp(middle + before))
            before = before + last
        table = enter + leave + first + [jnp.exp(before)]
        table = table + [jnp.zeros_like(before)] * (ROWS - 1 - len(table)) + [skip]
        rows_ref[s] = mm(parts_of(jnp.concatenate(table, axis=0)), rise_band)


def front_kernel(
    x_hbm, step_hbm, decay_hbm, skip_hbm, sums_hbm, bands_hbm,
    x_ref, weighted_ref, both_ref, rows_ref, bands, step, decay, skip, sums, sems,
):
    seqs, length, channels = x_ref.shape
    heads = decay.shape[1]
    pairs = [
        (decay_hbm, decay), (step_hbm, step), (sums_hbm, sums), (skip_hbm, skip), (bands_hbm, bands)
    ]
    small = len(pairs)
    pairs += [(x_hbm.at[s], x_ref.at[s]) for s in range(seqs)]
    copies = [
        pltpu.make_async_copy(source, target, sems.at[i])
        for i, (source, target) in enumerate(pairs)
    ]
    for copy in copies:
        copy.start()
    for copy in copies[:small]:
        copy.wait()
    fill_tables(step, decay, skip, sums, bands[2 * heads:], both_ref, rows_ref)
    for s in range(seqs):
        copies[small + s].wait()
        for k in range(length // SPAN):
            rows = slice(k * SPAN, (k + 1) * SPAN)
            both = both_ref[s, rows]
            for lo in range(0, channels, HALF):
                sl = slice(lo, lo + HALF)
                wide = mm(both, bands[:4 * heads, sl]).astype(BF16)
                weighted_ref[s, rows, sl] = x_ref[s, rows, sl] * wide


def front(features, step_size, log_decay, skip, sums, bands):
    seqs, length, channels = features.shape
    heads = step_size.shape[1]
    operands = [features, step_size, log_decay, skip, sums, bands]
    return pl.pallas_call(
        front_kernel,
        in_specs=[ANYWHERE] * 6,
        out_specs=[WHOLE] * 5,
        out_shape=[
            pltpu.VMEM(features.shape, BF16),
            pltpu.VMEM(features.shape, BF16),
            pltpu.VMEM((seqs, length, 4 * heads), BF16),
            pltpu.VMEM((seqs, ROWS, channels), F32),
            pltpu.VMEM(bands.shape, BF16),
        ],
        scratch_shapes=[
            pltpu.VMEM(step_size.shape, F32),
            pltpu.VMEM(log_decay.shape, F32),
            pltpu.VMEM(skip.shape, F32),
            pltpu.VMEM(sums.shape, BF16),
            pltpu.SemaphoreType.DMA((seqs + 5,)),
        ],
        compiler_params=PARAMS,
        cost_estimate=COST,
        name="front",
    )(*[in_hbm(operand) for operand in operands])


def state_kernel(b_ref, weighted_ref, rows_ref, entering_ref, state_ref):
    seqs, length, channels = weighted_ref.shape
    blocks = length // SPAN
    for s in range(seqs):
        for lo in range(0, channels, HALF):
            sl = slice(lo, lo + HALF)
            state = None
            for k in range(blocks):
                rows = slice(k * SPAN, (k + 1) * SPAN)
                added = mm(b_ref[s, :, rows], weighted_ref[s, rows, sl])
                if k > 0:
                    at = ENTER * blocks + k
                    entering = rows_ref[s, at:at + 1, sl] * state
                    entering_ref[s, k - 1, :, sl] = entering.astype(BF16)
                    added = added + entering
                at = LEAVE * blocks + k
                state = rows_ref[s, at:at + 1, sl] * added
            state_ref[s, :, sl] = state.astype(BF16)


def own_states(b, weighted, rows):
    seqs, states, length = b.shape
    channels = weighted.shape[2]
    return pl.pallas_call(
        state_kernel,
        in_specs=[WHOLE] * 3,
        out_specs=[WHOLE] * 2,
        out_shape=[
            pltpu.VMEM((seqs, length // SPAN - 1, states, channels), BF16),
            pltpu.VMEM((seqs, states, channels), BF16),
        ],
        compiler_params=PARAMS,
        cost_estimate=COST,
        name="own_states",
    )(b, in_vmem(weighted), in_vmem(rows))


def gate_kernel(gate_ref, x_ref, both_ref, bands_ref, rows_ref, lift_ref, skipped_ref):
    seqs, length, channels = lift_ref.shape
    heads4 = both_ref.shape[2]
    band = slice(heads4 // 2, heads4 // 2 + heads4)
    for s in range(seqs):
        for k in range(length // SPAN):
            rows = slice(k * SPAN, (k + 1) * SPAN)
            both = both_ref[s, rows]
            for lo in range(0, channels, HALF):
                sl = slice(lo, lo + HALF)
                half = 0.5 * gate_ref[s, rows, sl].astype(F32)
                gate = (half * jnp.tanh(half) + half).astype(BF16)
                lift_ref[s, rows, sl] = mm(both, bands_ref[band, sl]).astype(BF16) * gate
                skip = rows_ref[s, ROWS - 1:ROWS, sl].astype(BF16) * x_ref[s, rows, sl]
                skipped_ref[s, rows, sl] = skip * gate


def gates(gate_in, x, both, bands, rows):
    return pl.pallas_call(
        gate_kernel,
        in_specs=[WHOLE] * 5,
        out_specs=[WHOLE, WHOLE],
        out_shape=[pltpu.VMEM(gate_in.shape, BF16)] * 2,
        compiler_params=PARAMS,
        cost_estimate=GATES_COST,
        name="gates",
    )(in_vmem(gate_in), in_vmem(x), in_vmem(both), in_vmem(bands), in_vmem(rows))


def left_kernel(b_ref, c_ref, left_ref):
    seqs, states, length = b_ref.shape
    row, col = iotas((SPAN, SPAN))
    for s in range(seqs):
        for k in range(length // SPAN):
            rows = slice(k * SPAN, (k + 1) * SPAN)
            c_t = c_ref[s, :, rows].T
            affinity = mm(c_t, b_ref[s, :, rows])
            left_ref[s, rows, :SPAN] = jnp.where(row >= col, affinity, 0.0).astype(BF16)
            left_ref[s, rows, SPAN:] = c_t


def left_of(b, c):
    seqs, states, length = b.shape
    return pl.pallas_call(
        left_kernel,
        in_specs=[WHOLE] * 2,
        out_specs=WHOLE,
        out_shape=pltpu.VMEM((seqs, length, SPAN + states), BF16),
        compiler_params=PARAMS,
        cost_estimate=LEFT_COST,
        name="left",
    )(b, c)


def final_kernel(
    seq_ref, weighted_ref, near_ref, far_ref, lift_ref, skipped_ref, left_ref, rows_ref,
    incoming_ref, gated_ref, square_ref,
):
    length, channels = gated_ref.shape
    blocks = length // SPAN
    s = seq_ref[0]
    for k in range(blocks):
        rows = slice(k * SPAN, (k + 1) * SPAN)
        left = left_ref[s, rows]
        squares = jnp.zeros((SPAN, 128), F32)
        at = FIRST * blocks + k
        for lo in range(0, channels, HALF):
            sl = slice(lo, lo + HALF)
            entering = rows_ref[s, at:at + 1, sl].astype(BF16) * incoming_ref[:, sl]
            if k > 0:
                entering = entering + jnp.concatenate(
                    [near_ref[s, k - 1, :, sl], far_ref[s, k - 1, :, sl]], axis=0
                )
            right = jnp.concatenate([weighted_ref[s, rows, sl], entering], axis=0)
            mixed = mm(left, right).astype(BF16)
            gated = lift_ref[s, rows, sl] * mixed + skipped_ref[s, rows, sl]
            gated_ref[rows, sl] = gated
            power = gated * gated
            pair = sum(power[:, half:half + 128] for half in range(0, HALF, 128))
            squares = squares + pair.astype(F32)
        square_ref[k:k + 1] = jnp.sum(squares.T, axis=0, keepdims=True)
    unused = square_ref.shape[0] - blocks
    if unused:
        square_ref[blocks:] = jnp.zeros((unused, SPAN), F32)


def final(seq, weighted, near, far, lift, skipped, left, rows, incoming):
    _, length, channels = lift.shape
    return pl.pallas_call(
        final_kernel,
        in_specs=[pl.BlockSpec(memory_space=pltpu.SMEM)] + [WHOLE] * 8,
        out_specs=[WHOLE] * 2,
        out_shape=[
            pltpu.VMEM((length, channels), BF16),
            pltpu.VMEM((-(-length // SPAN // 8) * 8, SPAN), F32),
        ],
        compiler_params=PARAMS,
        cost_estimate=COST,
        name="final",
    )(
        seq, in_vmem(weighted), in_vmem(near), in_vmem(far), in_vmem(lift), in_vmem(skipped),
        in_vmem(left), in_vmem(rows), incoming,
    )


def norm_kernel(all_channels, seq_ref, square_ref, gain_ref, *refs):
    gated_refs, (out_hbm, staged, sems) = refs[:-3], refs[-3:]
    length, channels = gated_refs[0].shape
    blocks = length // SPAN
    stride = square_ref.shape[0] // len(gated_refs)
    copies = []
    for number, gated_ref in enumerate(gated_refs):
        s = lax.rem(seq_ref[0] + number, len(gated_refs))
        for k in range(blocks):
            rows = slice(k * SPAN, (k + 1) * SPAN)
            at = number * stride + k
            inverse = lax.rsqrt(square_ref[at:at + 1] / all_channels + 1e-05)
            column = jnp.broadcast_to(inverse, (128, SPAN)).T
            for lo in range(0, channels, 128):
                sl = slice(lo, lo + 128)
                staged[number, rows, sl] = (
                    gated_ref[rows, sl].astype(F32) * column * gain_ref[:, sl]
                ).astype(BF16)
            place = pl.ds(k * SPAN, SPAN)
            copies.append(
                pltpu.make_async_copy(
                    staged.at[number, place], out_hbm.at[s, place], sems.at[number * blocks + k]
                )
            )
            copies[-1].start(priority=k % 2)
    for copy in copies:
        copy.wait()


def normed(first, gated, squares, gain_row, all_channels):
    seqs = len(gated)
    length, channels = gated[0].shape
    return pl.pallas_call(
        functools.partial(norm_kernel, all_channels),
        in_specs=[pl.BlockSpec(memory_space=pltpu.SMEM)] + [WHOLE] * (2 + seqs),
        out_specs=ANYWHERE,
        out_shape=jax.ShapeDtypeStruct((seqs, length, channels), BF16),
        scratch_shapes=[
            pltpu.VMEM((seqs, length, channels), BF16),
            pltpu.SemaphoreType.DMA((seqs * (length // SPAN),)),
        ],
        compiler_params=STAGING_PARAMS,
        cost_estimate=COST,
        name="normed",
    )(first, squares, gain_row, *[in_vmem(one) for one in gated])


def from_all(shard, axis):
    devices = lax.axis_size(axis)
    paired = devices & (devices - 1) == 0
    return [shard] + [
        lax.ppermute(
            shard, axis, [(i, i ^ by if paired else (i + by) % devices) for i in range(devices)]
        )
        for by in range(1, devices)
    ]


def summed_over(value, axis):
    devices = lax.axis_size(axis)
    if devices & (devices - 1):
        return lax.psum(value, axis)
    by = 1
    while by < devices:
        value = value + lax.ppermute(value, axis, [(i, i ^ by) for i in range(devices)])
        by *= 2
    return value


def as_parts(row):
    high = row.astype(BF16)
    low = (row - high.astype(F32)).astype(BF16)
    return jnp.concatenate([high, low, jnp.zeros((14, row.shape[1]), BF16)], axis=0)


def body(features, gate_in, state_proj, step_size, log_decay, skip_gain, norm_gain):
    seqs, length, channels = features.shape
    heads = step_size.shape[1]
    pair = np.repeat(np.concatenate([np.eye(heads)] * 2), channels // heads, axis=1)
    bands = jnp.asarray(np.concatenate([0 * pair, pair, 0 * pair]), BF16)
    until = np.tril(np.ones((SPAN, SPAN)))
    sums = jnp.asarray(np.concatenate([np.tile(until, 2), np.tile(np.eye(SPAN), 2)]), BF16)
    b_own, c_own = lax.optimization_barrier((state_proj[0], state_proj[1]))
    b_far = from_all(b_own, "head")[1:]
    x, weighted, both, rows, bands = front(
        features, step_size, log_decay, skip_gain[None, :], sums, bands
    )

    place = lax.axis_index("ctx")
    even = place % 2 == 0
    mine = (place % 2).astype(jnp.int32)[None]
    devices = lax.axis_size("ctx")
    swap = [(i, i ^ 1) for i in range(devices)]
    total_at = TOTAL * (length // SPAN)
    decays = [rows[s, total_at:total_at + 1] for s in range(seqs)]
    decay = jnp.where(even, decays[0], decays[1])

    def past_chip(end, other, decay_other):
        return jnp.where(even, other + decay_other * end, end + decay * other)

    def across(past, entered, hop):
        sent = past if entered is None else past + decay_past * entered.astype(F32)
        sent = sent.astype(BF16)
        return sent, lax.ppermute(sent, "ctx", [(hop, hop + 2), (hop + 1, hop + 3)])

    near, near_ends = own_states(b_own, weighted, rows)
    own_rows = b_own.shape[1]
    other = lax.ppermute(
        jnp.concatenate([
            jnp.where(even, near_ends[1], near_ends[0]),
            as_parts(jnp.where(even, decays[1], decays[0])),
        ]),
        "ctx", swap,
    )
    b_far, _ = lax.optimization_barrier((b_far, near_ends))
    b_far = jnp.concatenate(b_far, axis=1)
    far, far_ends = own_states(b_far, weighted, rows)
    far_other = lax.ppermute(jnp.where(even, far_ends[1], far_ends[0]), "ctx", swap)
    other, _ = lax.optimization_barrier((other, far_ends))
    near_other = other[:own_rows].astype(F32)
    decay_other = (
        other[own_rows:own_rows + 1].astype(F32) + other[own_rows + 1:own_rows + 2].astype(F32)
    )
    decay_past = decay_other * decay
    near_end = jnp.where(even, near_ends[0], near_ends[1]).astype(F32)
    near_past = past_chip(near_end, near_other, decay_other)
    near_sent, near_got = across(near_past, None, 0)
    far_other, _ = lax.optimization_barrier((far_other, near_sent))
    far_other = far_other.astype(F32)
    far_end = jnp.where(even, far_ends[0], far_ends[1]).astype(F32)
    far_past = past_chip(far_end, far_other, decay_other)
    far_sent, far_got = across(far_past, None, 0)
    c_own, x, _ = lax.optimization_barrier((c_own, x, far_sent))
    c = from_all(c_own, "head")
    gated_by = gates(gate_in, x, both, bands, rows)
    c, gated_by = lax.optimization_barrier((c, gated_by))
    left = left_of(jnp.concatenate([b_own, b_far], axis=1), jnp.concatenate(c, axis=1))
    near_got, far_got, left = lax.optimization_barrier((near_got, far_got, left))
    for hop in range(2, devices - 2, 2):
        near_got = near_got + across(near_past, near_got, hop)[1]
        far_got = far_got + across(far_past, far_got, hop)[1]
    entered = jnp.concatenate([near_got, far_got])
    entered32 = entered.astype(F32)
    end = jnp.concatenate([near_end, far_end])
    end_other = jnp.concatenate([near_other, far_other])
    shared = lax.ppermute(
        jnp.where(even, end + decay * entered32, entered32).astype(BF16), "ctx", swap
    )
    incoming = jnp.where(even, entered32, end_other + decay_other * entered32).astype(BF16)
    operands = (weighted, near, far, *gated_by, left, rows)
    gated, squares = final(mine, *operands, incoming)
    shared, _ = lax.optimization_barrier((shared, squares))
    gated_next, squares_next = final(1 - mine, *operands, shared)
    squares = summed_over(jnp.concatenate([squares, squares_next]), "head")
    return normed(
        mine, [gated, gated_next], squares, norm_gain[None, :],
        channels * lax.axis_size("head"),
    )


def solution(mesh):
    in_specs = (
        P("groups", "ctx", "head"),
        P("groups", "ctx", "head"),
        P(None, "groups", "head", "ctx"),
        P("groups", "head", "ctx"),
        P("groups", "head", "ctx"),
        P("head"),
        P("head"),
    )
    out_specs = P("groups", "ctx", "head")
    return jax.shard_map(body, mesh=mesh, in_specs=in_specs, out_specs=out_specs, check_vma=False)
```

time: 57 us -> 51.1 us (0.90)
  Pallas kernels: 23.6 us -> 20 us
  waiting for transfers between devices: 9.96 us -> 8.65 us
    ppermute x9 -> x6, starting transfers between devices: 14.7 us -> 10.1 us  [from_all(): lax.ppermute(shard, axis, [(i, i ^ by if paired else (i + by) % devices)...]
    ppermute x1 -> x3, starting transfers between devices: 0.07 us -> 4.25 us  [the longest x2 4.18 us: summed_over(): lax.ppermute(value, axis, [(i, i ^ by) for i in range(devices)])]
    ppermute x2, waiting for transfers between devices: 2.9 us -> 0.01 us  [across(): lax.ppermute(sent, 'ctx', [(hop, hop + 2), (hop + 1, hop + 3)])]
    ppermute x1 -> x3, waiting for transfers between devices: 1.87 us -> 4.08 us  [the longest x2 4.08 us: summed_over(): lax.ppermute(value, axis, [(i, i ^ by) for i in range(devices)])]
    pallas_call x1, Pallas kernels: 6.43 us -> 4.56 us  [front(): pl.pallas_call(front_kernel, in_specs=[ANYWHERE] * 6, out_specs=[WHOLE] *...]
    pallas_call x6 -> x5, Pallas kernels: 14.6 us -> 12.9 us  [the longest x1 5.01 us: gates(): pl.pallas_call(gate_kernel, in_specs=[WHOLE] * 5, out_specs=[WHOLE, WHOLE...]
    ppermute x1, waiting for transfers between devices: 1.34 us -> 0.01 us  [body(): lax.ppermute(jnp.where(even, far_ends[1], far_ends[0]), 'ctx', swap)]
    ppermute x9 -> x6, waiting for transfers between devices: 3.85 us -> 4.55 us  [from_all(): lax.ppermute(shard, axis, [(i, i ^ by if paired else (i + by) % devices)...]
  transfers between devices with their start and end apart: 14 -> 13, of which waited for: 6 -> 4; matrix products, arithmetic and copies ran while one was open for 1% -> 2% of each run, Pallas kernels for 31% -> 29%
where the time goes in v9:
time: 51.1 us; the launch traced here: 50.9 us
  Pallas kernels  20 us (39%)
  starting transfers between devices  19.7 us (39%)
  waiting for transfers between devices  8.65 us (17%)
  other arithmetic  1.1 us (2%)
  local copies, waits for them, and re-layouts  1.06 us (2%)
    ppermute x6, starting transfers between devices, from_all(): lax.ppermute(shard, axis, [(i, i ^ by if paired else (i + by) % devices)...  10.1 us
    ppermute x2, starting transfers between devices, across(): lax.ppermute(sent, 'ctx', [(hop, hop + 2), (hop + 1, hop + 3)])  5.16 us
    pallas_call x1, Pallas kernels, gates(): pl.pallas_call(gate_kernel, in_specs=[WHOLE] * 5, out_specs=[WHOLE, WHOLE...  5.01 us
    pallas_call x1, Pallas kernels, front(): pl.pallas_call(front_kernel, in_specs=[ANYWHERE] * 6, out_specs=[WHOLE] *...  4.56 us
    ppermute x6, waiting for transfers between devices, from_all(): lax.ppermute(shard, axis, [(i, i ^ by if paired else (i + by) % devices)...  4.55 us
    pallas_call x2, Pallas kernels, final(): pl.pallas_call(final_kernel, in_specs=[pl.BlockSpec(memory_space=pltpu.SM...  4.49 us
    ppermute x2, starting transfers between devices, summed_over(): lax.ppermute(value, axis, [(i, i ^ by) for i in range(devices)])  4.18 us
    ppermute x2, waiting for transfers between devices, summed_over(): lax.ppermute(value, axis, [(i, i ^ by) for i in range(devices)])  4.08 us
  transfers between devices with their start and end apart: 13, of which 4 were waited for; matrix products, arithmetic and copies ran while one was open for 2% of the time, Pallas kernels for 29%

profile of v9, /device:TPU:0, one launch (start us, length us, event | category | flops | bytes accessed | tf_op | source)
XLA Modules:
  0.0 50.9 jit_solution(4607339183287937897)
XLA Ops:
  0.0 1.0 %slice_bitcast_fusion = (bf16[2,32,768]{2,1,0:T(8,128)(2,1)S(1)}, bf16[2,32,768]{2,1,0:T(8,128)(2,1)S(1)}) fusion(bf16[2,2,32,768]{3,2,1,0:T(8,128)(2,1)} %param.11), kind=kLoop, calls=%fused_computation.20 | loop fusion | bytes 393216 | tf_op jit(solution)/shard_map/squeeze | solution.py:375
  1.0 3.1 %collective-permute-start = (bf16[2,32,768]{2,1,0:T(8,128)(2,1)S(1)}, bf16[2,32,768]{2,1,0:T(8,128)(2,1)S(1)}, u32[]{:S(2)}, u32[]{:S(2)}) collective-permute-start(bf16[2,32,768]{2,1,0:T(8,128)(2,1)S(1)} %get-tuple-element.40.b_ref), channel_id=1, source_target_pairs={{0,1},{1,0},{2,3},{3,2},{4,5},{5,4},{6,7},{7,6},{8,9},{9,8},{10,11... | collective-permute-start | bytes 294920 | tf_op jit(solution)/shard_map/ppermute | solution.py:344
  4.0 2.6 %collective-permute-start.1 = (bf16[2,32,768]{2,1,0:T(8,128)(2,1)S(1)}, bf16[2,32,768]{2,1,0:T(8,128)(2,1)S(1)}, u32[]{:S(2)}, u32[]{:S(2)}) collective-permute-start(bf16[2,32,768]{2,1,0:T(8,128)(2,1)S(1)} %get-tuple-element.40.b_ref), channel_id=1, source_target_pairs={{0,2},{1,3},{2,0},{3,1},{4,6},{5,7},{6,4},{7,5},{8,10},{9,11},{10,... | collective-permute-start | bytes 294920 | tf_op jit(solution)/shard_map/ppermute | solution.py:344
  6.6 4.6 %front.1 = (bf16[2,768,2048]{2,1,0:T(8,128)(2,1)S(1)}, bf16[2,768,2048]{2,1,0:T(8,128)(2,1)S(1)}, bf16[2,768,128]{2,1,0:T(8,128)(2,1)S(1)}, f32[2,32,2048]{2,1,0:T(8,128)S(1)}, bf16[192,2048]{1,0:T(8,128)(2,1)S(1)}) custom-call(bf16[2,768,2048]{2,1,0:T(8,128)(2,1)} %x_hbm.1, f32[2,32,768]{2,1,0:T(8,128)} %step_hbm.1, f32[2,32,768]{2,1,0:T(8,128)} %decay_hbm.1, ...), custom_call_target="tpu_custom_call" | custom-call | flops 1000 | bytes 1000 | tf_op jit(solution)/shard_map/front/pallas_call | solution.py:127
  11.3 1.0 %own_states.2 = (bf16[2,5,32,2048]{3,2,1,0:T(8,128)(2,1)S(1)}, bf16[2,32,2048]{2,1,0:T(8,128)(2,1)S(1)}) custom-call(bf16[2,32,768]{2,1,0:T(8,128)(2,1)S(1)} %get-tuple-element.40.b_ref, bf16[2,768,2048]{2,1,0:T(8,128)(2,1)S(1)} %get-tuple-element.39.weighted_ref, f32[2,32,2048]{2,1,0:T(8,128)S(1)} %get-tuple-element.41.rows_ref), custom_call_target="tpu_custom_call" | custom-call | flops 1000 | bytes 1000 | tf_op jit(solution)/shard_map/own_states/pallas_call | solution.py:174
  12.3 0.1 pad.17.clone
  12.4 0.1 maximum_maximum_fusion
  12.5 0.1 collective-permute-start.4
  12.6 1.9 %collective-permute-done.1 = bf16[2,32,768]{2,1,0:T(8,128)(2,1)S(1)} collective-permute-done((bf16[2,32,768]{2,1,0:T(8,128)(2,1)S(1)}, bf16[2,32,768]{2,1,0:T(8,128)(2,1)S(1)}, u32[]{:S(2)}, u32[]{:S(2)}) %collective-permute-start.1) | collective-permute-done | bytes 98336 | tf_op jit(solution)/shard_map/ppermute | solution.py:344
  14.5 1.5 %own_states.3 = (bf16[2,5,96,2048]{3,2,1,0:T(8,128)(2,1)S(1)}, bf16[2,96,2048]{2,1,0:T(8,128)(2,1)S(1)}) custom-call(bf16[2,96,768]{2,1,0:T(8,128)(2,1)S(1)} %pad_maximum_fusion.3.b_ref, bf16[2,768,2048]{2,1,0:T(8,128)(2,1)S(1)} %get-tuple-element.39.weighted_ref, f32[2,32,2048]{2,1,0:T(8,128)S(1)} %get-tuple-element.41.rows_ref), custom_call_target="tpu_custom_call" | custom-call | flops 1000 | bytes 1000 | tf_op jit(solution)/shard_map/own_states/pallas_call | solution.py:174
  16.1 0.1 bitcast_convert_fusion
  16.1 0.1 collective-permute-start.3
  16.3 0.1 select_convert_fusion.1
  16.3 3.5 %collective-permute-start.8 = (bf16[32,2048]{1,0:T(8,128)(2,1)S(1)}, bf16[32,2048]{1,0:T(8,128)(2,1)S(1)}, u32[]{:S(2)}, u32[]{:S(2)}) collective-permute-start(bf16[32,2048]{1,0:T(8,128)(2,1)S(1)} %select_convert_fusion.1), channel_id=1, source_target_pairs={{0,8},{4,12},{1,9},{5,13},{2,10},{6,14},{3,11},{7,15},{16,24},{20,... | collective-permute-start | bytes 393224 | tf_op jit(solution)/shard_map/ppermute | solution.py:396
  19.9 0.2 select_convert_fusion
  20.2 1.6 %collective-permute-start.9 = (bf16[96,2048]{1,0:T(8,128)(2,1)S(1)}, bf16[96,2048]{1,0:T(8,128)(2,1)S(1)}, u32[]{:S(2)}, u32[]{:S(2)}) collective-permute-start(bf16[96,2048]{1,0:T(8,128)(2,1)S(1)} %select_convert_fusion), channel_id=1, source_target_pairs={{0,8},{4,12},{1,9},{5,13},{2,10},{6,14},{3,11},{7,15},{16,24},{20,... | collective-permute-start | bytes 1179656 | tf_op jit(solution)/shard_map/ppermute | solution.py:396
  21.8 1.7 %collective-permute-start.5 = (bf16[2,32,768]{2,1,0:T(8,128)(2,1)S(1)}, bf16[2,32,768]{2,1,0:T(8,128)(2,1)S(1)}, u32[]{:S(2)}, u32[]{:S(2)}) collective-permute-start(bf16[2,32,768]{2,1,0:T(8,128)(2,1)S(1)} %get-tuple-element.61), channel_id=1, source_target_pairs={{0,1},{1,0},{2,3},{3,2},{4,5},{5,4},{6,7},{7,6},{8,9},{9,8},{10,11... | collective-permute-start | bytes 294920 | tf_op jit(solution)/shard_map/ppermute | solution.py:344
  23.5 1.4 %collective-permute-start.6 = (bf16[2,32,768]{2,1,0:T(8,128)(2,1)S(1)}, bf16[2,32,768]{2,1,0:T(8,128)(2,1)S(1)}, u32[]{:S(2)}, u32[]{:S(2)}) collective-permute-start(bf16[2,32,768]{2,1,0:T(8,128)(2,1)S(1)} %get-tuple-element.61), channel_id=1, source_target_pairs={{0,2},{1,3},{2,0},{3,1},{4,6},{5,7},{6,4},{7,5},{8,10},{9,11},{10,... | collective-permute-start | bytes 294920 | tf_op jit(solution)/shard_map/ppermute | solution.py:344
  24.9 1.3 %collective-permute-start.7 = (bf16[2,32,768]{2,1,0:T(8,128)(2,1)S(1)}, bf16[2,32,768]{2,1,0:T(8,128)(2,1)S(1)}, u32[]{:S(2)}, u32[]{:S(2)}) collective-permute-start(bf16[2,32,768]{2,1,0:T(8,128)(2,1)S(1)} %get-tuple-element.61), channel_id=1, source_target_pairs={{0,3},{1,2},{2,1},{3,0},{4,7},{5,6},{6,5},{7,4},{8,11},{9,10},{10,... | collective-permute-start | bytes 294920 | tf_op jit(solution)/shard_map/ppermute | solution.py:344
  26.3 0.1 convert_element_type.85
  26.4 5.0 %gates.1 = (bf16[2,768,2048]{2,1,0:T(8,128)(2,1)S(1)}, bf16[2,768,2048]{2,1,0:T(8,128)(2,1)S(1)}) custom-call(bf16[2,768,2048]{2,1,0:T(8,128)(2,1)S(1)} %bitcast.30, bf16[2,768,2048]{2,1,0:T(8,128)(2,1)S(1)} %get-tuple-element.54.x_ref, bf16[2,768,128]{2,1,0:T(8,128)(2,1)S(1)} %get-tuple-element.55.both_ref, ...), custom_call_target="tpu_custom_call" | custom-call | flops 2000000000 | bytes 25000000 | tf_op jit(solution)/shard_map/gates/pallas_call | solution.py:206
  31.4 2.7 %collective-permute-done.6 = bf16[2,32,768]{2,1,0:T(8,128)(2,1)S(1)} collective-permute-done((bf16[2,32,768]{2,1,0:T(8,128)(2,1)S(1)}, bf16[2,32,768]{2,1,0:T(8,128)(2,1)S(1)}, u32[]{:S(2)}, u32[]{:S(2)}) %collective-permute-start.6) | collective-permute-done | bytes 98336 | tf_op jit(solution)/shard_map/ppermute | solution.py:344
  34.1 0.3 left.1.left_ref
  34.5 0.3 fusion.3
  34.8 0.1 collective-permute-start.10
  34.9 2.2 %final.2 = (bf16[768,2048]{1,0:T(8,128)(2,1)S(1)}, f32[8,128]{1,0:T(8,128)S(1)}) custom-call(s32[1]{0:T(128)} %bitcast.seq_ref, bf16[2,768,2048]{2,1,0:T(8,128)(2,1)S(1)} %get-tuple-element.39.weighted_ref, bf16[2,5,32,2048]{3,2,1,0:T(8,128)(2,1)S(1)} %get-tuple-element.42.near_ref, bf16[2,5,96,2048]{3,2,1,0:T(8,128)(2,1)S(1)} %get-tuple-element.47.far_ref, ...), custom_call_target="tpu_custom_call" | custom-call | flops 1000 | bytes 1000 | tf_op jit(solution)/shard_map/final/pallas_call | solution.py:276
  37.1 2.2 %final.3 = (bf16[768,2048]{1,0:T(8,128)(2,1)S(1)}, f32[8,128]{1,0:T(8,128)S(1)}) custom-call(s32[1]{0:T(128)S(6)} %sub.15.seq_ref, bf16[2,768,2048]{2,1,0:T(8,128)(2,1)S(1)} %get-tuple-element.39.weighted_ref, bf16[2,5,32,2048]{3,2,1,0:T(8,128)(2,1)S(1)} %get-tuple-element.42.near_ref, bf16[2,5,96,2048]{3,2,1,0:T(8,128)(2,1)S(1)} %get-tuple-element.47.far_ref, ...), custom_call_target="tpu_custom_call" | custom-call | flops 1000 | bytes 1000 | tf_op jit(solution)/shard_map/final/pallas_call | solution.py:276
  39.4 1.7 %collective-permute-start.11 = (f32[16,128]{1,0:T(8,128)S(1)}, f32[16,128]{1,0:T(8,128)S(1)}, u32[]{:S(2)}, u32[]{:S(2)}) collective-permute-start(f32[16,128]{1,0:T(8,128)S(1)} %constant_dynamic-update-slice_fusion), channel_id=1, source_target_pairs={{0,1},{1,0},{2,3},{3,2},{4,5},{5,4},{6,7},{7,6},{8,9},{9,8},{10,11... | collective-permute-start | bytes 24584 | tf_op jit(solution)/shard_map/ppermute | solution.py:357
  41.1 2.0 %collective-permute-done.11 = f32[16,128]{1,0:T(8,128)S(1)} collective-permute-done((f32[16,128]{1,0:T(8,128)S(1)}, f32[16,128]{1,0:T(8,128)S(1)}, u32[]{:S(2)}, u32[]{:S(2)}) %collective-permute-start.11) | collective-permute-done | bytes 8224 | tf_op jit(solution)/shard_map/ppermute | solution.py:357
  43.1 2.5 %collective-permute-start.12 = (f32[16,128]{1,0:T(8,128)S(1)}, f32[16,128]{1,0:T(8,128)S(1)}, u32[]{:S(2)}, u32[]{:S(2)}) collective-permute-start(f32[16,128]{1,0:T(8,128)S(1)} %add.40), channel_id=1, source_target_pairs={{0,2},{1,3},{2,0},{3,1},{4,6},{5,7},{6,4},{7,5},{8,10},{9,11},{10,... | collective-permute-start | bytes 24584 | tf_op jit(solution)/shard_map/ppermute | solution.py:357
  45.6 2.0 %collective-permute-done.12 = f32[16,128]{1,0:T(8,128)S(1)} collective-permute-done((f32[16,128]{1,0:T(8,128)S(1)}, f32[16,128]{1,0:T(8,128)S(1)}, u32[]{:S(2)}, u32[]{:S(2)}) %collective-permute-start.12) | collective-permute-done | bytes 8224 | tf_op jit(solution)/shard_map/ppermute | solution.py:357
  47.7 3.1 %normed.1 = bf16[2,768,2048]{2,1,0:T(8,128)(2,1)} custom-call(s32[1]{0:T(128)} %bitcast.seq_ref, f32[16,128]{1,0:T(8,128)S(1)} %add.41.square_ref, f32[1,2048]{1,0:T(1,128)S(1)} %bitcast.31, bf16[768,2048]{1,0:T(8,128)(2,1)S(1)} %get-tuple-element.71.refs_0_, bf16[768,2048]{1,0:T(8,128)(2,1)S(1)} %get-tuple-element.72.refs_1_), custom_call_target="tpu_custom_call" | custom-call | flops 1000 | bytes 1000 | tf_op jit(solution)/shard_map/normed/pallas_call | solution.py:325
  (30 shorter events, 0.3 us)
Async XLA Ops:
  1.0 11.6 %collective-permute-start = (bf16[2,32,768]{2,1,0:T(8,128)(2,1)S(1)}, bf16[2,32,768]{2,1,0:T(8,128)(2,1)S(1)}, u32[]{:S(2)}, u32[]{:S(2)}) collective-permute-start(bf16[2,32,768]{2,1,0:T(8,128)(2,1)S(1)} %get-tuple-element.40.b_ref), channel_id=1, source_target_pairs={{0,1},{1,0},{2,3},{3,2},{4,5},{5,4},{6,7},{7,6},{8,9},{9,8},{10,11... | collective-permute-start | bytes 294920 | tf_op jit(solution)/shard_map/ppermute | solution.py:344
  4.0 10.4 %collective-permute-start.1 = (bf16[2,32,768]{2,1,0:T(8,128)(2,1)S(1)}, bf16[2,32,768]{2,1,0:T(8,128)(2,1)S(1)}, u32[]{:S(2)}, u32[]{:S(2)}) collective-permute-start(bf16[2,32,768]{2,1,0:T(8,128)(2,1)S(1)} %get-tuple-element.40.b_ref), channel_id=1, source_target_pairs={{0,2},{1,3},{2,0},{3,1},{4,6},{5,7},{6,4},{7,5},{8,10},{9,11},{10,... | collective-permute-start | bytes 294920 | tf_op jit(solution)/shard_map/ppermute | solution.py:344
  6.6 7.8 %collective-permute-start.2 = (bf16[2,32,768]{2,1,0:T(8,128)(2,1)S(1)}, bf16[2,32,768]{2,1,0:T(8,128)(2,1)S(1)}, u32[]{:S(2)}, u32[]{:S(2)}) collective-permute-start(bf16[2,32,768]{2,1,0:T(8,128)(2,1)S(1)} %get-tuple-element.40.b_ref), channel_id=1, source_target_pairs={{0,3},{1,2},{2,1},{3,0},{4,7},{5,6},{6,5},{7,4},{8,11},{9,10},{10,... | collective-permute-start | bytes 294920 | tf_op jit(solution)/shard_map/ppermute | solution.py:344
  12.5 3.7 %collective-permute-start.4 = (bf16[48,2048]{1,0:T(8,128)(2,1)S(1)}, bf16[48,2048]{1,0:T(8,128)(2,1)S(1)}, u32[]{:S(2)}, u32[]{:S(2)}) collective-permute-start(bf16[48,2048]{1,0:T(8,128)(2,1)S(1)} %maximum_maximum_fusion), channel_id=1, source_target_pairs={{0,4},{4,0},{8,12},{12,8},{1,5},{5,1},{9,13},{13,9},{2,6},{6,2},{1... | collective-permute-start | bytes 589832 | tf_op jit(solution)/shard_map/ppermute | solution.py:400
  14.5 11.8 %slice-start = ((s8[6291456]{0:T(1024)(128)(4,1)}), s8[4194304]{0:T(1024)(128)(4,1)S(1)}, s32[]{:S(2)}) async-start(s8[6291456]{0:T(1024)(128)(4,1)} %bitcast.29), calls=%async_computation | async-start | bytes 8388608
  14.5 11.8 %slice-start.1 = ((s8[6291456]{0:T(1024)(128)(4,1)}), s8[2097152]{0:T(1024)(128)(4,1)S(1)}, s32[]{:S(2)}) async-start(s8[6291456]{0:T(1024)(128)(4,1)} %bitcast.29), calls=%async_computation.1 | async-start | bytes 4194304
  16.1 3.7 %collective-permute-start.3 = (bf16[96,2048]{1,0:T(8,128)(2,1)S(1)}, bf16[96,2048]{1,0:T(8,128)(2,1)S(1)}, u32[]{:S(2)}, u32[]{:S(2)}) collective-permute-start(bf16[96,2048]{1,0:T(8,128)(2,1)S(1)} %get-tuple-element.74), channel_id=1, source_target_pairs={{0,4},{4,0},{8,12},{12,8},{1,5},{5,1},{9,13},{13,9},{2,6},{6,2},{1... | collective-permute-start | bytes 1179656 | tf_op jit(solution)/shard_map/ppermute | solution.py:410
  16.3 18.1 %collective-permute-start.8 = (bf16[32,2048]{1,0:T(8,128)(2,1)S(1)}, bf16[32,2048]{1,0:T(8,128)(2,1)S(1)}, u32[]{:S(2)}, u32[]{:S(2)}) collective-permute-start(bf16[32,2048]{1,0:T(8,128)(2,1)S(1)} %select_convert_fusion.1), channel_id=1, source_target_pairs={{0,8},{4,12},{1,9},{5,13},{2,10},{6,14},{3,11},{7,15},{16,24},{20,... | collective-permute-start | bytes 393224 | tf_op jit(solution)/shard_map/ppermute | solution.py:396
  20.2 14.3 %collective-permute-start.9 = (bf16[96,2048]{1,0:T(8,128)(2,1)S(1)}, bf16[96,2048]{1,0:T(8,128)(2,1)S(1)}, u32[]{:S(2)}, u32[]{:S(2)}) collective-permute-start(bf16[96,2048]{1,0:T(8,128)(2,1)S(1)} %select_convert_fusion), channel_id=1, source_target_pairs={{0,8},{4,12},{1,9},{5,13},{2,10},{6,14},{3,11},{7,15},{16,24},{20,... | collective-permute-start | bytes 1179656 | tf_op jit(solution)/shard_map/ppermute | solution.py:396
  21.8 9.6 %collective-permute-start.5 = (bf16[2,32,768]{2,1,0:T(8,128)(2,1)S(1)}, bf16[2,32,768]{2,1,0:T(8,128)(2,1)S(1)}, u32[]{:S(2)}, u32[]{:S(2)}) collective-permute-start(bf16[2,32,768]{2,1,0:T(8,128)(2,1)S(1)} %get-tuple-element.61), channel_id=1, source_target_pairs={{0,1},{1,0},{2,3},{3,2},{4,5},{5,4},{6,7},{7,6},{8,9},{9,8},{10,11... | collective-permute-start | bytes 294920 | tf_op jit(solution)/shard_map/ppermute | solution.py:344
  23.5 10.6 %collective-permute-start.6 = (bf16[2,32,768]{2,1,0:T(8,128)(2,1)S(1)}, bf16[2,32,768]{2,1,0:T(8,128)(2,1)S(1)}, u32[]{:S(2)}, u32[]{:S(2)}) collective-permute-start(bf16[2,32,768]{2,1,0:T(8,128)(2,1)S(1)} %get-tuple-element.61), channel_id=1, source_target_pairs={{0,2},{1,3},{2,0},{3,1},{4,6},{5,7},{6,4},{7,5},{8,10},{9,11},{10,... | collective-permute-start | bytes 294920 | tf_op jit(solution)/shard_map/ppermute | solution.py:344
  24.9 9.2 %collective-permute-start.7 = (bf16[2,32,768]{2,1,0:T(8,128)(2,1)S(1)}, bf16[2,32,768]{2,1,0:T(8,128)(2,1)S(1)}, u32[]{:S(2)}, u32[]{:S(2)}) collective-permute-start(bf16[2,32,768]{2,1,0:T(8,128)(2,1)S(1)} %get-tuple-element.61), channel_id=1, source_target_pairs={{0,3},{1,2},{2,1},{3,0},{4,7},{5,6},{6,5},{7,4},{8,11},{9,10},{10,... | collective-permute-start | bytes 294920 | tf_op jit(solution)/shard_map/ppermute | solution.py:344
  34.8 2.3 %collective-permute-start.10 = (bf16[128,2048]{1,0:T(8,128)(2,1)S(1)}, bf16[128,2048]{1,0:T(8,128)(2,1)S(1)}, u32[]{:S(2)}, u32[]{:S(2)}) collective-permute-start(bf16[128,2048]{1,0:T(8,128)(2,1)S(1)} %get-tuple-element.75), channel_id=1, source_target_pairs={{0,4},{4,0},{8,12},{12,8},{1,5},{5,1},{9,13},{13,9},{2,6},{6,2},{1... | collective-permute-start | bytes 1572872 | tf_op jit(solution)/shard_map/ppermute | solution.py:438
  37.1 10.6 %copy-start = (f32[2048]{0:T(1024)S(1)}, f32[2048]{0:T(1024)}, u32[]{:S(2)}) copy-start(f32[2048]{0:T(1024)} %param.15) | copy-start | bytes 24580
  39.4 3.7 %collective-permute-start.11 = (f32[16,128]{1,0:T(8,128)S(1)}, f32[16,128]{1,0:T(8,128)S(1)}, u32[]{:S(2)}, u32[]{:S(2)}) collective-permute-start(f32[16,128]{1,0:T(8,128)S(1)} %constant_dynamic-update-slice_fusion), channel_id=1, source_target_pairs={{0,1},{1,0},{2,3},{3,2},{4,5},{5,4},{6,7},{7,6},{8,9},{9,8},{10,11... | collective-permute-start | bytes 24584 | tf_op jit(solution)/shard_map/ppermute | solution.py:357
  43.1 4.5 %collective-permute-start.12 = (f32[16,128]{1,0:T(8,128)S(1)}, f32[16,128]{1,0:T(8,128)S(1)}, u32[]{:S(2)}, u32[]{:S(2)}) collective-permute-start(f32[16,128]{1,0:T(8,128)S(1)} %add.40), channel_id=1, source_target_pairs={{0,2},{1,3},{2,0},{3,1},{4,6},{5,7},{6,4},{7,5},{8,10},{9,11},{10,... | collective-permute-start | bytes 24584 | tf_op jit(solution)/shard_map/ppermute | solution.py:357

commit v10 on v9

--- a/solution.py
+++ b/solution.py
@@ -15,7 +15,7 @@
 MIB = 1024 * 1024
 PARAMS = pltpu.CompilerParams(vmem_limit_bytes=4 * MIB)
 COST = pl.CostEstimate(flops=1000, bytes_accessed=1000, transcendentals=0)
-GATES_COST = pl.CostEstimate(flops=2 * 10**9, bytes_accessed=25 * 10**6, transcendentals=3 * 10**6)
+GATES_COST = pl.CostEstimate(flops=10**9, bytes_accessed=12 * 10**6, transcendentals=15 * 10**5)
 LEFT_COST = pl.CostEstimate(flops=5 * 10**7, bytes_accessed=16 * 10**5, transcendentals=0)
 STAGING_PARAMS = pltpu.CompilerParams(vmem_limit_bytes=10 * MIB)
 ENTER, LEAVE, FIRST, TOTAL = range(4)
@@ -185,33 +185,34 @@
     )(b, in_vmem(weighted), in_vmem(rows))
 
 
-def gate_kernel(gate_ref, x_ref, both_ref, bands_ref, rows_ref, lift_ref, skipped_ref):
-    seqs, length, channels = lift_ref.shape
+def gate_kernel(seq_ref, gate_ref, x_ref, both_ref, bands_ref, rows_ref, lift_ref, skipped_ref):
+    length, channels = lift_ref.shape
     heads4 = both_ref.shape[2]
     band = slice(heads4 // 2, heads4 // 2 + heads4)
-    for s in range(seqs):
-        for k in range(length // SPAN):
-            rows = slice(k * SPAN, (k + 1) * SPAN)
-            both = both_ref[s, rows]
-            for lo in range(0, channels, HALF):
-                sl = slice(lo, lo + HALF)
-                half = 0.5 * gate_ref[s, rows, sl].astype(F32)
-                gate = (half * jnp.tanh(half) + half).astype(BF16)
-                lift_ref[s, rows, sl] = mm(both, bands_ref[band, sl]).astype(BF16) * gate
-                skip = rows_ref[s, ROWS - 1:ROWS, sl].astype(BF16) * x_ref[s, rows, sl]
-                skipped_ref[s, rows, sl] = skip * gate
-
-
-def gates(gate_in, x, both, bands, rows):
+    seq = seq_ref[0]
+    for k in range(length // SPAN):
+        rows = slice(k * SPAN, (k + 1) * SPAN)
+        both = both_ref[seq, rows]
+        for lo in range(0, channels, HALF):
+            sl = slice(lo, lo + HALF)
+            half = 0.5 * gate_ref[seq, rows, sl].astype(F32)
+            gate = (half * jnp.tanh(half) + half).astype(BF16)
+            lift_ref[rows, sl] = mm(both, bands_ref[band, sl]).astype(BF16) * gate
+            skip = rows_ref[seq, ROWS - 1:ROWS, sl].astype(BF16) * x_ref[seq, rows, sl]
+            skipped_ref[rows, sl] = skip * gate
+
+
+def gates(seq, gate_in, x, both, bands, rows):
+    _, length, channels = gate_in.shape
     return pl.pallas_call(
         gate_kernel,
-        in_specs=[WHOLE] * 5,
+        in_specs=[pl.BlockSpec(memory_space=pltpu.SMEM)] + [WHOLE] * 5,
         out_specs=[WHOLE, WHOLE],
-        out_shape=[pltpu.VMEM(gate_in.shape, BF16)] * 2,
+        out_shape=[pltpu.VMEM((length, channels), BF16)] * 2,
         compiler_params=PARAMS,
         cost_estimate=GATES_COST,
         name="gates",
-    )(in_vmem(gate_in), in_vmem(x), in_vmem(both), in_vmem(bands), in_vmem(rows))
+    )(seq, in_vmem(gate_in), in_vmem(x), in_vmem(both), in_vmem(bands), in_vmem(rows))
 
 
 def left_kernel(b_ref, c_ref, left_ref):
@@ -240,7 +241,7 @@
 
 
 def final_kernel(
-    seq_ref, weighted_ref, near_ref, far_ref, lift_ref, skipped_ref, left_ref, rows_ref,
+    seq_ref, weighted_ref, near_ref, far_ref, left_ref, rows_ref, lift_ref, skipped_ref,
     incoming_ref, gated_ref, square_ref,
 ):
     length, channels = gated_ref.shape
@@ -260,7 +261,7 @@
                 )
             right = jnp.concatenate([weighted_ref[s, rows, sl], entering], axis=0)
             mixed = mm(left, right).astype(BF16)
-            gated = lift_ref[s, rows, sl] * mixed + skipped_ref[s, rows, sl]
+            gated = lift_ref[rows, sl] * mixed + skipped_ref[rows, sl]
             gated_ref[rows, sl] = gated
             power = gated * gated
             pair = sum(power[:, half:half + 128] for half in range(0, HALF, 128))
@@ -271,8 +272,8 @@
         square_ref[blocks:] = jnp.zeros((unused, SPAN), F32)
 
 
-def final(seq, weighted, near, far, lift, skipped, left, rows, incoming):
-    _, length, channels = lift.shape
+def final(seq, weighted, near, far, left, rows, lift, skipped, incoming):
+    length, channels = lift.shape
     return pl.pallas_call(
         final_kernel,
         in_specs=[pl.BlockSpec(memory_space=pltpu.SMEM)] + [WHOLE] * 8,
@@ -285,8 +286,8 @@
         cost_estimate=COST,
         name="final",
     )(
-        seq, in_vmem(weighted), in_vmem(near), in_vmem(far), in_vmem(lift), in_vmem(skipped),
-        in_vmem(left), in_vmem(rows), incoming,
+        seq, in_vmem(weighted), in_vmem(near), in_vmem(far), in_vmem(left), in_vmem(rows),
+        in_vmem(lift), in_vmem(skipped), incoming,
     )
 
 
@@ -348,17 +349,6 @@
     ]
 
 
-def summed_over(value, axis):
-    devices = lax.axis_size(axis)
-    if devices & (devices - 1):
-        return lax.psum(value, axis)
-    by = 1
-    while by < devices:
-        value = value + lax.ppermute(value, axis, [(i, i ^ by) for i in range(devices)])
-        by *= 2
-    return value
-
-
 def as_parts(row):
     high = row.astype(BF16)
     low = (row - high.astype(F32)).astype(BF16)
@@ -373,7 +363,7 @@
     until = np.tril(np.ones((SPAN, SPAN)))
     sums = jnp.asarray(np.concatenate([np.tile(until, 2), np.tile(np.eye(SPAN), 2)]), BF16)
     b_own, c_own = lax.optimization_barrier((state_proj[0], state_proj[1]))
-    b_far = from_all(b_own, "head")[1:]
+    b_pieces = from_all(b_own, "head")
     x, weighted, both, rows, bands = front(
         features, step_size, log_decay, skip_gain[None, :], sums, bands
     )
@@ -395,8 +385,9 @@
         sent = sent.astype(BF16)
         return sent, lax.ppermute(sent, "ctx", [(hop, hop + 2), (hop + 1, hop + 3)])
 
-    near, near_ends = own_states(b_own, weighted, rows)
-    own_rows = b_own.shape[1]
+    b_near = jnp.concatenate(b_pieces[:2], axis=1)
+    near, near_ends = own_states(b_near, weighted, rows)
+    near_rows = b_near.shape[1]
     other = lax.ppermute(
         jnp.concatenate([
             jnp.where(even, near_ends[1], near_ends[0]),
@@ -404,29 +395,29 @@
         ]),
         "ctx", swap,
     )
-    b_far, _ = lax.optimization_barrier((b_far, near_ends))
-    b_far = jnp.concatenate(b_far, axis=1)
-    far, far_ends = own_states(b_far, weighted, rows)
-    far_other = lax.ppermute(jnp.where(even, far_ends[1], far_ends[0]), "ctx", swap)
-    other, _ = lax.optimization_barrier((other, far_ends))
-    near_other = other[:own_rows].astype(F32)
+    near_other = other[:near_rows].astype(F32)
     decay_other = (
-        other[own_rows:own_rows + 1].astype(F32) + other[own_rows + 1:own_rows + 2].astype(F32)
+        other[near_rows:near_rows + 1].astype(F32) + other[near_rows + 1:near_rows + 2].astype(F32)
     )
     decay_past = decay_other * decay
     near_end = jnp.where(even, near_ends[0], near_ends[1]).astype(F32)
     near_past = past_chip(near_end, near_other, decay_other)
     near_sent, near_got = across(near_past, None, 0)
-    far_other, _ = lax.optimization_barrier((far_other, near_sent))
-    far_other = far_other.astype(F32)
+    b_far, _ = lax.optimization_barrier((b_pieces[2:], near_sent))
+    b_far = jnp.concatenate(b_far, axis=1)
+    far, far_ends = own_states(b_far, weighted, rows)
+    far_other = lax.ppermute(jnp.where(even, far_ends[1], far_ends[0]), "ctx", swap).astype(F32)
     far_end = jnp.where(even, far_ends[0], far_ends[1]).astype(F32)
     far_past = past_chip(far_end, far_other, decay_other)
     far_sent, far_got = across(far_past, None, 0)
-    c_own, x, _ = lax.optimization_barrier((c_own, x, far_sent))
+    c_own, _ = lax.optimization_barrier((c_own, near_ends))
     c = from_all(c_own, "head")
-    gated_by = gates(gate_in, x, both, bands, rows)
-    c, gated_by = lax.optimization_barrier((c, gated_by))
-    left = left_of(jnp.concatenate([b_own, b_far], axis=1), jnp.concatenate(c, axis=1))
+    x, _ = lax.optimization_barrier((x, far_sent))
+    lifts = gates(mine, gate_in, x, both, bands, rows)
+    x, lifts, c = lax.optimization_barrier((x, lifts, c))
+    lifts_next = gates(1 - mine, gate_in, x, both, bands, rows)
+    left = left_of(jnp.concatenate([b_near, b_far], axis=1), jnp.concatenate(c, axis=1))
+    left, lifts_next = lax.optimization_barrier((left, lifts_next))
     near_got, far_got, left = lax.optimization_barrier((near_got, far_got, left))
     for hop in range(2, devices - 2, 2):
         near_got = near_got + across(near_past, near_got, hop)[1]
@@ -439,11 +430,11 @@
         jnp.where(even, end + decay * entered32, entered32).astype(BF16), "ctx", swap
     )
     incoming = jnp.where(even, entered32, end_other + decay_other * entered32).astype(BF16)
-    operands = (weighted, near, far, *gated_by, left, rows)
-    gated, squares = final(mine, *operands, incoming)
+    operands = (weighted, near, far, left, rows)
+    gated, squares = final(mine, *operands, *lifts, incoming)
     shared, _ = lax.optimization_barrier((shared, squares))
-    gated_next, squares_next = final(1 - mine, *operands, shared)
-    squares = summed_over(jnp.concatenate([squares, squares_next]), "head")
+    gated_next, squares_next = final(1 - mine, *operands, *lifts_next, shared)
+    squares = sum(from_all(jnp.concatenate([squares, squares_next]), "head"))
     return normed(
         mine, [gated, gated_next], squares, norm_gain[None, :],
         channels * lax.axis_size("head"),

time: 51.1 us -> 49 us (0.959)
  waiting for transfers between devices: 8.65 us -> 5.4 us
  starting transfers between devices: 19.7 us -> 20.9 us
    ppermute x6 -> x9, starting transfers between devices: 10.1 us -> 15.5 us  [from_all(): lax.ppermute(shard, axis, [(i, i ^ by if paired else (i + by) % devices)...]
    ppermute x2 -> x0, starting transfers between devices: 4.18 us -> none  [summed_over(): lax.ppermute(value, axis, [(i, i ^ by) for i in range(devices)])]
    ppermute x2 -> x0, waiting for transfers between devices: 4.08 us -> none  [summed_over(): lax.ppermute(value, axis, [(i, i ^ by) for i in range(devices)])]
    ppermute x6 -> x9, waiting for transfers between devices: 4.55 us -> 2.83 us  [from_all(): lax.ppermute(shard, axis, [(i, i ^ by if paired else (i + by) % devices)...]
    ppermute x1, waiting for transfers between devices: 0.01 us -> 1.48 us  [body(): lax.ppermute(jnp.where(even, far_ends[1], far_ends[0]), 'ctx', swap)]
    ppermute x2, waiting for transfers between devices: 0.01 us -> 1.08 us  [across(): lax.ppermute(sent, 'ctx', [(hop, hop + 2), (hop + 1, hop + 3)])]
    pallas_call x1 -> x2, Pallas kernels: 5.01 us -> 4.99 us  [gates(): pl.pallas_call(gate_kernel, in_specs=[pl.BlockSpec(memory_space=pltpu.SME...]
  transfers between devices with their start and end apart: 13 -> 14, of which waited for: 4 -> 4; matrix products, arithmetic and copies ran while one was open for 2% -> 2% of each run, Pallas kernels for 29% -> 30%
where the time goes in v10:
time: 49 us; the launch traced here: 48.9 us
  starting transfers between devices  20.9 us (43%)
  Pallas kernels  19.9 us (41%)
  waiting for transfers between devices  5.4 us (11%)
  other arithmetic  1.12 us (2%)
  local copies, waits for them, and re-layouts  1.06 us (2%)
  between operations  0.49 us (1%)
    ppermute x9, starting transfers between devices, from_all(): lax.ppermute(shard, axis, [(i, i ^ by if paired else (i + by) % devices)...  15.5 us
    ppermute x2, starting transfers between devices, across(): lax.ppermute(sent, 'ctx', [(hop, hop + 2), (hop + 1, hop + 3)])  5.15 us
    pallas_call x2, Pallas kernels, gates(): pl.pallas_call(gate_kernel, in_specs=[pl.BlockSpec(memory_space=pltpu.SME...  4.99 us
    pallas_call x1, Pallas kernels, front(): pl.pallas_call(front_kernel, in_specs=[ANYWHERE] * 6, out_specs=[WHOLE] *...  4.55 us
    pallas_call x2, Pallas kernels, final(): pl.pallas_call(final_kernel, in_specs=[pl.BlockSpec(memory_space=pltpu.SM...  4.47 us
    pallas_call x1, Pallas kernels, normed(): pl.pallas_call(functools.partial(norm_kernel, all_channels), in_specs=[pl...  3.1 us
    ppermute x9, waiting for transfers between devices, from_all(): lax.ppermute(shard, axis, [(i, i ^ by if paired else (i + by) % devices)...  2.83 us
    pallas_call x2, Pallas kernels, own_states(): pl.pallas_call(state_kernel, in_specs=[WHOLE] * 3, out_specs=[WHOLE] * 2,...  2.48 us
  transfers between devices with their start and end apart: 14, of which 4 were waited for; matrix products, arithmetic and copies ran while one was open for 2% of the time, Pallas kernels for 30%

profile of v10, /device:TPU:0, one launch (start us, length us, event | category | flops | bytes accessed | tf_op | source)
XLA Modules:
  0.0 48.9 jit_solution(8671582595542004843)
XLA Ops:
  0.0 1.0 %slice_bitcast_fusion = (bf16[2,32,768]{2,1,0:T(8,128)(2,1)S(1)}, bf16[2,32,768]{2,1,0:T(8,128)(2,1)S(1)}) fusion(bf16[2,2,32,768]{3,2,1,0:T(8,128)(2,1)} %param.11), kind=kLoop, calls=%fused_computation.21 | loop fusion | bytes 393216 | tf_op jit(solution)/shard_map/squeeze | solution.py:365
  1.0 3.1 %collective-permute-start = (bf16[2,32,768]{2,1,0:T(8,128)(2,1)S(1)}, bf16[2,32,768]{2,1,0:T(8,128)(2,1)S(1)}, u32[]{:S(2)}, u32[]{:S(2)}) collective-permute-start(bf16[2,32,768]{2,1,0:T(8,128)(2,1)S(1)} %get-tuple-element.43), channel_id=1, source_target_pairs={{0,1},{1,0},{2,3},{3,2},{4,5},{5,4},{6,7},{7,6},{8,9},{9,8},{10,11... | collective-permute-start | bytes 294920 | tf_op jit(solution)/shard_map/ppermute | solution.py:345
  4.0 2.6 %collective-permute-start.1 = (bf16[2,32,768]{2,1,0:T(8,128)(2,1)S(1)}, bf16[2,32,768]{2,1,0:T(8,128)(2,1)S(1)}, u32[]{:S(2)}, u32[]{:S(2)}) collective-permute-start(bf16[2,32,768]{2,1,0:T(8,128)(2,1)S(1)} %get-tuple-element.43), channel_id=1, source_target_pairs={{0,2},{1,3},{2,0},{3,1},{4,6},{5,7},{6,4},{7,5},{8,10},{9,11},{10,... | collective-permute-start | bytes 294920 | tf_op jit(solution)/shard_map/ppermute | solution.py:345
  6.6 4.5 %front.1 = (bf16[2,768,2048]{2,1,0:T(8,128)(2,1)S(1)}, bf16[2,768,2048]{2,1,0:T(8,128)(2,1)S(1)}, bf16[2,768,128]{2,1,0:T(8,128)(2,1)S(1)}, f32[2,32,2048]{2,1,0:T(8,128)S(1)}, bf16[192,2048]{1,0:T(8,128)(2,1)S(1)}) custom-call(bf16[2,768,2048]{2,1,0:T(8,128)(2,1)} %x_hbm.1, f32[2,32,768]{2,1,0:T(8,128)} %step_hbm.1, f32[2,32,768]{2,1,0:T(8,128)} %decay_hbm.1, ...), custom_call_target="tpu_custom_call" | custom-call | flops 1000 | bytes 1000 | tf_op jit(solution)/shard_map/front/pallas_call | solution.py:127
  11.3 0.1 pad.19.clone
  11.4 1.2 %own_states.2 = (bf16[2,5,64,2048]{3,2,1,0:T(8,128)(2,1)S(1)}, bf16[2,64,2048]{2,1,0:T(8,128)(2,1)S(1)}) custom-call(bf16[2,64,768]{2,1,0:T(8,128)(2,1)S(1)} %pad_maximum_fusion.3.b_ref, bf16[2,768,2048]{2,1,0:T(8,128)(2,1)S(1)} %get-tuple-element.42.weighted_ref, f32[2,32,2048]{2,1,0:T(8,128)S(1)} %get-tuple-element.44.rows_ref), custom_call_target="tpu_custom_call" | custom-call | flops 1000 | bytes 1000 | tf_op jit(solution)/shard_map/own_states/pallas_call | solution.py:174
  12.7 0.1 maximum_maximum_fusion
  12.8 0.1 collective-permute-start.3
  12.9 1.0 %collective-permute-start.7 = (bf16[2,32,768]{2,1,0:T(8,128)(2,1)S(1)}, bf16[2,32,768]{2,1,0:T(8,128)(2,1)S(1)}, u32[]{:S(2)}, u32[]{:S(2)}) collective-permute-start(bf16[2,32,768]{2,1,0:T(8,128)(2,1)S(1)} %get-tuple-element.59), channel_id=1, source_target_pairs={{0,1},{1,0},{2,3},{3,2},{4,5},{5,4},{6,7},{7,6},{8,9},{9,8},{10,11... | collective-permute-start | bytes 294920 | tf_op jit(solution)/shard_map/ppermute | solution.py:345
  13.9 3.5 %collective-permute-start.8 = (bf16[2,32,768]{2,1,0:T(8,128)(2,1)S(1)}, bf16[2,32,768]{2,1,0:T(8,128)(2,1)S(1)}, u32[]{:S(2)}, u32[]{:S(2)}) collective-permute-start(bf16[2,32,768]{2,1,0:T(8,128)(2,1)S(1)} %get-tuple-element.59), channel_id=1, source_target_pairs={{0,2},{1,3},{2,0},{3,1},{4,6},{5,7},{6,4},{7,5},{8,10},{9,11},{10,... | collective-permute-start | bytes 294920 | tf_op jit(solution)/shard_map/ppermute | solution.py:345
  17.3 1.0 %collective-permute-start.9 = (bf16[2,32,768]{2,1,0:T(8,128)(2,1)S(1)}, bf16[2,32,768]{2,1,0:T(8,128)(2,1)S(1)}, u32[]{:S(2)}, u32[]{:S(2)}) collective-permute-start(bf16[2,32,768]{2,1,0:T(8,128)(2,1)S(1)} %get-tuple-element.59), channel_id=1, source_target_pairs={{0,3},{1,2},{2,1},{3,0},{4,7},{5,6},{6,5},{7,4},{8,11},{9,10},{10,... | collective-permute-start | bytes 294920 | tf_op jit(solution)/shard_map/ppermute | solution.py:345
  18.3 0.2 select_convert_fusion.1
  18.6 3.7 %collective-permute-start.4 = (bf16[64,2048]{1,0:T(8,128)(2,1)S(1)}, bf16[64,2048]{1,0:T(8,128)(2,1)S(1)}, u32[]{:S(2)}, u32[]{:S(2)}) collective-permute-start(bf16[64,2048]{1,0:T(8,128)(2,1)S(1)} %select_convert_fusion.1), channel_id=1, source_target_pairs={{0,8},{4,12},{1,9},{5,13},{2,10},{6,14},{3,11},{7,15},{16,24},{20,... | collective-permute-start | bytes 786440 | tf_op jit(solution)/shard_map/ppermute | solution.py:386
  22.2 1.3 %own_states.3 = (bf16[2,5,64,2048]{3,2,1,0:T(8,128)(2,1)S(1)}, bf16[2,64,2048]{2,1,0:T(8,128)(2,1)S(1)}) custom-call(bf16[2,64,768]{2,1,0:T(8,128)(2,1)S(1)} %pad_maximum_fusion.4.b_ref, bf16[2,768,2048]{2,1,0:T(8,128)(2,1)S(1)} %get-tuple-element.42.weighted_ref, f32[2,32,2048]{2,1,0:T(8,128)S(1)} %get-tuple-element.44.rows_ref), custom_call_target="tpu_custom_call" | custom-call | flops 1000 | bytes 1000 | tf_op jit(solution)/shard_map/own_states/pallas_call | solution.py:174
  23.5 0.1 bitcast_convert_fusion
  23.6 0.1 collective-permute-start.5
  23.7 1.5 %collective-permute-done.5 = bf16[64,2048]{1,0:T(8,128)(2,1)S(1)} collective-permute-done((bf16[64,2048]{1,0:T(8,128)(2,1)S(1)}, bf16[64,2048]{1,0:T(8,128)(2,1)S(1)}, u32[]{:S(2)}, u32[]{:S(2)}) %collective-permute-start.5) | collective-permute-done | bytes 262176 | tf_op jit(solution)/shard_map/ppermute | solution.py:409
  25.2 0.2 select_convert_fusion
  25.3 1.5 %collective-permute-start.6 = (bf16[64,2048]{1,0:T(8,128)(2,1)S(1)}, bf16[64,2048]{1,0:T(8,128)(2,1)S(1)}, u32[]{:S(2)}, u32[]{:S(2)}) collective-permute-start(bf16[64,2048]{1,0:T(8,128)(2,1)S(1)} %select_convert_fusion), channel_id=1, source_target_pairs={{0,8},{4,12},{1,9},{5,13},{2,10},{6,14},{3,11},{7,15},{16,24},{20,... | collective-permute-start | bytes 786440 | tf_op jit(solution)/shard_map/ppermute | solution.py:386
  26.9 2.5 %gates.2 = (bf16[768,2048]{1,0:T(8,128)(2,1)S(1)}, bf16[768,2048]{1,0:T(8,128)(2,1)S(1)}) custom-call(s32[1]{0:T(128)} %bitcast.seq_ref, bf16[2,768,2048]{2,1,0:T(8,128)(2,1)S(1)} %bitcast.30, bf16[2,768,2048]{2,1,0:T(8,128)(2,1)S(1)} %get-tuple-element.63.x_ref, bf16[2,768,128]{2,1,0:T(8,128)(2,1)S(1)} %get-tuple-element.53.both_ref, ...), custom_call_target="tpu_custom_call" | custom-call | flops 1000000000 | bytes 12000000 | tf_op jit(solution)/shard_map/gates/pallas_call | solution.py:207
  29.5 0.3 left.1.left_ref
  29.8 2.5 %gates.3 = (bf16[768,2048]{1,0:T(8,128)(2,1)S(1)}, bf16[768,2048]{1,0:T(8,128)(2,1)S(1)}) custom-call(s32[1]{0:T(128)S(6)} %sub.16.seq_ref, bf16[2,768,2048]{2,1,0:T(8,128)(2,1)S(1)} %bitcast.30, bf16[2,768,2048]{2,1,0:T(8,128)(2,1)S(1)} %get-tuple-element.63.x_ref, bf16[2,768,128]{2,1,0:T(8,128)(2,1)S(1)} %get-tuple-element.53.both_ref, ...), custom_call_target="tpu_custom_call" | custom-call | flops 1000000000 | bytes 12000000 | tf_op jit(solution)/shard_map/gates/pallas_call | solution.py:207
  32.3 1.1 %collective-permute-done.6 = bf16[64,2048]{1,0:T(8,128)(2,1)S(1)} collective-permute-done((bf16[64,2048]{1,0:T(8,128)(2,1)S(1)}, bf16[64,2048]{1,0:T(8,128)(2,1)S(1)}, u32[]{:S(2)}, u32[]{:S(2)}) %collective-permute-start.6) | collective-permute-done | bytes 262176 | tf_op jit(solution)/shard_map/ppermute | solution.py:386
  33.4 0.3 fusion.3
  33.7 0.1 collective-permute-start.10
  33.8 2.2 %final.2 = (bf16[768,2048]{1,0:T(8,128)(2,1)S(1)}, f32[8,128]{1,0:T(8,128)S(1)}) custom-call(s32[1]{0:T(128)} %bitcast.seq_ref, bf16[2,768,2048]{2,1,0:T(8,128)(2,1)S(1)} %get-tuple-element.42.weighted_ref, bf16[2,5,64,2048]{3,2,1,0:T(8,128)(2,1)S(1)} %get-tuple-element.45.near_ref, bf16[2,5,64,2048]{3,2,1,0:T(8,128)(2,1)S(1)} %get-tuple-element.49.far_ref, ...), custom_call_target="tpu_custom_call" | custom-call | flops 1000 | bytes 1000 | tf_op jit(solution)/shard_map/final/pallas_call | solution.py:277
  36.1 2.2 %final.3 = (bf16[768,2048]{1,0:T(8,128)(2,1)S(1)}, f32[8,128]{1,0:T(8,128)S(1)}) custom-call(s32[1]{0:T(128)S(6)} %sub.16.seq_ref, bf16[2,768,2048]{2,1,0:T(8,128)(2,1)S(1)} %get-tuple-element.42.weighted_ref, bf16[2,5,64,2048]{3,2,1,0:T(8,128)(2,1)S(1)} %get-tuple-element.45.near_ref, bf16[2,5,64,2048]{3,2,1,0:T(8,128)(2,1)S(1)} %get-tuple-element.49.far_ref, ...), custom_call_target="tpu_custom_call" | custom-call | flops 1000 | bytes 1000 | tf_op jit(solution)/shard_map/final/pallas_call | solution.py:277
  38.3 2.7 %collective-permute-start.13 = (f32[16,128]{1,0:T(8,128)S(1)}, f32[16,128]{1,0:T(8,128)S(1)}, u32[]{:S(2)}, u32[]{:S(2)}) collective-permute-start(f32[16,128]{1,0:T(8,128)S(1)} %constant_dynamic-update-slice_fusion), channel_id=1, source_target_pairs={{0,3},{1,2},{2,1},{3,0},{4,7},{5,6},{6,5},{7,4},{8,11},{9,10},{10,... | collective-permute-start | bytes 24584 | tf_op jit(solution)/shard_map/ppermute | solution.py:345
  41.0 1.7 %collective-permute-start.11 = (f32[16,128]{1,0:T(8,128)S(1)}, f32[16,128]{1,0:T(8,128)S(1)}, u32[]{:S(2)}, u32[]{:S(2)}) collective-permute-start(f32[16,128]{1,0:T(8,128)S(1)} %constant_dynamic-update-slice_fusion), channel_id=1, source_target_pairs={{0,1},{1,0},{2,3},{3,2},{4,5},{5,4},{6,7},{7,6},{8,9},{9,8},{10,11... | collective-permute-start | bytes 24584 | tf_op jit(solution)/shard_map/ppermute | solution.py:345
  42.8 1.1 %collective-permute-done.13 = f32[16,128]{1,0:T(8,128)S(1)} collective-permute-done((f32[16,128]{1,0:T(8,128)S(1)}, f32[16,128]{1,0:T(8,128)S(1)}, u32[]{:S(2)}, u32[]{:S(2)}) %collective-permute-start.13) | collective-permute-done | bytes 8224 | tf_op jit(solution)/shard_map/ppermute | solution.py:345
  43.8 1.8 %collective-permute-done.12 = f32[16,128]{1,0:T(8,128)S(1)} collective-permute-done((f32[16,128]{1,0:T(8,128)S(1)}, f32[16,128]{1,0:T(8,128)S(1)}, u32[]{:S(2)}, u32[]{:S(2)}) %collective-permute-start.12) | collective-permute-done | bytes 8224 | tf_op jit(solution)/shard_map/ppermute | solution.py:345
  45.6 3.1 %normed.1 = bf16[2,768,2048]{2,1,0:T(8,128)(2,1)} custom-call(s32[1]{0:T(128)} %bitcast.seq_ref, f32[16,128]{1,0:T(8,128)S(1)} %add_add_fusion.square_ref, f32[1,2048]{1,0:T(1,128)S(1)} %bitcast.31, bf16[768,2048]{1,0:T(8,128)(2,1)S(1)} %get-tuple-element.77.refs_0_, bf16[768,2048]{1,0:T(8,128)(2,1)S(1)} %get-tuple-element.78.refs_1_), custom_call_target="tpu_custom_call" | custom-call | flops 1000 | bytes 1000 | tf_op jit(solution)/shard_map/normed/pallas_call | solution.py:326
  (33 shorter events, 0.4 us)
Async XLA Ops:
  1.0 10.4 %collective-permute-start = (bf16[2,32,768]{2,1,0:T(8,128)(2,1)S(1)}, bf16[2,32,768]{2,1,0:T(8,128)(2,1)S(1)}, u32[]{:S(2)}, u32[]{:S(2)}) collective-permute-start(bf16[2,32,768]{2,1,0:T(8,128)(2,1)S(1)} %get-tuple-element.43), channel_id=1, source_target_pairs={{0,1},{1,0},{2,3},{3,2},{4,5},{5,4},{6,7},{7,6},{8,9},{9,8},{10,11... | collective-permute-start | bytes 294920 | tf_op jit(solution)/shard_map/ppermute | solution.py:345
  4.0 14.5 %collective-permute-start.1 = (bf16[2,32,768]{2,1,0:T(8,128)(2,1)S(1)}, bf16[2,32,768]{2,1,0:T(8,128)(2,1)S(1)}, u32[]{:S(2)}, u32[]{:S(2)}) collective-permute-start(bf16[2,32,768]{2,1,0:T(8,128)(2,1)S(1)} %get-tuple-element.43), channel_id=1, source_target_pairs={{0,2},{1,3},{2,0},{3,1},{4,6},{5,7},{6,4},{7,5},{8,10},{9,11},{10,... | collective-permute-start | bytes 294920 | tf_op jit(solution)/shard_map/ppermute | solution.py:345
  6.6 11.9 %collective-permute-start.2 = (bf16[2,32,768]{2,1,0:T(8,128)(2,1)S(1)}, bf16[2,32,768]{2,1,0:T(8,128)(2,1)S(1)}, u32[]{:S(2)}, u32[]{:S(2)}) collective-permute-start(bf16[2,32,768]{2,1,0:T(8,128)(2,1)S(1)} %get-tuple-element.43), channel_id=1, source_target_pairs={{0,3},{1,2},{2,1},{3,0},{4,7},{5,6},{6,5},{7,4},{8,11},{9,10},{10,... | collective-permute-start | bytes 294920 | tf_op jit(solution)/shard_map/ppermute | solution.py:345
  12.8 4.6 %collective-permute-start.3 = (bf16[80,2048]{1,0:T(8,128)(2,1)S(1)}, bf16[80,2048]{1,0:T(8,128)(2,1)S(1)}, u32[]{:S(2)}, u32[]{:S(2)}) collective-permute-start(bf16[80,2048]{1,0:T(8,128)(2,1)S(1)} %maximum_maximum_fusion), channel_id=1, source_target_pairs={{0,4},{4,0},{8,12},{12,8},{1,5},{5,1},{9,13},{13,9},{2,6},{6,2},{1... | collective-permute-start | bytes 983048 | tf_op jit(solution)/shard_map/ppermute | solution.py:391
  12.9 16.5 %collective-permute-start.7 = (bf16[2,32,768]{2,1,0:T(8,128)(2,1)S(1)}, bf16[2,32,768]{2,1,0:T(8,128)(2,1)S(1)}, u32[]{:S(2)}, u32[]{:S(2)}) collective-permute-start(bf16[2,32,768]{2,1,0:T(8,128)(2,1)S(1)} %get-tuple-element.59), channel_id=1, source_target_pairs={{0,1},{1,0},{2,3},{3,2},{4,5},{5,4},{6,7},{7,6},{8,9},{9,8},{10,11... | collective-permute-start | bytes 294920 | tf_op jit(solution)/shard_map/ppermute | solution.py:345
  13.9 15.5 %collective-permute-start.8 = (bf16[2,32,768]{2,1,0:T(8,128)(2,1)S(1)}, bf16[2,32,768]{2,1,0:T(8,128)(2,1)S(1)}, u32[]{:S(2)}, u32[]{:S(2)}) collective-permute-start(bf16[2,32,768]{2,1,0:T(8,128)(2,1)S(1)} %get-tuple-element.59), channel_id=1, source_target_pairs={{0,2},{1,3},{2,0},{3,1},{4,6},{5,7},{6,4},{7,5},{8,10},{9,11},{10,... | collective-permute-start | bytes 294920 | tf_op jit(solution)/shard_map/ppermute | solution.py:345
  17.3 12.0 %collective-permute-start.9 = (bf16[2,32,768]{2,1,0:T(8,128)(2,1)S(1)}, bf16[2,32,768]{2,1,0:T(8,128)(2,1)S(1)}, u32[]{:S(2)}, u32[]{:S(2)}) collective-permute-start(bf16[2,32,768]{2,1,0:T(8,128)(2,1)S(1)} %get-tuple-element.59), channel_id=1, source_target_pairs={{0,3},{1,2},{2,1},{3,0},{4,7},{5,6},{6,5},{7,4},{8,11},{9,10},{10,... | collective-permute-start | bytes 294920 | tf_op jit(solution)/shard_map/ppermute | solution.py:345
  18.3 8.5 %slice-start = ((s8[6291456]{0:T(1024)(128)(4,1)}), s8[4194304]{0:T(1024)(128)(4,1)S(1)}, s32[]{:S(2)}) async-start(s8[6291456]{0:T(1024)(128)(4,1)} %bitcast.29), calls=%async_computation | async-start | bytes 8388608
  18.5 8.3 %slice-start.1 = ((s8[6291456]{0:T(1024)(128)(4,1)}), s8[2097152]{0:T(1024)(128)(4,1)S(1)}, s32[]{:S(2)}) async-start(s8[6291456]{0:T(1024)(128)(4,1)} %bitcast.29), calls=%async_computation.1 | async-start | bytes 4194304
  18.6 13.8 %collective-permute-start.4 = (bf16[64,2048]{1,0:T(8,128)(2,1)S(1)}, bf16[64,2048]{1,0:T(8,128)(2,1)S(1)}, u32[]{:S(2)}, u32[]{:S(2)}) collective-permute-start(bf16[64,2048]{1,0:T(8,128)(2,1)S(1)} %select_convert_fusion.1), channel_id=1, source_target_pairs={{0,8},{4,12},{1,9},{5,13},{2,10},{6,14},{3,11},{7,15},{16,24},{20,... | collective-permute-start | bytes 786440 | tf_op jit(solution)/shard_map/ppermute | solution.py:386
  23.6 1.6 %collective-permute-start.5 = (bf16[64,2048]{1,0:T(8,128)(2,1)S(1)}, bf16[64,2048]{1,0:T(8,128)(2,1)S(1)}, u32[]{:S(2)}, u32[]{:S(2)}) collective-permute-start(bf16[64,2048]{1,0:T(8,128)(2,1)S(1)} %get-tuple-element.84), channel_id=1, source_target_pairs={{0,4},{4,0},{8,12},{12,8},{1,5},{5,1},{9,13},{13,9},{2,6},{6,2},{1... | collective-permute-start | bytes 786440 | tf_op jit(solution)/shard_map/ppermute | solution.py:409
  25.3 8.1 %collective-permute-start.6 = (bf16[64,2048]{1,0:T(8,128)(2,1)S(1)}, bf16[64,2048]{1,0:T(8,128)(2,1)S(1)}, u32[]{:S(2)}, u32[]{:S(2)}) collective-permute-start(bf16[64,2048]{1,0:T(8,128)(2,1)S(1)} %select_convert_fusion), channel_id=1, source_target_pairs={{0,8},{4,12},{1,9},{5,13},{2,10},{6,14},{3,11},{7,15},{16,24},{20,... | collective-permute-start | bytes 786440 | tf_op jit(solution)/shard_map/ppermute | solution.py:386
  33.7 2.3 %collective-permute-start.10 = (bf16[128,2048]{1,0:T(8,128)(2,1)S(1)}, bf16[128,2048]{1,0:T(8,128)(2,1)S(1)}, u32[]{:S(2)}, u32[]{:S(2)}) collective-permute-start(bf16[128,2048]{1,0:T(8,128)(2,1)S(1)} %get-tuple-element.79), channel_id=1, source_target_pairs={{0,4},{4,0},{8,12},{12,8},{1,5},{5,1},{9,13},{13,9},{2,6},{6,2},{1... | collective-permute-start | bytes 1572872 | tf_op jit(solution)/shard_map/ppermute | solution.py:429
  36.0 9.6 %copy-start = (f32[2048]{0:T(1024)S(1)}, f32[2048]{0:T(1024)}, u32[]{:S(2)}) copy-start(f32[2048]{0:T(1024)} %param.15) | copy-start | bytes 24580
  38.3 5.5 %collective-permute-start.13 = (f32[16,128]{1,0:T(8,128)S(1)}, f32[16,128]{1,0:T(8,128)S(1)}, u32[]{:S(2)}, u32[]{:S(2)}) collective-permute-start(f32[16,128]{1,0:T(8,128)S(1)} %constant_dynamic-update-slice_fusion), channel_id=1, source_target_pairs={{0,3},{1,2},{2,1},{3,0},{4,7},{5,6},{6,5},{7,4},{8,11},{9,10},{10,... | collective-permute-start | bytes 24584 | tf_op jit(solution)/shard_map/ppermute | solution.py:345
  41.0 4.5 %collective-permute-start.12 = (f32[16,128]{1,0:T(8,128)S(1)}, f32[16,128]{1,0:T(8,128)S(1)}, u32[]{:S(2)}, u32[]{:S(2)}) collective-permute-start(f32[16,128]{1,0:T(8,128)S(1)} %constant_dynamic-update-slice_fusion), channel_id=1, source_target_pairs={{0,2},{1,3},{2,0},{3,1},{4,6},{5,7},{6,4},{7,5},{8,10},{9,11},{10,... | collective-permute-start | bytes 24584 | tf_op jit(solution)/shard_map/ppermute | solution.py:345
  41.0 4.5 %collective-permute-start.11 = (f32[16,128]{1,0:T(8,128)S(1)}, f32[16,128]{1,0:T(8,128)S(1)}, u32[]{:S(2)}, u32[]{:S(2)}) collective-permute-start(f32[16,128]{1,0:T(8,128)S(1)} %constant_dynamic-update-slice_fusion), channel_id=1, source_target_pairs={{0,1},{1,0},{2,3},{3,2},{4,5},{5,4},{6,7},{7,6},{8,9},{9,8},{10,11... | collective-permute-start | bytes 24584 | tf_op jit(solution)/shard_map/ppermute | solution.py:345

commit v11 on v10

--- a/solution.py
+++ b/solution.py
@@ -338,15 +338,16 @@
     )(first, squares, gain_row, *[in_vmem(one) for one in gated])
 
 
-def from_all(shard, axis):
+def from_partner(shard, axis, by):
     devices = lax.axis_size(axis)
     paired = devices & (devices - 1) == 0
-    return [shard] + [
-        lax.ppermute(
-            shard, axis, [(i, i ^ by if paired else (i + by) % devices) for i in range(devices)]
-        )
-        for by in range(1, devices)
-    ]
+    return lax.ppermute(
+        shard, axis, [(i, i ^ by if paired else (i + by) % devices) for i in range(devices)]
+    )
+
+
+def from_all(shard, axis):
+    return [shard] + [from_partner(shard, axis, by) for by in range(1, lax.axis_size(axis))]
 
 
 def as_parts(row):
@@ -363,10 +364,13 @@
     until = np.tril(np.ones((SPAN, SPAN)))
     sums = jnp.asarray(np.concatenate([np.tile(until, 2), np.tile(np.eye(SPAN), 2)]), BF16)
     b_own, c_own = lax.optimization_barrier((state_proj[0], state_proj[1]))
-    b_pieces = from_all(b_own, "head")
+    b_next = from_partner(b_own, "head", 1)
     x, weighted, both, rows, bands = front(
         features, step_size, log_decay, skip_gain[None, :], sums, bands
     )
+
+    b_own, rows = lax.optimization_barrier((b_own, rows))
+    b_far = [from_partner(b_own, "head", by) for by in range(2, lax.axis_size("head"))]
 
     place = lax.axis_index("ctx")
     even = place % 2 == 0
@@ -385,7 +389,7 @@
         sent = sent.astype(BF16)
         return sent, lax.ppermute(sent, "ctx", [(hop, hop + 2), (hop + 1, hop + 3)])
 
-    b_near = jnp.concatenate(b_pieces[:2], axis=1)
+    b_near = jnp.concatenate([b_own, b_next], axis=1)
     near, near_ends = own_states(b_near, weighted, rows)
     near_rows = b_near.shape[1]
     other = lax.ppermute(
@@ -403,14 +407,14 @@
     near_end = jnp.where(even, near_ends[0], near_ends[1]).astype(F32)
     near_past = past_chip(near_end, near_other, decay_other)
     near_sent, near_got = across(near_past, None, 0)
-    b_far, _ = lax.optimization_barrier((b_pieces[2:], near_sent))
+    b_far, _ = lax.optimization_barrier((b_far, near_sent))
     b_far = jnp.concatenate(b_far, axis=1)
     far, far_ends = own_states(b_far, weighted, rows)
     far_other = lax.ppermute(jnp.where(even, far_ends[1], far_ends[0]), "ctx", swap).astype(F32)
     far_end = jnp.where(even, far_ends[0], far_ends[1]).astype(F32)
     far_past = past_chip(far_end, far_other, decay_other)
     far_sent, far_got = across(far_past, None, 0)
-    c_own, _ = lax.optimization_barrier((c_own, near_ends))
+    c_own, _ = lax.optimization_barrier((c_own, near_sent))
     c = from_all(c_own, "head")
     x, _ = lax.optimization_barrier((x, far_sent))
     lifts = gates(mine, gate_in, x, both, bands, rows)

time: 49 us -> 61.5 us (1.26)
  local copies, waits for them, and re-layouts: 1.06 us -> 12.6 us
  waiting for transfers between devices: 5.4 us -> 6.88 us
  starting transfers between devices: 20.9 us -> 20.2 us
    unnamed x7 -> x25, local copies, waits for them, and re-layouts: 0.03 us -> 11.5 us
    ppermute x1, waiting for transfers between devices: 0.01 us -> 1.59 us  [body(): lax.ppermute(jnp.concatenate([jnp.where(even, near_ends[1], near_ends[0])...]
    ppermute x2, waiting for transfers between devices: 1.08 us -> 0.01 us  [across(): lax.ppermute(sent, 'ctx', [(hop, hop + 2), (hop + 1, hop + 3)])]
    ppermute x9, waiting for transfers between devices: 2.83 us -> 3.8 us  [from_partner(): lax.ppermute(shard, axis, [(i, i ^ by if paired else (i + by) % devices)...]
    ppermute x9, starting transfers between devices: 15.5 us -> 14.7 us  [from_partner(): lax.ppermute(shard, axis, [(i, i ^ by if paired else (i + by) % devices)...]
  transfers between devices with their start and end apart: 14 -> 14, of which waited for: 4 -> 5; matrix products, arithmetic and copies ran while one was open for 2% -> 1% of each run, Pallas kernels for 30% -> 24%
where the time goes in v11:
time: 61.5 us; the launch traced here: 61.3 us
  starting transfers between devices  20.2 us (33%)
  Pallas kernels  20 us (33%)
  local copies, waits for them, and re-layouts  12.6 us (20%)
  waiting for transfers between devices  6.88 us (11%)
  other arithmetic  1.12 us (2%)
    ppermute x9, starting transfers between devices, from_partner(): lax.ppermute(shard, axis, [(i, i ^ by if paired else (i + by) % devices)...  14.7 us
    unnamed x25, local copies, waits for them, and re-layouts  11.5 us
    ppermute x2, starting transfers between devices, across(): lax.ppermute(sent, 'ctx', [(hop, hop + 2), (hop + 1, hop + 3)])  5.38 us
    pallas_call x2, Pallas kernels, gates(): pl.pallas_call(gate_kernel, in_specs=[pl.BlockSpec(memory_space=pltpu.SME...  4.99 us
    pallas_call x2, Pallas kernels, final(): pl.pallas_call(final_kernel, in_specs=[pl.BlockSpec(memory_space=pltpu.SM...  4.58 us
    pallas_call x1, Pallas kernels, front(): pl.pallas_call(front_kernel, in_specs=[ANYWHERE] * 6, out_specs=[WHOLE] *...  4.45 us
    ppermute x9, waiting for transfers between devices, from_partner(): lax.ppermute(shard, axis, [(i, i ^ by if paired else (i + by) % devices)...  3.8 us
    pallas_call x1, Pallas kernels, normed(): pl.pallas_call(functools.partial(norm_kernel, all_channels), in_specs=[pl...  3.1 us
  transfers between devices with their start and end apart: 14, of which 5 were waited for; matrix products, arithmetic and copies ran while one was open for 1% of the time, Pallas kernels for 24%

profile of v11, /device:TPU:0, one launch (start us, length us, event | category | flops | bytes accessed | tf_op | source)
XLA Modules:
  0.0 61.3 jit_solution(340877126470361999)
XLA Ops:
  0.0 1.0 %slice_bitcast_fusion = (bf16[2,32,768]{2,1,0:T(8,128)(2,1)S(1)}, bf16[2,32,768]{2,1,0:T(8,128)(2,1)S(1)}) fusion(bf16[2,2,32,768]{3,2,1,0:T(8,128)(2,1)} %param.11), kind=kLoop, calls=%fused_computation.21 | loop fusion | bytes 393216 | tf_op jit(solution)/shard_map/squeeze | solution.py:366
  1.0 3.1 %collective-permute-start = (bf16[2,32,768]{2,1,0:T(8,128)(2,1)S(1)}, bf16[2,32,768]{2,1,0:T(8,128)(2,1)S(1)}, u32[]{:S(2)}, u32[]{:S(2)}) collective-permute-start(bf16[2,32,768]{2,1,0:T(8,128)(2,1)S(1)} %get-tuple-element.47), channel_id=1, source_target_pairs={{0,1},{1,0},{2,3},{3,2},{4,5},{5,4},{6,7},{7,6},{8,9},{9,8},{10,11... | collective-permute-start | bytes 294920 | tf_op jit(solution)/shard_map/ppermute | solution.py:344
  4.0 4.5 %front.1 = (bf16[2,768,2048]{2,1,0:T(8,128)(2,1)S(1)}, bf16[2,768,2048]{2,1,0:T(8,128)(2,1)S(1)}, bf16[2,768,128]{2,1,0:T(8,128)(2,1)S(1)}, f32[2,32,2048]{2,1,0:T(8,128)S(1)}, bf16[192,2048]{1,0:T(8,128)(2,1)S(1)}) custom-call(bf16[2,768,2048]{2,1,0:T(8,128)(2,1)} %x_hbm.1, f32[2,32,768]{2,1,0:T(8,128)} %step_hbm.1, f32[2,32,768]{2,1,0:T(8,128)} %decay_hbm.1, ...), custom_call_target="tpu_custom_call" | custom-call | flops 1000 | bytes 1000 | tf_op jit(solution)/shard_map/front/pallas_call | solution.py:127
  8.5 2.7 %copy-done = bf16[2,768,2048]{2,1,0:T(8,128)(2,1)} copy-done((bf16[2,768,2048]{2,1,0:T(8,128)(2,1)}, bf16[2,768,2048]{2,1,0:T(8,128)(2,1)S(1)}, u32[]{:S(2)}) %copy-start) | copy-done | bytes 6291480
  11.2 2.6 %copy-done.3 = bf16[2,768,2048]{2,1,0:T(8,128)(2,1)} copy-done((bf16[2,768,2048]{2,1,0:T(8,128)(2,1)}, bf16[2,768,2048]{2,1,0:T(8,128)(2,1)S(1)}, u32[]{:S(2)}) %copy-start.3) | copy-done | bytes 6291480
  13.9 2.6 %collective-permute-start.1 = (bf16[2,32,768]{2,1,0:T(8,128)(2,1)S(1)}, bf16[2,32,768]{2,1,0:T(8,128)(2,1)S(1)}, u32[]{:S(2)}, u32[]{:S(2)}) collective-permute-start(bf16[2,32,768]{2,1,0:T(8,128)(2,1)S(1)} %get-tuple-element.47), channel_id=1, source_target_pairs={{0,2},{1,3},{2,0},{3,1},{4,6},{5,7},{6,4},{7,5},{8,10},{9,11},{10,... | collective-permute-start | bytes 294920 | tf_op jit(solution)/shard_map/ppermute | solution.py:344
  16.6 2.8 %copy-done.1 = bf16[2,768,2048]{2,1,0:T(8,128)(2,1)S(1)} copy-done((bf16[2,768,2048]{2,1,0:T(8,128)(2,1)S(1)}, bf16[2,768,2048]{2,1,0:T(8,128)(2,1)}, u32[]{:S(2)}) %copy-start.1) | copy-done | bytes 6291480
  19.4 1.3 %own_states.2 = (bf16[2,5,64,2048]{3,2,1,0:T(8,128)(2,1)S(1)}, bf16[2,64,2048]{2,1,0:T(8,128)(2,1)S(1)}) custom-call(bf16[2,64,768]{2,1,0:T(8,128)(2,1)S(1)} %pad_maximum_fusion.3.b_ref, bf16[2,768,2048]{2,1,0:T(8,128)(2,1)S(1)} %copy-done.1, f32[2,32,2048]{2,1,0:T(8,128)S(1)} %get-tuple-element.48.rows_ref), custom_call_target="tpu_custom_call" | custom-call | flops 1000 | bytes 1000 | tf_op jit(solution)/shard_map/own_states/pallas_call | solution.py:174
  21.0 1.6 %collective-permute-done.3 = bf16[80,2048]{1,0:T(8,128)(2,1)S(1)} collective-permute-done((bf16[80,2048]{1,0:T(8,128)(2,1)S(1)}, bf16[80,2048]{1,0:T(8,128)(2,1)S(1)}, u32[]{:S(2)}, u32[]{:S(2)}) %collective-permute-start.3) | collective-permute-done | bytes 327712 | tf_op jit(solution)/shard_map/ppermute | solution.py:395
  22.6 0.2 select_convert_fusion.1
  22.8 3.9 %collective-permute-start.4 = (bf16[64,2048]{1,0:T(8,128)(2,1)S(1)}, bf16[64,2048]{1,0:T(8,128)(2,1)S(1)}, u32[]{:S(2)}, u32[]{:S(2)}) collective-permute-start(bf16[64,2048]{1,0:T(8,128)(2,1)S(1)} %select_convert_fusion.1), channel_id=1, source_target_pairs={{0,8},{4,12},{1,9},{5,13},{2,10},{6,14},{3,11},{7,15},{16,24},{20,... | collective-permute-start | bytes 786440 | tf_op jit(solution)/shard_map/ppermute | solution.py:390
  26.7 0.7 %collective-permute-start.7 = (bf16[2,32,768]{2,1,0:T(8,128)(2,1)S(1)}, bf16[2,32,768]{2,1,0:T(8,128)(2,1)S(1)}, u32[]{:S(2)}, u32[]{:S(2)}) collective-permute-start(bf16[2,32,768]{2,1,0:T(8,128)(2,1)S(1)} %get-tuple-element.63), channel_id=1, source_target_pairs={{0,1},{1,0},{2,3},{3,2},{4,5},{5,4},{6,7},{7,6},{8,9},{9,8},{10,11... | collective-permute-start | bytes 294920 | tf_op jit(solution)/shard_map/ppermute | solution.py:344
  27.4 3.5 %collective-permute-start.8 = (bf16[2,32,768]{2,1,0:T(8,128)(2,1)S(1)}, bf16[2,32,768]{2,1,0:T(8,128)(2,1)S(1)}, u32[]{:S(2)}, u32[]{:S(2)}) collective-permute-start(bf16[2,32,768]{2,1,0:T(8,128)(2,1)S(1)} %get-tuple-element.63), channel_id=1, source_target_pairs={{0,2},{1,3},{2,0},{3,1},{4,6},{5,7},{6,4},{7,5},{8,10},{9,11},{10,... | collective-permute-start | bytes 294920 | tf_op jit(solution)/shard_map/ppermute | solution.py:344
  31.0 0.3 collective-permute-start.9
  31.3 1.3 %own_states.3 = (bf16[2,5,64,2048]{3,2,1,0:T(8,128)(2,1)S(1)}, bf16[2,64,2048]{2,1,0:T(8,128)(2,1)S(1)}) custom-call(bf16[2,64,768]{2,1,0:T(8,128)(2,1)S(1)} %pad_maximum_fusion.4.b_ref, bf16[2,768,2048]{2,1,0:T(8,128)(2,1)S(1)} %copy-done.2, f32[2,32,2048]{2,1,0:T(8,128)S(1)} %get-tuple-element.48.rows_ref), custom_call_target="tpu_custom_call" | custom-call | flops 1000 | bytes 1000 | tf_op jit(solution)/shard_map/own_states/pallas_call | solution.py:174
  32.7 1.5 %collective-permute-done.5 = bf16[64,2048]{1,0:T(8,128)(2,1)S(1)} collective-permute-done((bf16[64,2048]{1,0:T(8,128)(2,1)S(1)}, bf16[64,2048]{1,0:T(8,128)(2,1)S(1)}, u32[]{:S(2)}, u32[]{:S(2)}) %collective-permute-start.5) | collective-permute-done | bytes 262176 | tf_op jit(solution)/shard_map/ppermute | solution.py:413
  34.4 1.5 %collective-permute-start.6 = (bf16[64,2048]{1,0:T(8,128)(2,1)S(1)}, bf16[64,2048]{1,0:T(8,128)(2,1)S(1)}, u32[]{:S(2)}, u32[]{:S(2)}) collective-permute-start(bf16[64,2048]{1,0:T(8,128)(2,1)S(1)} %select_convert_fusion), channel_id=1, source_target_pairs={{0,8},{4,12},{1,9},{5,13},{2,10},{6,14},{3,11},{7,15},{16,24},{20,... | collective-permute-start | bytes 786440 | tf_op jit(solution)/shard_map/ppermute | solution.py:390
  35.9 2.5 %gates.2 = (bf16[768,2048]{1,0:T(8,128)(2,1)S(1)}, bf16[768,2048]{1,0:T(8,128)(2,1)S(1)}) custom-call(s32[1]{0:T(128)} %bitcast.seq_ref, bf16[2,768,2048]{2,1,0:T(8,128)(2,1)S(1)} %bitcast.30, bf16[2,768,2048]{2,1,0:T(8,128)(2,1)S(1)} %copy-done.4, bf16[2,768,128]{2,1,0:T(8,128)(2,1)S(1)} %get-tuple-element.57.both_ref, ...), custom_call_target="tpu_custom_call" | custom-call | flops 1000000000 | bytes 12000000 | tf_op jit(solution)/shard_map/gates/pallas_call | solution.py:207
  38.4 0.2 collective-permute-done.8
  38.7 0.3 left.1.left_ref
  39.0 2.5 %gates.3 = (bf16[768,2048]{1,0:T(8,128)(2,1)S(1)}, bf16[768,2048]{1,0:T(8,128)(2,1)S(1)}) custom-call(s32[1]{0:T(128)S(6)} %sub.16.seq_ref, bf16[2,768,2048]{2,1,0:T(8,128)(2,1)S(1)} %bitcast.30, bf16[2,768,2048]{2,1,0:T(8,128)(2,1)S(1)} %copy-done.4, bf16[2,768,128]{2,1,0:T(8,128)(2,1)S(1)} %get-tuple-element.57.both_ref, ...), custom_call_target="tpu_custom_call" | custom-call | flops 1000000000 | bytes 12000000 | tf_op jit(solution)/shard_map/gates/pallas_call | solution.py:207
  41.5 1.7 %copy-done.5 = bf16[768,2048]{1,0:T(8,128)(2,1)} copy-done((bf16[768,2048]{1,0:T(8,128)(2,1)}, bf16[768,2048]{1,0:T(8,128)(2,1)S(1)}, u32[]{:S(2)}) %copy-start.5) | copy-done | bytes 3145752
  43.2 0.3 fusion.3
  43.6 1.2 %copy-done.7 = bf16[768,2048]{1,0:T(8,128)(2,1)} copy-done((bf16[768,2048]{1,0:T(8,128)(2,1)}, bf16[768,2048]{1,0:T(8,128)(2,1)S(1)}, u32[]{:S(2)}) %copy-start.7) | copy-done | bytes 3145752
  44.8 2.2 %final.2 = (bf16[768,2048]{1,0:T(8,128)(2,1)S(1)}, f32[8,128]{1,0:T(8,128)S(1)}) custom-call(s32[1]{0:T(128)} %bitcast.seq_ref, bf16[2,768,2048]{2,1,0:T(8,128)(2,1)S(1)} %copy-done.2, bf16[2,5,64,2048]{3,2,1,0:T(8,128)(2,1)S(1)} %get-tuple-element.49.near_ref, bf16[2,5,64,2048]{3,2,1,0:T(8,128)(2,1)S(1)} %get-tuple-element.53.far_ref, ...), custom_call_target="tpu_custom_call" | custom-call | flops 1000 | bytes 1000 | tf_op jit(solution)/shard_map/final/pallas_call | solution.py:277
  47.1 0.6 copy-done.8
  47.6 2.3 %final.3 = (bf16[768,2048]{1,0:T(8,128)(2,1)S(1)}, f32[8,128]{1,0:T(8,128)S(1)}) custom-call(s32[1]{0:T(128)S(6)} %sub.16.seq_ref, bf16[2,768,2048]{2,1,0:T(8,128)(2,1)S(1)} %copy-done.2, bf16[2,5,64,2048]{3,2,1,0:T(8,128)(2,1)S(1)} %get-tuple-element.49.near_ref, bf16[2,5,64,2048]{3,2,1,0:T(8,128)(2,1)S(1)} %get-tuple-element.53.far_ref, ...), custom_call_target="tpu_custom_call" | custom-call | flops 1000 | bytes 1000 | tf_op jit(solution)/shard_map/final/pallas_call | solution.py:277
  50.0 3.5 %collective-permute-start.13 = (f32[16,128]{1,0:T(8,128)S(1)}, f32[16,128]{1,0:T(8,128)S(1)}, u32[]{:S(2)}, u32[]{:S(2)}) collective-permute-start(f32[16,128]{1,0:T(8,128)S(1)} %constant_dynamic-update-slice_fusion), channel_id=1, source_target_pairs={{0,3},{1,2},{2,1},{3,0},{4,7},{5,6},{6,5},{7,4},{8,11},{9,10},{10,... | collective-permute-start | bytes 24584 | tf_op jit(solution)/shard_map/ppermute | solution.py:344
  53.5 1.0 %collective-permute-start.11 = (f32[16,128]{1,0:T(8,128)S(1)}, f32[16,128]{1,0:T(8,128)S(1)}, u32[]{:S(2)}, u32[]{:S(2)}) collective-permute-start(f32[16,128]{1,0:T(8,128)S(1)} %constant_dynamic-update-slice_fusion), channel_id=1, source_target_pairs={{0,1},{1,0},{2,3},{3,2},{4,5},{5,4},{6,7},{7,6},{8,9},{9,8},{10,11... | collective-permute-start | bytes 24584 | tf_op jit(solution)/shard_map/ppermute | solution.py:344
  54.4 1.1 %collective-permute-done.13 = f32[16,128]{1,0:T(8,128)S(1)} collective-permute-done((f32[16,128]{1,0:T(8,128)S(1)}, f32[16,128]{1,0:T(8,128)S(1)}, u32[]{:S(2)}, u32[]{:S(2)}) %collective-permute-start.13) | collective-permute-done | bytes 8224 | tf_op jit(solution)/shard_map/ppermute | solution.py:344
  55.5 2.5 %collective-permute-done.12 = f32[16,128]{1,0:T(8,128)S(1)} collective-permute-done((f32[16,128]{1,0:T(8,128)S(1)}, f32[16,128]{1,0:T(8,128)S(1)}, u32[]{:S(2)}, u32[]{:S(2)}) %collective-permute-start.12) | collective-permute-done | bytes 8224 | tf_op jit(solution)/shard_map/ppermute | solution.py:344
  58.0 3.1 %normed.1 = bf16[2,768,2048]{2,1,0:T(8,128)(2,1)} custom-call(s32[1]{0:T(128)} %bitcast.seq_ref, f32[16,128]{1,0:T(8,128)S(1)} %add_add_fusion.square_ref, f32[1,2048]{1,0:T(1,128)S(1)} %bitcast.31, bf16[768,2048]{1,0:T(8,128)(2,1)S(1)} %get-tuple-element.81.refs_0_, bf16[768,2048]{1,0:T(8,128)(2,1)S(1)} %get-tuple-element.82.refs_1_), custom_call_target="tpu_custom_call" | custom-call | flops 1000 | bytes 1000 | tf_op jit(solution)/shard_map/normed/pallas_call | solution.py:326
  (51 shorter events, 1.0 us)
Async XLA Ops:
  1.0 15.6 %collective-permute-start = (bf16[2,32,768]{2,1,0:T(8,128)(2,1)S(1)}, bf16[2,32,768]{2,1,0:T(8,128)(2,1)S(1)}, u32[]{:S(2)}, u32[]{:S(2)}) collective-permute-start(bf16[2,32,768]{2,1,0:T(8,128)(2,1)S(1)} %get-tuple-element.47), channel_id=1, source_target_pairs={{0,1},{1,0},{2,3},{3,2},{4,5},{5,4},{6,7},{7,6},{8,9},{9,8},{10,11... | collective-permute-start | bytes 294920 | tf_op jit(solution)/shard_map/ppermute | solution.py:344
  8.5 2.7 %copy-start = (bf16[2,768,2048]{2,1,0:T(8,128)(2,1)}, bf16[2,768,2048]{2,1,0:T(8,128)(2,1)S(1)}, u32[]{:S(2)}) copy-start(bf16[2,768,2048]{2,1,0:T(8,128)(2,1)S(1)} %get-tuple-element.44.weighted_ref) | copy-start | bytes 18874372
  11.2 2.6 %copy-start.3 = (bf16[2,768,2048]{2,1,0:T(8,128)(2,1)}, bf16[2,768,2048]{2,1,0:T(8,128)(2,1)S(1)}, u32[]{:S(2)}) copy-start(bf16[2,768,2048]{2,1,0:T(8,128)(2,1)S(1)} %get-tuple-element.67.x_ref) | copy-start | bytes 18874372
  13.9 17.1 %collective-permute-start.1 = (bf16[2,32,768]{2,1,0:T(8,128)(2,1)S(1)}, bf16[2,32,768]{2,1,0:T(8,128)(2,1)S(1)}, u32[]{:S(2)}, u32[]{:S(2)}) collective-permute-start(bf16[2,32,768]{2,1,0:T(8,128)(2,1)S(1)} %get-tuple-element.47), channel_id=1, source_target_pairs={{0,2},{1,3},{2,0},{3,1},{4,6},{5,7},{6,4},{7,5},{8,10},{9,11},{10,... | collective-permute-start | bytes 294920 | tf_op jit(solution)/shard_map/ppermute | solution.py:344
  16.4 14.5 %collective-permute-start.2 = (bf16[2,32,768]{2,1,0:T(8,128)(2,1)S(1)}, bf16[2,32,768]{2,1,0:T(8,128)(2,1)S(1)}, u32[]{:S(2)}, u32[]{:S(2)}) collective-permute-start(bf16[2,32,768]{2,1,0:T(8,128)(2,1)S(1)} %get-tuple-element.47), channel_id=1, source_target_pairs={{0,3},{1,2},{2,1},{3,0},{4,7},{5,6},{6,5},{7,4},{8,11},{9,10},{10,... | collective-permute-start | bytes 294920 | tf_op jit(solution)/shard_map/ppermute | solution.py:344
  16.6 2.8 %copy-start.1 = (bf16[2,768,2048]{2,1,0:T(8,128)(2,1)S(1)}, bf16[2,768,2048]{2,1,0:T(8,128)(2,1)}, u32[]{:S(2)}) copy-start(bf16[2,768,2048]{2,1,0:T(8,128)(2,1)} %copy-done) | copy-start | bytes 18874372
  19.4 11.9 %copy-start.2 = (bf16[2,768,2048]{2,1,0:T(8,128)(2,1)S(1)}, bf16[2,768,2048]{2,1,0:T(8,128)(2,1)}, u32[]{:S(2)}) copy-start(bf16[2,768,2048]{2,1,0:T(8,128)(2,1)} %copy-done) | copy-start | bytes 18874372
  20.7 15.2 %copy-start.4 = (bf16[2,768,2048]{2,1,0:T(8,128)(2,1)S(1)}, bf16[2,768,2048]{2,1,0:T(8,128)(2,1)}, u32[]{:S(2)}) copy-start(bf16[2,768,2048]{2,1,0:T(8,128)(2,1)} %copy-done.3) | copy-start | bytes 18874372
  20.9 1.7 %collective-permute-start.3 = (bf16[80,2048]{1,0:T(8,128)(2,1)S(1)}, bf16[80,2048]{1,0:T(8,128)(2,1)S(1)}, u32[]{:S(2)}, u32[]{:S(2)}) collective-permute-start(bf16[80,2048]{1,0:T(8,128)(2,1)S(1)} %maximum_maximum_fusion), channel_id=1, source_target_pairs={{0,4},{4,0},{8,12},{12,8},{1,5},{5,1},{9,13},{13,9},{2,6},{6,2},{1... | collective-permute-start | bytes 983048 | tf_op jit(solution)/shard_map/ppermute | solution.py:395
  22.6 13.3 %slice-start = ((s8[6291456]{0:T(1024)(128)(4,1)}), s8[4194304]{0:T(1024)(128)(4,1)S(1)}, s32[]{:S(2)}) async-start(s8[6291456]{0:T(1024)(128)(4,1)} %bitcast.29), calls=%async_computation | async-start | bytes 8388608
  22.8 20.4 %collective-permute-start.4 = (bf16[64,2048]{1,0:T(8,128)(2,1)S(1)}, bf16[64,2048]{1,0:T(8,128)(2,1)S(1)}, u32[]{:S(2)}, u32[]{:S(2)}) collective-permute-start(bf16[64,2048]{1,0:T(8,128)(2,1)S(1)} %select_convert_fusion.1), channel_id=1, source_target_pairs={{0,8},{4,12},{1,9},{5,13},{2,10},{6,14},{3,11},{7,15},{16,24},{20,... | collective-permute-start | bytes 786440 | tf_op jit(solution)/shard_map/ppermute | solution.py:390
  26.7 11.7 %collective-permute-start.7 = (bf16[2,32,768]{2,1,0:T(8,128)(2,1)S(1)}, bf16[2,32,768]{2,1,0:T(8,128)(2,1)S(1)}, u32[]{:S(2)}, u32[]{:S(2)}) collective-permute-start(bf16[2,32,768]{2,1,0:T(8,128)(2,1)S(1)} %get-tuple-element.63), channel_id=1, source_target_pairs={{0,1},{1,0},{2,3},{3,2},{4,5},{5,4},{6,7},{7,6},{8,9},{9,8},{10,11... | collective-permute-start | bytes 294920 | tf_op jit(solution)/shard_map/ppermute | solution.py:344
  27.4 11.2 %collective-permute-start.8 = (bf16[2,32,768]{2,1,0:T(8,128)(2,1)S(1)}, bf16[2,32,768]{2,1,0:T(8,128)(2,1)S(1)}, u32[]{:S(2)}, u32[]{:S(2)}) collective-permute-start(bf16[2,32,768]{2,1,0:T(8,128)(2,1)S(1)} %get-tuple-element.63), channel_id=1, source_target_pairs={{0,2},{1,3},{2,0},{3,1},{4,6},{5,7},{6,4},{7,5},{8,10},{9,11},{10,... | collective-permute-start | bytes 294920 | tf_op jit(solution)/shard_map/ppermute | solution.py:344
  31.0 4.9 %slice-start.1 = ((s8[6291456]{0:T(1024)(128)(4,1)}), s8[2097152]{0:T(1024)(128)(4,1)S(1)}, s32[]{:S(2)}) async-start(s8[6291456]{0:T(1024)(128)(4,1)} %bitcast.29), calls=%async_computation.1 | async-start | bytes 4194304
  31.0 7.7 %collective-permute-start.9 = (bf16[2,32,768]{2,1,0:T(8,128)(2,1)S(1)}, bf16[2,32,768]{2,1,0:T(8,128)(2,1)S(1)}, u32[]{:S(2)}, u32[]{:S(2)}) collective-permute-start(bf16[2,32,768]{2,1,0:T(8,128)(2,1)S(1)} %get-tuple-element.63), channel_id=1, source_target_pairs={{0,3},{1,2},{2,1},{3,0},{4,7},{5,6},{6,5},{7,4},{8,11},{9,10},{10,... | collective-permute-start | bytes 294920 | tf_op jit(solution)/shard_map/ppermute | solution.py:344
  32.6 1.6 %collective-permute-start.5 = (bf16[64,2048]{1,0:T(8,128)(2,1)S(1)}, bf16[64,2048]{1,0:T(8,128)(2,1)S(1)}, u32[]{:S(2)}, u32[]{:S(2)}) collective-permute-start(bf16[64,2048]{1,0:T(8,128)(2,1)S(1)} %get-tuple-element.88), channel_id=1, source_target_pairs={{0,4},{4,0},{8,12},{12,8},{1,5},{5,1},{9,13},{13,9},{2,6},{6,2},{1... | collective-permute-start | bytes 786440 | tf_op jit(solution)/shard_map/ppermute | solution.py:413
  34.4 8.9 %collective-permute-start.6 = (bf16[64,2048]{1,0:T(8,128)(2,1)S(1)}, bf16[64,2048]{1,0:T(8,128)(2,1)S(1)}, u32[]{:S(2)}, u32[]{:S(2)}) collective-permute-start(bf16[64,2048]{1,0:T(8,128)(2,1)S(1)} %select_convert_fusion), channel_id=1, source_target_pairs={{0,8},{4,12},{1,9},{5,13},{2,10},{6,14},{3,11},{7,15},{16,24},{20,... | collective-permute-start | bytes 786440 | tf_op jit(solution)/shard_map/ppermute | solution.py:390
  41.5 1.7 %copy-start.5 = (bf16[768,2048]{1,0:T(8,128)(2,1)}, bf16[768,2048]{1,0:T(8,128)(2,1)S(1)}, u32[]{:S(2)}) copy-start(bf16[768,2048]{1,0:T(8,128)(2,1)S(1)} %get-tuple-element.77.lift_ref) | copy-start | bytes 9437188
  43.2 1.6 %copy-start.7 = (bf16[768,2048]{1,0:T(8,128)(2,1)}, bf16[768,2048]{1,0:T(8,128)(2,1)S(1)}, u32[]{:S(2)}) copy-start(bf16[768,2048]{1,0:T(8,128)(2,1)S(1)} %get-tuple-element.78.skipped_ref) | copy-start | bytes 9437188
  43.5 3.5 %collective-permute-start.10 = (bf16[128,2048]{1,0:T(8,128)(2,1)S(1)}, bf16[128,2048]{1,0:T(8,128)(2,1)S(1)}, u32[]{:S(2)}, u32[]{:S(2)}) collective-permute-start(bf16[128,2048]{1,0:T(8,128)(2,1)S(1)} %get-tuple-element.83), channel_id=1, source_target_pairs={{0,4},{4,0},{8,12},{12,8},{1,5},{5,1},{9,13},{13,9},{2,6},{6,2},{1... | collective-permute-start | bytes 1572872 | tf_op jit(solution)/shard_map/ppermute | solution.py:433
  44.8 2.3 %copy-start.6 = (bf16[768,2048]{1,0:T(8,128)(2,1)S(1)}, bf16[768,2048]{1,0:T(8,128)(2,1)}, u32[]{:S(2)}) copy-start(bf16[768,2048]{1,0:T(8,128)(2,1)} %copy-done.5) | copy-start | bytes 9437188
  44.8 2.8 %copy-start.8 = (bf16[768,2048]{1,0:T(8,128)(2,1)S(1)}, bf16[768,2048]{1,0:T(8,128)(2,1)}, u32[]{:S(2)}) copy-start(bf16[768,2048]{1,0:T(8,128)(2,1)} %copy-done.7) | copy-start | bytes 9437188
  47.0 11.0 %copy-start.9 = (f32[2048]{0:T(1024)S(1)}, f32[2048]{0:T(1024)}, u32[]{:S(2)}) copy-start(f32[2048]{0:T(1024)} %param.15) | copy-start | bytes 24580
  50.0 5.5 %collective-permute-start.13 = (f32[16,128]{1,0:T(8,128)S(1)}, f32[16,128]{1,0:T(8,128)S(1)}, u32[]{:S(2)}, u32[]{:S(2)}) collective-permute-start(f32[16,128]{1,0:T(8,128)S(1)} %constant_dynamic-update-slice_fusion), channel_id=1, source_target_pairs={{0,3},{1,2},{2,1},{3,0},{4,7},{5,6},{6,5},{7,4},{8,11},{9,10},{10,... | collective-permute-start | bytes 24584 | tf_op jit(solution)/shard_map/ppermute | solution.py:344
  53.5 4.5 %collective-permute-start.12 = (f32[16,128]{1,0:T(8,128)S(1)}, f32[16,128]{1,0:T(8,128)S(1)}, u32[]{:S(2)}, u32[]{:S(2)}) collective-permute-start(f32[16,128]{1,0:T(8,128)S(1)} %constant_dynamic-update-slice_fusion), channel_id=1, source_target_pairs={{0,2},{1,3},{2,0},{3,1},{4,6},{5,7},{6,4},{7,5},{8,10},{9,11},{10,... | collective-permute-start | bytes 24584 | tf_op jit(solution)/shard_map/ppermute | solution.py:344
  53.5 4.5 %collective-permute-start.11 = (f32[16,128]{1,0:T(8,128)S(1)}, f32[16,128]{1,0:T(8,128)S(1)}, u32[]{:S(2)}, u32[]{:S(2)}) collective-permute-start(f32[16,128]{1,0:T(8,128)S(1)} %constant_dynamic-update-slice_fusion), channel_id=1, source_target_pairs={{0,1},{1,0},{2,3},{3,2},{4,5},{5,4},{6,7},{7,6},{8,9},{9,8},{10,11... | collective-permute-start | bytes 24584 | tf_op jit(solution)/shard_map/ppermute | solution.py:344

commit v12 on v11

--- a/solution.py
+++ b/solution.py
@@ -91,15 +91,15 @@
 
 def front_kernel(
     x_hbm, step_hbm, decay_hbm, skip_hbm, sums_hbm, bands_hbm,
-    x_ref, weighted_ref, both_ref, rows_ref, bands, step, decay, skip, sums, sems,
+    weighted_ref, both_ref, rows_ref, bands, step, decay, skip, sums, sems,
 ):
-    seqs, length, channels = x_ref.shape
+    seqs, length, channels = weighted_ref.shape
     heads = decay.shape[1]
     pairs = [
         (decay_hbm, decay), (step_hbm, step), (sums_hbm, sums), (skip_hbm, skip), (bands_hbm, bands)
     ]
     small = len(pairs)
-    pairs += [(x_hbm.at[s], x_ref.at[s]) for s in range(seqs)]
+    pairs += [(x_hbm.at[s], weighted_ref.at[s]) for s in range(seqs)]
     copies = [
         pltpu.make_async_copy(source, target, sems.at[i])
         for i, (source, target) in enumerate(pairs)
@@ -117,7 +117,7 @@
             for lo in range(0, channels, HALF):
                 sl = slice(lo, lo + HALF)
                 wide = mm(both, bands[:4 * heads, sl]).astype(BF16)
-                weighted_ref[s, rows, sl] = x_ref[s, rows, sl] * wide
+                weighted_ref[s, rows, sl] = weighted_ref[s, rows, sl] * wide
 
 
 def front(features, step_size, log_decay, skip, sums, bands):
@@ -127,9 +127,8 @@
     return pl.pallas_call(
         front_kernel,
         in_specs=[ANYWHERE] * 6,
-        out_specs=[WHOLE] * 5,
+        out_specs=[WHOLE] * 4,
         out_shape=[
-            pltpu.VMEM(features.shape, BF16),
             pltpu.VMEM(features.shape, BF16),
             pltpu.VMEM((seqs, length, 4 * heads), BF16),
             pltpu.VMEM((seqs, ROWS, channels), F32),
@@ -339,11 +338,13 @@
 
 
 def from_partner(shard, axis, by):
-    devices = lax.axis_size(axis)
-    paired = devices & (devices - 1) == 0
-    return lax.ppermute(
-        shard, axis, [(i, i ^ by if paired else (i + by) % devices) for i in range(devices)]
-    )
+    return lax.ppermute(shard, axis, [(i, i ^ by) for i in range(lax.axis_size(axis))])
+
+
+def doubled(block, axis, by, behind=()):
+    other = from_partner(block, axis, by)
+    other, _ = lax.optimization_barrier((other, behind))
+    return jnp.concatenate([block, other], axis=1)
 
 
 def from_all(shard, axis):
@@ -364,13 +365,11 @@
     until = np.tril(np.ones((SPAN, SPAN)))
     sums = jnp.asarray(np.concatenate([np.tile(until, 2), np.tile(np.eye(SPAN), 2)]), BF16)
     b_own, c_own = lax.optimization_barrier((state_proj[0], state_proj[1]))
-    b_next = from_partner(b_own, "head", 1)
-    x, weighted, both, rows, bands = front(
+    b_near = doubled(b_own, "head", 1)
+    c_near = doubled(c_own, "head", 1)
+    weighted, both, rows, bands = front(
         features, step_size, log_decay, skip_gain[None, :], sums, bands
     )
-
-    b_own, rows = lax.optimization_barrier((b_own, rows))
-    b_far = [from_partner(b_own, "head", by) for by in range(2, lax.axis_size("head"))]
 
     place = lax.axis_index("ctx")
     even = place % 2 == 0
@@ -389,7 +388,6 @@
         sent = sent.astype(BF16)
         return sent, lax.ppermute(sent, "ctx", [(hop, hop + 2), (hop + 1, hop + 3)])
 
-    b_near = jnp.concatenate([b_own, b_next], axis=1)
     near, near_ends = own_states(b_near, weighted, rows)
     near_rows = b_near.shape[1]
     other = lax.ppermute(
@@ -407,20 +405,23 @@
     near_end = jnp.where(even, near_ends[0], near_ends[1]).astype(F32)
     near_past = past_chip(near_end, near_other, decay_other)
     near_sent, near_got = across(near_past, None, 0)
-    b_far, _ = lax.optimization_barrier((b_far, near_sent))
-    b_far = jnp.concatenate(b_far, axis=1)
+    b = b_near
+    for by in (1 << i for i in range(1, (lax.axis_size("head") - 1).bit_length())):
+        b = doubled(b, "head", by, near_sent)
+    b_far = b[:, near_rows:]
     far, far_ends = own_states(b_far, weighted, rows)
     far_other = lax.ppermute(jnp.where(even, far_ends[1], far_ends[0]), "ctx", swap).astype(F32)
     far_end = jnp.where(even, far_ends[0], far_ends[1]).astype(F32)
     far_past = past_chip(far_end, far_other, decay_other)
     far_sent, far_got = across(far_past, None, 0)
-    c_own, _ = lax.optimization_barrier((c_own, near_sent))
-    c = from_all(c_own, "head")
-    x, _ = lax.optimization_barrier((x, far_sent))
-    lifts = gates(mine, gate_in, x, both, bands, rows)
-    x, lifts, c = lax.optimization_barrier((x, lifts, c))
-    lifts_next = gates(1 - mine, gate_in, x, both, bands, rows)
-    left = left_of(jnp.concatenate([b_near, b_far], axis=1), jnp.concatenate(c, axis=1))
+    c, _ = lax.optimization_barrier((c_near, near_sent))
+    both, _ = lax.optimization_barrier((both, far_sent))
+    lifts = gates(mine, gate_in, features, both, bands, rows)
+    for by in (1 << i for i in range(1, (lax.axis_size("head") - 1).bit_length())):
+        c = doubled(c, "head", by, lifts)
+    both, c = lax.optimization_barrier((both, c))
+    lifts_next = gates(1 - mine, gate_in, features, both, bands, rows)
+    left = left_of(b, c)
     left, lifts_next = lax.optimization_barrier((left, lifts_next))
     near_got, far_got, left = lax.optimization_barrier((near_got, far_got, left))
     for hop in range(2, devices - 2, 2):

time: 61.5 us -> 53.3 us (0.87)
  local copies, waits for them, and re-layouts: 12.6 us -> 1.08 us
  waiting for transfers between devices: 6.88 us -> 12.2 us
  starting transfers between devices: 20.2 us -> 18.2 us
    unnamed x25 -> x11, local copies, waits for them, and re-layouts: 11.5 us -> 0.04 us
    ppermute x9 -> x7, waiting for transfers between devices: 3.8 us -> 10.7 us  [from_partner(): lax.ppermute(shard, axis, [(i, i ^ by) for i in range(lax.axis_size(axis))])]
    ppermute x9 -> x7, starting transfers between devices: 14.7 us -> 10.6 us  [from_partner(): lax.ppermute(shard, axis, [(i, i ^ by) for i in range(lax.axis_size(axis))])]
    ppermute x2, starting transfers between devices: 5.38 us -> 7.34 us  [across(): lax.ppermute(sent, 'ctx', [(hop, hop + 2), (hop + 1, hop + 3)])]
    ppermute x1, waiting for transfers between devices: 1.59 us -> 0.01 us  [body(): lax.ppermute(jnp.concatenate([jnp.where(even, near_ends[1], near_ends[0])...]
  transfers between devices with their start and end apart: 14 -> 12, of which waited for: 5 -> 6; matrix products, arithmetic and copies ran while one was open for 1% -> 2% of each run, Pallas kernels for 24% -> 28%
where the time goes in v12:
time: 53.3 us; the launch traced here: 53.2 us
  Pallas kernels  20.1 us (38%)
  starting transfers between devices  18.2 us (34%)
  waiting for transfers between devices  12.2 us (23%)
  other arithmetic  1.12 us (2%)
  local copies, waits for them, and re-layouts  1.08 us (2%)
    ppermute x7, waiting for transfers between devices, from_partner(): lax.ppermute(shard, axis, [(i, i ^ by) for i in range(lax.axis_size(axis))])  10.7 us
    ppermute x7, starting transfers between devices, from_partner(): lax.ppermute(shard, axis, [(i, i ^ by) for i in range(lax.axis_size(axis))])  10.6 us
    ppermute x2, starting transfers between devices, across(): lax.ppermute(sent, 'ctx', [(hop, hop + 2), (hop + 1, hop + 3)])  7.34 us
    pallas_call x2, Pallas kernels, gates(): pl.pallas_call(gate_kernel, in_specs=[pl.BlockSpec(memory_space=pltpu.SME...  5.05 us
    pallas_call x1, Pallas kernels, front(): pl.pallas_call(front_kernel, in_specs=[ANYWHERE] * 6, out_specs=[WHOLE] *...  4.64 us
    pallas_call x2, Pallas kernels, final(): pl.pallas_call(final_kernel, in_specs=[pl.BlockSpec(memory_space=pltpu.SM...  4.55 us
    pallas_call x1, Pallas kernels, normed(): pl.pallas_call(functools.partial(norm_kernel, all_channels), in_specs=[pl...  3.1 us
    pallas_call x2, Pallas kernels, own_states(): pl.pallas_call(state_kernel, in_specs=[WHOLE] * 3, out_specs=[WHOLE] * 2,...  2.47 us
  transfers between devices with their start and end apart: 12, of which 6 were waited for; matrix products, arithmetic and copies ran while one was open for 2% of the time, Pallas kernels for 28%

profile of v12, /device:TPU:0, one launch (start us, length us, event | category | flops | bytes accessed | tf_op | source)
XLA Modules:
  0.0 53.2 jit_solution(3138689183645893961)
XLA Ops:
  0.0 1.0 %slice_bitcast_fusion = (bf16[2,32,768]{2,1,0:T(8,128)(2,1)S(1)}, bf16[2,32,768]{2,1,0:T(8,128)(2,1)S(1)}) fusion(bf16[2,2,32,768]{3,2,1,0:T(8,128)(2,1)} %param.11), kind=kLoop, calls=%fused_computation.21 | loop fusion | bytes 393216 | tf_op jit(solution)/shard_map/squeeze | solution.py:367
  1.0 3.1 %collective-permute-start.6 = (bf16[2,32,768]{2,1,0:T(8,128)(2,1)S(1)}, bf16[2,32,768]{2,1,0:T(8,128)(2,1)S(1)}, u32[]{:S(2)}, u32[]{:S(2)}) collective-permute-start(bf16[2,32,768]{2,1,0:T(8,128)(2,1)S(1)} %get-tuple-element.46), channel_id=1, source_target_pairs={{0,1},{1,0},{2,3},{3,2},{4,5},{5,4},{6,7},{7,6},{8,9},{9,8},{10,11... | collective-permute-start | bytes 294920 | tf_op jit(solution)/shard_map/ppermute | solution.py:341
  4.0 0.1 collective-permute-start
  4.1 4.6 %front.1 = (bf16[2,768,2048]{2,1,0:T(8,128)(2,1)S(1)}, bf16[2,768,128]{2,1,0:T(8,128)(2,1)S(1)}, f32[2,32,2048]{2,1,0:T(8,128)S(1)}, bf16[192,2048]{1,0:T(8,128)(2,1)S(1)}) custom-call(bf16[2,768,2048]{2,1,0:T(8,128)(2,1)} %x_ref.3, f32[2,32,768]{2,1,0:T(8,128)} %step_hbm.1, f32[2,32,768]{2,1,0:T(8,128)} %decay_hbm.1, f32[1,32]{1,0:T(1,128)} %bitcast.40, ...), custom_call_target="tpu_custom_call" | custom-call | flops 1000 | bytes 1000 | tf_op jit(solution)/shard_map/front/pallas_call | solution.py:127
  8.8 0.1 pad.16.clone
  9.0 1.3 %own_states.2 = (bf16[2,5,64,2048]{3,2,1,0:T(8,128)(2,1)S(1)}, bf16[2,64,2048]{2,1,0:T(8,128)(2,1)S(1)}) custom-call(bf16[2,64,768]{2,1,0:T(8,128)(2,1)S(1)} %pad_maximum_fusion.3.b_ref, bf16[2,768,2048]{2,1,0:T(8,128)(2,1)S(1)} %get-tuple-element.36.weighted_ref, f32[2,32,2048]{2,1,0:T(8,128)S(1)} %get-tuple-element.38.rows_ref), custom_call_target="tpu_custom_call" | custom-call | flops 1000 | bytes 1000 | tf_op jit(solution)/shard_map/own_states/pallas_call | solution.py:173
  10.3 0.1 maximum_maximum_fusion
  10.4 0.1 collective-permute-start.2
  10.5 3.0 %collective-permute-start.1 = (bf16[2,64,768]{2,1,0:T(8,128)(2,1)S(1)}, bf16[2,64,768]{2,1,0:T(8,128)(2,1)S(1)}, u32[]{:S(2)}, u32[]{:S(2)}) collective-permute-start(bf16[2,64,768]{2,1,0:T(8,128)(2,1)S(1)} %pad_maximum_fusion.3.b_ref), channel_id=1, source_target_pairs={{0,2},{1,3},{2,0},{3,1},{4,6},{5,7},{6,4},{7,5},{8,10},{9,11},{10,... | collective-permute-start | bytes 589832 | tf_op jit(solution)/shard_map/ppermute | solution.py:341
  13.6 0.2 select_convert_fusion.1
  13.8 3.7 %collective-permute-start.3 = (bf16[64,2048]{1,0:T(8,128)(2,1)S(1)}, bf16[64,2048]{1,0:T(8,128)(2,1)S(1)}, u32[]{:S(2)}, u32[]{:S(2)}) collective-permute-start(bf16[64,2048]{1,0:T(8,128)(2,1)S(1)} %select_convert_fusion.1), channel_id=1, source_target_pairs={{0,8},{4,12},{1,9},{5,13},{2,10},{6,14},{3,11},{7,15},{16,24},{20,... | collective-permute-start | bytes 786440 | tf_op jit(solution)/shard_map/ppermute | solution.py:389
  17.5 5.8 %collective-permute-done.1.b_ref = bf16[2,64,768]{2,1,0:T(8,128)(2,1)S(1)} collective-permute-done((bf16[2,64,768]{2,1,0:T(8,128)(2,1)S(1)}, bf16[2,64,768]{2,1,0:T(8,128)(2,1)S(1)}, u32[]{:S(2)}, u32[]{:S(2)}) %collective-permute-start.1) | collective-permute-done | bytes 196640 | tf_op jit(solution)/shard_map/ppermute | solution.py:341
  23.3 1.2 %own_states.3 = (bf16[2,5,64,2048]{3,2,1,0:T(8,128)(2,1)S(1)}, bf16[2,64,2048]{2,1,0:T(8,128)(2,1)S(1)}) custom-call(bf16[2,64,768]{2,1,0:T(8,128)(2,1)S(1)} %collective-permute-done.1.b_ref, bf16[2,768,2048]{2,1,0:T(8,128)(2,1)S(1)} %get-tuple-element.36.weighted_ref, f32[2,32,2048]{2,1,0:T(8,128)S(1)} %get-tuple-element.38.rows_ref), custom_call_target="tpu_custom_call" | custom-call | flops 1000 | bytes 1000 | tf_op jit(solution)/shard_map/own_states/pallas_call | solution.py:173
  24.6 0.1 collective-permute-start.4
  24.8 1.4 %collective-permute-done.4 = bf16[64,2048]{1,0:T(8,128)(2,1)S(1)} collective-permute-done((bf16[64,2048]{1,0:T(8,128)(2,1)S(1)}, bf16[64,2048]{1,0:T(8,128)(2,1)S(1)}, u32[]{:S(2)}, u32[]{:S(2)}) %collective-permute-start.4) | collective-permute-done | bytes 262176 | tf_op jit(solution)/shard_map/ppermute | solution.py:413
  26.2 0.2 select_convert_fusion
  26.4 3.7 %collective-permute-start.5 = (bf16[64,2048]{1,0:T(8,128)(2,1)S(1)}, bf16[64,2048]{1,0:T(8,128)(2,1)S(1)}, u32[]{:S(2)}, u32[]{:S(2)}) collective-permute-start(bf16[64,2048]{1,0:T(8,128)(2,1)S(1)} %select_convert_fusion), channel_id=1, source_target_pairs={{0,8},{4,12},{1,9},{5,13},{2,10},{6,14},{3,11},{7,15},{16,24},{20,... | collective-permute-start | bytes 786440 | tf_op jit(solution)/shard_map/ppermute | solution.py:389
  30.1 2.5 %gates.2 = (bf16[768,2048]{1,0:T(8,128)(2,1)S(1)}, bf16[768,2048]{1,0:T(8,128)(2,1)S(1)}) custom-call(s32[1]{0:T(128)} %bitcast.seq_ref, bf16[2,768,2048]{2,1,0:T(8,128)(2,1)S(1)} %bitcast.32, bf16[2,768,2048]{2,1,0:T(8,128)(2,1)S(1)} %bitcast.30, bf16[2,768,128]{2,1,0:T(8,128)(2,1)S(1)} %get-tuple-element.53.both_ref, ...), custom_call_target="tpu_custom_call" | custom-call | flops 1000000000 | bytes 12000000 | tf_op jit(solution)/shard_map/gates/pallas_call | solution.py:206
  32.6 2.5 %collective-permute-done.7 = bf16[2,64,768]{2,1,0:T(8,128)(2,1)S(1)} collective-permute-done((bf16[2,64,768]{2,1,0:T(8,128)(2,1)S(1)}, bf16[2,64,768]{2,1,0:T(8,128)(2,1)S(1)}, u32[]{:S(2)}, u32[]{:S(2)}) %collective-permute-start.7) | collective-permute-done | bytes 196640 | tf_op jit(solution)/shard_map/ppermute | solution.py:341
  35.2 0.3 left.1.left_ref
  35.5 2.5 %gates.3 = (bf16[768,2048]{1,0:T(8,128)(2,1)S(1)}, bf16[768,2048]{1,0:T(8,128)(2,1)S(1)}) custom-call(s32[1]{0:T(128)S(6)} %sub.16.seq_ref, bf16[2,768,2048]{2,1,0:T(8,128)(2,1)S(1)} %bitcast.32, bf16[2,768,2048]{2,1,0:T(8,128)(2,1)S(1)} %bitcast.30, bf16[2,768,128]{2,1,0:T(8,128)(2,1)S(1)} %get-tuple-element.53.both_ref, ...), custom_call_target="tpu_custom_call" | custom-call | flops 1000000000 | bytes 12000000 | tf_op jit(solution)/shard_map/gates/pallas_call | solution.py:206
  38.1 0.3 fusion.3
  38.4 0.1 collective-permute-start.8
  38.5 2.3 %final.2 = (bf16[768,2048]{1,0:T(8,128)(2,1)S(1)}, f32[8,128]{1,0:T(8,128)S(1)}) custom-call(s32[1]{0:T(128)} %bitcast.seq_ref, bf16[2,768,2048]{2,1,0:T(8,128)(2,1)S(1)} %get-tuple-element.36.weighted_ref, bf16[2,5,64,2048]{3,2,1,0:T(8,128)(2,1)S(1)} %get-tuple-element.39.near_ref, bf16[2,5,64,2048]{3,2,1,0:T(8,128)(2,1)S(1)} %get-tuple-element.42.far_ref, ...), custom_call_target="tpu_custom_call" | custom-call | flops 1000 | bytes 1000 | tf_op jit(solution)/shard_map/final/pallas_call | solution.py:276
  40.8 2.2 %final.3 = (bf16[768,2048]{1,0:T(8,128)(2,1)S(1)}, f32[8,128]{1,0:T(8,128)S(1)}) custom-call(s32[1]{0:T(128)S(6)} %sub.16.seq_ref, bf16[2,768,2048]{2,1,0:T(8,128)(2,1)S(1)} %get-tuple-element.36.weighted_ref, bf16[2,5,64,2048]{3,2,1,0:T(8,128)(2,1)S(1)} %get-tuple-element.39.near_ref, bf16[2,5,64,2048]{3,2,1,0:T(8,128)(2,1)S(1)} %get-tuple-element.42.far_ref, ...), custom_call_target="tpu_custom_call" | custom-call | flops 1000 | bytes 1000 | tf_op jit(solution)/shard_map/final/pallas_call | solution.py:276
  43.1 1.3 %collective-permute-start.11 = (f32[16,128]{1,0:T(8,128)S(1)}, f32[16,128]{1,0:T(8,128)S(1)}, u32[]{:S(2)}, u32[]{:S(2)}) collective-permute-start(f32[16,128]{1,0:T(8,128)S(1)} %constant_dynamic-update-slice_fusion), channel_id=1, source_target_pairs={{0,3},{1,2},{2,1},{3,0},{4,7},{5,6},{6,5},{7,4},{8,11},{9,10},{10,... | collective-permute-start | bytes 24584 | tf_op jit(solution)/shard_map/ppermute | solution.py:341
  44.3 1.9 %collective-permute-start.10 = (f32[16,128]{1,0:T(8,128)S(1)}, f32[16,128]{1,0:T(8,128)S(1)}, u32[]{:S(2)}, u32[]{:S(2)}) collective-permute-start(f32[16,128]{1,0:T(8,128)S(1)} %constant_dynamic-update-slice_fusion), channel_id=1, source_target_pairs={{0,2},{1,3},{2,0},{3,1},{4,6},{5,7},{6,4},{7,5},{8,10},{9,11},{10,... | collective-permute-start | bytes 24584 | tf_op jit(solution)/shard_map/ppermute | solution.py:341
  46.2 1.3 %collective-permute-start.9 = (f32[16,128]{1,0:T(8,128)S(1)}, f32[16,128]{1,0:T(8,128)S(1)}, u32[]{:S(2)}, u32[]{:S(2)}) collective-permute-start(f32[16,128]{1,0:T(8,128)S(1)} %constant_dynamic-update-slice_fusion), channel_id=1, source_target_pairs={{0,1},{1,0},{2,3},{3,2},{4,5},{5,4},{6,7},{7,6},{8,9},{9,8},{10,11... | collective-permute-start | bytes 24584 | tf_op jit(solution)/shard_map/ppermute | solution.py:341
  47.5 1.1 %collective-permute-done.11 = f32[16,128]{1,0:T(8,128)S(1)} collective-permute-done((f32[16,128]{1,0:T(8,128)S(1)}, f32[16,128]{1,0:T(8,128)S(1)}, u32[]{:S(2)}, u32[]{:S(2)}) %collective-permute-start.11) | collective-permute-done | bytes 8224 | tf_op jit(solution)/shard_map/ppermute | solution.py:341
  48.6 0.4 collective-permute-done.10
  49.0 0.9 %collective-permute-done.9 = f32[16,128]{1,0:T(8,128)S(1)} collective-permute-done((f32[16,128]{1,0:T(8,128)S(1)}, f32[16,128]{1,0:T(8,128)S(1)}, u32[]{:S(2)}, u32[]{:S(2)}) %collective-permute-start.9) | collective-permute-done | bytes 8224 | tf_op jit(solution)/shard_map/ppermute | solution.py:341
  49.9 3.1 %normed.1 = bf16[2,768,2048]{2,1,0:T(8,128)(2,1)} custom-call(s32[1]{0:T(128)} %bitcast.seq_ref, f32[16,128]{1,0:T(8,128)S(1)} %add_add_fusion.square_ref, f32[1,2048]{1,0:T(1,128)S(1)} %bitcast.33, bf16[768,2048]{1,0:T(8,128)(2,1)S(1)} %get-tuple-element.65.refs_0_, bf16[768,2048]{1,0:T(8,128)(2,1)S(1)} %get-tuple-element.66.refs_1_), custom_call_target="tpu_custom_call" | custom-call | flops 1000 | bytes 1000 | tf_op jit(solution)/shard_map/normed/pallas_call | solution.py:325
  (35 shorter events, 0.4 us)
Async XLA Ops:
  1.0 12.6 %collective-permute-start.6 = (bf16[2,32,768]{2,1,0:T(8,128)(2,1)S(1)}, bf16[2,32,768]{2,1,0:T(8,128)(2,1)S(1)}, u32[]{:S(2)}, u32[]{:S(2)}) collective-permute-start(bf16[2,32,768]{2,1,0:T(8,128)(2,1)S(1)} %get-tuple-element.46), channel_id=1, source_target_pairs={{0,1},{1,0},{2,3},{3,2},{4,5},{5,4},{6,7},{7,6},{8,9},{9,8},{10,11... | collective-permute-start | bytes 294920 | tf_op jit(solution)/shard_map/ppermute | solution.py:341
  4.0 4.9 %collective-permute-start = (bf16[2,32,768]{2,1,0:T(8,128)(2,1)S(1)}, bf16[2,32,768]{2,1,0:T(8,128)(2,1)S(1)}, u32[]{:S(2)}, u32[]{:S(2)}) collective-permute-start(bf16[2,32,768]{2,1,0:T(8,128)(2,1)S(1)} %get-tuple-element.37), channel_id=1, source_target_pairs={{0,1},{1,0},{2,3},{3,2},{4,5},{5,4},{6,7},{7,6},{8,9},{9,8},{10,11... | collective-permute-start | bytes 294920 | tf_op jit(solution)/shard_map/ppermute | solution.py:341
  4.1 25.9 %slice-start.2 = ((s8[6291456]{0:T(1024)(128)(4,1)}), s8[4194304]{0:T(1024)(128)(4,1)S(1)}, s32[]{:S(2)}) async-start(s8[6291456]{0:T(1024)(128)(4,1)} %bitcast.31), calls=%async_computation.2 | async-start | bytes 8388608
  9.0 21.1 %slice-start.3 = ((s8[6291456]{0:T(1024)(128)(4,1)}), s8[2097152]{0:T(1024)(128)(4,1)S(1)}, s32[]{:S(2)}) async-start(s8[6291456]{0:T(1024)(128)(4,1)} %bitcast.31), calls=%async_computation.3 | async-start | bytes 4194304
  10.4 3.1 %collective-permute-start.2 = (bf16[80,2048]{1,0:T(8,128)(2,1)S(1)}, bf16[80,2048]{1,0:T(8,128)(2,1)S(1)}, u32[]{:S(2)}, u32[]{:S(2)}) collective-permute-start(bf16[80,2048]{1,0:T(8,128)(2,1)S(1)} %maximum_maximum_fusion), channel_id=1, source_target_pairs={{0,4},{4,0},{8,12},{12,8},{1,5},{5,1},{9,13},{13,9},{2,6},{6,2},{1... | collective-permute-start | bytes 983048 | tf_op jit(solution)/shard_map/ppermute | solution.py:393
  10.5 12.8 %collective-permute-start.1 = (bf16[2,64,768]{2,1,0:T(8,128)(2,1)S(1)}, bf16[2,64,768]{2,1,0:T(8,128)(2,1)S(1)}, u32[]{:S(2)}, u32[]{:S(2)}) collective-permute-start(bf16[2,64,768]{2,1,0:T(8,128)(2,1)S(1)} %pad_maximum_fusion.3.b_ref), channel_id=1, source_target_pairs={{0,2},{1,3},{2,0},{3,1},{4,6},{5,7},{6,4},{7,5},{8,10},{9,11},{10,... | collective-permute-start | bytes 589832 | tf_op jit(solution)/shard_map/ppermute | solution.py:341
  13.6 16.5 %slice-start = ((s8[6291456]{0:T(1024)(128)(4,1)}), s8[4194304]{0:T(1024)(128)(4,1)S(1)}, s32[]{:S(2)}) async-start(s8[6291456]{0:T(1024)(128)(4,1)} %bitcast.29), calls=%async_computation | async-start | bytes 8388608
  13.8 16.3 %slice-start.1 = ((s8[6291456]{0:T(1024)(128)(4,1)}), s8[2097152]{0:T(1024)(128)(4,1)S(1)}, s32[]{:S(2)}) async-start(s8[6291456]{0:T(1024)(128)(4,1)} %bitcast.29), calls=%async_computation.1 | async-start | bytes 4194304
  13.8 24.3 %collective-permute-start.3 = (bf16[64,2048]{1,0:T(8,128)(2,1)S(1)}, bf16[64,2048]{1,0:T(8,128)(2,1)S(1)}, u32[]{:S(2)}, u32[]{:S(2)}) collective-permute-start(bf16[64,2048]{1,0:T(8,128)(2,1)S(1)} %select_convert_fusion.1), channel_id=1, source_target_pairs={{0,8},{4,12},{1,9},{5,13},{2,10},{6,14},{3,11},{7,15},{16,24},{20,... | collective-permute-start | bytes 786440 | tf_op jit(solution)/shard_map/ppermute | solution.py:389
  23.3 11.8 %collective-permute-start.7 = (bf16[2,64,768]{2,1,0:T(8,128)(2,1)S(1)}, bf16[2,64,768]{2,1,0:T(8,128)(2,1)S(1)}, u32[]{:S(2)}, u32[]{:S(2)}) collective-permute-start(bf16[2,64,768]{2,1,0:T(8,128)(2,1)S(1)} %pad_maximum_fusion.4), channel_id=1, source_target_pairs={{0,2},{1,3},{2,0},{3,1},{4,6},{5,7},{6,4},{7,5},{8,10},{9,11},{10,... | collective-permute-start | bytes 589832 | tf_op jit(solution)/shard_map/ppermute | solution.py:341
  24.6 1.6 %collective-permute-start.4 = (bf16[64,2048]{1,0:T(8,128)(2,1)S(1)}, bf16[64,2048]{1,0:T(8,128)(2,1)S(1)}, u32[]{:S(2)}, u32[]{:S(2)}) collective-permute-start(bf16[64,2048]{1,0:T(8,128)(2,1)S(1)} %get-tuple-element.72), channel_id=1, source_target_pairs={{0,4},{4,0},{8,12},{12,8},{1,5},{5,1},{9,13},{13,9},{2,6},{6,2},{1... | collective-permute-start | bytes 786440 | tf_op jit(solution)/shard_map/ppermute | solution.py:413
  26.4 11.7 %collective-permute-start.5 = (bf16[64,2048]{1,0:T(8,128)(2,1)S(1)}, bf16[64,2048]{1,0:T(8,128)(2,1)S(1)}, u32[]{:S(2)}, u32[]{:S(2)}) collective-permute-start(bf16[64,2048]{1,0:T(8,128)(2,1)S(1)} %select_convert_fusion), channel_id=1, source_target_pairs={{0,8},{4,12},{1,9},{5,13},{2,10},{6,14},{3,11},{7,15},{16,24},{20,... | collective-permute-start | bytes 786440 | tf_op jit(solution)/shard_map/ppermute | solution.py:389
  38.4 2.4 %collective-permute-start.8 = (bf16[128,2048]{1,0:T(8,128)(2,1)S(1)}, bf16[128,2048]{1,0:T(8,128)(2,1)S(1)}, u32[]{:S(2)}, u32[]{:S(2)}) collective-permute-start(bf16[128,2048]{1,0:T(8,128)(2,1)S(1)} %get-tuple-element.67), channel_id=1, source_target_pairs={{0,4},{4,0},{8,12},{12,8},{1,5},{5,1},{9,13},{13,9},{2,6},{6,2},{1... | collective-permute-start | bytes 1572872 | tf_op jit(solution)/shard_map/ppermute | solution.py:434
  40.8 9.1 %copy-start = (f32[2048]{0:T(1024)S(1)}, f32[2048]{0:T(1024)}, u32[]{:S(2)}) copy-start(f32[2048]{0:T(1024)} %param.15) | copy-start | bytes 24580
  43.1 5.5 %collective-permute-start.11 = (f32[16,128]{1,0:T(8,128)S(1)}, f32[16,128]{1,0:T(8,128)S(1)}, u32[]{:S(2)}, u32[]{:S(2)}) collective-permute-start(f32[16,128]{1,0:T(8,128)S(1)} %constant_dynamic-update-slice_fusion), channel_id=1, source_target_pairs={{0,3},{1,2},{2,1},{3,0},{4,7},{5,6},{6,5},{7,4},{8,11},{9,10},{10,... | collective-permute-start | bytes 24584 | tf_op jit(solution)/shard_map/ppermute | solution.py:341
  44.3 4.6 %collective-permute-start.10 = (f32[16,128]{1,0:T(8,128)S(1)}, f32[16,128]{1,0:T(8,128)S(1)}, u32[]{:S(2)}, u32[]{:S(2)}) collective-permute-start(f32[16,128]{1,0:T(8,128)S(1)} %constant_dynamic-update-slice_fusion), channel_id=1, source_target_pairs={{0,2},{1,3},{2,0},{3,1},{4,6},{5,7},{6,4},{7,5},{8,10},{9,11},{10,... | collective-permute-start | bytes 24584 | tf_op jit(solution)/shard_map/ppermute | solution.py:341
  46.2 3.7 %collective-permute-start.9 = (f32[16,128]{1,0:T(8,128)S(1)}, f32[16,128]{1,0:T(8,128)S(1)}, u32[]{:S(2)}, u32[]{:S(2)}) collective-permute-start(f32[16,128]{1,0:T(8,128)S(1)} %constant_dynamic-update-slice_fusion), channel_id=1, source_target_pairs={{0,1},{1,0},{2,3},{3,2},{4,5},{5,4},{6,7},{7,6},{8,9},{9,8},{10,11... | collective-permute-start | bytes 24584 | tf_op jit(solution)/shard_map/ppermute | solution.py:341

commit v13 on v12

--- a/solution.py
+++ b/solution.py
@@ -365,8 +365,8 @@
     until = np.tril(np.ones((SPAN, SPAN)))
     sums = jnp.asarray(np.concatenate([np.tile(until, 2), np.tile(np.eye(SPAN), 2)]), BF16)
     b_own, c_own = lax.optimization_barrier((state_proj[0], state_proj[1]))
-    b_near = doubled(b_own, "head", 1)
-    c_near = doubled(c_own, "head", 1)
+    b_pieces = from_all(b_own, "head")
+    b_near = jnp.concatenate(b_pieces[:2], axis=1)
     weighted, both, rows, bands = front(
         features, step_size, log_decay, skip_gain[None, :], sums, bands
     )
@@ -405,23 +405,22 @@
     near_end = jnp.where(even, near_ends[0], near_ends[1]).astype(F32)
     near_past = past_chip(near_end, near_other, decay_other)
     near_sent, near_got = across(near_past, None, 0)
-    b = b_near
-    for by in (1 << i for i in range(1, (lax.axis_size("head") - 1).bit_length())):
-        b = doubled(b, "head", by, near_sent)
-    b_far = b[:, near_rows:]
+    b_far, _ = lax.optimization_barrier((b_pieces[2:], near_sent))
+    b_far = jnp.concatenate(b_far, axis=1)
     far, far_ends = own_states(b_far, weighted, rows)
     far_other = lax.ppermute(jnp.where(even, far_ends[1], far_ends[0]), "ctx", swap).astype(F32)
     far_end = jnp.where(even, far_ends[0], far_ends[1]).astype(F32)
     far_past = past_chip(far_end, far_other, decay_other)
     far_sent, far_got = across(far_past, None, 0)
-    c, _ = lax.optimization_barrier((c_near, near_sent))
+    c_own, _ = lax.optimization_barrier((c_own, near_ends))
+    c = doubled(c_own, "head", 1, near_sent)
     both, _ = lax.optimization_barrier((both, far_sent))
     lifts = gates(mine, gate_in, features, both, bands, rows)
     for by in (1 << i for i in range(1, (lax.axis_size("head") - 1).bit_length())):
         c = doubled(c, "head", by, lifts)
     both, c = lax.optimization_barrier((both, c))
     lifts_next = gates(1 - mine, gate_in, features, both, bands, rows)
-    left = left_of(b, c)
+    left = left_of(jnp.concatenate([b_near, b_far], axis=1), c)
     left, lifts_next = lax.optimization_barrier((left, lifts_next))
     near_got, far_got, left = lax.optimization_barrier((near_got, far_got, left))
     for hop in range(2, devices - 2, 2):

time: 53.3 us -> 49.9 us (0.936)
  waiting for transfers between devices: 12.2 us -> 6.1 us
  starting transfers between devices: 18.2 us -> 20.8 us
    ppermute x7 -> x8, waiting for transfers between devices: 10.7 us -> 4.65 us  [from_partner(): lax.ppermute(shard, axis, [(i, i ^ by) for i in range(lax.axis_size(axis))])]
    ppermute x7 -> x8, starting transfers between devices: 10.6 us -> 13.8 us  [from_partner(): lax.ppermute(shard, axis, [(i, i ^ by) for i in range(lax.axis_size(axis))])]
  transfers between devices with their start and end apart: 12 -> 13, of which waited for: 6 -> 5; matrix products, arithmetic and copies ran while one was open for 2% -> 2% of each run, Pallas kernels for 28% -> 30%
where the time goes in v13:
time: 49.9 us; the launch traced here: 49.7 us
  starting transfers between devices  20.8 us (42%)
  Pallas kernels  20.1 us (40%)
  waiting for transfers between devices  6.1 us (12%)
  other arithmetic  1.14 us (2%)
  local copies, waits for them, and re-layouts  1.08 us (2%)
  between operations  0.52 us (1%)
    ppermute x8, starting transfers between devices, from_partner(): lax.ppermute(shard, axis, [(i, i ^ by) for i in range(lax.axis_size(axis))])  13.8 us
    ppermute x2, starting transfers between devices, across(): lax.ppermute(sent, 'ctx', [(hop, hop + 2), (hop + 1, hop + 3)])  6.81 us
    pallas_call x2, Pallas kernels, gates(): pl.pallas_call(gate_kernel, in_specs=[pl.BlockSpec(memory_space=pltpu.SME...  5.05 us
    pallas_call x1, Pallas kernels, front(): pl.pallas_call(front_kernel, in_specs=[ANYWHERE] * 6, out_specs=[WHOLE] *...  4.66 us
    ppermute x8, waiting for transfers between devices, from_partner(): lax.ppermute(shard, axis, [(i, i ^ by) for i in range(lax.axis_size(axis))])  4.65 us
    pallas_call x2, Pallas kernels, final(): pl.pallas_call(final_kernel, in_specs=[pl.BlockSpec(memory_space=pltpu.SM...  4.47 us
    pallas_call x1, Pallas kernels, normed(): pl.pallas_call(functools.partial(norm_kernel, all_channels), in_specs=[pl...  3.1 us
    pallas_call x2, Pallas kernels, own_states(): pl.pallas_call(state_kernel, in_specs=[WHOLE] * 3, out_specs=[WHOLE] * 2,...  2.52 us
  transfers between devices with their start and end apart: 13, of which 5 were waited for; matrix products, arithmetic and copies ran while one was open for 2% of the time, Pallas kernels for 30%

profile of v13, /device:TPU:0, one launch (start us, length us, event | category | flops | bytes accessed | tf_op | source)
XLA Modules:
  0.0 49.7 jit_solution(5177767692288276733)
XLA Ops:
  0.0 1.0 %slice_bitcast_fusion = (bf16[2,32,768]{2,1,0:T(8,128)(2,1)S(1)}, bf16[2,32,768]{2,1,0:T(8,128)(2,1)S(1)}) fusion(bf16[2,2,32,768]{3,2,1,0:T(8,128)(2,1)} %param.11), kind=kLoop, calls=%fused_computation.22 | loop fusion | bytes 393216 | tf_op jit(solution)/shard_map/squeeze | solution.py:367
  1.0 5.1 %collective-permute-start.2 = (bf16[2,32,768]{2,1,0:T(8,128)(2,1)S(1)}, bf16[2,32,768]{2,1,0:T(8,128)(2,1)S(1)}, u32[]{:S(2)}, u32[]{:S(2)}) collective-permute-start(bf16[2,32,768]{2,1,0:T(8,128)(2,1)S(1)} %get-tuple-element.39), channel_id=1, source_target_pairs={{0,3},{1,2},{2,1},{3,0},{4,7},{5,6},{6,5},{7,4},{8,11},{9,10},{10,... | collective-permute-start | bytes 294920 | tf_op jit(solution)/shard_map/ppermute | solution.py:341
  6.1 0.6 %collective-permute-start = (bf16[2,32,768]{2,1,0:T(8,128)(2,1)S(1)}, bf16[2,32,768]{2,1,0:T(8,128)(2,1)S(1)}, u32[]{:S(2)}, u32[]{:S(2)}) collective-permute-start(bf16[2,32,768]{2,1,0:T(8,128)(2,1)S(1)} %get-tuple-element.39), channel_id=1, source_target_pairs={{0,1},{1,0},{2,3},{3,2},{4,5},{5,4},{6,7},{7,6},{8,9},{9,8},{10,11... | collective-permute-start | bytes 294920 | tf_op jit(solution)/shard_map/ppermute | solution.py:341
  6.7 4.7 %front.1 = (bf16[2,768,2048]{2,1,0:T(8,128)(2,1)S(1)}, bf16[2,768,128]{2,1,0:T(8,128)(2,1)S(1)}, f32[2,32,2048]{2,1,0:T(8,128)S(1)}, bf16[192,2048]{1,0:T(8,128)(2,1)S(1)}) custom-call(bf16[2,768,2048]{2,1,0:T(8,128)(2,1)} %x_ref.3, f32[2,32,768]{2,1,0:T(8,128)} %step_hbm.1, f32[2,32,768]{2,1,0:T(8,128)} %decay_hbm.1, f32[1,32]{1,0:T(1,128)} %bitcast.40, ...), custom_call_target="tpu_custom_call" | custom-call | flops 1000 | bytes 1000 | tf_op jit(solution)/shard_map/front/pallas_call | solution.py:127
  11.5 0.1 pad.20.clone
  11.5 0.9 %collective-permute-done = bf16[2,32,768]{2,1,0:T(8,128)(2,1)S(1)} collective-permute-done((bf16[2,32,768]{2,1,0:T(8,128)(2,1)S(1)}, bf16[2,32,768]{2,1,0:T(8,128)(2,1)S(1)}, u32[]{:S(2)}, u32[]{:S(2)}) %collective-permute-start) | collective-permute-done | bytes 98336 | tf_op jit(solution)/shard_map/ppermute | solution.py:341
  12.4 1.3 %own_states.2 = (bf16[2,5,64,2048]{3,2,1,0:T(8,128)(2,1)S(1)}, bf16[2,64,2048]{2,1,0:T(8,128)(2,1)S(1)}) custom-call(bf16[2,64,768]{2,1,0:T(8,128)(2,1)S(1)} %pad_maximum_fusion.3.b_ref, bf16[2,768,2048]{2,1,0:T(8,128)(2,1)S(1)} %get-tuple-element.38.weighted_ref, f32[2,32,2048]{2,1,0:T(8,128)S(1)} %get-tuple-element.40.rows_ref), custom_call_target="tpu_custom_call" | custom-call | flops 1000 | bytes 1000 | tf_op jit(solution)/shard_map/own_states/pallas_call | solution.py:173
  13.7 0.1 bitcast_convert_fusion.1
  13.7 0.1 maximum_maximum_fusion
  13.9 0.1 collective-permute-start.3
  14.0 2.6 %collective-permute-start.7 = (bf16[2,32,768]{2,1,0:T(8,128)(2,1)S(1)}, bf16[2,32,768]{2,1,0:T(8,128)(2,1)S(1)}, u32[]{:S(2)}, u32[]{:S(2)}) collective-permute-start(bf16[2,32,768]{2,1,0:T(8,128)(2,1)S(1)} %get-tuple-element.50), channel_id=1, source_target_pairs={{0,1},{1,0},{2,3},{3,2},{4,5},{5,4},{6,7},{7,6},{8,9},{9,8},{10,11... | collective-permute-start | bytes 294920 | tf_op jit(solution)/shard_map/ppermute | solution.py:341
  16.5 0.2 select_convert_fusion.1
  16.7 3.4 %collective-permute-start.4 = (bf16[64,2048]{1,0:T(8,128)(2,1)S(1)}, bf16[64,2048]{1,0:T(8,128)(2,1)S(1)}, u32[]{:S(2)}, u32[]{:S(2)}) collective-permute-start(bf16[64,2048]{1,0:T(8,128)(2,1)S(1)} %select_convert_fusion.1), channel_id=1, source_target_pairs={{0,8},{4,12},{1,9},{5,13},{2,10},{6,14},{3,11},{7,15},{16,24},{20,... | collective-permute-start | bytes 786440 | tf_op jit(solution)/shard_map/ppermute | solution.py:389
  20.2 1.0 %collective-permute-start.8 = (bf16[2,64,768]{2,1,0:T(8,128)(2,1)S(1)}, bf16[2,64,768]{2,1,0:T(8,128)(2,1)S(1)}, u32[]{:S(2)}, u32[]{:S(2)}) collective-permute-start(bf16[2,64,768]{2,1,0:T(8,128)(2,1)S(1)} %pad_maximum_fusion.5), channel_id=1, source_target_pairs={{0,2},{1,3},{2,0},{3,1},{4,6},{5,7},{6,4},{7,5},{8,10},{9,11},{10,... | collective-permute-start | bytes 589832 | tf_op jit(solution)/shard_map/ppermute | solution.py:341
  21.3 1.3 %own_states.3 = (bf16[2,5,64,2048]{3,2,1,0:T(8,128)(2,1)S(1)}, bf16[2,64,2048]{2,1,0:T(8,128)(2,1)S(1)}) custom-call(bf16[2,64,768]{2,1,0:T(8,128)(2,1)S(1)} %pad_maximum_fusion.4.b_ref, bf16[2,768,2048]{2,1,0:T(8,128)(2,1)S(1)} %get-tuple-element.38.weighted_ref, f32[2,32,2048]{2,1,0:T(8,128)S(1)} %get-tuple-element.40.rows_ref), custom_call_target="tpu_custom_call" | custom-call | flops 1000 | bytes 1000 | tf_op jit(solution)/shard_map/own_states/pallas_call | solution.py:173
  22.6 0.1 collective-permute-start.5
  22.8 1.4 %collective-permute-done.5 = bf16[64,2048]{1,0:T(8,128)(2,1)S(1)} collective-permute-done((bf16[64,2048]{1,0:T(8,128)(2,1)S(1)}, bf16[64,2048]{1,0:T(8,128)(2,1)S(1)}, u32[]{:S(2)}, u32[]{:S(2)}) %collective-permute-start.5) | collective-permute-done | bytes 262176 | tf_op jit(solution)/shard_map/ppermute | solution.py:411
  24.2 0.2 select_convert_fusion
  24.4 3.4 %collective-permute-start.6 = (bf16[64,2048]{1,0:T(8,128)(2,1)S(1)}, bf16[64,2048]{1,0:T(8,128)(2,1)S(1)}, u32[]{:S(2)}, u32[]{:S(2)}) collective-permute-start(bf16[64,2048]{1,0:T(8,128)(2,1)S(1)} %select_convert_fusion), channel_id=1, source_target_pairs={{0,8},{4,12},{1,9},{5,13},{2,10},{6,14},{3,11},{7,15},{16,24},{20,... | collective-permute-start | bytes 786440 | tf_op jit(solution)/shard_map/ppermute | solution.py:389
  27.8 2.5 %gates.2 = (bf16[768,2048]{1,0:T(8,128)(2,1)S(1)}, bf16[768,2048]{1,0:T(8,128)(2,1)S(1)}) custom-call(s32[1]{0:T(128)} %bitcast.seq_ref, bf16[2,768,2048]{2,1,0:T(8,128)(2,1)S(1)} %bitcast.32, bf16[2,768,2048]{2,1,0:T(8,128)(2,1)S(1)} %bitcast.30, bf16[2,768,128]{2,1,0:T(8,128)(2,1)S(1)} %get-tuple-element.57.both_ref, ...), custom_call_target="tpu_custom_call" | custom-call | flops 1000000000 | bytes 12000000 | tf_op jit(solution)/shard_map/gates/pallas_call | solution.py:206
  30.4 1.8 %collective-permute-done.8 = bf16[2,64,768]{2,1,0:T(8,128)(2,1)S(1)} collective-permute-done((bf16[2,64,768]{2,1,0:T(8,128)(2,1)S(1)}, bf16[2,64,768]{2,1,0:T(8,128)(2,1)S(1)}, u32[]{:S(2)}, u32[]{:S(2)}) %collective-permute-start.8) | collective-permute-done | bytes 196640 | tf_op jit(solution)/shard_map/ppermute | solution.py:341
  32.2 0.3 left.1.left_ref
  32.5 2.5 %gates.3 = (bf16[768,2048]{1,0:T(8,128)(2,1)S(1)}, bf16[768,2048]{1,0:T(8,128)(2,1)S(1)}) custom-call(s32[1]{0:T(128)S(6)} %sub.16.seq_ref, bf16[2,768,2048]{2,1,0:T(8,128)(2,1)S(1)} %bitcast.32, bf16[2,768,2048]{2,1,0:T(8,128)(2,1)S(1)} %bitcast.30, bf16[2,768,128]{2,1,0:T(8,128)(2,1)S(1)} %get-tuple-element.57.both_ref, ...), custom_call_target="tpu_custom_call" | custom-call | flops 1000000000 | bytes 12000000 | tf_op jit(solution)/shard_map/gates/pallas_call | solution.py:206
  35.1 0.3 fusion.3
  35.4 0.1 collective-permute-start.9
  35.5 2.2 %final.2 = (bf16[768,2048]{1,0:T(8,128)(2,1)S(1)}, f32[8,128]{1,0:T(8,128)S(1)}) custom-call(s32[1]{0:T(128)} %bitcast.seq_ref, bf16[2,768,2048]{2,1,0:T(8,128)(2,1)S(1)} %get-tuple-element.38.weighted_ref, bf16[2,5,64,2048]{3,2,1,0:T(8,128)(2,1)S(1)} %get-tuple-element.41.near_ref, bf16[2,5,64,2048]{3,2,1,0:T(8,128)(2,1)S(1)} %get-tuple-element.45.far_ref, ...), custom_call_target="tpu_custom_call" | custom-call | flops 1000 | bytes 1000 | tf_op jit(solution)/shard_map/final/pallas_call | solution.py:276
  37.8 2.2 %final.3 = (bf16[768,2048]{1,0:T(8,128)(2,1)S(1)}, f32[8,128]{1,0:T(8,128)S(1)}) custom-call(s32[1]{0:T(128)S(6)} %sub.16.seq_ref, bf16[2,768,2048]{2,1,0:T(8,128)(2,1)S(1)} %get-tuple-element.38.weighted_ref, bf16[2,5,64,2048]{3,2,1,0:T(8,128)(2,1)S(1)} %get-tuple-element.41.near_ref, bf16[2,5,64,2048]{3,2,1,0:T(8,128)(2,1)S(1)} %get-tuple-element.45.far_ref, ...), custom_call_target="tpu_custom_call" | custom-call | flops 1000 | bytes 1000 | tf_op jit(solution)/shard_map/final/pallas_call | solution.py:276
  40.0 1.9 %collective-permute-start.12 = (f32[16,128]{1,0:T(8,128)S(1)}, f32[16,128]{1,0:T(8,128)S(1)}, u32[]{:S(2)}, u32[]{:S(2)}) collective-permute-start(f32[16,128]{1,0:T(8,128)S(1)} %constant_dynamic-update-slice_fusion), channel_id=1, source_target_pairs={{0,3},{1,2},{2,1},{3,0},{4,7},{5,6},{6,5},{7,4},{8,11},{9,10},{10,... | collective-permute-start | bytes 24584 | tf_op jit(solution)/shard_map/ppermute | solution.py:341
  41.9 2.5 %collective-permute-start.10 = (f32[16,128]{1,0:T(8,128)S(1)}, f32[16,128]{1,0:T(8,128)S(1)}, u32[]{:S(2)}, u32[]{:S(2)}) collective-permute-start(f32[16,128]{1,0:T(8,128)S(1)} %constant_dynamic-update-slice_fusion), channel_id=1, source_target_pairs={{0,1},{1,0},{2,3},{3,2},{4,5},{5,4},{6,7},{7,6},{8,9},{9,8},{10,11... | collective-permute-start | bytes 24584 | tf_op jit(solution)/shard_map/ppermute | solution.py:341
  44.5 1.1 %collective-permute-done.12 = f32[16,128]{1,0:T(8,128)S(1)} collective-permute-done((f32[16,128]{1,0:T(8,128)S(1)}, f32[16,128]{1,0:T(8,128)S(1)}, u32[]{:S(2)}, u32[]{:S(2)}) %collective-permute-start.12) | collective-permute-done | bytes 8224 | tf_op jit(solution)/shard_map/ppermute | solution.py:341
  45.5 0.9 %collective-permute-done.11 = f32[16,128]{1,0:T(8,128)S(1)} collective-permute-done((f32[16,128]{1,0:T(8,128)S(1)}, f32[16,128]{1,0:T(8,128)S(1)}, u32[]{:S(2)}, u32[]{:S(2)}) %collective-permute-start.11) | collective-permute-done | bytes 8224 | tf_op jit(solution)/shard_map/ppermute | solution.py:341
  46.5 3.1 %normed.1 = bf16[2,768,2048]{2,1,0:T(8,128)(2,1)} custom-call(s32[1]{0:T(128)} %bitcast.seq_ref, f32[16,128]{1,0:T(8,128)S(1)} %add_add_fusion.square_ref, f32[1,2048]{1,0:T(1,128)S(1)} %bitcast.33, bf16[768,2048]{1,0:T(8,128)(2,1)S(1)} %get-tuple-element.69.refs_0_, bf16[768,2048]{1,0:T(8,128)(2,1)S(1)} %get-tuple-element.70.refs_1_), custom_call_target="tpu_custom_call" | custom-call | flops 1000 | bytes 1000 | tf_op jit(solution)/shard_map/normed/pallas_call | solution.py:325
  (38 shorter events, 0.4 us)
Async XLA Ops:
  1.0 19.2 %collective-permute-start.2 = (bf16[2,32,768]{2,1,0:T(8,128)(2,1)S(1)}, bf16[2,32,768]{2,1,0:T(8,128)(2,1)S(1)}, u32[]{:S(2)}, u32[]{:S(2)}) collective-permute-start(bf16[2,32,768]{2,1,0:T(8,128)(2,1)S(1)} %get-tuple-element.39), channel_id=1, source_target_pairs={{0,3},{1,2},{2,1},{3,0},{4,7},{5,6},{6,5},{7,4},{8,11},{9,10},{10,... | collective-permute-start | bytes 294920 | tf_op jit(solution)/shard_map/ppermute | solution.py:341
  6.1 14.1 %collective-permute-start.1 = (bf16[2,32,768]{2,1,0:T(8,128)(2,1)S(1)}, bf16[2,32,768]{2,1,0:T(8,128)(2,1)S(1)}, u32[]{:S(2)}, u32[]{:S(2)}) collective-permute-start(bf16[2,32,768]{2,1,0:T(8,128)(2,1)S(1)} %get-tuple-element.39), channel_id=1, source_target_pairs={{0,2},{1,3},{2,0},{3,1},{4,6},{5,7},{6,4},{7,5},{8,10},{9,11},{10,... | collective-permute-start | bytes 294920 | tf_op jit(solution)/shard_map/ppermute | solution.py:341
  6.1 6.3 %collective-permute-start = (bf16[2,32,768]{2,1,0:T(8,128)(2,1)S(1)}, bf16[2,32,768]{2,1,0:T(8,128)(2,1)S(1)}, u32[]{:S(2)}, u32[]{:S(2)}) collective-permute-start(bf16[2,32,768]{2,1,0:T(8,128)(2,1)S(1)} %get-tuple-element.39), channel_id=1, source_target_pairs={{0,1},{1,0},{2,3},{3,2},{4,5},{5,4},{6,7},{7,6},{8,9},{9,8},{10,11... | collective-permute-start | bytes 294920 | tf_op jit(solution)/shard_map/ppermute | solution.py:341
  6.7 21.1 %slice-start.2 = ((s8[6291456]{0:T(1024)(128)(4,1)}), s8[4194304]{0:T(1024)(128)(4,1)S(1)}, s32[]{:S(2)}) async-start(s8[6291456]{0:T(1024)(128)(4,1)} %bitcast.31), calls=%async_computation.2 | async-start | bytes 8388608
  12.4 15.4 %slice-start.3 = ((s8[6291456]{0:T(1024)(128)(4,1)}), s8[2097152]{0:T(1024)(128)(4,1)S(1)}, s32[]{:S(2)}) async-start(s8[6291456]{0:T(1024)(128)(4,1)} %bitcast.31), calls=%async_computation.3 | async-start | bytes 4194304
  13.9 2.7 %collective-permute-start.3 = (bf16[80,2048]{1,0:T(8,128)(2,1)S(1)}, bf16[80,2048]{1,0:T(8,128)(2,1)S(1)}, u32[]{:S(2)}, u32[]{:S(2)}) collective-permute-start(bf16[80,2048]{1,0:T(8,128)(2,1)S(1)} %maximum_maximum_fusion), channel_id=1, source_target_pairs={{0,4},{4,0},{8,12},{12,8},{1,5},{5,1},{9,13},{13,9},{2,6},{6,2},{1... | collective-permute-start | bytes 983048 | tf_op jit(solution)/shard_map/ppermute | solution.py:393
  14.0 6.2 %collective-permute-start.7 = (bf16[2,32,768]{2,1,0:T(8,128)(2,1)S(1)}, bf16[2,32,768]{2,1,0:T(8,128)(2,1)S(1)}, u32[]{:S(2)}, u32[]{:S(2)}) collective-permute-start(bf16[2,32,768]{2,1,0:T(8,128)(2,1)S(1)} %get-tuple-element.50), channel_id=1, source_target_pairs={{0,1},{1,0},{2,3},{3,2},{4,5},{5,4},{6,7},{7,6},{8,9},{9,8},{10,11... | collective-permute-start | bytes 294920 | tf_op jit(solution)/shard_map/ppermute | solution.py:341
  16.7 18.4 %collective-permute-start.4 = (bf16[64,2048]{1,0:T(8,128)(2,1)S(1)}, bf16[64,2048]{1,0:T(8,128)(2,1)S(1)}, u32[]{:S(2)}, u32[]{:S(2)}) collective-permute-start(bf16[64,2048]{1,0:T(8,128)(2,1)S(1)} %select_convert_fusion.1), channel_id=1, source_target_pairs={{0,8},{4,12},{1,9},{5,13},{2,10},{6,14},{3,11},{7,15},{16,24},{20,... | collective-permute-start | bytes 786440 | tf_op jit(solution)/shard_map/ppermute | solution.py:389
  20.2 7.6 %slice-start = ((s8[6291456]{0:T(1024)(128)(4,1)}), s8[4194304]{0:T(1024)(128)(4,1)S(1)}, s32[]{:S(2)}) async-start(s8[6291456]{0:T(1024)(128)(4,1)} %bitcast.29), calls=%async_computation | async-start | bytes 8388608
  20.2 7.6 %slice-start.1 = ((s8[6291456]{0:T(1024)(128)(4,1)}), s8[2097152]{0:T(1024)(128)(4,1)S(1)}, s32[]{:S(2)}) async-start(s8[6291456]{0:T(1024)(128)(4,1)} %bitcast.29), calls=%async_computation.1 | async-start | bytes 4194304
  20.2 11.9 %collective-permute-start.8 = (bf16[2,64,768]{2,1,0:T(8,128)(2,1)S(1)}, bf16[2,64,768]{2,1,0:T(8,128)(2,1)S(1)}, u32[]{:S(2)}, u32[]{:S(2)}) collective-permute-start(bf16[2,64,768]{2,1,0:T(8,128)(2,1)S(1)} %pad_maximum_fusion.5), channel_id=1, source_target_pairs={{0,2},{1,3},{2,0},{3,1},{4,6},{5,7},{6,4},{7,5},{8,10},{9,11},{10,... | collective-permute-start | bytes 589832 | tf_op jit(solution)/shard_map/ppermute | solution.py:341
  22.6 1.6 %collective-permute-start.5 = (bf16[64,2048]{1,0:T(8,128)(2,1)S(1)}, bf16[64,2048]{1,0:T(8,128)(2,1)S(1)}, u32[]{:S(2)}, u32[]{:S(2)}) collective-permute-start(bf16[64,2048]{1,0:T(8,128)(2,1)S(1)} %get-tuple-element.76), channel_id=1, source_target_pairs={{0,4},{4,0},{8,12},{12,8},{1,5},{5,1},{9,13},{13,9},{2,6},{6,2},{1... | collective-permute-start | bytes 786440 | tf_op jit(solution)/shard_map/ppermute | solution.py:411
  24.4 10.7 %collective-permute-start.6 = (bf16[64,2048]{1,0:T(8,128)(2,1)S(1)}, bf16[64,2048]{1,0:T(8,128)(2,1)S(1)}, u32[]{:S(2)}, u32[]{:S(2)}) collective-permute-start(bf16[64,2048]{1,0:T(8,128)(2,1)S(1)} %select_convert_fusion), channel_id=1, source_target_pairs={{0,8},{4,12},{1,9},{5,13},{2,10},{6,14},{3,11},{7,15},{16,24},{20,... | collective-permute-start | bytes 786440 | tf_op jit(solution)/shard_map/ppermute | solution.py:389
  35.4 2.3 %collective-permute-start.9 = (bf16[128,2048]{1,0:T(8,128)(2,1)S(1)}, bf16[128,2048]{1,0:T(8,128)(2,1)S(1)}, u32[]{:S(2)}, u32[]{:S(2)}) collective-permute-start(bf16[128,2048]{1,0:T(8,128)(2,1)S(1)} %get-tuple-element.71), channel_id=1, source_target_pairs={{0,4},{4,0},{8,12},{12,8},{1,5},{5,1},{9,13},{13,9},{2,6},{6,2},{1... | collective-permute-start | bytes 1572872 | tf_op jit(solution)/shard_map/ppermute | solution.py:433
  37.7 8.7 %copy-start = (f32[2048]{0:T(1024)S(1)}, f32[2048]{0:T(1024)}, u32[]{:S(2)}) copy-start(f32[2048]{0:T(1024)} %param.15) | copy-start | bytes 24580
  40.0 5.5 %collective-permute-start.12 = (f32[16,128]{1,0:T(8,128)S(1)}, f32[16,128]{1,0:T(8,128)S(1)}, u32[]{:S(2)}, u32[]{:S(2)}) collective-permute-start(f32[16,128]{1,0:T(8,128)S(1)} %constant_dynamic-update-slice_fusion), channel_id=1, source_target_pairs={{0,3},{1,2},{2,1},{3,0},{4,7},{5,6},{6,5},{7,4},{8,11},{9,10},{10,... | collective-permute-start | bytes 24584 | tf_op jit(solution)/shard_map/ppermute | solution.py:341
  41.9 4.5 %collective-permute-start.11 = (f32[16,128]{1,0:T(8,128)S(1)}, f32[16,128]{1,0:T(8,128)S(1)}, u32[]{:S(2)}, u32[]{:S(2)}) collective-permute-start(f32[16,128]{1,0:T(8,128)S(1)} %constant_dynamic-update-slice_fusion), channel_id=1, source_target_pairs={{0,2},{1,3},{2,0},{3,1},{4,6},{5,7},{6,4},{7,5},{8,10},{9,11},{10,... | collective-permute-start | bytes 24584 | tf_op jit(solution)/shard_map/ppermute | solution.py:341
  41.9 4.5 %collective-permute-start.10 = (f32[16,128]{1,0:T(8,128)S(1)}, f32[16,128]{1,0:T(8,128)S(1)}, u32[]{:S(2)}, u32[]{:S(2)}) collective-permute-start(f32[16,128]{1,0:T(8,128)S(1)} %constant_dynamic-update-slice_fusion), channel_id=1, source_target_pairs={{0,1},{1,0},{2,3},{3,2},{4,5},{5,4},{6,7},{7,6},{8,9},{9,8},{10,11... | collective-permute-start | bytes 24584 | tf_op jit(solution)/shard_map/ppermute | solution.py:341

commit v14 on v13

--- a/solution.py
+++ b/solution.py
@@ -408,20 +408,19 @@
     b_far, _ = lax.optimization_barrier((b_pieces[2:], near_sent))
     b_far = jnp.concatenate(b_far, axis=1)
     far, far_ends = own_states(b_far, weighted, rows)
-    far_other = lax.ppermute(jnp.where(even, far_ends[1], far_ends[0]), "ctx", swap).astype(F32)
+    far_swap = jnp.where(even, far_ends[1], far_ends[0])
+    far_other = lax.ppermute(far_swap, "ctx", swap).astype(F32)
     far_end = jnp.where(even, far_ends[0], far_ends[1]).astype(F32)
     far_past = past_chip(far_end, far_other, decay_other)
     far_sent, far_got = across(far_past, None, 0)
     c_own, _ = lax.optimization_barrier((c_own, near_ends))
-    c = doubled(c_own, "head", 1, near_sent)
+    c = doubled(c_own, "head", 1, far_swap)
     both, _ = lax.optimization_barrier((both, far_sent))
     lifts = gates(mine, gate_in, features, both, bands, rows)
+    lifts_next = gates(1 - mine, gate_in, features, both, bands, rows)
     for by in (1 << i for i in range(1, (lax.axis_size("head") - 1).bit_length())):
-        c = doubled(c, "head", by, lifts)
-    both, c = lax.optimization_barrier((both, c))
-    lifts_next = gates(1 - mine, gate_in, features, both, bands, rows)
+        c = doubled(c, "head", by, (lifts, lifts_next))
     left = left_of(jnp.concatenate([b_near, b_far], axis=1), c)
-    left, lifts_next = lax.optimization_barrier((left, lifts_next))
     near_got, far_got, left = lax.optimization_barrier((near_got, far_got, left))
     for hop in range(2, devices - 2, 2):
         near_got = near_got + across(near_past, near_got, hop)[1]

time: 49.9 us -> 49.7 us (level)
  starting transfers between devices: 20.8 us -> 19.2 us
  waiting for transfers between devices: 6.1 us -> 7.51 us
    ppermute x8, waiting for transfers between devices: 4.65 us -> 7.11 us  [from_partner(): lax.ppermute(shard, axis, [(i, i ^ by) for i in range(lax.axis_size(axis))])]
    ppermute x2, starting transfers between devices: 6.81 us -> 5.16 us  [across(): lax.ppermute(sent, 'ctx', [(hop, hop + 2), (hop + 1, hop + 3)])]
    ppermute x1, waiting for transfers between devices: 1.44 us -> 0.39 us  [body(): far_other = lax.ppermute(far_swap, 'ctx', swap).astype(F32)]
where the time goes in v14:
time: 49.7 us; the launch traced here: 49.5 us
  Pallas kernels  20.1 us (40%)
  starting transfers between devices  19.2 us (39%)
  waiting for transfers between devices  7.51 us (15%)
  other arithmetic  1.15 us (2%)
  local copies, waits for them, and re-layouts  1.08 us (2%)
  between operations  0.52 us (1%)
    ppermute x8, starting transfers between devices, from_partner(): lax.ppermute(shard, axis, [(i, i ^ by) for i in range(lax.axis_size(axis))])  13.8 us
    ppermute x8, waiting for transfers between devices, from_partner(): lax.ppermute(shard, axis, [(i, i ^ by) for i in range(lax.axis_size(axis))])  7.11 us
    ppermute x2, starting transfers between devices, across(): lax.ppermute(sent, 'ctx', [(hop, hop + 2), (hop + 1, hop + 3)])  5.16 us
    pallas_call x2, Pallas kernels, gates(): pl.pallas_call(gate_kernel, in_specs=[pl.BlockSpec(memory_space=pltpu.SME...  5.05 us
    pallas_call x1, Pallas kernels, front(): pl.pallas_call(front_kernel, in_specs=[ANYWHERE] * 6, out_specs=[WHOLE] *...  4.66 us
    pallas_call x2, Pallas kernels, final(): pl.pallas_call(final_kernel, in_specs=[pl.BlockSpec(memory_space=pltpu.SM...  4.48 us
    pallas_call x1, Pallas kernels, normed(): pl.pallas_call(functools.partial(norm_kernel, all_channels), in_specs=[pl...  3.1 us
    pallas_call x2, Pallas kernels, own_states(): pl.pallas_call(state_kernel, in_specs=[WHOLE] * 3, out_specs=[WHOLE] * 2,...  2.53 us
  transfers between devices with their start and end apart: 13, of which 5 were waited for; matrix products, arithmetic and copies ran while one was open for 2% of the time, Pallas kernels for 30%

profile of v14, /device:TPU:0, one launch (start us, length us, event | category | flops | bytes accessed | tf_op | source)
XLA Modules:
  0.0 49.5 jit_solution(1575938665884802397)
XLA Ops:
  0.0 1.0 %slice_bitcast_fusion = (bf16[2,32,768]{2,1,0:T(8,128)(2,1)S(1)}, bf16[2,32,768]{2,1,0:T(8,128)(2,1)S(1)}) fusion(bf16[2,2,32,768]{3,2,1,0:T(8,128)(2,1)} %param.11), kind=kLoop, calls=%fused_computation.22 | loop fusion | bytes 393216 | tf_op jit(solution)/shard_map/squeeze | solution.py:367
  1.0 5.1 %collective-permute-start.2 = (bf16[2,32,768]{2,1,0:T(8,128)(2,1)S(1)}, bf16[2,32,768]{2,1,0:T(8,128)(2,1)S(1)}, u32[]{:S(2)}, u32[]{:S(2)}) collective-permute-start(bf16[2,32,768]{2,1,0:T(8,128)(2,1)S(1)} %get-tuple-element.34), channel_id=1, source_target_pairs={{0,3},{1,2},{2,1},{3,0},{4,7},{5,6},{6,5},{7,4},{8,11},{9,10},{10,... | collective-permute-start | bytes 294920 | tf_op jit(solution)/shard_map/ppermute | solution.py:341
  6.1 0.6 %collective-permute-start = (bf16[2,32,768]{2,1,0:T(8,128)(2,1)S(1)}, bf16[2,32,768]{2,1,0:T(8,128)(2,1)S(1)}, u32[]{:S(2)}, u32[]{:S(2)}) collective-permute-start(bf16[2,32,768]{2,1,0:T(8,128)(2,1)S(1)} %get-tuple-element.34), channel_id=1, source_target_pairs={{0,1},{1,0},{2,3},{3,2},{4,5},{5,4},{6,7},{7,6},{8,9},{9,8},{10,11... | collective-permute-start | bytes 294920 | tf_op jit(solution)/shard_map/ppermute | solution.py:341
  6.7 4.7 %front.1 = (bf16[2,768,2048]{2,1,0:T(8,128)(2,1)S(1)}, bf16[2,768,128]{2,1,0:T(8,128)(2,1)S(1)}, f32[2,32,2048]{2,1,0:T(8,128)S(1)}, bf16[192,2048]{1,0:T(8,128)(2,1)S(1)}) custom-call(bf16[2,768,2048]{2,1,0:T(8,128)(2,1)} %x_ref.3, f32[2,32,768]{2,1,0:T(8,128)} %step_hbm.1, f32[2,32,768]{2,1,0:T(8,128)} %decay_hbm.1, f32[1,32]{1,0:T(1,128)} %bitcast.40, ...), custom_call_target="tpu_custom_call" | custom-call | flops 1000 | bytes 1000 | tf_op jit(solution)/shard_map/front/pallas_call | solution.py:127
  11.5 0.1 pad.20.clone
  11.5 0.9 %collective-permute-done = bf16[2,32,768]{2,1,0:T(8,128)(2,1)S(1)} collective-permute-done((bf16[2,32,768]{2,1,0:T(8,128)(2,1)S(1)}, bf16[2,32,768]{2,1,0:T(8,128)(2,1)S(1)}, u32[]{:S(2)}, u32[]{:S(2)}) %collective-permute-start) | collective-permute-done | bytes 98336 | tf_op jit(solution)/shard_map/ppermute | solution.py:341
  12.4 1.3 %own_states.2 = (bf16[2,5,64,2048]{3,2,1,0:T(8,128)(2,1)S(1)}, bf16[2,64,2048]{2,1,0:T(8,128)(2,1)S(1)}) custom-call(bf16[2,64,768]{2,1,0:T(8,128)(2,1)S(1)} %pad_maximum_fusion.3.b_ref, bf16[2,768,2048]{2,1,0:T(8,128)(2,1)S(1)} %get-tuple-element.33.weighted_ref, f32[2,32,2048]{2,1,0:T(8,128)S(1)} %get-tuple-element.35.rows_ref), custom_call_target="tpu_custom_call" | custom-call | flops 1000 | bytes 1000 | tf_op jit(solution)/shard_map/own_states/pallas_call | solution.py:173
  13.7 0.1 bitcast_convert_fusion.1
  13.7 0.1 maximum_maximum_fusion
  13.9 0.1 collective-permute-start.3
  14.0 2.6 %collective-permute-start.7 = (bf16[2,32,768]{2,1,0:T(8,128)(2,1)S(1)}, bf16[2,32,768]{2,1,0:T(8,128)(2,1)S(1)}, u32[]{:S(2)}, u32[]{:S(2)}) collective-permute-start(bf16[2,32,768]{2,1,0:T(8,128)(2,1)S(1)} %get-tuple-element.43), channel_id=1, source_target_pairs={{0,1},{1,0},{2,3},{3,2},{4,5},{5,4},{6,7},{7,6},{8,9},{9,8},{10,11... | collective-permute-start | bytes 294920 | tf_op jit(solution)/shard_map/ppermute | solution.py:341
  16.5 0.2 select_convert_fusion.1
  16.8 3.7 %collective-permute-start.4 = (bf16[64,2048]{1,0:T(8,128)(2,1)S(1)}, bf16[64,2048]{1,0:T(8,128)(2,1)S(1)}, u32[]{:S(2)}, u32[]{:S(2)}) collective-permute-start(bf16[64,2048]{1,0:T(8,128)(2,1)S(1)} %select_convert_fusion.1), channel_id=1, source_target_pairs={{0,8},{4,12},{1,9},{5,13},{2,10},{6,14},{3,11},{7,15},{16,24},{20,... | collective-permute-start | bytes 786440 | tf_op jit(solution)/shard_map/ppermute | solution.py:389
  20.5 1.3 %own_states.3 = (bf16[2,5,64,2048]{3,2,1,0:T(8,128)(2,1)S(1)}, bf16[2,64,2048]{2,1,0:T(8,128)(2,1)S(1)}) custom-call(bf16[2,64,768]{2,1,0:T(8,128)(2,1)S(1)} %pad_maximum_fusion.4.b_ref, bf16[2,768,2048]{2,1,0:T(8,128)(2,1)S(1)} %get-tuple-element.33.weighted_ref, f32[2,32,2048]{2,1,0:T(8,128)S(1)} %get-tuple-element.35.rows_ref), custom_call_target="tpu_custom_call" | custom-call | flops 1000 | bytes 1000 | tf_op jit(solution)/shard_map/own_states/pallas_call | solution.py:173
  21.8 0.1 collective-permute-start.5
  21.9 1.0 %collective-permute-start.8 = (bf16[2,64,768]{2,1,0:T(8,128)(2,1)S(1)}, bf16[2,64,768]{2,1,0:T(8,128)(2,1)S(1)}, u32[]{:S(2)}, u32[]{:S(2)}) collective-permute-start(bf16[2,64,768]{2,1,0:T(8,128)(2,1)S(1)} %pad_maximum_fusion.5), channel_id=1, source_target_pairs={{0,2},{1,3},{2,0},{3,1},{4,6},{5,7},{6,4},{7,5},{8,10},{9,11},{10,... | collective-permute-start | bytes 589832 | tf_op jit(solution)/shard_map/ppermute | solution.py:341
  23.0 0.4 collective-permute-done.5
  23.4 0.2 select_convert_fusion
  23.6 1.5 %collective-permute-start.6 = (bf16[64,2048]{1,0:T(8,128)(2,1)S(1)}, bf16[64,2048]{1,0:T(8,128)(2,1)S(1)}, u32[]{:S(2)}, u32[]{:S(2)}) collective-permute-start(bf16[64,2048]{1,0:T(8,128)(2,1)S(1)} %select_convert_fusion), channel_id=1, source_target_pairs={{0,8},{4,12},{1,9},{5,13},{2,10},{6,14},{3,11},{7,15},{16,24},{20,... | collective-permute-start | bytes 786440 | tf_op jit(solution)/shard_map/ppermute | solution.py:389
  25.1 2.5 %gates.2 = (bf16[768,2048]{1,0:T(8,128)(2,1)S(1)}, bf16[768,2048]{1,0:T(8,128)(2,1)S(1)}) custom-call(s32[1]{0:T(128)} %bitcast.seq_ref, bf16[2,768,2048]{2,1,0:T(8,128)(2,1)S(1)} %bitcast.32, bf16[2,768,2048]{2,1,0:T(8,128)(2,1)S(1)} %bitcast.30, bf16[2,768,128]{2,1,0:T(8,128)(2,1)S(1)} %get-tuple-element.46.both_ref, ...), custom_call_target="tpu_custom_call" | custom-call | flops 1000000000 | bytes 12000000 | tf_op jit(solution)/shard_map/gates/pallas_call | solution.py:206
  27.7 2.5 %gates.3 = (bf16[768,2048]{1,0:T(8,128)(2,1)S(1)}, bf16[768,2048]{1,0:T(8,128)(2,1)S(1)}) custom-call(s32[1]{0:T(128)S(6)} %sub.16.seq_ref, bf16[2,768,2048]{2,1,0:T(8,128)(2,1)S(1)} %bitcast.32, bf16[2,768,2048]{2,1,0:T(8,128)(2,1)S(1)} %bitcast.30, bf16[2,768,128]{2,1,0:T(8,128)(2,1)S(1)} %get-tuple-element.46.both_ref, ...), custom_call_target="tpu_custom_call" | custom-call | flops 1000000000 | bytes 12000000 | tf_op jit(solution)/shard_map/gates/pallas_call | solution.py:206
  30.2 4.2 %collective-permute-done.8 = bf16[2,64,768]{2,1,0:T(8,128)(2,1)S(1)} collective-permute-done((bf16[2,64,768]{2,1,0:T(8,128)(2,1)S(1)}, bf16[2,64,768]{2,1,0:T(8,128)(2,1)S(1)}, u32[]{:S(2)}, u32[]{:S(2)}) %collective-permute-start.8) | collective-permute-done | bytes 196640 | tf_op jit(solution)/shard_map/ppermute | solution.py:341
  34.5 0.3 left.1.left_ref
  34.8 0.3 fusion.3
  35.1 0.1 collective-permute-start.9
  35.2 2.2 %final.2 = (bf16[768,2048]{1,0:T(8,128)(2,1)S(1)}, f32[8,128]{1,0:T(8,128)S(1)}) custom-call(s32[1]{0:T(128)} %bitcast.seq_ref, bf16[2,768,2048]{2,1,0:T(8,128)(2,1)S(1)} %get-tuple-element.33.weighted_ref, bf16[2,5,64,2048]{3,2,1,0:T(8,128)(2,1)S(1)} %get-tuple-element.36.near_ref, bf16[2,5,64,2048]{3,2,1,0:T(8,128)(2,1)S(1)} %get-tuple-element.40.far_ref, ...), custom_call_target="tpu_custom_call" | custom-call | flops 1000 | bytes 1000 | tf_op jit(solution)/shard_map/final/pallas_call | solution.py:276
  37.5 2.2 %final.3 = (bf16[768,2048]{1,0:T(8,128)(2,1)S(1)}, f32[8,128]{1,0:T(8,128)S(1)}) custom-call(s32[1]{0:T(128)S(6)} %sub.16.seq_ref, bf16[2,768,2048]{2,1,0:T(8,128)(2,1)S(1)} %get-tuple-element.33.weighted_ref, bf16[2,5,64,2048]{3,2,1,0:T(8,128)(2,1)S(1)} %get-tuple-element.36.near_ref, bf16[2,5,64,2048]{3,2,1,0:T(8,128)(2,1)S(1)} %get-tuple-element.40.far_ref, ...), custom_call_target="tpu_custom_call" | custom-call | flops 1000 | bytes 1000 | tf_op jit(solution)/shard_map/final/pallas_call | solution.py:276
  39.7 2.0 %collective-permute-start.12 = (f32[16,128]{1,0:T(8,128)S(1)}, f32[16,128]{1,0:T(8,128)S(1)}, u32[]{:S(2)}, u32[]{:S(2)}) collective-permute-start(f32[16,128]{1,0:T(8,128)S(1)} %constant_dynamic-update-slice_fusion), channel_id=1, source_target_pairs={{0,3},{1,2},{2,1},{3,0},{4,7},{5,6},{6,5},{7,4},{8,11},{9,10},{10,... | collective-permute-start | bytes 24584 | tf_op jit(solution)/shard_map/ppermute | solution.py:341
  41.7 2.5 %collective-permute-start.10 = (f32[16,128]{1,0:T(8,128)S(1)}, f32[16,128]{1,0:T(8,128)S(1)}, u32[]{:S(2)}, u32[]{:S(2)}) collective-permute-start(f32[16,128]{1,0:T(8,128)S(1)} %constant_dynamic-update-slice_fusion), channel_id=1, source_target_pairs={{0,1},{1,0},{2,3},{3,2},{4,5},{5,4},{6,7},{7,6},{8,9},{9,8},{10,11... | collective-permute-start | bytes 24584 | tf_op jit(solution)/shard_map/ppermute | solution.py:341
  44.2 1.1 %collective-permute-done.12 = f32[16,128]{1,0:T(8,128)S(1)} collective-permute-done((f32[16,128]{1,0:T(8,128)S(1)}, f32[16,128]{1,0:T(8,128)S(1)}, u32[]{:S(2)}, u32[]{:S(2)}) %collective-permute-start.12) | collective-permute-done | bytes 8224 | tf_op jit(solution)/shard_map/ppermute | solution.py:341
  45.3 1.0 %collective-permute-done.11 = f32[16,128]{1,0:T(8,128)S(1)} collective-permute-done((f32[16,128]{1,0:T(8,128)S(1)}, f32[16,128]{1,0:T(8,128)S(1)}, u32[]{:S(2)}, u32[]{:S(2)}) %collective-permute-start.11) | collective-permute-done | bytes 8224 | tf_op jit(solution)/shard_map/ppermute | solution.py:341
  46.3 3.1 %normed.1 = bf16[2,768,2048]{2,1,0:T(8,128)(2,1)} custom-call(s32[1]{0:T(128)} %bitcast.seq_ref, f32[16,128]{1,0:T(8,128)S(1)} %add_add_fusion.square_ref, f32[1,2048]{1,0:T(1,128)S(1)} %bitcast.33, bf16[768,2048]{1,0:T(8,128)(2,1)S(1)} %get-tuple-element.59.refs_0_, bf16[768,2048]{1,0:T(8,128)(2,1)S(1)} %get-tuple-element.60.refs_1_), custom_call_target="tpu_custom_call" | custom-call | flops 1000 | bytes 1000 | tf_op jit(solution)/shard_map/normed/pallas_call | solution.py:325
  (38 shorter events, 0.4 us)
Async XLA Ops:
  1.0 15.8 %collective-permute-start.2 = (bf16[2,32,768]{2,1,0:T(8,128)(2,1)S(1)}, bf16[2,32,768]{2,1,0:T(8,128)(2,1)S(1)}, u32[]{:S(2)}, u32[]{:S(2)}) collective-permute-start(bf16[2,32,768]{2,1,0:T(8,128)(2,1)S(1)} %get-tuple-element.34), channel_id=1, source_target_pairs={{0,3},{1,2},{2,1},{3,0},{4,7},{5,6},{6,5},{7,4},{8,11},{9,10},{10,... | collective-permute-start | bytes 294920 | tf_op jit(solution)/shard_map/ppermute | solution.py:341
  6.1 10.7 %collective-permute-start.1 = (bf16[2,32,768]{2,1,0:T(8,128)(2,1)S(1)}, bf16[2,32,768]{2,1,0:T(8,128)(2,1)S(1)}, u32[]{:S(2)}, u32[]{:S(2)}) collective-permute-start(bf16[2,32,768]{2,1,0:T(8,128)(2,1)S(1)} %get-tuple-element.34), channel_id=1, source_target_pairs={{0,2},{1,3},{2,0},{3,1},{4,6},{5,7},{6,4},{7,5},{8,10},{9,11},{10,... | collective-permute-start | bytes 294920 | tf_op jit(solution)/shard_map/ppermute | solution.py:341
  6.1 6.3 %collective-permute-start = (bf16[2,32,768]{2,1,0:T(8,128)(2,1)S(1)}, bf16[2,32,768]{2,1,0:T(8,128)(2,1)S(1)}, u32[]{:S(2)}, u32[]{:S(2)}) collective-permute-start(bf16[2,32,768]{2,1,0:T(8,128)(2,1)S(1)} %get-tuple-element.34), channel_id=1, source_target_pairs={{0,1},{1,0},{2,3},{3,2},{4,5},{5,4},{6,7},{7,6},{8,9},{9,8},{10,11... | collective-permute-start | bytes 294920 | tf_op jit(solution)/shard_map/ppermute | solution.py:341
  6.7 18.4 %slice-start.2 = ((s8[6291456]{0:T(1024)(128)(4,1)}), s8[4194304]{0:T(1024)(128)(4,1)S(1)}, s32[]{:S(2)}) async-start(s8[6291456]{0:T(1024)(128)(4,1)} %bitcast.31), calls=%async_computation.2 | async-start | bytes 8388608
  12.4 12.7 %slice-start.3 = ((s8[6291456]{0:T(1024)(128)(4,1)}), s8[2097152]{0:T(1024)(128)(4,1)S(1)}, s32[]{:S(2)}) async-start(s8[6291456]{0:T(1024)(128)(4,1)} %bitcast.31), calls=%async_computation.3 | async-start | bytes 4194304
  13.9 2.7 %collective-permute-start.3 = (bf16[80,2048]{1,0:T(8,128)(2,1)S(1)}, bf16[80,2048]{1,0:T(8,128)(2,1)S(1)}, u32[]{:S(2)}, u32[]{:S(2)}) collective-permute-start(bf16[80,2048]{1,0:T(8,128)(2,1)S(1)} %maximum_maximum_fusion), channel_id=1, source_target_pairs={{0,4},{4,0},{8,12},{12,8},{1,5},{5,1},{9,13},{13,9},{2,6},{6,2},{1... | collective-permute-start | bytes 983048 | tf_op jit(solution)/shard_map/ppermute | solution.py:393
  14.0 7.9 %collective-permute-start.7 = (bf16[2,32,768]{2,1,0:T(8,128)(2,1)S(1)}, bf16[2,32,768]{2,1,0:T(8,128)(2,1)S(1)}, u32[]{:S(2)}, u32[]{:S(2)}) collective-permute-start(bf16[2,32,768]{2,1,0:T(8,128)(2,1)S(1)} %get-tuple-element.43), channel_id=1, source_target_pairs={{0,1},{1,0},{2,3},{3,2},{4,5},{5,4},{6,7},{7,6},{8,9},{9,8},{10,11... | collective-permute-start | bytes 294920 | tf_op jit(solution)/shard_map/ppermute | solution.py:341
  16.7 8.4 %slice-start = ((s8[6291456]{0:T(1024)(128)(4,1)}), s8[4194304]{0:T(1024)(128)(4,1)S(1)}, s32[]{:S(2)}) async-start(s8[6291456]{0:T(1024)(128)(4,1)} %bitcast.29), calls=%async_computation | async-start | bytes 8388608
  16.8 8.3 %slice-start.1 = ((s8[6291456]{0:T(1024)(128)(4,1)}), s8[2097152]{0:T(1024)(128)(4,1)S(1)}, s32[]{:S(2)}) async-start(s8[6291456]{0:T(1024)(128)(4,1)} %bitcast.29), calls=%async_computation.1 | async-start | bytes 4194304
  16.8 18.0 %collective-permute-start.4 = (bf16[64,2048]{1,0:T(8,128)(2,1)S(1)}, bf16[64,2048]{1,0:T(8,128)(2,1)S(1)}, u32[]{:S(2)}, u32[]{:S(2)}) collective-permute-start(bf16[64,2048]{1,0:T(8,128)(2,1)S(1)} %select_convert_fusion.1), channel_id=1, source_target_pairs={{0,8},{4,12},{1,9},{5,13},{2,10},{6,14},{3,11},{7,15},{16,24},{20,... | collective-permute-start | bytes 786440 | tf_op jit(solution)/shard_map/ppermute | solution.py:389
  21.8 1.6 %collective-permute-start.5 = (bf16[64,2048]{1,0:T(8,128)(2,1)S(1)}, bf16[64,2048]{1,0:T(8,128)(2,1)S(1)}, u32[]{:S(2)}, u32[]{:S(2)}) collective-permute-start(bf16[64,2048]{1,0:T(8,128)(2,1)S(1)} %get-tuple-element.66), channel_id=1, source_target_pairs={{0,4},{4,0},{8,12},{12,8},{1,5},{5,1},{9,13},{13,9},{2,6},{6,2},{1... | collective-permute-start | bytes 786440 | tf_op jit(solution)/shard_map/ppermute | solution.py:412
  21.9 12.5 %collective-permute-start.8 = (bf16[2,64,768]{2,1,0:T(8,128)(2,1)S(1)}, bf16[2,64,768]{2,1,0:T(8,128)(2,1)S(1)}, u32[]{:S(2)}, u32[]{:S(2)}) collective-permute-start(bf16[2,64,768]{2,1,0:T(8,128)(2,1)S(1)} %pad_maximum_fusion.5), channel_id=1, source_target_pairs={{0,2},{1,3},{2,0},{3,1},{4,6},{5,7},{6,4},{7,5},{8,10},{9,11},{10,... | collective-permute-start | bytes 589832 | tf_op jit(solution)/shard_map/ppermute | solution.py:341
  23.6 11.2 %collective-permute-start.6 = (bf16[64,2048]{1,0:T(8,128)(2,1)S(1)}, bf16[64,2048]{1,0:T(8,128)(2,1)S(1)}, u32[]{:S(2)}, u32[]{:S(2)}) collective-permute-start(bf16[64,2048]{1,0:T(8,128)(2,1)S(1)} %select_convert_fusion), channel_id=1, source_target_pairs={{0,8},{4,12},{1,9},{5,13},{2,10},{6,14},{3,11},{7,15},{16,24},{20,... | collective-permute-start | bytes 786440 | tf_op jit(solution)/shard_map/ppermute | solution.py:389
  35.1 2.3 %collective-permute-start.9 = (bf16[128,2048]{1,0:T(8,128)(2,1)S(1)}, bf16[128,2048]{1,0:T(8,128)(2,1)S(1)}, u32[]{:S(2)}, u32[]{:S(2)}) collective-permute-start(bf16[128,2048]{1,0:T(8,128)(2,1)S(1)} %get-tuple-element.61), channel_id=1, source_target_pairs={{0,4},{4,0},{8,12},{12,8},{1,5},{5,1},{9,13},{13,9},{2,6},{6,2},{1... | collective-permute-start | bytes 1572872 | tf_op jit(solution)/shard_map/ppermute | solution.py:432
  37.5 8.8 %copy-start = (f32[2048]{0:T(1024)S(1)}, f32[2048]{0:T(1024)}, u32[]{:S(2)}) copy-start(f32[2048]{0:T(1024)} %param.15) | copy-start | bytes 24580
  39.7 5.5 %collective-permute-start.12 = (f32[16,128]{1,0:T(8,128)S(1)}, f32[16,128]{1,0:T(8,128)S(1)}, u32[]{:S(2)}, u32[]{:S(2)}) collective-permute-start(f32[16,128]{1,0:T(8,128)S(1)} %constant_dynamic-update-slice_fusion), channel_id=1, source_target_pairs={{0,3},{1,2},{2,1},{3,0},{4,7},{5,6},{6,5},{7,4},{8,11},{9,10},{10,... | collective-permute-start | bytes 24584 | tf_op jit(solution)/shard_map/ppermute | solution.py:341
  41.7 4.5 %collective-permute-start.11 = (f32[16,128]{1,0:T(8,128)S(1)}, f32[16,128]{1,0:T(8,128)S(1)}, u32[]{:S(2)}, u32[]{:S(2)}) collective-permute-start(f32[16,128]{1,0:T(8,128)S(1)} %constant_dynamic-update-slice_fusion), channel_id=1, source_target_pairs={{0,2},{1,3},{2,0},{3,1},{4,6},{5,7},{6,4},{7,5},{8,10},{9,11},{10,... | collective-permute-start | bytes 24584 | tf_op jit(solution)/shard_map/ppermute | solution.py:341
  41.7 4.5 %collective-permute-start.10 = (f32[16,128]{1,0:T(8,128)S(1)}, f32[16,128]{1,0:T(8,128)S(1)}, u32[]{:S(2)}, u32[]{:S(2)}) collective-permute-start(f32[16,128]{1,0:T(8,128)S(1)} %constant_dynamic-update-slice_fusion), channel_id=1, source_target_pairs={{0,1},{1,0},{2,3},{3,2},{4,5},{5,4},{6,7},{7,6},{8,9},{9,8},{10,11... | collective-permute-start | bytes 24584 | tf_op jit(solution)/shard_map/ppermute | solution.py:341

commit v15 on v13

--- a/solution.py
+++ b/solution.py
@@ -214,53 +214,67 @@
     )(seq, in_vmem(gate_in), in_vmem(x), in_vmem(both), in_vmem(bands), in_vmem(rows))
 
 
-def left_kernel(b_ref, c_ref, left_ref):
-    seqs, states, length = b_ref.shape
-    row, col = iotas((SPAN, SPAN))
-    for s in range(seqs):
-        for k in range(length // SPAN):
-            rows = slice(k * SPAN, (k + 1) * SPAN)
-            c_t = c_ref[s, :, rows].T
-            affinity = mm(c_t, b_ref[s, :, rows])
-            left_ref[s, rows, :SPAN] = jnp.where(row >= col, affinity, 0.0).astype(BF16)
-            left_ref[s, rows, SPAN:] = c_t
-
-
-def left_of(b, c):
-    seqs, states, length = b.shape
-    return pl.pallas_call(
-        left_kernel,
-        in_specs=[WHOLE] * 2,
-        out_specs=WHOLE,
-        out_shape=pltpu.VMEM((seqs, length, SPAN + states), BF16),
-        compiler_params=PARAMS,
-        cost_estimate=LEFT_COST,
-        name="left",
-    )(b, c)
-
-
-def final_kernel(
-    seq_ref, weighted_ref, near_ref, far_ref, left_ref, rows_ref, lift_ref, skipped_ref,
-    incoming_ref, gated_ref, square_ref,
+def local_kernel(
+    seq_ref, weighted_ref, near_ref, far_ref, lift_ref, skipped_ref, b_ref, c_ref, rows_ref,
+    own_ref, factor_ref, c_t_ref,
 ):
-    length, channels = gated_ref.shape
+    length, channels = own_ref.shape
     blocks = length // SPAN
     s = seq_ref[0]
+    row, col = iotas((SPAN, SPAN))
     for k in range(blocks):
         rows = slice(k * SPAN, (k + 1) * SPAN)
-        left = left_ref[s, rows]
-        squares = jnp.zeros((SPAN, 128), F32)
+        c_t = c_ref[s, :, rows].T
+        c_t_ref[rows] = c_t
+        affinity = mm(c_t, b_ref[s, :, rows])
+        left = jnp.where(row >= col, affinity, 0.0).astype(BF16)
+        if k > 0:
+            left = jnp.concatenate([left, c_t], axis=1)
         at = FIRST * blocks + k
         for lo in range(0, channels, HALF):
             sl = slice(lo, lo + HALF)
-            entering = rows_ref[s, at:at + 1, sl].astype(BF16) * incoming_ref[:, sl]
+            right = weighted_ref[s, rows, sl]
             if k > 0:
-                entering = entering + jnp.concatenate(
-                    [near_ref[s, k - 1, :, sl], far_ref[s, k - 1, :, sl]], axis=0
+                right = jnp.concatenate(
+                    [right, near_ref[s, k - 1, :, sl], far_ref[s, k - 1, :, sl]], axis=0
                 )
-            right = jnp.concatenate([weighted_ref[s, rows, sl], entering], axis=0)
-            mixed = mm(left, right).astype(BF16)
-            gated = lift_ref[rows, sl] * mixed + skipped_ref[rows, sl]
+            lift = lift_ref[rows, sl]
+            own_ref[rows, sl] = lift * mm(left, right).astype(BF16) + skipped_ref[rows, sl]
+            factor_ref[rows, sl] = lift * rows_ref[s, at:at + 1, sl].astype(BF16)
+
+
+def local_terms(seq, weighted, near, far, lift, skipped, b, c, rows):
+    length, channels = lift.shape
+    states = b.shape[1]
+    return pl.pallas_call(
+        local_kernel,
+        in_specs=[pl.BlockSpec(memory_space=pltpu.SMEM)] + [WHOLE] * 8,
+        out_specs=[WHOLE] * 3,
+        out_shape=[
+            pltpu.VMEM(lift.shape, BF16),
+            pltpu.VMEM(lift.shape, BF16),
+            pltpu.VMEM((length, states), BF16),
+        ],
+        compiler_params=PARAMS,
+        cost_estimate=LEFT_COST,
+        name="local_terms",
+    )(
+        seq, in_vmem(weighted), in_vmem(near), in_vmem(far), in_vmem(lift), in_vmem(skipped),
+        b, c, in_vmem(rows),
+    )
+
+
+def joined_kernel(own_ref, factor_ref, c_t_ref, incoming_ref, gated_ref, square_ref):
+    length, channels = own_ref.shape
+    blocks = length // SPAN
+    for k in range(blocks):
+        rows = slice(k * SPAN, (k + 1) * SPAN)
+        c_t = c_t_ref[rows]
+        squares = jnp.zeros((SPAN, 128), F32)
+        for lo in range(0, channels, HALF):
+            sl = slice(lo, lo + HALF)
+            carried = mm(c_t, incoming_ref[:, sl]).astype(BF16)
+            gated = own_ref[rows, sl] + factor_ref[rows, sl] * carried
             gated_ref[rows, sl] = gated
             power = gated * gated
             pair = sum(power[:, half:half + 128] for half in range(0, HALF, 128))
@@ -271,11 +285,11 @@
         square_ref[blocks:] = jnp.zeros((unused, SPAN), F32)
 
 
-def final(seq, weighted, near, far, left, rows, lift, skipped, incoming):
-    length, channels = lift.shape
-    return pl.pallas_call(
-        final_kernel,
-        in_specs=[pl.BlockSpec(memory_space=pltpu.SMEM)] + [WHOLE] * 8,
+def joined(own, factor, c_t, incoming):
+    length, channels = own.shape
+    return pl.pallas_call(
+        joined_kernel,
+        in_specs=[WHOLE] * 4,
         out_specs=[WHOLE] * 2,
         out_shape=[
             pltpu.VMEM((length, channels), BF16),
@@ -283,11 +297,8 @@
         ],
         compiler_params=PARAMS,
         cost_estimate=COST,
-        name="final",
-    )(
-        seq, in_vmem(weighted), in_vmem(near), in_vmem(far), in_vmem(left), in_vmem(rows),
-        in_vmem(lift), in_vmem(skipped), incoming,
-    )
+        name="joined",
+    )(in_vmem(own), in_vmem(factor), in_vmem(c_t), incoming)
 
 
 def norm_kernel(all_channels, seq_ref, square_ref, gain_ref, *refs):
@@ -341,12 +352,6 @@
     return lax.ppermute(shard, axis, [(i, i ^ by) for i in range(lax.axis_size(axis))])
 
 
-def doubled(block, axis, by, behind=()):
-    other = from_partner(block, axis, by)
-    other, _ = lax.optimization_barrier((other, behind))
-    return jnp.concatenate([block, other], axis=1)
-
-
 def from_all(shard, axis):
     return [shard] + [from_partner(shard, axis, by) for by in range(1, lax.axis_size(axis))]
 
@@ -413,16 +418,19 @@
     far_past = past_chip(far_end, far_other, decay_other)
     far_sent, far_got = across(far_past, None, 0)
     c_own, _ = lax.optimization_barrier((c_own, near_ends))
-    c = doubled(c_own, "head", 1, near_sent)
+    c = from_all(c_own, "head")
     both, _ = lax.optimization_barrier((both, far_sent))
     lifts = gates(mine, gate_in, features, both, bands, rows)
-    for by in (1 << i for i in range(1, (lax.axis_size("head") - 1).bit_length())):
-        c = doubled(c, "head", by, lifts)
-    both, c = lax.optimization_barrier((both, c))
+    both, lifts, c = lax.optimization_barrier((both, lifts, c))
     lifts_next = gates(1 - mine, gate_in, features, both, bands, rows)
-    left = left_of(jnp.concatenate([b_near, b_far], axis=1), c)
-    left, lifts_next = lax.optimization_barrier((left, lifts_next))
-    near_got, far_got, left = lax.optimization_barrier((near_got, far_got, left))
+    c, lifts_next = lax.optimization_barrier((c, lifts_next))
+    b = jnp.concatenate([b_near, b_far], axis=1)
+    c = jnp.concatenate(c, axis=1)
+    terms = local_terms(mine, weighted, near, far, *lifts, b, c, rows)
+    terms_next = local_terms(1 - mine, weighted, near, far, *lifts_next, b, c, rows)
+    near_got, far_got, terms, terms_next = lax.optimization_barrier(
+        (near_got, far_got, terms, terms_next)
+    )
     for hop in range(2, devices - 2, 2):
         near_got = near_got + across(near_past, near_got, hop)[1]
         far_got = far_got + across(far_past, far_got, hop)[1]
@@ -434,10 +442,9 @@
         jnp.where(even, end + decay * entered32, entered32).astype(BF16), "ctx", swap
     )
     incoming = jnp.where(even, entered32, end_other + decay_other * entered32).astype(BF16)
-    operands = (weighted, near, far, left, rows)
-    gated, squares = final(mine, *operands, *lifts, incoming)
+    gated, squares = joined(*terms, incoming)
     shared, _ = lax.optimization_barrier((shared, squares))
-    gated_next, squares_next = final(1 - mine, *operands, *lifts_next, shared)
+    gated_next, squares_next = joined(*terms_next, shared)
     squares = sum(from_all(jnp.concatenate([squares, squares_next]), "head"))
     return normed(
         mine, [gated, gated_next], squares, norm_gain[None, :],

time: 49.9 us -> 52.2 us (1.046)
  Pallas kernels: 20.1 us -> 22.1 us
    pallas_call x3 -> x4, Pallas kernels: 4.77 us -> 6.93 us  [the longest x2 3.75 us: local_terms(): pl.pallas_call(local_kernel, in_specs=[pl.BlockSpec(memory_space=pltpu.SM...]
    ppermute x8 -> x9, starting transfers between devices: 13.8 us -> 15.5 us  [from_partner(): lax.ppermute(shard, axis, [(i, i ^ by) for i in range(lax.axis_size(axis))])]
    ppermute x2, starting transfers between devices: 6.81 us -> 5.17 us  [across(): lax.ppermute(sent, 'ctx', [(hop, hop + 2), (hop + 1, hop + 3)])]
    ppermute x8 -> x9, waiting for transfers between devices: 4.65 us -> 4.56 us  [from_partner(): lax.ppermute(shard, axis, [(i, i ^ by) for i in range(lax.axis_size(axis))])]
  transfers between devices with their start and end apart: 13 -> 14, of which waited for: 5 -> 4; matrix products, arithmetic and copies ran while one was open for 2% -> 2% of each run, Pallas kernels for 30% -> 33%
where the time goes in v15:
time: 52.2 us; the launch traced here: 52 us
  Pallas kernels  22.1 us (42%)
  starting transfers between devices  21 us (40%)
  waiting for transfers between devices  6.23 us (12%)
  local copies, waits for them, and re-layouts  1.14 us (2%)
  other arithmetic  1.06 us (2%)
  between operations  0.55 us (1%)
    ppermute x9, starting transfers between devices, from_partner(): lax.ppermute(shard, axis, [(i, i ^ by) for i in range(lax.axis_size(axis))])  15.5 us
    ppermute x2, starting transfers between devices, across(): lax.ppermute(sent, 'ctx', [(hop, hop + 2), (hop + 1, hop + 3)])  5.17 us
    pallas_call x2, Pallas kernels, gates(): pl.pallas_call(gate_kernel, in_specs=[pl.BlockSpec(memory_space=pltpu.SME...  5 us
    pallas_call x1, Pallas kernels, front(): pl.pallas_call(front_kernel, in_specs=[ANYWHERE] * 6, out_specs=[WHOLE] *...  4.59 us
    ppermute x9, waiting for transfers between devices, from_partner(): lax.ppermute(shard, axis, [(i, i ^ by) for i in range(lax.axis_size(axis))])  4.56 us
    pallas_call x2, Pallas kernels, local_terms(): pl.pallas_call(local_kernel, in_specs=[pl.BlockSpec(memory_space=pltpu.SM...  3.75 us
    pallas_call x2, Pallas kernels, joined(): pl.pallas_call(joined_kernel, in_specs=[WHOLE] * 4, out_specs=[WHOLE] * 2...  3.19 us
    pallas_call x1, Pallas kernels, normed(): pl.pallas_call(functools.partial(norm_kernel, all_channels), in_specs=[pl...  3.1 us
  transfers between devices with their start and end apart: 14, of which 4 were waited for; matrix products, arithmetic and copies ran while one was open for 2% of the time, Pallas kernels for 33%

profile of v15, /device:TPU:0, one launch (start us, length us, event | category | flops | bytes accessed | tf_op | source)
XLA Modules:
  0.0 52.0 jit_solution(6383136717004141516)
XLA Ops:
  0.0 1.0 %slice_bitcast_fusion = (bf16[2,32,768]{2,1,0:T(8,128)(2,1)S(1)}, bf16[2,32,768]{2,1,0:T(8,128)(2,1)S(1)}) fusion(bf16[2,2,32,768]{3,2,1,0:T(8,128)(2,1)} %param.11), kind=kLoop, calls=%fused_computation.19 | loop fusion | bytes 393216 | tf_op jit(solution)/shard_map/squeeze | solution.py:372
  1.0 3.1 %collective-permute-start = (bf16[2,32,768]{2,1,0:T(8,128)(2,1)S(1)}, bf16[2,32,768]{2,1,0:T(8,128)(2,1)S(1)}, u32[]{:S(2)}, u32[]{:S(2)}) collective-permute-start(bf16[2,32,768]{2,1,0:T(8,128)(2,1)S(1)} %get-tuple-element.55), channel_id=1, source_target_pairs={{0,1},{1,0},{2,3},{3,2},{4,5},{5,4},{6,7},{7,6},{8,9},{9,8},{10,11... | collective-permute-start | bytes 294920 | tf_op jit(solution)/shard_map/ppermute | solution.py:352
  4.0 2.6 %collective-permute-start.3 = (bf16[2,32,768]{2,1,0:T(8,128)(2,1)S(1)}, bf16[2,32,768]{2,1,0:T(8,128)(2,1)S(1)}, u32[]{:S(2)}, u32[]{:S(2)}) collective-permute-start(bf16[2,32,768]{2,1,0:T(8,128)(2,1)S(1)} %get-tuple-element.55), channel_id=1, source_target_pairs={{0,2},{1,3},{2,0},{3,1},{4,6},{5,7},{6,4},{7,5},{8,10},{9,11},{10,... | collective-permute-start | bytes 294920 | tf_op jit(solution)/shard_map/ppermute | solution.py:352
  6.6 4.6 %front.1 = (bf16[2,768,2048]{2,1,0:T(8,128)(2,1)S(1)}, bf16[2,768,128]{2,1,0:T(8,128)(2,1)S(1)}, f32[2,32,2048]{2,1,0:T(8,128)S(1)}, bf16[192,2048]{1,0:T(8,128)(2,1)S(1)}) custom-call(bf16[2,768,2048]{2,1,0:T(8,128)(2,1)} %x_ref.3, f32[2,32,768]{2,1,0:T(8,128)} %step_hbm.1, f32[2,32,768]{2,1,0:T(8,128)} %decay_hbm.1, f32[1,32]{1,0:T(1,128)} %bitcast.40, ...), custom_call_target="tpu_custom_call" | custom-call | flops 1000 | bytes 1000 | tf_op jit(solution)/shard_map/front/pallas_call | solution.py:127
  11.3 0.1 pad.11.clone
  11.4 1.2 %own_states.2 = (bf16[2,5,64,2048]{3,2,1,0:T(8,128)(2,1)S(1)}, bf16[2,64,2048]{2,1,0:T(8,128)(2,1)S(1)}) custom-call(bf16[2,64,768]{2,1,0:T(8,128)(2,1)S(1)} %pad_maximum_fusion.1.b_ref, bf16[2,768,2048]{2,1,0:T(8,128)(2,1)S(1)} %get-tuple-element.56.weighted_ref, f32[2,32,2048]{2,1,0:T(8,128)S(1)} %get-tuple-element.57.rows_ref), custom_call_target="tpu_custom_call" | custom-call | flops 1000 | bytes 1000 | tf_op jit(solution)/shard_map/own_states/pallas_call | solution.py:173
  12.7 0.1 maximum_maximum_fusion
  12.8 0.1 collective-permute-start.1
  13.0 1.0 %collective-permute-start.7 = (bf16[2,32,768]{2,1,0:T(8,128)(2,1)S(1)}, bf16[2,32,768]{2,1,0:T(8,128)(2,1)S(1)}, u32[]{:S(2)}, u32[]{:S(2)}) collective-permute-start(bf16[2,32,768]{2,1,0:T(8,128)(2,1)S(1)} %get-tuple-element.80), channel_id=1, source_target_pairs={{0,1},{1,0},{2,3},{3,2},{4,5},{5,4},{6,7},{7,6},{8,9},{9,8},{10,11... | collective-permute-start | bytes 294920 | tf_op jit(solution)/shard_map/ppermute | solution.py:352
  13.9 3.5 %collective-permute-start.8 = (bf16[2,32,768]{2,1,0:T(8,128)(2,1)S(1)}, bf16[2,32,768]{2,1,0:T(8,128)(2,1)S(1)}, u32[]{:S(2)}, u32[]{:S(2)}) collective-permute-start(bf16[2,32,768]{2,1,0:T(8,128)(2,1)S(1)} %get-tuple-element.80), channel_id=1, source_target_pairs={{0,2},{1,3},{2,0},{3,1},{4,6},{5,7},{6,4},{7,5},{8,10},{9,11},{10,... | collective-permute-start | bytes 294920 | tf_op jit(solution)/shard_map/ppermute | solution.py:352
  17.4 0.9 %collective-permute-start.9 = (bf16[2,32,768]{2,1,0:T(8,128)(2,1)S(1)}, bf16[2,32,768]{2,1,0:T(8,128)(2,1)S(1)}, u32[]{:S(2)}, u32[]{:S(2)}) collective-permute-start(bf16[2,32,768]{2,1,0:T(8,128)(2,1)S(1)} %get-tuple-element.80), channel_id=1, source_target_pairs={{0,3},{1,2},{2,1},{3,0},{4,7},{5,6},{6,5},{7,4},{8,11},{9,10},{10,... | collective-permute-start | bytes 294920 | tf_op jit(solution)/shard_map/ppermute | solution.py:352
  18.4 0.2 select_convert_fusion.1
  18.6 3.7 %collective-permute-start.2 = (bf16[64,2048]{1,0:T(8,128)(2,1)S(1)}, bf16[64,2048]{1,0:T(8,128)(2,1)S(1)}, u32[]{:S(2)}, u32[]{:S(2)}) collective-permute-start(bf16[64,2048]{1,0:T(8,128)(2,1)S(1)} %select_convert_fusion.1), channel_id=1, source_target_pairs={{0,8},{4,12},{1,9},{5,13},{2,10},{6,14},{3,11},{7,15},{16,24},{20,... | collective-permute-start | bytes 786440 | tf_op jit(solution)/shard_map/ppermute | solution.py:394
  22.3 1.2 %own_states.3 = (bf16[2,5,64,2048]{3,2,1,0:T(8,128)(2,1)S(1)}, bf16[2,64,2048]{2,1,0:T(8,128)(2,1)S(1)}) custom-call(bf16[2,64,768]{2,1,0:T(8,128)(2,1)S(1)} %pad_maximum_fusion.2.b_ref, bf16[2,768,2048]{2,1,0:T(8,128)(2,1)S(1)} %get-tuple-element.56.weighted_ref, f32[2,32,2048]{2,1,0:T(8,128)S(1)} %get-tuple-element.57.rows_ref), custom_call_target="tpu_custom_call" | custom-call | flops 1000 | bytes 1000 | tf_op jit(solution)/shard_map/own_states/pallas_call | solution.py:173
  23.6 0.1 collective-permute-start.5
  23.7 1.5 %collective-permute-done.5 = bf16[64,2048]{1,0:T(8,128)(2,1)S(1)} collective-permute-done((bf16[64,2048]{1,0:T(8,128)(2,1)S(1)}, bf16[64,2048]{1,0:T(8,128)(2,1)S(1)}, u32[]{:S(2)}, u32[]{:S(2)}) %collective-permute-start.5) | collective-permute-done | bytes 262176 | tf_op jit(solution)/shard_map/ppermute | solution.py:416
  25.2 0.2 select_convert_fusion
  25.4 1.5 %collective-permute-start.6 = (bf16[64,2048]{1,0:T(8,128)(2,1)S(1)}, bf16[64,2048]{1,0:T(8,128)(2,1)S(1)}, u32[]{:S(2)}, u32[]{:S(2)}) collective-permute-start(bf16[64,2048]{1,0:T(8,128)(2,1)S(1)} %select_convert_fusion), channel_id=1, source_target_pairs={{0,8},{4,12},{1,9},{5,13},{2,10},{6,14},{3,11},{7,15},{16,24},{20,... | collective-permute-start | bytes 786440 | tf_op jit(solution)/shard_map/ppermute | solution.py:394
  26.9 2.5 %gates.2 = (bf16[768,2048]{1,0:T(8,128)(2,1)S(1)}, bf16[768,2048]{1,0:T(8,128)(2,1)S(1)}) custom-call(s32[1]{0:T(128)} %bitcast.seq_ref, bf16[2,768,2048]{2,1,0:T(8,128)(2,1)S(1)} %bitcast.32, bf16[2,768,2048]{2,1,0:T(8,128)(2,1)S(1)} %bitcast.30, bf16[2,768,128]{2,1,0:T(8,128)(2,1)S(1)} %get-tuple-element.77.both_ref, ...), custom_call_target="tpu_custom_call" | custom-call | flops 1000000000 | bytes 12000000 | tf_op jit(solution)/shard_map/gates/pallas_call | solution.py:206
  29.5 2.5 %gates.3 = (bf16[768,2048]{1,0:T(8,128)(2,1)S(1)}, bf16[768,2048]{1,0:T(8,128)(2,1)S(1)}) custom-call(s32[1]{0:T(128)S(6)} %sub.16.seq_ref, bf16[2,768,2048]{2,1,0:T(8,128)(2,1)S(1)} %bitcast.32, bf16[2,768,2048]{2,1,0:T(8,128)(2,1)S(1)} %bitcast.30, bf16[2,768,128]{2,1,0:T(8,128)(2,1)S(1)} %get-tuple-element.77.both_ref, ...), custom_call_target="tpu_custom_call" | custom-call | flops 1000000000 | bytes 12000000 | tf_op jit(solution)/shard_map/gates/pallas_call | solution.py:206
  32.1 1.9 %local_terms.3 = (bf16[768,2048]{1,0:T(8,128)(2,1)S(1)}, bf16[768,2048]{1,0:T(8,128)(2,1)S(1)}, bf16[768,128]{1,0:T(8,128)(2,1)S(1)}) custom-call(s32[1]{0:T(128)S(6)} %sub.16.seq_ref, bf16[2,768,2048]{2,1,0:T(8,128)(2,1)S(1)} %get-tuple-element.56.weighted_ref, bf16[2,5,64,2048]{3,2,1,0:T(8,128)(2,1)S(1)} %get-tuple-element.62.near_ref, ...), custom_call_target="tpu_custom_call" | custom-call | flops 50000000 | bytes 1600000 | tf_op jit(solution)/shard_map/local_terms/pallas_call | solution.py:249
  34.0 1.9 %local_terms.2 = (bf16[768,2048]{1,0:T(8,128)(2,1)S(1)}, bf16[768,2048]{1,0:T(8,128)(2,1)S(1)}, bf16[768,128]{1,0:T(8,128)(2,1)S(1)}) custom-call(s32[1]{0:T(128)} %bitcast.seq_ref, bf16[2,768,2048]{2,1,0:T(8,128)(2,1)S(1)} %get-tuple-element.56.weighted_ref, bf16[2,5,64,2048]{3,2,1,0:T(8,128)(2,1)S(1)} %get-tuple-element.62.near_ref, ...), custom_call_target="tpu_custom_call" | custom-call | flops 50000000 | bytes 1600000 | tf_op jit(solution)/shard_map/local_terms/pallas_call | solution.py:249
  35.9 0.3 fusion.3
  36.2 0.2 collective-permute-start.10
  36.3 1.6 %joined.2 = (bf16[768,2048]{1,0:T(8,128)(2,1)S(1)}, f32[8,128]{1,0:T(8,128)S(1)}) custom-call(bf16[768,2048]{1,0:T(8,128)(2,1)S(1)} %get-tuple-element.92.own_ref, bf16[768,2048]{1,0:T(8,128)(2,1)S(1)} %get-tuple-element.93.factor_ref, bf16[768,128]{1,0:T(8,128)(2,1)S(1)} %get-tuple-element.94.c_t_ref, bf16[128,2048]{1,0:T(8,128)(2,1)S(1)} %get-tuple-element.106.incoming_ref), custom_call_target="tpu_custom_call" | custom-call | flops 1000 | bytes 1000 | tf_op jit(solution)/shard_map/joined/pallas_call | solution.py:290
  38.0 0.2 collective-permute-done.10.incoming_ref
  38.1 1.6 %joined.3 = (bf16[768,2048]{1,0:T(8,128)(2,1)S(1)}, f32[8,128]{1,0:T(8,128)S(1)}) custom-call(bf16[768,2048]{1,0:T(8,128)(2,1)S(1)} %get-tuple-element.98.own_ref, bf16[768,2048]{1,0:T(8,128)(2,1)S(1)} %get-tuple-element.99.factor_ref, bf16[768,128]{1,0:T(8,128)(2,1)S(1)} %get-tuple-element.100.c_t_ref, ...), custom_call_target="tpu_custom_call" | custom-call | flops 1000 | bytes 1000 | tf_op jit(solution)/shard_map/joined/pallas_call | solution.py:290
  39.8 3.5 %collective-permute-start.12 = (f32[16,128]{1,0:T(8,128)S(1)}, f32[16,128]{1,0:T(8,128)S(1)}, u32[]{:S(2)}, u32[]{:S(2)}) collective-permute-start(f32[16,128]{1,0:T(8,128)S(1)} %constant_dynamic-update-slice_fusion.8), channel_id=1, source_target_pairs={{0,2},{1,3},{2,0},{3,1},{4,6},{5,7},{6,4},{7,5},{8,10},{9,11},{10,... | collective-permute-start | bytes 24584 | tf_op jit(solution)/shard_map/ppermute | solution.py:352
  43.3 0.9 %collective-permute-start.13 = (f32[16,128]{1,0:T(8,128)S(1)}, f32[16,128]{1,0:T(8,128)S(1)}, u32[]{:S(2)}, u32[]{:S(2)}) collective-permute-start(f32[16,128]{1,0:T(8,128)S(1)} %constant_dynamic-update-slice_fusion.8), channel_id=1, source_target_pairs={{0,3},{1,2},{2,1},{3,0},{4,7},{5,6},{6,5},{7,4},{8,11},{9,10},{10,... | collective-permute-start | bytes 24584 | tf_op jit(solution)/shard_map/ppermute | solution.py:352
  44.2 0.7 %collective-permute-done.12 = f32[16,128]{1,0:T(8,128)S(1)} collective-permute-done((f32[16,128]{1,0:T(8,128)S(1)}, f32[16,128]{1,0:T(8,128)S(1)}, u32[]{:S(2)}, u32[]{:S(2)}) %collective-permute-start.12) | collective-permute-done | bytes 8224 | tf_op jit(solution)/shard_map/ppermute | solution.py:352
  44.9 3.8 %collective-permute-done.13 = f32[16,128]{1,0:T(8,128)S(1)} collective-permute-done((f32[16,128]{1,0:T(8,128)S(1)}, f32[16,128]{1,0:T(8,128)S(1)}, u32[]{:S(2)}, u32[]{:S(2)}) %collective-permute-start.13) | collective-permute-done | bytes 8224 | tf_op jit(solution)/shard_map/ppermute | solution.py:352
  48.8 3.1 %normed.1 = bf16[2,768,2048]{2,1,0:T(8,128)(2,1)} custom-call(s32[1]{0:T(128)} %bitcast.seq_ref, f32[16,128]{1,0:T(8,128)S(1)} %add_add_fusion.square_ref, f32[1,2048]{1,0:T(1,128)S(1)} %bitcast.33, bf16[768,2048]{1,0:T(8,128)(2,1)S(1)} %get-tuple-element.103.refs_0_, bf16[768,2048]{1,0:T(8,128)(2,1)S(1)} %get-tuple-element.104.refs_1_), custom_call_target="tpu_custom_call" | custom-call | flops 1000 | bytes 1000 | tf_op jit(solution)/shard_map/normed/pallas_call | solution.py:336
  (45 shorter events, 0.5 us)
Async XLA Ops:
  1.0 10.4 %collective-permute-start = (bf16[2,32,768]{2,1,0:T(8,128)(2,1)S(1)}, bf16[2,32,768]{2,1,0:T(8,128)(2,1)S(1)}, u32[]{:S(2)}, u32[]{:S(2)}) collective-permute-start(bf16[2,32,768]{2,1,0:T(8,128)(2,1)S(1)} %get-tuple-element.55), channel_id=1, source_target_pairs={{0,1},{1,0},{2,3},{3,2},{4,5},{5,4},{6,7},{7,6},{8,9},{9,8},{10,11... | collective-permute-start | bytes 294920 | tf_op jit(solution)/shard_map/ppermute | solution.py:352
  4.0 14.5 %collective-permute-start.3 = (bf16[2,32,768]{2,1,0:T(8,128)(2,1)S(1)}, bf16[2,32,768]{2,1,0:T(8,128)(2,1)S(1)}, u32[]{:S(2)}, u32[]{:S(2)}) collective-permute-start(bf16[2,32,768]{2,1,0:T(8,128)(2,1)S(1)} %get-tuple-element.55), channel_id=1, source_target_pairs={{0,2},{1,3},{2,0},{3,1},{4,6},{5,7},{6,4},{7,5},{8,10},{9,11},{10,... | collective-permute-start | bytes 294920 | tf_op jit(solution)/shard_map/ppermute | solution.py:352
  6.6 11.9 %collective-permute-start.4 = (bf16[2,32,768]{2,1,0:T(8,128)(2,1)S(1)}, bf16[2,32,768]{2,1,0:T(8,128)(2,1)S(1)}, u32[]{:S(2)}, u32[]{:S(2)}) collective-permute-start(bf16[2,32,768]{2,1,0:T(8,128)(2,1)S(1)} %get-tuple-element.55), channel_id=1, source_target_pairs={{0,3},{1,2},{2,1},{3,0},{4,7},{5,6},{6,5},{7,4},{8,11},{9,10},{10,... | collective-permute-start | bytes 294920 | tf_op jit(solution)/shard_map/ppermute | solution.py:352
  6.6 20.2 %slice-start.2 = ((s8[6291456]{0:T(1024)(128)(4,1)}), s8[4194304]{0:T(1024)(128)(4,1)S(1)}, s32[]{:S(2)}) async-start(s8[6291456]{0:T(1024)(128)(4,1)} %bitcast.31), calls=%async_computation.2 | async-start | bytes 8388608
  11.4 15.5 %slice-start.3 = ((s8[6291456]{0:T(1024)(128)(4,1)}), s8[2097152]{0:T(1024)(128)(4,1)S(1)}, s32[]{:S(2)}) async-start(s8[6291456]{0:T(1024)(128)(4,1)} %bitcast.31), calls=%async_computation.3 | async-start | bytes 4194304
  12.8 4.6 %collective-permute-start.1 = (bf16[80,2048]{1,0:T(8,128)(2,1)S(1)}, bf16[80,2048]{1,0:T(8,128)(2,1)S(1)}, u32[]{:S(2)}, u32[]{:S(2)}) collective-permute-start(bf16[80,2048]{1,0:T(8,128)(2,1)S(1)} %maximum_maximum_fusion), channel_id=1, source_target_pairs={{0,4},{4,0},{8,12},{12,8},{1,5},{5,1},{9,13},{13,9},{2,6},{6,2},{1... | collective-permute-start | bytes 983048 | tf_op jit(solution)/shard_map/ppermute | solution.py:398
  13.0 16.5 %collective-permute-start.7 = (bf16[2,32,768]{2,1,0:T(8,128)(2,1)S(1)}, bf16[2,32,768]{2,1,0:T(8,128)(2,1)S(1)}, u32[]{:S(2)}, u32[]{:S(2)}) collective-permute-start(bf16[2,32,768]{2,1,0:T(8,128)(2,1)S(1)} %get-tuple-element.80), channel_id=1, source_target_pairs={{0,1},{1,0},{2,3},{3,2},{4,5},{5,4},{6,7},{7,6},{8,9},{9,8},{10,11... | collective-permute-start | bytes 294920 | tf_op jit(solution)/shard_map/ppermute | solution.py:352
  13.9 15.5 %collective-permute-start.8 = (bf16[2,32,768]{2,1,0:T(8,128)(2,1)S(1)}, bf16[2,32,768]{2,1,0:T(8,128)(2,1)S(1)}, u32[]{:S(2)}, u32[]{:S(2)}) collective-permute-start(bf16[2,32,768]{2,1,0:T(8,128)(2,1)S(1)} %get-tuple-element.80), channel_id=1, source_target_pairs={{0,2},{1,3},{2,0},{3,1},{4,6},{5,7},{6,4},{7,5},{8,10},{9,11},{10,... | collective-permute-start | bytes 294920 | tf_op jit(solution)/shard_map/ppermute | solution.py:352
  17.4 12.0 %collective-permute-start.9 = (bf16[2,32,768]{2,1,0:T(8,128)(2,1)S(1)}, bf16[2,32,768]{2,1,0:T(8,128)(2,1)S(1)}, u32[]{:S(2)}, u32[]{:S(2)}) collective-permute-start(bf16[2,32,768]{2,1,0:T(8,128)(2,1)S(1)} %get-tuple-element.80), channel_id=1, source_target_pairs={{0,3},{1,2},{2,1},{3,0},{4,7},{5,6},{6,5},{7,4},{8,11},{9,10},{10,... | collective-permute-start | bytes 294920 | tf_op jit(solution)/shard_map/ppermute | solution.py:352
  18.4 8.5 %slice-start = ((s8[6291456]{0:T(1024)(128)(4,1)}), s8[4194304]{0:T(1024)(128)(4,1)S(1)}, s32[]{:S(2)}) async-start(s8[6291456]{0:T(1024)(128)(4,1)} %bitcast.29), calls=%async_computation | async-start | bytes 8388608
  18.6 8.3 %slice-start.1 = ((s8[6291456]{0:T(1024)(128)(4,1)}), s8[2097152]{0:T(1024)(128)(4,1)S(1)}, s32[]{:S(2)}) async-start(s8[6291456]{0:T(1024)(128)(4,1)} %bitcast.29), calls=%async_computation.1 | async-start | bytes 4194304
  18.6 17.2 %collective-permute-start.2 = (bf16[64,2048]{1,0:T(8,128)(2,1)S(1)}, bf16[64,2048]{1,0:T(8,128)(2,1)S(1)}, u32[]{:S(2)}, u32[]{:S(2)}) collective-permute-start(bf16[64,2048]{1,0:T(8,128)(2,1)S(1)} %select_convert_fusion.1), channel_id=1, source_target_pairs={{0,8},{4,12},{1,9},{5,13},{2,10},{6,14},{3,11},{7,15},{16,24},{20,... | collective-permute-start | bytes 786440 | tf_op jit(solution)/shard_map/ppermute | solution.py:394
  23.6 1.6 %collective-permute-start.5 = (bf16[64,2048]{1,0:T(8,128)(2,1)S(1)}, bf16[64,2048]{1,0:T(8,128)(2,1)S(1)}, u32[]{:S(2)}, u32[]{:S(2)}) collective-permute-start(bf16[64,2048]{1,0:T(8,128)(2,1)S(1)} %get-tuple-element.110), channel_id=1, source_target_pairs={{0,4},{4,0},{8,12},{12,8},{1,5},{5,1},{9,13},{13,9},{2,6},{6,2},{1... | collective-permute-start | bytes 786440 | tf_op jit(solution)/shard_map/ppermute | solution.py:416
  25.4 10.5 %collective-permute-start.6 = (bf16[64,2048]{1,0:T(8,128)(2,1)S(1)}, bf16[64,2048]{1,0:T(8,128)(2,1)S(1)}, u32[]{:S(2)}, u32[]{:S(2)}) collective-permute-start(bf16[64,2048]{1,0:T(8,128)(2,1)S(1)} %select_convert_fusion), channel_id=1, source_target_pairs={{0,8},{4,12},{1,9},{5,13},{2,10},{6,14},{3,11},{7,15},{16,24},{20,... | collective-permute-start | bytes 786440 | tf_op jit(solution)/shard_map/ppermute | solution.py:394
  36.2 2.0 %collective-permute-start.10 = (bf16[128,2048]{1,0:T(8,128)(2,1)S(1)}, bf16[128,2048]{1,0:T(8,128)(2,1)S(1)}, u32[]{:S(2)}, u32[]{:S(2)}) collective-permute-start(bf16[128,2048]{1,0:T(8,128)(2,1)S(1)} %get-tuple-element.105), channel_id=1, source_target_pairs={{0,4},{4,0},{8,12},{12,8},{1,5},{5,1},{9,13},{13,9},{2,6},{6,2},{1... | collective-permute-start | bytes 1572872 | tf_op jit(solution)/shard_map/ppermute | solution.py:441
  37.9 10.8 %copy-start = (f32[2048]{0:T(1024)S(1)}, f32[2048]{0:T(1024)}, u32[]{:S(2)}) copy-start(f32[2048]{0:T(1024)} %param.15) | copy-start | bytes 24580
  39.8 4.5 %collective-permute-start.11 = (f32[16,128]{1,0:T(8,128)S(1)}, f32[16,128]{1,0:T(8,128)S(1)}, u32[]{:S(2)}, u32[]{:S(2)}) collective-permute-start(f32[16,128]{1,0:T(8,128)S(1)} %constant_dynamic-update-slice_fusion.8), channel_id=1, source_target_pairs={{0,1},{1,0},{2,3},{3,2},{4,5},{5,4},{6,7},{7,6},{8,9},{9,8},{10,11... | collective-permute-start | bytes 24584 | tf_op jit(solution)/shard_map/ppermute | solution.py:352
  39.8 5.1 %collective-permute-start.12 = (f32[16,128]{1,0:T(8,128)S(1)}, f32[16,128]{1,0:T(8,128)S(1)}, u32[]{:S(2)}, u32[]{:S(2)}) collective-permute-start(f32[16,128]{1,0:T(8,128)S(1)} %constant_dynamic-update-slice_fusion.8), channel_id=1, source_target_pairs={{0,2},{1,3},{2,0},{3,1},{4,6},{5,7},{6,4},{7,5},{8,10},{9,11},{10,... | collective-permute-start | bytes 24584 | tf_op jit(solution)/shard_map/ppermute | solution.py:352
  43.3 5.4 %collective-permute-start.13 = (f32[16,128]{1,0:T(8,128)S(1)}, f32[16,128]{1,0:T(8,128)S(1)}, u32[]{:S(2)}, u32[]{:S(2)}) collective-permute-start(f32[16,128]{1,0:T(8,128)S(1)} %constant_dynamic-update-slice_fusion.8), channel_id=1, source_target_pairs={{0,3},{1,2},{2,1},{3,0},{4,7},{5,6},{6,5},{7,4},{8,11},{9,10},{10,... | collective-permute-start | bytes 24584 | tf_op jit(solution)/shard_map/ppermute | solution.py:352
